TPU v7x, 32 devices: a whole 2x2x4 slice. The times are simulated.
32 devices in a mesh: seq: 2 (over x), pos: 16 (over z, y, core).
Axes of the slice: x: 2, y: 2, z: 4, core: 2. Of those that a mesh axis runs over, the one named last changes fastest.
Arguments:
- skip_stream_input: bfloat16 [8, 128, 768], P('seq', 'pos'), may hold values from -6 to 6
- lateral_asking_vectors: bfloat16 [8, 128, 768], P('seq', 'pos'), may hold values from -30 to 30
- lateral_matched_vectors: bfloat16 [8, 128, 768], P('seq', 'pos'), may hold values from -6 to 6
- lateral_carried_vectors: bfloat16 [8, 128, 768], P('seq', 'pos'), may hold values from -6 to 6
- lateral_closing_linear: bfloat16 [768, 768], replicated, may hold values from -0.21875 to 0.21875
- upright_normalizer_multiplier: float32 [768], replicated, may hold values from 0.1 to 1.9
- upright_threefold_linear: bfloat16 [768, 2304], P(None, 'seq'), may hold values from -0.21875 to 0.21875
- upright_closing_linear: bfloat16 [768, 768], replicated, may hold values from -0.21875 to 0.21875
- regression_factors: float32 [12], replicated, may hold values from -192 to 192
- regression_offset: float32 [1], replicated, may hold values from -3 to 3
Outputs:
- alignment_output: bfloat16 [8, 128, 768], P('seq', 'pos')
- pairing_chances: float32 [128, 128], P('pos', 'seq')
All inputs are finite; a program needn't handle non-finite values.
Results may differ from a plain program's by a relative error of at most 0.004.
Values may be sent and summed in bfloat16 or wider, within the bound.
No kernel may reach another device: no remote copies, remote signals or barrier semaphores. Data moves between devices by JAX's collectives and lax.ppermute only.
A program may use at most 64 MiB of HBM per device.

v0:
```python
import math

import jax
import jax.numpy as jnp
from jax import lax
from jax.sharding import PartitionSpec as P


def layer_norm(values, scaling):
    average = jnp.mean(values, axis=-1, keepdims=True)
    centered = values - average
    spread = jnp.mean(centered * centered, axis=-1, keepdims=True)
    return centered * lax.rsqrt(spread + 1e-05) * scaling


def column_attend(query_part, key_part, value_part, factor):
    scores = (
        jnp.einsum("sphd,tphd->phst", query_part, key_part, preferred_element_type=jnp.float32)
        * factor
    )
    exponent = jnp.exp(scores)
    col_weights = (exponent / jnp.sum(exponent, axis=-1, keepdims=True)).astype(jnp.bfloat16)
    return jnp.einsum(
        "phst,tphd->sphd", col_weights, value_part, preferred_element_type=jnp.float32
    ).astype(jnp.bfloat16)


def per_device(
    skip_stream_input,
    lateral_asking_vectors,
    lateral_matched_vectors,
    lateral_carried_vectors,
    lateral_closing_linear,
    upright_normalizer_multiplier,
    upright_threefold_linear,
    upright_closing_linear,
    regression_factors,
    regression_offset,
):
    upper_limit = lax.Precision.HIGHEST
    local_homolog_number, local_site_number, embedding_breadth = lateral_asking_vectors.shape
    focus_group_tally = regression_factors.shape[0]
    head_size = embedding_breadth // focus_group_tally
    seq_count = lax.axis_size("seq")
    pos_count = lax.axis_size("pos")
    total_len = local_site_number * pos_count
    queries = lateral_asking_vectors.reshape(
        local_homolog_number, local_site_number, focus_group_tally, head_size
    )
    shard_rows = lax.all_gather(lateral_matched_vectors, "pos", axis=1, tiled=True)
    key_part = shard_rows.reshape(
        local_homolog_number, shard_rows.shape[1], focus_group_tally, head_size
    )
    partial_value = jnp.einsum(
        "rihd,rjhd->hij", queries, key_part, preferred_element_type=jnp.float32
    )
    factor = 1.0 / (math.sqrt(head_size) * math.sqrt(local_homolog_number * seq_count))
    logits = lax.psum(partial_value, "seq") * factor
    row_peak = jnp.max(logits, axis=2, keepdims=True)
    exponent = jnp.exp(logits - row_peak)
    affinity_shares = (exponent / jnp.sum(exponent, axis=2, keepdims=True)).astype(jnp.bfloat16)
    shard_rows = lax.all_gather(lateral_carried_vectors, "pos", axis=1, tiled=True)
    row_count = shard_rows.shape[1]
    value_part = shard_rows.reshape(local_homolog_number, row_count, focus_group_tally, head_size)
    mixture = jnp.einsum(
        "hij,rjhd->rihd", affinity_shares, value_part, preferred_element_type=jnp.float32
    )
    horizontal_mixed_result = mixture.astype(jnp.bfloat16).reshape(
        local_homolog_number * local_site_number, embedding_breadth
    )
    residue_embedding = skip_stream_input.reshape(
        local_homolog_number * local_site_number, embedding_breadth
    ).astype(jnp.float32) + jnp.dot(
        horizontal_mixed_result, lateral_closing_linear, preferred_element_type=jnp.float32
    )
    normed = layer_norm(residue_embedding, upright_normalizer_multiplier).astype(jnp.bfloat16)
    full_projection = lax.all_gather(upright_threefold_linear, "seq", axis=1, tiled=True)
    col_factor = 1.0 / math.sqrt(head_size)
    all_seqs = local_homolog_number * seq_count
    projected = jnp.dot(normed, full_projection, preferred_element_type=jnp.float32).astype(
        jnp.bfloat16
    )
    projected = projected.reshape(local_homolog_number, local_site_number, 3 * embedding_breadth)
    col_query = projected[:, :, :embedding_breadth].reshape(
        local_homolog_number, local_site_number, focus_group_tally, head_size
    )
    key_value = projected[:, :, embedding_breadth:]
    all_key_value = lax.all_gather(key_value, "seq", axis=0, tiled=True)
    all_key_value = all_key_value.reshape(
        all_seqs, local_site_number, 2, focus_group_tally, head_size
    )
    attended = column_attend(col_query, all_key_value[:, :, 0], all_key_value[:, :, 1], col_factor)
    column_mixing = attended.reshape(local_homolog_number * local_site_number, embedding_breadth)
    alignment_output = (
        residue_embedding
        + jnp.dot(column_mixing, upright_closing_linear, preferred_element_type=jnp.float32)
    ).astype(jnp.bfloat16)
    alignment_output = alignment_output.reshape(
        local_homolog_number, local_site_number, embedding_breadth
    )
    pos_index = lax.axis_index("pos")
    seq_index = lax.axis_index("seq")
    row_begin = pos_index * local_site_number
    col_part = jnp.sum(affinity_shares, axis=1, dtype=jnp.float32)
    row_part = jnp.sum(affinity_shares, axis=2, dtype=jnp.float32)
    own_cols = lax.dynamic_slice_in_dim(col_part, row_begin, local_site_number, 1)
    local_sums = lax.dynamic_update_slice_in_dim(col_part, own_cols + row_part, row_begin, 1)
    couple_amount = lax.psum(local_sums, "pos")
    focus_group_amount = jnp.sum(couple_amount, axis=1)
    combined_groups = jnp.einsum(
        "f,feg->eg", regression_factors, affinity_shares.astype(jnp.float32), precision=upper_limit
    )
    mirrored = lax.all_to_all(combined_groups, "pos", split_axis=1, concat_axis=0, tiled=True)
    slab_width = total_len // seq_count
    slab_begin = seq_index * slab_width
    resident_block = lax.dynamic_slice_in_dim(combined_groups, slab_begin, slab_width, 1)
    transposed_share = jnp.transpose(lax.dynamic_slice_in_dim(mirrored, slab_begin, slab_width, 0))
    row_factors = lax.dynamic_slice_in_dim(couple_amount, row_begin, local_site_number, 1)
    col_factors = lax.dynamic_slice_in_dim(couple_amount, slab_begin, slab_width, 1)
    product_adjuster = jnp.einsum(
        "q,qz,qd->zd",
        regression_factors / focus_group_amount,
        row_factors,
        col_factors,
        precision=upper_limit,
    )
    pairing_chances = jax.nn.sigmoid(
        resident_block + transposed_share - product_adjuster + regression_offset[0]
    )
    return (alignment_output, pairing_chances)


def solution(mesh):
    placed = (
        P("seq", "pos", None),
        P("seq", "pos", None),
        P("seq", "pos", None),
        P("seq", "pos", None),
        P(),
        P(),
        P(None, "seq"),
        P(),
        P(),
        P(),
    )
    return jax.shard_map(
        per_device,
        mesh=mesh,
        in_specs=placed,
        out_specs=(P("seq", "pos", None), P("pos", "seq")),
        check_vma=False,
    )
```

profile of v0, /device:TPU:0, one launch (start us, length us, event | category | flops | bytes accessed | tf_op | source)
XLA Modules:
  0.0 127.7 jit_solution(10048367500120693676)
XLA Ops:
  7.2 0.0 copy-start
  7.2 0.0 copy-start.3
  7.2 0.0 all-gather.2.cloned.1.call-start
  7.2 0.7 all-gather.2.cloned.1.call-update
  7.9 0.1 copy-done.3
  8.1 0.0 copy-start.5
  8.1 25.5 %all_gather.12 = bf16[4,128,768]{2,0,1:T(4,128)(2,1)S(1)} all-gather(bf16[4,8,768]{2,0,1:T(4,128)(2,1)S(1)} %copy.39), channel_id=1, replica_groups=mesh['seq'=2,'pos'=16] {'pos'}, dimensions={1}, use_global_device_ids=true | all-gather | bytes 835584 | tf_op jit(solution)/shard_map/all_gather | solution.py:50
  33.6 0.7 copy.40
  34.2 0.0 copy-done.5
  34.3 0.0 copy-start.4
  34.3 0.1 reshape.53
  34.4 0.3 convolution_bitcast_fusion
  34.7 9.7 %psum.14 = f32[12,8,128]{2,1,0:T(8,128)S(1)} all-reduce(f32[12,8,128]{2,1,0:T(8,128)S(1)} %convolution_bitcast_fusion), channel_id=1, replica_groups=mesh['seq'=2,'pos'=16] {'seq'}, use_global_device_ids=true, to_apply=%region_0.0 | all-reduce | flops 12288 | bytes 98304 | tf_op jit(solution)/shard_map/psum | solution.py:58
  44.3 1.9 %fusion.37 = (f32[12,8]{1,0:T(8,128)S(1)}, f32[12,8,128]{2,1,0:T(8,128)S(1)}) fusion(f32[12,8,128]{2,1,0:T(8,128)S(1)} %psum.14), kind=kOutput, calls=%fused_computation.58 | output fusion | flops 36991 | bytes 98688 | tf_op jit(solution)/shard_map/sub | solution.py:60
  46.3 0.2 convert_reduce_fusion
  46.5 0.0 copy-done.7
  46.5 0.1 fusion.24
  46.6 0.1 all_to_all.14
  46.7 0.6 copy.51
  47.4 3.5 %all-to-all-start = ((f32[8,16,8]{2,0,1:T(8,128)}), f32[8,16,8]{2,0,1:T(8,128)S(1)}, u32[]{:S(2)}, u32[]{:S(2)}) async-start(f32[8,16,8]{2,0,1:T(8,128)} %copy.51), calls=%async_computation | async-start | bytes 131072 | tf_op jit(solution)/shard_map/all_to_all | solution.py:113
  50.9 0.0 copy-done.4
  50.9 24.0 %all_gather.13 = bf16[4,128,768]{2,0,1:T(4,128)(2,1)S(1)} all-gather(bf16[4,8,768]{2,0,1:T(4,128)(2,1)S(1)} %copy.43), channel_id=1, replica_groups=mesh['seq'=2,'pos'=16] {'pos'}, dimensions={1}, use_global_device_ids=true | all-gather | bytes 835584 | tf_op jit(solution)/shard_map/all_gather | solution.py:62
  74.9 0.7 copy.44
  75.6 0.7 fusion.4
  76.3 0.1 copy.46
  76.4 0.1 reshape.56
  76.5 0.0 copy-done
  76.5 0.0 copy-done.2
  76.5 0.4 fusion.38
  77.0 0.2 multiply_reduce_fusion
  77.2 0.1 dynamic-slice_add_fusion
  77.2 0.2 dynamic_update_slice.3
  77.4 30.4 %psum.15 = f32[12,128]{1,0:T(8,128)S(1)} all-reduce(f32[12,128]{1,0:T(8,128)S(1)} %dynamic_update_slice.3), channel_id=1, replica_groups=mesh['seq'=2,'pos'=16] {'pos'}, use_global_device_ids=true, to_apply=%region_8.0 | all-reduce | flops 1536 | bytes 12288 | tf_op jit(solution)/shard_map/psum | solution.py:108
  107.8 0.1 reduce_sum.69
  108.6 0.0 all-to-all-done
  108.6 0.1 copy.60
  108.7 0.9 fusion.13
  109.6 0.0 copy-done.6
  109.6 2.8 %fusion.1 = bf16[4,8,2304]{2,1,0:T(8,128)(2,1)S(1)} fusion(bf16[768,2304]{1,0:T(8,128)(2,1)} %all-gather.2.cloned.1.call-done, f32[32,768]{1,0:T(8,128)S(1)} %get-tuple-element.10, f32[768]{0:T(1024)S(1)} %copy-done.6, f32[32]{0:T(128)S(1)} %add_rsqrt_fusion, f32[32]{0:T(128)S(1)} %broadcast_multiply_fusion), kind=kOutput, calls=%fused_computation.2 | convolution fusion | flops 113418240 | bytes 3788032 | tf_op jit(solution)/shard_map/dot_general | solution.py:80
  112.4 5.3 %all_gather.15 = bf16[8,8,1536]{2,1,0:T(8,128)(2,1)S(1)} all-gather(bf16[4,8,1536]{2,1,0:T(8,128)(2,1)S(1)} %slice.16), channel_id=1, replica_groups=mesh['seq'=2,'pos'=16] {'seq'}, dimensions={0}, use_global_device_ids=true | all-gather | bytes 294912 | tf_op jit(solution)/shard_map/all_gather | solution.py:88
  117.7 0.4 reshape.58
  118.2 0.1 reshape.59
  118.3 0.3 fusion.2
  118.6 0.0 copy-start.1
  118.6 0.3 fusion.3
  119.0 0.1 reshape.60
  119.1 0.8 copy-done.1
  119.9 0.9 fusion.7
  (14 shorter events, 0.2 us)
Async XLA Ops:
  7.2 69.3 %copy-start = (bf16[768,768]{1,0:T(8,128)(2,1)S(1)}, bf16[768,768]{1,0:T(8,128)(2,1)}, u32[]{:S(2)}) copy-start(bf16[768,768]{1,0:T(8,128)(2,1)} %param.14) | copy-start | bytes 3538948
  7.2 0.9 copy-start.3
  7.2 102.4 %all-gather.2.cloned.1.call-start = ((), (), s32[]{:S(2)}) async-start(), calls=%async_computation.1 | async-start | bytes 5308416 | tf_op jit(solution)/shard_map/all_gather | solution.py:77
  8.1 26.1 %copy-start.5 = (bf16[4,8,768]{2,1,0:T(8,128)(2,1)S(1)}, bf16[4,8,768]{2,1,0:T(8,128)(2,1)}, u32[]{:S(2)}) copy-start(bf16[4,8,768]{2,1,0:T(8,128)(2,1)} %param.11) | copy-start | bytes 147460
  33.6 12.9 %copy-start.7 = (f32[12]{0:T(128)S(1)}, f32[12]{0:T(128)}, u32[]{:S(2)}) copy-start(f32[12]{0:T(128)} %param.18) | copy-start | bytes 148
  34.3 16.6 %copy-start.4 = (bf16[4,8,768]{2,1,0:T(8,128)(2,1)S(1)}, bf16[4,8,768]{2,1,0:T(8,128)(2,1)}, u32[]{:S(2)}) copy-start(bf16[4,8,768]{2,1,0:T(8,128)(2,1)} %param.13) | copy-start | bytes 147460
  47.4 61.2 %all-to-all-start = ((f32[8,16,8]{2,0,1:T(8,128)}), f32[8,16,8]{2,0,1:T(8,128)S(1)}, u32[]{:S(2)}, u32[]{:S(2)}) async-start(f32[8,16,8]{2,0,1:T(8,128)} %copy.51), calls=%async_computation | async-start | bytes 131072 | tf_op jit(solution)/shard_map/all_to_all | solution.py:113
  74.9 1.6 %copy-start.2 = (bf16[4,8,768]{2,1,0:T(8,128)(2,1)S(1)}, bf16[4,8,768]{2,1,0:T(8,128)(2,1)}, u32[]{:S(2)}) copy-start(bf16[4,8,768]{2,1,0:T(8,128)(2,1)} %param.10) | copy-start | bytes 147460
  76.3 33.3 %copy-start.6 = (f32[768]{0:T(1024)S(1)}, f32[768]{0:T(1024)}, u32[]{:S(2)}) copy-start(f32[768]{0:T(1024)} %param.15) | copy-start | bytes 9220
  118.6 1.3 copy-start.1
Sparse Core Ops, SparseCore 0:
  9.6 53.1 all-gather.1
where the time goes:
time: 128 us
  blocking collectives  94.8 us (74%)
  between operations  15 us (12%)
  matrix products  6.76 us (5%)
  local copies, waits for them, and re-layouts  4.39 us (3%)
  starting transfers between devices  3.54 us (3%)
  other arithmetic  2.54 us (2%)
    psum x1, blocking collectives, per_device(): couple_amount = lax.psum(local_sums, 'pos')  30.4 us
    all_gather x1, blocking collectives, per_device(): lax.all_gather(lateral_matched_vectors, 'pos', axis=1, tiled=True)  25.5 us
    all_gather x1, blocking collectives, per_device(): lax.all_gather(lateral_carried_vectors, 'pos', axis=1, tiled=True)  24 us
    psum x1, blocking collectives, per_device(): logits = lax.psum(partial_value, 'seq') * factor  9.67 us
    all_gather x1, blocking collectives, per_device(): all_key_value = lax.all_gather(key_value, 'seq', axis=0, tiled=True)  5.29 us
    all_to_all x1, starting transfers between devices, per_device(): lax.all_to_all(combined_groups, 'pos', split_axis=1, concat_axis=0, tiled...  3.5 us
    dot_general x1, matrix products, per_device(): jnp.dot(normed, full_projection, preferred_element_type=jnp.float32)  2.77 us
  transfers between devices with their start and end apart: 2, of which 0 were waited for; matrix products, arithmetic and copies ran while one was open for 6% of the time, Pallas kernels for 0%

commit v1 on v0

v1 whole, which is shorter than its diff:
```python
import functools
import math

import jax
import jax.numpy as jnp
from jax import lax
from jax.experimental import pallas as pl
from jax.experimental.pallas import tpu as pltpu
from jax.sharding import PartitionSpec as P

F32 = jnp.float32
BF16 = jnp.bfloat16
HIGHEST = lax.Precision.HIGHEST
LANE_BLOCK = 256


def dot_nn(a, b, precision=None):
    return lax.dot_general(
        a, b, (((1,), (0,)), ((), ())), precision=precision, preferred_element_type=F32
    )


def dot_nt(a, b, precision=None):
    return lax.dot_general(
        a, b, (((1,), (1,)), ((), ())), precision=precision, preferred_element_type=F32
    )


def round_up(n, m):
    return -(-n // m) * m


def lane_block(embed, head):
    return LANE_BLOCK if embed % LANE_BLOCK == 0 and LANE_BLOCK % head == 0 else head


def logits_kernel(head, part_count, *refs):
    q_ref, k_refs, out_ref = refs[0], refs[1 : 1 + part_count], refs[-1]
    rows, sites, embed = q_ref.shape
    width = lane_block(embed, head)
    group = width // head
    lane_head = lax.broadcasted_iota(jnp.int32, (group * sites, width), 1) // head
    row_head = lax.broadcasted_iota(jnp.int32, (group * sites, width), 0) // sites
    own_head = lane_head == row_head
    for block in range(embed // width):
        cols = slice(block * width, (block + 1) * width)
        total = None
        for r in range(rows):
            q = q_ref[r, :, cols].astype(F32)
            q = jnp.where(own_head, jnp.concatenate([q] * group, axis=0), 0.0).astype(BF16)
            keys = jnp.concatenate([k[r, :, cols] for k in k_refs], axis=0)
            term = dot_nt(q, keys)
            total = term if total is None else total + term
        out_ref[block * group * sites : (block + 1) * group * sites, :] = total


def softmax_kernel(factor, heads, part_count, *refs):
    parts, (factor_ref, order_ref, w_ref, pair_ref, held) = refs[:part_count], refs[part_count:]
    rows, length = w_ref.shape
    sites = rows // heads
    logits = parts[0][...]
    for part in parts[1:]:
        logits = logits + part[...]
    logits = logits * factor
    exponent = jnp.exp(logits - jnp.max(logits, axis=1, keepdims=True))
    shares = (exponent / jnp.sum(exponent, axis=1, keepdims=True)).astype(BF16)
    w_ref[...] = shares
    shares = shares.astype(F32)
    row_sum = jnp.sum(shares, axis=1, keepdims=True)
    lane = lax.broadcasted_iota(jnp.int32, (rows, length), 1)
    row = lax.broadcasted_iota(jnp.int32, (rows, length), 0) % sites
    both = (shares + jnp.where(lane == row, row_sum, 0.0)).reshape(heads, sites, length)
    head_rows = round_up(heads, 8)
    held[...] = jnp.zeros_like(held)
    held[0:heads, :] = jnp.sum(both, axis=1)
    merged = shares[0:sites, :] * factor_ref[0]
    for h in range(1, heads):
        merged = merged + shares[h * sites : (h + 1) * sites, :] * factor_ref[h]
    held[head_rows : head_rows + sites, :] = merged
    pair_ref[...] = dot_nn(held[...], order_ref[...], HIGHEST)


def mix_kernel(head, split, v_count, w_count, *refs):
    scalar_ref, w_ref = refs[:2]
    v_refs = refs[2 : 2 + v_count]
    closing_ref, skip_ref, gain_ref = refs[2 + v_count : 5 + v_count]
    weight_refs = refs[5 + v_count : 5 + v_count + w_count]
    hidden_ref, query_ref, kv_ref, mixed, normed, projected = refs[5 + v_count + w_count :]
    rows, sites, embed = skip_ref.shape
    width = lane_block(embed, head)
    group = width // head
    lane_head = lax.broadcasted_iota(jnp.int32, (sites, width), 1) // head
    for block in range(embed // width):
        cols = slice(block * width, (block + 1) * width)
        shares = w_ref[block * group * sites : (block + 1) * group * sites, :]
        for r in range(rows):
            values = jnp.concatenate([v[r, :, cols] for v in v_refs], axis=0)
            product = dot_nn(shares, values)
            own = product[0:sites, :]
            for g in range(1, group):
                own = jnp.where(lane_head == g, product[g * sites : (g + 1) * sites, :], own)
            mixed[r * sites : (r + 1) * sites, cols] = own
    hidden = skip_ref[...].astype(F32).reshape(rows * sites, embed) + dot_nn(
        mixed[...].astype(BF16), closing_ref[...]
    )
    hidden_ref[...] = hidden
    centered = hidden - jnp.mean(hidden, axis=1, keepdims=True)
    spread = jnp.mean(centered * centered, axis=1, keepdims=True)
    unit = (centered * lax.rsqrt(spread + 1e-05) * gain_ref[...]).astype(BF16)
    if split:
        own_ref, first_ref, second_ref = weight_refs
        columns, half = own_ref.shape[1], first_ref.shape[0]
        normed[...] = unit
        own_at = pl.multiple_of(scalar_ref[0] * columns, 128)
        other_at = pl.multiple_of((1 - scalar_ref[0]) * columns, 128)
        first = normed[:, pl.ds(pl.multiple_of(scalar_ref[1] * half, 128), half)]
        second = normed[:, pl.ds(pl.multiple_of((1 - scalar_ref[1]) * half, 128), half)]
        projected[:, pl.ds(own_at, columns)] = dot_nn(unit, own_ref[...]).astype(BF16)
        projected[:, pl.ds(other_at, columns)] = (
            dot_nn(first, first_ref[...]) + dot_nn(second, second_ref[...])
        ).astype(BF16)
    else:
        projected[...] = dot_nn(unit, weight_refs[0][...]).astype(BF16)
    query_ref[...] = projected[:, 0:embed]
    kv_ref[...] = projected[:, embed:]


def column_kernel(head, factor, part_count, *refs):
    q_ref, kv_refs = refs[0], refs[1 : 1 + part_count]
    hidden_ref, closing_ref, out_ref, products, mixed = refs[1 + part_count :]
    rows, sites, embed = out_ref.shape
    heads = embed // head
    padded = round_up(heads, 128)
    pick = (
        lax.broadcasted_iota(jnp.int32, (embed, padded), 0) // head
        == lax.broadcasted_iota(jnp.int32, (embed, padded), 1)
    ).astype(BF16)
    spread = (
        lax.broadcasted_iota(jnp.int32, (padded, embed), 1) // head
        == lax.broadcasted_iota(jnp.int32, (padded, embed), 0)
    ).astype(BF16)
    query = q_ref[...].astype(F32)
    key_values = [kv[...].astype(F32) for kv in kv_refs]
    keys, values = [], []
    for kv in key_values:
        for t in range(kv.shape[0] // sites):
            keys.append(kv[t * sites : (t + 1) * sites, 0:embed])
            values.append(kv[t * sites : (t + 1) * sites, embed:])
    seqs = len(keys)
    for s in range(rows):
        for t in range(seqs):
            at = (s * seqs + t) * sites
            products[at : at + sites, :] = query[s * sites : (s + 1) * sites, :] * keys[t]
    product = products[...]
    high = product.astype(BF16)
    low = (product - high.astype(F32)).astype(BF16)
    scores = (dot_nn(high, pick) + dot_nn(low, pick)) * factor
    exponent = jnp.exp(scores).reshape(rows, seqs, sites, padded)
    shares = (exponent / jnp.sum(exponent, axis=1, keepdims=True)).astype(BF16)
    wide = dot_nn(shares.reshape(rows * seqs * sites, padded), spread)
    for s in range(rows):
        total = None
        for t in range(seqs):
            at = (s * seqs + t) * sites
            term = wide[at : at + sites, :] * values[t]
            total = term if total is None else total + term
        mixed[s * sites : (s + 1) * sites, :] = total
    out = hidden_ref[...] + dot_nn(mixed[...].astype(BF16), closing_ref[...])
    out_ref[...] = out.reshape(rows, sites, embed).astype(BF16)


def contact_kernel(heads, sites, part_count, *refs):
    parts = refs[:part_count]
    factor_ref, offset_ref, own_ref, slab_ref, arrival_ref, out_ref, held, table = refs[part_count:]
    head_rows = round_up(heads, 8)
    step = head_rows + sites
    total, block = None, 0
    for part in parts:
        for at in range(0, part.shape[0], step):
            sums = part[at : at + head_rows, :]
            total = sums if total is None else total + sums
            table[block * sites : (block + 1) * sites, :] = part[at + head_rows : at + step, :]
            block += 1
    amount = jnp.sum(total, axis=1, keepdims=True)
    real = lax.broadcasted_iota(jnp.int32, (head_rows, 1), 0) < heads
    share = jnp.where(real, factor_ref[:, 0:1] / jnp.where(real, amount, 1.0), 0.0)
    held[0:head_rows, :] = total
    held[head_rows:step, :] = table[0:sites, :]
    slab = dot_nn(held[...], slab_ref[...], HIGHEST)
    own = dot_nt(own_ref[...], total * share, HIGHEST)
    mirrored = dot_nn(dot_nt(own_ref[...], table[...], HIGHEST), arrival_ref[...], HIGHEST)
    adjuster = dot_nn(own, slab[0:head_rows, :], HIGHEST)
    out_ref[...] = jax.nn.sigmoid(
        slab[head_rows:step, :] + mirrored - adjuster + offset_ref[0]
    )


def call(kernel, out_shape, operands, smem=(), scratch=(), flops=1000000, bytes_accessed=1000000):
    vmem = pl.BlockSpec(memory_space=pltpu.VMEM)
    specs = [
        pl.BlockSpec(memory_space=pltpu.SMEM) if i in smem else vmem for i in range(len(operands))
    ]
    return pl.pallas_call(
        kernel,
        out_shape=out_shape,
        in_specs=specs,
        out_specs=jax.tree.map(lambda _: vmem, out_shape),
        scratch_shapes=list(scratch),
        compiler_params=pltpu.CompilerParams(vmem_limit_bytes=24 * 1024 * 1024),
        cost_estimate=pl.CostEstimate(
            flops=flops, bytes_accessed=bytes_accessed, transcendentals=0
        ),
    )(*operands)


def stages_of(count):
    stages, stride = [], 1
    while count > 1 and len(stages) < 2 and count % 2 == 0:
        stages.append((stride, 2))
        stride, count = stride * 2, count // 2
    if count > 1:
        stages.append((stride, count))
    return stages[::-1]


def staged_gather(array, axis, count):
    parts = [array]
    for at, (stride, size) in enumerate(stages_of(count)):
        array = parts[0] if len(parts) == 1 else jnp.concatenate(parts, axis=axis)
        parts = [array]
        for delta in range(1, size):
            pairs = []
            for p in range(count):
                a = (p // stride) % size
                pairs.append((p, p + ((a + delta) % size - a) * stride))
            parts.append(lax.ppermute(array, "pos", pairs))
    return parts


def arrival_order(index, count):
    sources = [index]
    for stride, size in stages_of(count):
        grown = []
        for delta in range(size):
            for source in sources:
                a = (source // stride) % size
                grown.append(source + ((a - delta) % size - a) * stride)
        sources = grown
    return jnp.stack(sources)


def per_device(
    skip_stream_input,
    lateral_asking_vectors,
    lateral_matched_vectors,
    lateral_carried_vectors,
    lateral_closing_linear,
    upright_normalizer_multiplier,
    upright_threefold_linear,
    upright_closing_linear,
    regression_factors,
    regression_offset,
):
    rows, sites, embed = lateral_asking_vectors.shape
    heads = regression_factors.shape[0]
    head = embed // heads
    seq_count = lax.axis_size("seq")
    pos_count = lax.axis_size("pos")
    length = sites * pos_count
    slab_width = length // seq_count
    pos_index = lax.axis_index("pos").astype(jnp.int32)
    seq_index = lax.axis_index("seq").astype(jnp.int32)
    swap = [(s, 1 - s) for s in range(2)]
    embed_in, columns = upright_threefold_linear.shape
    split = seq_count == 2 and pos_count % 2 == 0 and columns % 128 == 0 and embed_in % 256 == 0

    key_parts = staged_gather(lateral_matched_vectors, 1, pos_count)
    value_parts = staged_gather(lateral_carried_vectors, 1, pos_count)

    origin = arrival_order(pos_index, pos_count)
    place = (origin[:, None] * sites + jnp.arange(sites, dtype=jnp.int32)[None, :]).reshape(length)
    every = jnp.arange(length, dtype=jnp.int32)
    slab_at = seq_index * slab_width + jnp.arange(slab_width, dtype=jnp.int32)
    order = (place[:, None] == every[None, :]).astype(F32)
    own_rows = pos_index * sites + jnp.arange(sites, dtype=jnp.int32)
    own_select = (own_rows[:, None] == every[None, :]).astype(F32)
    slab_select = (every[:, None] == slab_at[None, :]).astype(F32)
    arrival_select = (place[:, None] == slab_at[None, :]).astype(F32)
    scalars = jnp.stack([seq_index, pos_index % 2])

    if split:
        half = embed_in // 2
        sent = lax.dynamic_slice_in_dim(
            upright_threefold_linear, (pos_index % 2) * half, half, 0
        )
        first = lax.ppermute(sent, "seq", swap)
        second = lax.ppermute(first, "pos", [(p, p ^ 1) for p in range(pos_count)])
        weights = [upright_threefold_linear, first, second]
    else:
        weights = [lax.all_gather(upright_threefold_linear, "seq", axis=1, tiled=True)]

    partial = call(
        functools.partial(logits_kernel, head, len(key_parts)),
        jax.ShapeDtypeStruct((heads * sites, length), F32),
        [lateral_asking_vectors, *key_parts],
    )
    if seq_count == 2:
        partials = [partial, lax.ppermute(partial, "seq", swap)]
    else:
        partials = [lax.psum(partial, "seq")]
    head_rows = round_up(heads, 8)
    shares, pair_local = call(
        functools.partial(
            softmax_kernel,
            1.0 / (math.sqrt(head) * math.sqrt(rows * seq_count)),
            heads,
            len(partials),
        ),
        (
            jax.ShapeDtypeStruct((heads * sites, length), BF16),
            jax.ShapeDtypeStruct((head_rows + sites, length), F32),
        ),
        [*partials, regression_factors, order],
        smem=(len(partials),),
        scratch=[pltpu.VMEM((head_rows + sites, length), F32)],
    )
    pair_parts = staged_gather(pair_local, 0, pos_count)

    cells = rows * sites
    hidden, query, key_value = call(
        functools.partial(mix_kernel, head, split, len(value_parts), len(weights)),
        (
            jax.ShapeDtypeStruct((cells, embed), F32),
            jax.ShapeDtypeStruct((cells, embed), BF16),
            jax.ShapeDtypeStruct((cells, 2 * embed), BF16),
        ),
        [
            scalars,
            shares,
            *value_parts,
            lateral_closing_linear,
            skip_stream_input,
            upright_normalizer_multiplier.reshape(1, embed),
            *weights,
        ],
        smem=(0,),
        scratch=[
            pltpu.VMEM((cells, embed), F32),
            pltpu.VMEM((cells, embed), BF16),
            pltpu.VMEM((cells, 3 * embed), BF16),
        ],
    )
    if seq_count == 2:
        kv_parts = [key_value, lax.ppermute(key_value, "seq", swap)]
    else:
        kv_parts = [lax.all_gather(key_value, "seq", axis=0, tiled=True)]
    alignment_output = call(
        functools.partial(column_kernel, head, 1.0 / math.sqrt(head), len(kv_parts)),
        jax.ShapeDtypeStruct((rows, sites, embed), BF16),
        [query, *kv_parts, hidden, upright_closing_linear],
        scratch=[
            pltpu.VMEM((cells * rows * seq_count, embed), F32),
            pltpu.VMEM((cells, embed), F32),
        ],
    )

    factor_column = jnp.zeros((head_rows, 128), F32).at[:heads, :].set(regression_factors[:, None])
    n = len(pair_parts)
    pairing_chances = call(
        functools.partial(contact_kernel, heads, sites, n),
        jax.ShapeDtypeStruct((sites, slab_width), F32),
        [*pair_parts, factor_column, regression_offset, own_select, slab_select, arrival_select],
        smem=(n + 1,),
        scratch=[
            pltpu.VMEM((head_rows + sites, length), F32),
            pltpu.VMEM((length, length), F32),
        ],
    )
    return alignment_output, pairing_chances


def solution(mesh):
    cells = P("seq", "pos", None)
    return jax.shard_map(
        per_device,
        mesh=mesh,
        in_specs=(cells, cells, cells, cells, P(), P(), P(None, "seq"), P(), P(), P()),
        out_specs=(cells, P("pos", "seq")),
        check_vma=False,
    )
```

time: 128 us -> 62.1 us (0.49)
  blocking collectives: 94.8 us -> 0 us
  waiting for transfers between devices: 0.69 us -> 26.7 us
  starting transfers between devices: 3.54 us -> 23.9 us
  between operations: 15 us -> 1.61 us
  matrix products: 6.76 us -> 0 us
  Pallas kernels: 0 us -> 5.99 us
  other arithmetic: 2.54 us -> 0.44 us
    all_gather x3 -> x0, blocking collectives: 54.8 us -> none  [the longest x1 25.5 us: per_device(): lax.all_gather(lateral_matched_vectors, 'pos', axis=1, tiled=True)]
    psum x2 -> x0, blocking collectives: 40.1 us -> none  [the longest x1 30.4 us: per_device(): couple_amount = lax.psum(local_sums, 'pos')]
    ppermute x0 -> x19, waiting for transfers between devices: none -> 26.7 us  [the longest x15 11.8 us: staged_gather(): parts.append(lax.ppermute(array, 'pos', pairs))]
    ppermute x0 -> x19, starting transfers between devices: none -> 23.9 us  [the longest x15 19.3 us: staged_gather(): parts.append(lax.ppermute(array, 'pos', pairs))]
    dot_general x9 -> x0, matrix products: 6.76 us -> none  [the longest x1 2.77 us: per_device(): jnp.dot(normed, full_projection, preferred_element_type=jnp.float32)]
    pallas_call x0 -> x5, Pallas kernels: none -> 5.99 us  [call(): pl.pallas_call(kernel, out_shape=out_shape, in_specs=specs, out_specs=jax...]
    all_to_all x1 -> x0, starting transfers between devices: 3.5 us -> none  [per_device(): lax.all_to_all(combined_groups, 'pos', split_axis=1, concat_axis=0, tiled...]
    sub x1 -> x0, other arithmetic: 1.92 us -> none  [per_device(): exponent = jnp.exp(logits - row_peak)]
  transfers between devices with their start and end apart: 2 -> 19, of which waited for: 0 -> 8; matrix products, arithmetic and copies ran while one was open for 6% -> 6% of each run, Pallas kernels for 0% -> 7%
where the time goes in v1:
time: 62.1 us; the launch traced here: 61.9 us
  waiting for transfers between devices  26.7 us (43%)
  starting transfers between devices  23.9 us (38%)
  Pallas kernels  5.99 us (10%)
  local copies, waits for them, and re-layouts  3.23 us (5%)
  between operations  1.61 us (3%)
    ppermute x15, starting transfers between devices, staged_gather(): parts.append(lax.ppermute(array, 'pos', pairs))  19.3 us
    ppermute x15, waiting for transfers between devices, staged_gather(): parts.append(lax.ppermute(array, 'pos', pairs))  11.8 us
    ppermute x1, waiting for transfers between devices, per_device(): first = lax.ppermute(sent, 'seq', swap)  11 us
    pallas_call x5, Pallas kernels, call(): pl.pallas_call(kernel, out_shape=out_shape, in_specs=specs, out_specs=jax...  5.99 us
    ppermute x1, waiting for transfers between devices, per_device(): partials = [partial, lax.ppermute(partial, 'seq', swap)]  2.35 us
    unnamed x30, local copies, waits for them, and re-layouts  1.69 us
    ppermute x1, starting transfers between devices, per_device(): kv_parts = [key_value, lax.ppermute(key_value, 'seq', swap)]  1.56 us
    ppermute x1, starting transfers between devices, per_device(): first = lax.ppermute(sent, 'seq', swap)  1.56 us
  transfers between devices with their start and end apart: 19, of which 8 were waited for; matrix products, arithmetic and copies ran while one was open for 6% of the time, Pallas kernels for 7%

profile of v1, /device:TPU:0, one launch (start us, length us, event | category | flops | bytes accessed | tf_op | source)
XLA Modules:
  0.0 61.9 jit_solution(13931568187643507645)
XLA Ops:
  0.6 0.0 copy-start.7
  0.7 5.1 %collective-permute-start.2 = (bf16[4,8,768]{2,1,0:T(8,128)(2,1)}, bf16[4,8,768]{2,1,0:T(8,128)(2,1)S(1)}, u32[]{:S(2)}, u32[]{:S(2)}) collective-permute-start(bf16[4,8,768]{2,1,0:T(8,128)(2,1)} %param.14), channel_id=1, source_target_pairs={{0,12},{1,13},{2,14},{3,15},{4,0},{5,1},{6,2},{7,3},{8,4},{9,5},{1... | collective-permute-start | bytes 147464 | tf_op jit(solution)/shard_map/ppermute | solution.py:236
  5.8 0.0 collective-permute-start.1
  5.8 1.0 %collective-permute-start = (bf16[4,8,768]{2,1,0:T(8,128)(2,1)}, bf16[4,8,768]{2,1,0:T(8,128)(2,1)S(1)}, u32[]{:S(2)}, u32[]{:S(2)}) collective-permute-start(bf16[4,8,768]{2,1,0:T(8,128)(2,1)} %param.14), channel_id=1, source_target_pairs={{0,4},{1,5},{2,6},{3,7},{4,8},{5,9},{6,10},{7,11},{8,12},{9,13},{1... | collective-permute-start | bytes 147464 | tf_op jit(solution)/shard_map/ppermute | solution.py:236
  6.8 2.8 %collective-permute-start.8 = (bf16[4,8,768]{2,1,0:T(8,128)(2,1)}, bf16[4,8,768]{2,1,0:T(8,128)(2,1)S(1)}, u32[]{:S(2)}, u32[]{:S(2)}) collective-permute-start(bf16[4,8,768]{2,1,0:T(8,128)(2,1)} %param.15), channel_id=1, source_target_pairs={{0,12},{1,13},{2,14},{3,15},{4,0},{5,1},{6,2},{7,3},{8,4},{9,5},{1... | collective-permute-start | bytes 147464 | tf_op jit(solution)/shard_map/ppermute | solution.py:236
  9.6 1.1 %collective-permute-start.7 = (bf16[4,8,768]{2,1,0:T(8,128)(2,1)}, bf16[4,8,768]{2,1,0:T(8,128)(2,1)S(1)}, u32[]{:S(2)}, u32[]{:S(2)}) collective-permute-start(bf16[4,8,768]{2,1,0:T(8,128)(2,1)} %param.15), channel_id=1, source_target_pairs={{0,8},{1,9},{2,10},{3,11},{4,12},{5,13},{6,14},{7,15},{8,0},{9,1},... | collective-permute-start | bytes 147464 | tf_op jit(solution)/shard_map/ppermute | solution.py:236
  10.7 0.8 %constant_dynamic-update-slice_fusion.4 = bf16[4,64,768]{2,1,0:T(8,128)(2,1)S(1)} fusion(bf16[4,8,768]{2,1,0:T(8,128)(2,1)} %param.14), kind=kLoop, calls=%fused_computation.12 | loop fusion | bytes 98304
  11.5 0.8 %constant_dynamic-update-slice_fusion.9 = bf16[4,64,768]{2,1,0:T(8,128)(2,1)S(1)} fusion(bf16[4,8,768]{2,1,0:T(8,128)(2,1)} %param.15), kind=kLoop, calls=%fused_computation.17 | loop fusion | bytes 98304
  12.3 0.1 stack.79
  12.5 0.1 iota_add_fusion
  12.5 0.1 add.375
  12.6 0.1 fusion.refs_3_
  12.7 0.1 compare_convert_fusion
  12.8 0.0 copy-start.4
  12.8 1.2 %constant_dynamic-slice_fusion = bf16[384,1152]{1,0:T(8,128)(2,1)S(1)} fusion(bf16[768,1152]{1,0:T(8,128)(2,1)} %refs_7_.1, s32[]{:T(128)S(6)} %select_n.292), kind=kLoop, calls=%fused_computation.30 | loop fusion | bytes 1769476 | tf_op jit(solution)/shard_map/dynamic_slice | solution.py:293
  14.1 0.0 copy-start.5
  14.1 0.0 copy-start
  14.1 0.0 copy-start.2
  14.1 0.0 copy-start.3
  14.1 0.1 pad_add_fusion.refs_0_
  14.2 0.1 collective-permute-start.6
  14.3 1.6 %collective-permute-start.11 = (bf16[384,1152]{1,0:T(8,128)(2,1)S(1)}, bf16[384,1152]{1,0:T(8,128)(2,1)S(1)}, u32[]{:S(2)}, u32[]{:S(2)}) collective-permute-start(bf16[384,1152]{1,0:T(8,128)(2,1)S(1)} %constant_dynamic-slice_fusion), channel_id=1, source_target_pairs={{0,16},{16,0},{1,17},{17,1},{2,18},{18,2},{3,19},{19,3},{4,20},{20... | collective-permute-start | bytes 2654216 | tf_op jit(solution)/shard_map/ppermute | solution.py:296
  15.9 1.6 %collective-permute-start.3 = (bf16[4,32,768]{2,1,0:T(8,128)(2,1)S(1)}, bf16[4,32,768]{2,1,0:T(8,128)(2,1)S(1)}, u32[]{:S(2)}, u32[]{:S(2)}) collective-permute-start(bf16[4,32,768]{2,1,0:T(8,128)(2,1)S(1)} %pad_maximum_fusion), channel_id=1, source_target_pairs={{0,2},{1,3},{2,0},{3,1},{4,6},{5,7},{6,4},{7,5},{8,10},{9,11},{10,... | collective-permute-start | bytes 589832 | tf_op jit(solution)/shard_map/ppermute | solution.py:236
  17.5 4.1 %collective-permute-done.3 = bf16[4,32,768]{2,1,0:T(8,128)(2,1)S(1)} collective-permute-done((bf16[4,32,768]{2,1,0:T(8,128)(2,1)S(1)}, bf16[4,32,768]{2,1,0:T(8,128)(2,1)S(1)}, u32[]{:S(2)}, u32[]{:S(2)}) %collective-permute-start.3) | collective-permute-done | bytes 196640 | tf_op jit(solution)/shard_map/ppermute | solution.py:236
  21.6 0.1 collective-permute-start.4
  21.8 1.6 %collective-permute-start.9 = (bf16[4,32,768]{2,1,0:T(8,128)(2,1)S(1)}, bf16[4,32,768]{2,1,0:T(8,128)(2,1)S(1)}, u32[]{:S(2)}, u32[]{:S(2)}) collective-permute-start(bf16[4,32,768]{2,1,0:T(8,128)(2,1)S(1)} %pad_maximum_fusion.1), channel_id=1, source_target_pairs={{0,2},{1,3},{2,0},{3,1},{4,6},{5,7},{6,4},{7,5},{8,10},{9,11},{10,... | collective-permute-start | bytes 589832 | tf_op jit(solution)/shard_map/ppermute | solution.py:236
  23.4 11.0 %collective-permute-done.11.refs_8_ = bf16[384,1152]{1,0:T(8,128)(2,1)S(1)} collective-permute-done((bf16[384,1152]{1,0:T(8,128)(2,1)S(1)}, bf16[384,1152]{1,0:T(8,128)(2,1)S(1)}, u32[]{:S(2)}, u32[]{:S(2)}) %collective-permute-start.11) | collective-permute-done | bytes 884768 | tf_op jit(solution)/shard_map/ppermute | solution.py:296
  34.4 0.3 shard_map.113.refs_0_
  34.7 1.5 %collective-permute-start.5 = (f32[96,128]{1,0:T(8,128)S(1)}, f32[96,128]{1,0:T(8,128)S(1)}, u32[]{:S(2)}, u32[]{:S(2)}) collective-permute-start(f32[96,128]{1,0:T(8,128)S(1)} %shard_map.113.refs_0_), channel_id=1, source_target_pairs={{0,16},{16,0},{1,17},{17,1},{2,18},{18,2},{3,19},{19,3},{4,20},{20... | collective-permute-start | bytes 147464 | tf_op jit(solution)/shard_map/ppermute | solution.py:308
  36.3 0.3 collective-permute-start.10
  36.5 2.3 %collective-permute-done.5.refs_1_ = f32[96,128]{1,0:T(8,128)S(1)} collective-permute-done((f32[96,128]{1,0:T(8,128)S(1)}, f32[96,128]{1,0:T(8,128)S(1)}, u32[]{:S(2)}, u32[]{:S(2)}) %collective-permute-start.5) | collective-permute-done | bytes 49184 | tf_op jit(solution)/shard_map/ppermute | solution.py:308
  38.9 1.0 %shard_map.114 = (bf16[96,128]{1,0:T(8,128)(2,1)S(1)}, f32[24,128]{1,0:T(8,128)S(1)}) custom-call(f32[96,128]{1,0:T(8,128)S(1)} %shard_map.113.refs_0_, f32[96,128]{1,0:T(8,128)S(1)} %collective-permute-done.5.refs_1_, f32[12]{0:T(128)S(1)} %copy-done.5, f32[128,128]{1,0:T(8,128)S(1)} %fusion.refs_3_), custom_call_target="tpu_custom_call" | custom-call | flops 1000000 | bytes 1000000 | tf_op jit(solution)/shard_map/pallas_call | solution.py:203
  39.8 3.5 %collective-permute-start.16 = (f32[24,128]{1,0:T(8,128)S(1)}, f32[24,128]{1,0:T(8,128)S(1)}, u32[]{:S(2)}, u32[]{:S(2)}) collective-permute-start(f32[24,128]{1,0:T(8,128)S(1)} %get-tuple-element.23), channel_id=1, source_target_pairs={{0,12},{1,13},{2,14},{3,15},{4,0},{5,1},{6,2},{7,3},{8,4},{9,5},{1... | collective-permute-start | bytes 36872 | tf_op jit(solution)/shard_map/ppermute | solution.py:236
  43.3 0.3 collective-permute-start.15
  43.6 0.4 collective-permute-start.14
  44.0 0.8 %collective-permute-done.16 = f32[24,128]{1,0:T(8,128)S(1)} collective-permute-done((f32[24,128]{1,0:T(8,128)S(1)}, f32[24,128]{1,0:T(8,128)S(1)}, u32[]{:S(2)}, u32[]{:S(2)}) %collective-permute-start.16) | collective-permute-done | bytes 12320 | tf_op jit(solution)/shard_map/ppermute | solution.py:236
  44.7 3.2 %collective-permute-done.15 = f32[24,128]{1,0:T(8,128)S(1)} collective-permute-done((f32[24,128]{1,0:T(8,128)S(1)}, f32[24,128]{1,0:T(8,128)S(1)}, u32[]{:S(2)}, u32[]{:S(2)}) %collective-permute-start.15) | collective-permute-done | bytes 12320 | tf_op jit(solution)/shard_map/ppermute | solution.py:236
  47.9 1.2 %collective-permute-done.14 = f32[24,128]{1,0:T(8,128)S(1)} collective-permute-done((f32[24,128]{1,0:T(8,128)S(1)}, f32[24,128]{1,0:T(8,128)S(1)}, u32[]{:S(2)}, u32[]{:S(2)}) %collective-permute-start.14) | collective-permute-done | bytes 12320 | tf_op jit(solution)/shard_map/ppermute | solution.py:236
  49.1 1.5 %collective-permute-start.17 = (f32[96,128]{1,0:T(8,128)S(1)}, f32[96,128]{1,0:T(8,128)S(1)}, u32[]{:S(2)}, u32[]{:S(2)}) collective-permute-start(f32[96,128]{1,0:T(8,128)S(1)} %pad_maximum_fusion.2), channel_id=1, source_target_pairs={{0,2},{1,3},{2,0},{3,1},{4,6},{5,7},{6,4},{7,5},{8,10},{9,11},{10,... | collective-permute-start | bytes 147464 | tf_op jit(solution)/shard_map/ppermute | solution.py:236
  50.6 2.6 %collective-permute-done.17 = f32[96,128]{1,0:T(8,128)S(1)} collective-permute-done((f32[96,128]{1,0:T(8,128)S(1)}, f32[96,128]{1,0:T(8,128)S(1)}, u32[]{:S(2)}, u32[]{:S(2)}) %collective-permute-start.17) | collective-permute-done | bytes 49184 | tf_op jit(solution)/shard_map/ppermute | solution.py:236
  53.2 0.0 copy-start.1
  53.3 1.9 %shard_map.115 = (f32[32,768]{1,0:T(8,128)S(1)}, bf16[32,768]{1,0:T(8,128)(2,1)S(1)}, bf16[32,1536]{1,0:T(8,128)(2,1)S(1)}) custom-call(s32[2]{0:T(128)S(1)} %pad_add_fusion.refs_0_, bf16[96,128]{1,0:T(8,128)(2,1)S(1)} %get-tuple-element.19.refs_1_, bf16[4,64,768]{2,1,0:T(8,128)(2,1)S(1)} %constant_dynamic-update-slice_fusion.5.refs_2_, ...), custom_call_target="tpu_custom_call" | custom-call | flops 1000000 | bytes 1000000 | tf_op jit(solution)/shard_map/pallas_call | solution.py:203
  55.1 1.6 %collective-permute-start.13 = (bf16[32,1536]{1,0:T(8,128)(2,1)S(1)}, bf16[32,1536]{1,0:T(8,128)(2,1)S(1)}, u32[]{:S(2)}, u32[]{:S(2)}) collective-permute-start(bf16[32,1536]{1,0:T(8,128)(2,1)S(1)} %get-tuple-element.21.refs_1_), channel_id=1, source_target_pairs={{0,16},{16,0},{1,17},{17,1},{2,18},{18,2},{3,19},{19,3},{4,20},{20... | collective-permute-start | bytes 294920 | tf_op jit(solution)/shard_map/ppermute | solution.py:354
  56.7 0.1 fusion.2.refs_4_
  57.5 0.1 scatter.8.refs_2_
  57.5 1.3 %shard_map.117 = f32[8,64]{1,0:T(8,128)} custom-call(f32[192,128]{1,0:T(8,128)S(1)} %constant_dynamic-update-slice_fusion.10.refs_0_, f32[192,128]{1,0:T(8,128)S(1)} %collective-permute-done.18.refs_1_, f32[16,128]{1,0:T(8,128)S(1)} %scatter.8.refs_2_, f32[1]{0:T(128)S(6)} %copy.24.refs_3_, f32[8,128]{1,0:T(8,128)S(1)} %fusion.2.refs_4_, ...), custom_call_target="tpu_custom_call" | custom-call | flops 1000000 | bytes 1000000 | tf_op jit(solution)/shard_map/pallas_call | solution.py:203
  58.9 1.5 %collective-permute-done.13.refs_2_ = bf16[32,1536]{1,0:T(8,128)(2,1)S(1)} collective-permute-done((bf16[32,1536]{1,0:T(8,128)(2,1)S(1)}, bf16[32,1536]{1,0:T(8,128)(2,1)S(1)}, u32[]{:S(2)}, u32[]{:S(2)}) %collective-permute-start.13) | collective-permute-done | bytes 98336 | tf_op jit(solution)/shard_map/ppermute | solution.py:354
  60.4 1.5 %shard_map.116 = bf16[4,8,768]{2,1,0:T(8,128)(2,1)} custom-call(bf16[32,768]{1,0:T(8,128)(2,1)S(1)} %get-tuple-element.20.refs_0_, bf16[32,1536]{1,0:T(8,128)(2,1)S(1)} %get-tuple-element.21.refs_1_, bf16[32,1536]{1,0:T(8,128)(2,1)S(1)} %collective-permute-done.13.refs_2_, f32[32,768]{1,0:T(8,128)S(1)} %get-tuple-element.22.refs_3_, ...), custom_call_target="tpu_custom_call" | custom-call | flops 1000000 | bytes 1000000 | tf_op jit(solution)/shard_map/pallas_call | solution.py:203
  (45 shorter events, 0.2 us)
Async XLA Ops:
  0.6 15.2 %copy-start.6 = (bf16[4,8,768]{2,1,0:T(8,128)(2,1)S(1)}, bf16[4,8,768]{2,1,0:T(8,128)(2,1)}, u32[]{:S(2)}) copy-start(bf16[4,8,768]{2,1,0:T(8,128)(2,1)} %param.14) | copy-start | bytes 147460
  0.6 13.6 %copy-start.7 = (bf16[4,8,768]{2,1,0:T(8,128)(2,1)S(1)}, bf16[4,8,768]{2,1,0:T(8,128)(2,1)}, u32[]{:S(2)}) copy-start(bf16[4,8,768]{2,1,0:T(8,128)(2,1)} %param.15) | copy-start | bytes 147460
  0.7 13.5 %copy-start.8 = (f32[768]{0:T(1024)S(1)}, f32[768]{0:T(1024)}, u32[]{:S(2)}) copy-start(f32[768]{0:T(1024)} %param.17) | copy-start | bytes 9220
  0.7 13.5 %collective-permute-start.2 = (bf16[4,8,768]{2,1,0:T(8,128)(2,1)}, bf16[4,8,768]{2,1,0:T(8,128)(2,1)S(1)}, u32[]{:S(2)}, u32[]{:S(2)}) collective-permute-start(bf16[4,8,768]{2,1,0:T(8,128)(2,1)} %param.14), channel_id=1, source_target_pairs={{0,12},{1,13},{2,14},{3,15},{4,0},{5,1},{6,2},{7,3},{8,4},{9,5},{1... | collective-permute-start | bytes 147464 | tf_op jit(solution)/shard_map/ppermute | solution.py:236
  5.8 8.5 %collective-permute-start.1 = (bf16[4,8,768]{2,1,0:T(8,128)(2,1)}, bf16[4,8,768]{2,1,0:T(8,128)(2,1)S(1)}, u32[]{:S(2)}, u32[]{:S(2)}) collective-permute-start(bf16[4,8,768]{2,1,0:T(8,128)(2,1)} %param.14), channel_id=1, source_target_pairs={{0,8},{1,9},{2,10},{3,11},{4,12},{5,13},{6,14},{7,15},{8,0},{9,1},... | collective-permute-start | bytes 147464 | tf_op jit(solution)/shard_map/ppermute | solution.py:236
  5.8 10.1 %collective-permute-start = (bf16[4,8,768]{2,1,0:T(8,128)(2,1)}, bf16[4,8,768]{2,1,0:T(8,128)(2,1)S(1)}, u32[]{:S(2)}, u32[]{:S(2)}) collective-permute-start(bf16[4,8,768]{2,1,0:T(8,128)(2,1)} %param.14), channel_id=1, source_target_pairs={{0,4},{1,5},{2,6},{3,7},{4,8},{5,9},{6,10},{7,11},{8,12},{9,13},{1... | collective-permute-start | bytes 147464 | tf_op jit(solution)/shard_map/ppermute | solution.py:236
  6.8 14.9 %collective-permute-start.8 = (bf16[4,8,768]{2,1,0:T(8,128)(2,1)}, bf16[4,8,768]{2,1,0:T(8,128)(2,1)S(1)}, u32[]{:S(2)}, u32[]{:S(2)}) collective-permute-start(bf16[4,8,768]{2,1,0:T(8,128)(2,1)} %param.15), channel_id=1, source_target_pairs={{0,12},{1,13},{2,14},{3,15},{4,0},{5,1},{6,2},{7,3},{8,4},{9,5},{1... | collective-permute-start | bytes 147464 | tf_op jit(solution)/shard_map/ppermute | solution.py:236
  9.6 12.1 %collective-permute-start.7 = (bf16[4,8,768]{2,1,0:T(8,128)(2,1)}, bf16[4,8,768]{2,1,0:T(8,128)(2,1)S(1)}, u32[]{:S(2)}, u32[]{:S(2)}) collective-permute-start(bf16[4,8,768]{2,1,0:T(8,128)(2,1)} %param.15), channel_id=1, source_target_pairs={{0,8},{1,9},{2,10},{3,11},{4,12},{5,13},{6,14},{7,15},{8,0},{9,1},... | collective-permute-start | bytes 147464 | tf_op jit(solution)/shard_map/ppermute | solution.py:236
  12.8 21.6 %copy-start.4 = (bf16[4,8,768]{2,1,0:T(8,128)(2,1)S(1)}, bf16[4,8,768]{2,1,0:T(8,128)(2,1)}, u32[]{:S(2)}) copy-start(bf16[4,8,768]{2,1,0:T(8,128)(2,1)} %refs_0_.1) | copy-start | bytes 147460
  14.1 24.8 %copy-start.5 = (f32[12]{0:T(128)S(1)}, f32[12]{0:T(128)}, u32[]{:S(2)}) copy-start(f32[12]{0:T(128)} %refs_2_.1) | copy-start | bytes 148
  14.1 39.1 %copy-start = (bf16[768,1152]{1,0:T(8,128)(2,1)S(1)}, bf16[768,1152]{1,0:T(8,128)(2,1)}, u32[]{:S(2)}) copy-start(bf16[768,1152]{1,0:T(8,128)(2,1)} %refs_7_.1) | copy-start | bytes 5308420
  14.1 39.1 %copy-start.2 = (bf16[768,768]{1,0:T(8,128)(2,1)S(1)}, bf16[768,768]{1,0:T(8,128)(2,1)}, u32[]{:S(2)}) copy-start(bf16[768,768]{1,0:T(8,128)(2,1)} %refs_4_.2) | copy-start | bytes 3538948
  14.1 39.1 %copy-start.3 = (bf16[4,8,768]{2,1,0:T(8,128)(2,1)S(1)}, bf16[4,8,768]{2,1,0:T(8,128)(2,1)}, u32[]{:S(2)}) copy-start(bf16[4,8,768]{2,1,0:T(8,128)(2,1)} %refs_5_.1) | copy-start | bytes 147460
  14.2 7.5 %collective-permute-start.6 = (bf16[4,8,768]{2,1,0:T(8,128)(2,1)S(1)}, bf16[4,8,768]{2,1,0:T(8,128)(2,1)S(1)}, u32[]{:S(2)}, u32[]{:S(2)}) collective-permute-start(bf16[4,8,768]{2,1,0:T(8,128)(2,1)S(1)} %copy-done.7), channel_id=1, source_target_pairs={{0,4},{1,5},{2,6},{3,7},{4,8},{5,9},{6,10},{7,11},{8,12},{9,13},{1... | collective-permute-start | bytes 147464 | tf_op jit(solution)/shard_map/ppermute | solution.py:236
  14.3 20.1 %collective-permute-start.11 = (bf16[384,1152]{1,0:T(8,128)(2,1)S(1)}, bf16[384,1152]{1,0:T(8,128)(2,1)S(1)}, u32[]{:S(2)}, u32[]{:S(2)}) collective-permute-start(bf16[384,1152]{1,0:T(8,128)(2,1)S(1)} %constant_dynamic-slice_fusion), channel_id=1, source_target_pairs={{0,16},{16,0},{1,17},{17,1},{2,18},{18,2},{3,19},{19,3},{4,20},{20... | collective-permute-start | bytes 2654216 | tf_op jit(solution)/shard_map/ppermute | solution.py:296
  15.9 5.7 %collective-permute-start.3 = (bf16[4,32,768]{2,1,0:T(8,128)(2,1)S(1)}, bf16[4,32,768]{2,1,0:T(8,128)(2,1)S(1)}, u32[]{:S(2)}, u32[]{:S(2)}) collective-permute-start(bf16[4,32,768]{2,1,0:T(8,128)(2,1)S(1)} %pad_maximum_fusion), channel_id=1, source_target_pairs={{0,2},{1,3},{2,0},{3,1},{4,6},{5,7},{6,4},{7,5},{8,10},{9,11},{10,... | collective-permute-start | bytes 589832 | tf_op jit(solution)/shard_map/ppermute | solution.py:236
  21.6 12.7 %collective-permute-start.4 = (bf16[4,64,768]{2,1,0:T(8,128)(2,1)S(1)}, bf16[4,64,768]{2,1,0:T(8,128)(2,1)S(1)}, u32[]{:S(2)}, u32[]{:S(2)}) collective-permute-start(bf16[4,64,768]{2,1,0:T(8,128)(2,1)S(1)} %constant_dynamic-update-slice_fusion.refs_1_), channel_id=1, source_target_pairs={{0,1},{1,0},{2,3},{3,2},{4,5},{5,4},{6,7},{7,6},{8,9},{9,8},{10,11... | collective-permute-start | bytes 1179656 | tf_op jit(solution)/shard_map/ppermute | solution.py:236
  21.8 14.5 %collective-permute-start.9 = (bf16[4,32,768]{2,1,0:T(8,128)(2,1)S(1)}, bf16[4,32,768]{2,1,0:T(8,128)(2,1)S(1)}, u32[]{:S(2)}, u32[]{:S(2)}) collective-permute-start(bf16[4,32,768]{2,1,0:T(8,128)(2,1)S(1)} %pad_maximum_fusion.1), channel_id=1, source_target_pairs={{0,2},{1,3},{2,0},{3,1},{4,6},{5,7},{6,4},{7,5},{8,10},{9,11},{10,... | collective-permute-start | bytes 589832 | tf_op jit(solution)/shard_map/ppermute | solution.py:236
  34.4 18.9 %collective-permute-start.12 = (bf16[384,1152]{1,0:T(8,128)(2,1)S(1)}, bf16[384,1152]{1,0:T(8,128)(2,1)S(1)}, u32[]{:S(2)}, u32[]{:S(2)}) collective-permute-start(bf16[384,1152]{1,0:T(8,128)(2,1)S(1)} %collective-permute-done.11.refs_8_), channel_id=1, source_target_pairs={{0,1},{1,0},{2,3},{3,2},{4,5},{5,4},{6,7},{7,6},{8,9},{9,8},{10,11... | collective-permute-start | bytes 2654216 | tf_op jit(solution)/shard_map/ppermute | solution.py:297
  34.7 4.2 %collective-permute-start.5 = (f32[96,128]{1,0:T(8,128)S(1)}, f32[96,128]{1,0:T(8,128)S(1)}, u32[]{:S(2)}, u32[]{:S(2)}) collective-permute-start(f32[96,128]{1,0:T(8,128)S(1)} %shard_map.113.refs_0_), channel_id=1, source_target_pairs={{0,16},{16,0},{1,17},{17,1},{2,18},{18,2},{3,19},{19,3},{4,20},{20... | collective-permute-start | bytes 147464 | tf_op jit(solution)/shard_map/ppermute | solution.py:308
  36.3 16.9 %collective-permute-start.10 = (bf16[4,64,768]{2,1,0:T(8,128)(2,1)S(1)}, bf16[4,64,768]{2,1,0:T(8,128)(2,1)S(1)}, u32[]{:S(2)}, u32[]{:S(2)}) collective-permute-start(bf16[4,64,768]{2,1,0:T(8,128)(2,1)S(1)} %constant_dynamic-update-slice_fusion.5.refs_2_), channel_id=1, source_target_pairs={{0,1},{1,0},{2,3},{3,2},{4,5},{5,4},{6,7},{7,6},{8,9},{9,8},{10,11... | collective-permute-start | bytes 1179656 | tf_op jit(solution)/shard_map/ppermute | solution.py:236
  39.8 4.9 %collective-permute-start.16 = (f32[24,128]{1,0:T(8,128)S(1)}, f32[24,128]{1,0:T(8,128)S(1)}, u32[]{:S(2)}, u32[]{:S(2)}) collective-permute-start(f32[24,128]{1,0:T(8,128)S(1)} %get-tuple-element.23), channel_id=1, source_target_pairs={{0,12},{1,13},{2,14},{3,15},{4,0},{5,1},{6,2},{7,3},{8,4},{9,5},{1... | collective-permute-start | bytes 36872 | tf_op jit(solution)/shard_map/ppermute | solution.py:236
  43.3 4.6 %collective-permute-start.15 = (f32[24,128]{1,0:T(8,128)S(1)}, f32[24,128]{1,0:T(8,128)S(1)}, u32[]{:S(2)}, u32[]{:S(2)}) collective-permute-start(f32[24,128]{1,0:T(8,128)S(1)} %get-tuple-element.23), channel_id=1, source_target_pairs={{0,8},{1,9},{2,10},{3,11},{4,12},{5,13},{6,14},{7,15},{8,0},{9,1},... | collective-permute-start | bytes 36872 | tf_op jit(solution)/shard_map/ppermute | solution.py:236
  43.6 5.5 %collective-permute-start.14 = (f32[24,128]{1,0:T(8,128)S(1)}, f32[24,128]{1,0:T(8,128)S(1)}, u32[]{:S(2)}, u32[]{:S(2)}) collective-permute-start(f32[24,128]{1,0:T(8,128)S(1)} %get-tuple-element.23), channel_id=1, source_target_pairs={{0,4},{1,5},{2,6},{3,7},{4,8},{5,9},{6,10},{7,11},{8,12},{9,13},{1... | collective-permute-start | bytes 36872 | tf_op jit(solution)/shard_map/ppermute | solution.py:236
  49.1 4.1 %collective-permute-start.17 = (f32[96,128]{1,0:T(8,128)S(1)}, f32[96,128]{1,0:T(8,128)S(1)}, u32[]{:S(2)}, u32[]{:S(2)}) collective-permute-start(f32[96,128]{1,0:T(8,128)S(1)} %pad_maximum_fusion.2), channel_id=1, source_target_pairs={{0,2},{1,3},{2,0},{3,1},{4,6},{5,7},{6,4},{7,5},{8,10},{9,11},{10,... | collective-permute-start | bytes 147464 | tf_op jit(solution)/shard_map/ppermute | solution.py:236
  53.2 4.3 %collective-permute-start.18 = (f32[192,128]{1,0:T(8,128)S(1)}, f32[192,128]{1,0:T(8,128)S(1)}, u32[]{:S(2)}, u32[]{:S(2)}) collective-permute-start(f32[192,128]{1,0:T(8,128)S(1)} %constant_dynamic-update-slice_fusion.10.refs_0_), channel_id=1, source_target_pairs={{0,1},{1,0},{2,3},{3,2},{4,5},{5,4},{6,7},{7,6},{8,9},{9,8},{10,11... | collective-permute-start | bytes 294920 | tf_op jit(solution)/shard_map/ppermute | solution.py:236
  53.2 7.2 %copy-start.1 = (bf16[768,768]{1,0:T(8,128)(2,1)S(1)}, bf16[768,768]{1,0:T(8,128)(2,1)}, u32[]{:S(2)}) copy-start(bf16[768,768]{1,0:T(8,128)(2,1)} %refs_4_.3) | copy-start | bytes 3538948
  55.1 5.2 %collective-permute-start.13 = (bf16[32,1536]{1,0:T(8,128)(2,1)S(1)}, bf16[32,1536]{1,0:T(8,128)(2,1)S(1)}, u32[]{:S(2)}, u32[]{:S(2)}) collective-permute-start(bf16[32,1536]{1,0:T(8,128)(2,1)S(1)} %get-tuple-element.21.refs_1_), channel_id=1, source_target_pairs={{0,16},{16,0},{1,17},{17,1},{2,18},{18,2},{3,19},{19,3},{4,20},{20... | collective-permute-start | bytes 294920 | tf_op jit(solution)/shard_map/ppermute | solution.py:354

commit v2 on v1

--- a/solution.py
+++ b/solution.py
@@ -3,6 +3,7 @@
 
 import jax
 import jax.numpy as jnp
+import numpy as np
 from jax import lax
 from jax.experimental import pallas as pl
 from jax.experimental.pallas import tpu as pltpu
@@ -77,15 +78,14 @@
     for h in range(1, heads):
         merged = merged + shares[h * sites : (h + 1) * sites, :] * factor_ref[h]
     held[head_rows : head_rows + sites, :] = merged
-    pair_ref[...] = dot_nn(held[...], order_ref[...], HIGHEST)
-
-
-def mix_kernel(head, split, v_count, w_count, *refs):
-    scalar_ref, w_ref = refs[:2]
-    v_refs = refs[2 : 2 + v_count]
-    closing_ref, skip_ref, gain_ref = refs[2 + v_count : 5 + v_count]
-    weight_refs = refs[5 + v_count : 5 + v_count + w_count]
-    hidden_ref, query_ref, kv_ref, mixed, normed, projected = refs[5 + v_count + w_count :]
+    pair_ref[...] = jnp.broadcast_to(
+        dot_nn(held[...], order_ref[...], HIGHEST)[None], pair_ref.shape
+    )
+
+
+def mix_kernel(head, v_count, *refs):
+    w_ref, v_refs = refs[0], refs[1 : 1 + v_count]
+    closing_ref, skip_ref, gain_ref, hidden_ref, normed_ref, mixed = refs[1 + v_count :]
     rows, sites, embed = skip_ref.shape
     width = lane_block(embed, head)
     group = width // head
@@ -106,29 +106,31 @@
     hidden_ref[...] = hidden
     centered = hidden - jnp.mean(hidden, axis=1, keepdims=True)
     spread = jnp.mean(centered * centered, axis=1, keepdims=True)
-    unit = (centered * lax.rsqrt(spread + 1e-05) * gain_ref[...]).astype(BF16)
-    if split:
-        own_ref, first_ref, second_ref = weight_refs
-        columns, half = own_ref.shape[1], first_ref.shape[0]
-        normed[...] = unit
+    normed_ref[...] = (centered * lax.rsqrt(spread + 1e-05) * gain_ref[...]).astype(BF16)
+
+
+def project_kernel(part_count, *refs):
+    parts, (weight_ref, out_ref) = refs[:part_count], refs[part_count:]
+    normed = jnp.concatenate([part[...] for part in parts], axis=0)
+    out_ref[...] = dot_nn(normed, weight_ref[...]).astype(BF16)
+
+
+def column_kernel(head, factor, swapped, *refs):
+    if swapped:
+        scalar_ref, own_ref, other_ref = refs[:3]
+        full = refs[-1]
+        hidden_ref, closing_ref, out_ref, products, mixed = refs[3:-1]
+        cells, columns = own_ref.shape
         own_at = pl.multiple_of(scalar_ref[0] * columns, 128)
         other_at = pl.multiple_of((1 - scalar_ref[0]) * columns, 128)
-        first = normed[:, pl.ds(pl.multiple_of(scalar_ref[1] * half, 128), half)]
-        second = normed[:, pl.ds(pl.multiple_of((1 - scalar_ref[1]) * half, 128), half)]
-        projected[:, pl.ds(own_at, columns)] = dot_nn(unit, own_ref[...]).astype(BF16)
-        projected[:, pl.ds(other_at, columns)] = (
-            dot_nn(first, first_ref[...]) + dot_nn(second, second_ref[...])
-        ).astype(BF16)
-    else:
-        projected[...] = dot_nn(unit, weight_refs[0][...]).astype(BF16)
-    query_ref[...] = projected[:, 0:embed]
-    kv_ref[...] = projected[:, embed:]
-
-
-def column_kernel(head, factor, part_count, *refs):
-    q_ref, kv_refs = refs[0], refs[1 : 1 + part_count]
-    hidden_ref, closing_ref, out_ref, products, mixed = refs[1 + part_count :]
+        full[:, pl.ds(own_at, columns)] = own_ref[...]
+        full[0 : cells // 2, pl.ds(other_at, columns)] = other_ref[cells // 2 :, :]
+        full[cells // 2 :, pl.ds(other_at, columns)] = other_ref[0 : cells // 2, :]
+    else:
+        query_ref, full = refs[:2]
+        hidden_ref, closing_ref, out_ref, products, mixed = refs[2:]
     rows, sites, embed = out_ref.shape
+    own_rows = rows * sites
     heads = embed // head
     padded = round_up(heads, 128)
     pick = (
@@ -139,14 +141,15 @@
         lax.broadcasted_iota(jnp.int32, (padded, embed), 1) // head
         == lax.broadcasted_iota(jnp.int32, (padded, embed), 0)
     ).astype(BF16)
-    query = q_ref[...].astype(F32)
-    key_values = [kv[...].astype(F32) for kv in kv_refs]
-    keys, values = [], []
-    for kv in key_values:
-        for t in range(kv.shape[0] // sites):
-            keys.append(kv[t * sites : (t + 1) * sites, 0:embed])
-            values.append(kv[t * sites : (t + 1) * sites, embed:])
-    seqs = len(keys)
+    if swapped:
+        query = full[0:own_rows, 0:embed].astype(F32)
+        key, value = full[:, embed : 2 * embed].astype(F32), full[:, 2 * embed :].astype(F32)
+    else:
+        query = query_ref[...].astype(F32)
+        key, value = full[:, 0:embed].astype(F32), full[:, embed:].astype(F32)
+    seqs = key.shape[0] // sites
+    keys = [key[t * sites : (t + 1) * sites, :] for t in range(seqs)]
+    values = [value[t * sites : (t + 1) * sites, :] for t in range(seqs)]
     for s in range(rows):
         for t in range(seqs):
             at = (s * seqs + t) * sites
@@ -169,26 +172,26 @@
     out_ref[...] = out.reshape(rows, sites, embed).astype(BF16)
 
 
-def contact_kernel(heads, sites, part_count, *refs):
-    parts = refs[:part_count]
-    factor_ref, offset_ref, own_ref, slab_ref, arrival_ref, out_ref, held, table = refs[part_count:]
+def contact_kernel(heads, scalar_ref, pair_ref, factor_ref, offset_ref, own_ref, slab_ref, out_ref, held):
+    count, step, length = pair_ref.shape
     head_rows = round_up(heads, 8)
-    step = head_rows + sites
-    total, block = None, 0
-    for part in parts:
-        for at in range(0, part.shape[0], step):
-            sums = part[at : at + head_rows, :]
-            total = sums if total is None else total + sums
-            table[block * sites : (block + 1) * sites, :] = part[at + head_rows : at + step, :]
-            block += 1
+    sites = step - head_rows
+    blocks = slab_ref.shape[1] // sites
+    total = pair_ref[0, 0:head_rows, :]
+    for n in range(1, count):
+        total = total + pair_ref[n, 0:head_rows, :]
+    held[0:head_rows, :] = total
+    held[head_rows:step, :] = pair_ref[scalar_ref[1], head_rows:step, :]
+    first = scalar_ref[0] * blocks
+    table = jnp.concatenate(
+        [pair_ref[first + n, head_rows:step, :] for n in range(blocks)], axis=0
+    )
     amount = jnp.sum(total, axis=1, keepdims=True)
     real = lax.broadcasted_iota(jnp.int32, (head_rows, 1), 0) < heads
     share = jnp.where(real, factor_ref[:, 0:1] / jnp.where(real, amount, 1.0), 0.0)
-    held[0:head_rows, :] = total
-    held[head_rows:step, :] = table[0:sites, :]
     slab = dot_nn(held[...], slab_ref[...], HIGHEST)
     own = dot_nt(own_ref[...], total * share, HIGHEST)
-    mirrored = dot_nn(dot_nt(own_ref[...], table[...], HIGHEST), arrival_ref[...], HIGHEST)
+    mirrored = dot_nt(own_ref[...], table, HIGHEST)
     adjuster = dot_nn(own, slab[0:head_rows, :], HIGHEST)
     out_ref[...] = jax.nn.sigmoid(
         slab[head_rows:step, :] + mirrored - adjuster + offset_ref[0]
@@ -223,30 +226,40 @@
     return stages[::-1]
 
 
+def send_pos(array, count, stride, size, delta):
+    pairs = []
+    for p in range(count):
+        a = (p // stride) % size
+        pairs.append((p, p + ((a + delta) % size - a) * stride))
+    return lax.ppermute(array, "pos", pairs)
+
+
 def staged_gather(array, axis, count):
     parts = [array]
     for at, (stride, size) in enumerate(stages_of(count)):
-        array = parts[0] if len(parts) == 1 else jnp.concatenate(parts, axis=axis)
-        parts = [array]
-        for delta in range(1, size):
-            pairs = []
-            for p in range(count):
-                a = (p // stride) % size
-                pairs.append((p, p + ((a + delta) % size - a) * stride))
-            parts.append(lax.ppermute(array, "pos", pairs))
+        if at == 1:
+            parts = [jnp.concatenate(parts, axis=axis)]
+        parts = parts + [
+            send_pos(part, count, stride, size, delta)
+            for delta in range(1, size)
+            for part in parts
+        ]
     return parts
 
 
 def arrival_order(index, count):
-    sources = [index]
-    for stride, size in stages_of(count):
-        grown = []
-        for delta in range(size):
-            for source in sources:
-                a = (source // stride) % size
-                grown.append(source + ((a - delta) % size - a) * stride)
-        sources = grown
-    return jnp.stack(sources)
+    digits = [()]
+    for stage in stages_of(count):
+        digits = [d + (delta,) for delta in range(stage[1]) for d in digits]
+    origin = jnp.zeros((count,), jnp.int32)
+    for at, (stride, size) in enumerate(stages_of(count)):
+        delta = np.array([d[at] for d in digits], np.int32)
+        origin = origin + ((index // stride) % size + size - delta) % size * stride
+    return origin
+
+
+def after(array, *others):
+    return lax.optimization_barrier((array, *others))[0]
 
 
 def per_device(
@@ -268,14 +281,17 @@
     pos_count = lax.axis_size("pos")
     length = sites * pos_count
     slab_width = length // seq_count
+    cells = rows * sites
     pos_index = lax.axis_index("pos").astype(jnp.int32)
     seq_index = lax.axis_index("seq").astype(jnp.int32)
     swap = [(s, 1 - s) for s in range(2)]
-    embed_in, columns = upright_threefold_linear.shape
-    split = seq_count == 2 and pos_count % 2 == 0 and columns % 128 == 0 and embed_in % 256 == 0
+    columns = upright_threefold_linear.shape[1]
+    swapped = seq_count == 2 and columns % 128 == 0
 
     key_parts = staged_gather(lateral_matched_vectors, 1, pos_count)
-    value_parts = staged_gather(lateral_carried_vectors, 1, pos_count)
+    value_parts = staged_gather(
+        after(lateral_carried_vectors, key_parts[0]), 1, pos_count
+    )
 
     origin = arrival_order(pos_index, pos_count)
     place = (origin[:, None] * sites + jnp.arange(sites, dtype=jnp.int32)[None, :]).reshape(length)
@@ -285,19 +301,7 @@
     own_rows = pos_index * sites + jnp.arange(sites, dtype=jnp.int32)
     own_select = (own_rows[:, None] == every[None, :]).astype(F32)
     slab_select = (every[:, None] == slab_at[None, :]).astype(F32)
-    arrival_select = (place[:, None] == slab_at[None, :]).astype(F32)
-    scalars = jnp.stack([seq_index, pos_index % 2])
-
-    if split:
-        half = embed_in // 2
-        sent = lax.dynamic_slice_in_dim(
-            upright_threefold_linear, (pos_index % 2) * half, half, 0
-        )
-        first = lax.ppermute(sent, "seq", swap)
-        second = lax.ppermute(first, "pos", [(p, p ^ 1) for p in range(pos_count)])
-        weights = [upright_threefold_linear, first, second]
-    else:
-        weights = [lax.all_gather(upright_threefold_linear, "seq", axis=1, tiled=True)]
+    scalars = jnp.stack([seq_index, pos_index])
 
     partial = call(
         functools.partial(logits_kernel, head, len(key_parts)),
@@ -318,63 +322,66 @@
         ),
         (
             jax.ShapeDtypeStruct((heads * sites, length), BF16),
-            jax.ShapeDtypeStruct((head_rows + sites, length), F32),
+            jax.ShapeDtypeStruct((pos_count, head_rows + sites, length), F32),
         ),
         [*partials, regression_factors, order],
         smem=(len(partials),),
         scratch=[pltpu.VMEM((head_rows + sites, length), F32)],
     )
-    pair_parts = staged_gather(pair_local, 0, pos_count)
-
-    cells = rows * sites
-    hidden, query, key_value = call(
-        functools.partial(mix_kernel, head, split, len(value_parts), len(weights)),
+    pair_all = lax.all_to_all(pair_local, "pos", split_axis=0, concat_axis=0, tiled=True)
+
+    hidden, normed = call(
+        functools.partial(mix_kernel, head, len(value_parts)),
         (
             jax.ShapeDtypeStruct((cells, embed), F32),
             jax.ShapeDtypeStruct((cells, embed), BF16),
-            jax.ShapeDtypeStruct((cells, 2 * embed), BF16),
         ),
         [
-            scalars,
             shares,
             *value_parts,
             lateral_closing_linear,
             skip_stream_input,
             upright_normalizer_multiplier.reshape(1, embed),
-            *weights,
         ],
-        smem=(0,),
-        scratch=[
-            pltpu.VMEM((cells, embed), F32),
-            pltpu.VMEM((cells, embed), BF16),
-            pltpu.VMEM((cells, 3 * embed), BF16),
-        ],
-    )
-    if seq_count == 2:
-        kv_parts = [key_value, lax.ppermute(key_value, "seq", swap)]
-    else:
-        kv_parts = [lax.all_gather(key_value, "seq", axis=0, tiled=True)]
+        scratch=[pltpu.VMEM((cells, embed), F32)],
+    )
+    if swapped:
+        normed_all = [normed, lax.ppermute(normed, "seq", swap)]
+        weight = upright_threefold_linear
+    else:
+        normed_all = [normed]
+        weight = lax.all_gather(upright_threefold_linear, "seq", axis=1, tiled=True)
+    projected = call(
+        functools.partial(project_kernel, len(normed_all)),
+        jax.ShapeDtypeStruct((cells * len(normed_all), weight.shape[1]), BF16),
+        [*normed_all, weight],
+    )
+    if swapped:
+        column_inputs = [scalars, projected, lax.ppermute(projected, "seq", swap)]
+    else:
+        key_value = lax.all_gather(projected[:, embed:], "seq", axis=0, tiled=True)
+        column_inputs = [projected[:, :embed], key_value]
+    scratch = [
+        pltpu.VMEM((cells * rows * seq_count, embed), F32),
+        pltpu.VMEM((cells, embed), F32),
+    ]
+    if swapped:
+        scratch.append(pltpu.VMEM((cells * 2, columns * 2), BF16))
     alignment_output = call(
-        functools.partial(column_kernel, head, 1.0 / math.sqrt(head), len(kv_parts)),
+        functools.partial(column_kernel, head, 1.0 / math.sqrt(head), swapped),
         jax.ShapeDtypeStruct((rows, sites, embed), BF16),
-        [query, *kv_parts, hidden, upright_closing_linear],
-        scratch=[
-            pltpu.VMEM((cells * rows * seq_count, embed), F32),
-            pltpu.VMEM((cells, embed), F32),
-        ],
+        [*column_inputs, hidden, upright_closing_linear],
+        smem=(0,) if swapped else (),
+        scratch=scratch,
     )
 
     factor_column = jnp.zeros((head_rows, 128), F32).at[:heads, :].set(regression_factors[:, None])
-    n = len(pair_parts)
     pairing_chances = call(
-        functools.partial(contact_kernel, heads, sites, n),
+        functools.partial(contact_kernel, heads),
         jax.ShapeDtypeStruct((sites, slab_width), F32),
-        [*pair_parts, factor_column, regression_offset, own_select, slab_select, arrival_select],
-        smem=(n + 1,),
-        scratch=[
-            pltpu.VMEM((head_rows + sites, length), F32),
-            pltpu.VMEM((length, length), F32),
-        ],
+        [scalars, pair_all, factor_column, regression_offset, own_select, slab_select],
+        smem=(0, 3),
+        scratch=[pltpu.VMEM((head_rows + sites, length), F32)],
     )
     return alignment_output, pairing_chances
 

time: 62.1 us -> 56.9 us (0.916)
  waiting for transfers between devices: 26.7 us -> 17.5 us
  local copies, waits for them, and re-layouts: 3.23 us -> 9.33 us
  starting transfers between devices: 23.9 us -> 21 us
    ppermute x18 -> x14, waiting for transfers between devices: 24.3 us -> 15.8 us  [the longest x12 11.1 us: send_pos(): return lax.ppermute(array, 'pos', pairs)]
    ppermute x18 -> x14, starting transfers between devices: 22.4 us -> 15.8 us  [the longest x12 13.7 us: send_pos(): return lax.ppermute(array, 'pos', pairs)]
    unnamed x30 -> x32, local copies, waits for them, and re-layouts: 1.69 us -> 7.9 us
    all_to_all x0 -> x1, starting transfers between devices: none -> 3.65 us  [per_device(): lax.all_to_all(pair_local, 'pos', split_axis=0, concat_axis=0, tiled=True)]
    reshape x1, local copies, waits for them, and re-layouts: 0.01 us -> 1.27 us  [per_device(): upright_normalizer_multiplier.reshape(1, embed)]
    dynamic_slice x1 -> x0, local copies, waits for them, and re-layouts: 1.25 us -> none  [per_device(): lax.dynamic_slice_in_dim(upright_threefold_linear, pos_index % 2 * half,...]
    ppermute x1, waiting for transfers between devices: 2.35 us -> 1.37 us  [per_device(): partials = [partial, lax.ppermute(partial, 'seq', swap)]]
    mul x1, other arithmetic: 0.01 us -> 0.7 us  [per_device(): origin[:, None] * sites + jnp.arange(sites, dtype=jnp.int32)[None, :]]
  transfers between devices with their start and end apart: 19 -> 16, of which waited for: 8 -> 9; matrix products, arithmetic and copies ran while one was open for 6% -> 7% of each run, Pallas kernels for 7% -> 7%
where the time goes in v2:
time: 56.9 us; the launch traced here: 56.3 us
  starting transfers between devices  21 us (37%)
  waiting for transfers between devices  17.5 us (31%)
  local copies, waits for them, and re-layouts  9.33 us (16%)
  Pallas kernels  5.98 us (11%)
  between operations  1.44 us (3%)
  other arithmetic  1.02 us (2%)
    ppermute x12, starting transfers between devices, send_pos(): return lax.ppermute(array, 'pos', pairs)  13.7 us
    ppermute x12, waiting for transfers between devices, send_pos(): return lax.ppermute(array, 'pos', pairs)  11.1 us
    unnamed x32, local copies, waits for them, and re-layouts  7.9 us
    pallas_call x6, Pallas kernels, call(): pl.pallas_call(kernel, out_shape=out_shape, in_specs=specs, out_specs=jax...  5.98 us
    ppermute x1, waiting for transfers between devices, per_device(): column_inputs = [scalars, projected, lax.ppermute(projected, 'seq', swap)]  4.69 us
    all_to_all x1, starting transfers between devices, per_device(): lax.all_to_all(pair_local, 'pos', split_axis=0, concat_axis=0, tiled=True)  3.65 us
    ppermute x1, starting transfers between devices, per_device(): normed_all = [normed, lax.ppermute(normed, 'seq', swap)]  1.56 us
    ppermute x1, starting transfers between devices, per_device(): partials = [partial, lax.ppermute(partial, 'seq', swap)]  1.51 us
  transfers between devices with their start and end apart: 16, of which 9 were waited for; matrix products, arithmetic and copies ran while one was open for 7% of the time, Pallas kernels for 7%

profile of v2, /device:TPU:0, one launch (start us, length us, event | category | flops | bytes accessed | tf_op | source)
XLA Modules:
  0.0 56.3 jit_solution(12996033380384469551)
XLA Ops:
  0.6 3.1 %collective-permute-start = (bf16[4,8,768]{2,1,0:T(8,128)(2,1)}, bf16[4,8,768]{2,1,0:T(8,128)(2,1)S(1)}, u32[]{:S(2)}, u32[]{:S(2)}) collective-permute-start(bf16[4,8,768]{2,1,0:T(8,128)(2,1)} %param.17), channel_id=1, source_target_pairs={{0,4},{1,5},{2,6},{3,7},{4,8},{5,9},{6,10},{7,11},{8,12},{9,13},{1... | collective-permute-start | bytes 147464 | tf_op jit(solution)/shard_map/ppermute | solution.py:234
  3.7 2.6 %collective-permute-start.1 = (bf16[4,8,768]{2,1,0:T(8,128)(2,1)}, bf16[4,8,768]{2,1,0:T(8,128)(2,1)S(1)}, u32[]{:S(2)}, u32[]{:S(2)}) collective-permute-start(bf16[4,8,768]{2,1,0:T(8,128)(2,1)} %param.17), channel_id=1, source_target_pairs={{0,8},{1,9},{2,10},{3,11},{4,12},{5,13},{6,14},{7,15},{8,0},{9,1},... | collective-permute-start | bytes 147464 | tf_op jit(solution)/shard_map/ppermute | solution.py:234
  6.3 1.3 %collective-permute-start.2 = (bf16[4,8,768]{2,1,0:T(8,128)(2,1)}, bf16[4,8,768]{2,1,0:T(8,128)(2,1)S(1)}, u32[]{:S(2)}, u32[]{:S(2)}) collective-permute-start(bf16[4,8,768]{2,1,0:T(8,128)(2,1)} %param.17), channel_id=1, source_target_pairs={{0,12},{1,13},{2,14},{3,15},{4,0},{5,1},{6,2},{7,3},{8,4},{9,5},{1... | collective-permute-start | bytes 147464 | tf_op jit(solution)/shard_map/ppermute | solution.py:234
  7.7 0.8 %constant_dynamic-update-slice_fusion.3 = bf16[4,32,768]{2,1,0:T(8,128)(2,1)S(1)} fusion(bf16[4,8,768]{2,1,0:T(8,128)(2,1)} %param.17), kind=kLoop, calls=%fused_computation.7 | loop fusion | bytes 98304
  8.5 0.7 %fusion.10 = s32[16]{0:T(128)S(1)} fusion(s32[16]{0:T(128)} %constant.134, s32[16]{0:T(128)} %constant.133, s32[16]{0:T(128)} %constant.132, s32[]{:T(128)S(6)} %add.94, s32[]{:T(128)S(6)} %add.90, s32[]{:T(128)S(6)} %add.87), kind=kLoop, calls=%fused_computation.31 | loop fusion | flops 656 | bytes 268 | tf_op jit(solution)/shard_map/mul | solution.py:297
  9.2 0.1 iota_add_fusion
  9.3 0.1 add.100
  9.4 0.0 collective-permute-done
  9.4 0.7 %collective-permute-done.1 = bf16[4,8,768]{2,1,0:T(8,128)(2,1)S(1)} collective-permute-done((bf16[4,8,768]{2,1,0:T(8,128)(2,1)}, bf16[4,8,768]{2,1,0:T(8,128)(2,1)S(1)}, u32[]{:S(2)}, u32[]{:S(2)}) %collective-permute-start.1) | collective-permute-done | bytes 49184 | tf_op jit(solution)/shard_map/ppermute | solution.py:234
  10.1 0.5 collective-permute-done.2
  10.6 1.6 %collective-permute-start.3 = (bf16[4,32,768]{2,1,0:T(8,128)(2,1)S(1)}, bf16[4,32,768]{2,1,0:T(8,128)(2,1)S(1)}, u32[]{:S(2)}, u32[]{:S(2)}) collective-permute-start(bf16[4,32,768]{2,1,0:T(8,128)(2,1)S(1)} %constant_dynamic-update-slice_fusion.refs_1_), channel_id=1, source_target_pairs={{0,2},{1,3},{2,0},{3,1},{4,6},{5,7},{6,4},{7,5},{8,10},{9,11},{10,... | collective-permute-start | bytes 589832 | tf_op jit(solution)/shard_map/ppermute | solution.py:234
  12.3 0.7 %collective-permute-start.7 = (bf16[4,8,768]{2,1,0:T(8,128)(2,1)}, bf16[4,8,768]{2,1,0:T(8,128)(2,1)S(1)}, u32[]{:S(2)}, u32[]{:S(2)}) collective-permute-start(bf16[4,8,768]{2,1,0:T(8,128)(2,1)} %param.18), channel_id=1, source_target_pairs={{0,4},{1,5},{2,6},{3,7},{4,8},{5,9},{6,10},{7,11},{8,12},{9,13},{1... | collective-permute-start | bytes 147464 | tf_op jit(solution)/shard_map/ppermute | solution.py:234
  13.0 0.8 %constant_dynamic-update-slice_fusion.7 = bf16[4,32,768]{2,1,0:T(8,128)(2,1)S(1)} fusion(bf16[4,8,768]{2,1,0:T(8,128)(2,1)} %param.18), kind=kLoop, calls=%fused_computation.11 | loop fusion | bytes 98304
  13.8 2.9 %collective-permute-start.8 = (bf16[4,8,768]{2,1,0:T(8,128)(2,1)}, bf16[4,8,768]{2,1,0:T(8,128)(2,1)S(1)}, u32[]{:S(2)}, u32[]{:S(2)}) collective-permute-start(bf16[4,8,768]{2,1,0:T(8,128)(2,1)} %param.18), channel_id=1, source_target_pairs={{0,8},{1,9},{2,10},{3,11},{4,12},{5,13},{6,14},{7,15},{8,0},{9,1},... | collective-permute-start | bytes 147464 | tf_op jit(solution)/shard_map/ppermute | solution.py:234
  16.7 0.4 collective-permute-start.9
  17.1 1.7 %collective-permute-done.7 = bf16[4,8,768]{2,1,0:T(8,128)(2,1)S(1)} collective-permute-done((bf16[4,8,768]{2,1,0:T(8,128)(2,1)}, bf16[4,8,768]{2,1,0:T(8,128)(2,1)S(1)}, u32[]{:S(2)}, u32[]{:S(2)}) %collective-permute-start.7) | collective-permute-done | bytes 49184 | tf_op jit(solution)/shard_map/ppermute | solution.py:234
  18.7 1.9 %collective-permute-done.8 = bf16[4,8,768]{2,1,0:T(8,128)(2,1)S(1)} collective-permute-done((bf16[4,8,768]{2,1,0:T(8,128)(2,1)}, bf16[4,8,768]{2,1,0:T(8,128)(2,1)S(1)}, u32[]{:S(2)}, u32[]{:S(2)}) %collective-permute-start.8) | collective-permute-done | bytes 49184 | tf_op jit(solution)/shard_map/ppermute | solution.py:234
  20.7 0.8 %collective-permute-done.9 = bf16[4,8,768]{2,1,0:T(8,128)(2,1)S(1)} collective-permute-done((bf16[4,8,768]{2,1,0:T(8,128)(2,1)}, bf16[4,8,768]{2,1,0:T(8,128)(2,1)S(1)}, u32[]{:S(2)}, u32[]{:S(2)}) %collective-permute-start.9) | collective-permute-done | bytes 49184 | tf_op jit(solution)/shard_map/ppermute | solution.py:234
  21.4 0.5 collective-permute-start.10
  21.9 0.1 fusion.refs_3_
  22.0 0.6 %collective-permute-start.11 = (bf16[4,32,768]{2,1,0:T(8,128)(2,1)S(1)}, bf16[4,32,768]{2,1,0:T(8,128)(2,1)S(1)}, u32[]{:S(2)}, u32[]{:S(2)}) collective-permute-start(bf16[4,32,768]{2,1,0:T(8,128)(2,1)S(1)} %constant_dynamic-update-slice_fusion.4.refs_1_), channel_id=1, source_target_pairs={{0,1},{1,0},{2,3},{3,2},{4,5},{5,4},{6,7},{7,6},{8,9},{9,8},{10,11... | collective-permute-start | bytes 589832 | tf_op jit(solution)/shard_map/ppermute | solution.py:234
  22.6 5.5 %collective-permute-done.10.refs_2_ = bf16[4,32,768]{2,1,0:T(8,128)(2,1)S(1)} collective-permute-done((bf16[4,32,768]{2,1,0:T(8,128)(2,1)S(1)}, bf16[4,32,768]{2,1,0:T(8,128)(2,1)S(1)}, u32[]{:S(2)}, u32[]{:S(2)}) %collective-permute-start.10) | collective-permute-done | bytes 196640 | tf_op jit(solution)/shard_map/ppermute | solution.py:234
  28.1 0.0 copy-start.8
  28.1 0.8 %copy-done.8 = bf16[4,8,768]{2,1,0:T(8,128)(2,1)S(1)} copy-done((bf16[4,8,768]{2,1,0:T(8,128)(2,1)S(1)}, bf16[4,8,768]{2,1,0:T(8,128)(2,1)}, u32[]{:S(2)}) %copy-start.8) | copy-done | bytes 49176
  28.9 0.3 shard_map.140.refs_0_
  29.2 1.5 %collective-permute-start.6 = (f32[96,128]{1,0:T(8,128)S(1)}, f32[96,128]{1,0:T(8,128)S(1)}, u32[]{:S(2)}, u32[]{:S(2)}) collective-permute-start(f32[96,128]{1,0:T(8,128)S(1)} %shard_map.140.refs_0_), channel_id=1, source_target_pairs={{0,16},{16,0},{1,17},{17,1},{2,18},{18,2},{3,19},{19,3},{4,20},{20... | collective-permute-start | bytes 147464 | tf_op jit(solution)/shard_map/ppermute | solution.py:312
  30.7 1.3 %reshape.56.refs_7_ = f32[1,768]{1,0:T(1,128)} reshape(f32[768]{0:T(1024)} %param.20) | data formatting | bytes 6144 | tf_op jit(solution)/shard_map/reshape | solution.py:344
  32.0 1.4 %collective-permute-done.6.refs_1_ = f32[96,128]{1,0:T(8,128)S(1)} collective-permute-done((f32[96,128]{1,0:T(8,128)S(1)}, f32[96,128]{1,0:T(8,128)S(1)}, u32[]{:S(2)}, u32[]{:S(2)}) %collective-permute-start.6) | collective-permute-done | bytes 49184 | tf_op jit(solution)/shard_map/ppermute | solution.py:312
  33.4 0.7 %copy-done.11 = f32[12]{0:T(128)S(1)} copy-done((f32[12]{0:T(128)S(1)}, f32[12]{0:T(128)}, u32[]{:S(2)}) %copy-start.11) | copy-done | bytes 72
  34.0 1.0 %shard_map.141 = (bf16[96,128]{1,0:T(8,128)(2,1)S(1)}, f32[16,24,128]{2,1,0:T(8,128)S(1)}) custom-call(f32[96,128]{1,0:T(8,128)S(1)} %shard_map.140.refs_0_, f32[96,128]{1,0:T(8,128)S(1)} %collective-permute-done.6.refs_1_, f32[12]{0:T(128)S(1)} %copy-done.11, f32[128,128]{1,0:T(8,128)S(1)} %fusion.refs_3_), custom_call_target="tpu_custom_call" | custom-call | flops 1000000 | bytes 1000000 | tf_op jit(solution)/shard_map/pallas_call | solution.py:206
  35.0 0.7 %copy-done.3 = bf16[4,32,768]{2,1,0:T(8,128)(2,1)} copy-done((bf16[4,32,768]{2,1,0:T(8,128)(2,1)}, bf16[4,32,768]{2,1,0:T(8,128)(2,1)S(1)}, u32[]{:S(2)}) %copy-start.3) | copy-done | bytes 196632
  35.8 0.7 %copy-done.5 = bf16[4,32,768]{2,1,0:T(8,128)(2,1)} copy-done((bf16[4,32,768]{2,1,0:T(8,128)(2,1)}, bf16[4,32,768]{2,1,0:T(8,128)(2,1)S(1)}, u32[]{:S(2)}) %copy-start.5) | copy-done | bytes 196632
  36.5 0.9 %copy-done.4 = bf16[4,32,768]{2,1,0:T(8,128)(2,1)S(1)} copy-done((bf16[4,32,768]{2,1,0:T(8,128)(2,1)S(1)}, bf16[4,32,768]{2,1,0:T(8,128)(2,1)}, u32[]{:S(2)}) %copy-start.4) | copy-done | bytes 196632
  37.4 0.9 %copy-done.6 = bf16[4,32,768]{2,1,0:T(8,128)(2,1)S(1)} copy-done((bf16[4,32,768]{2,1,0:T(8,128)(2,1)S(1)}, bf16[4,32,768]{2,1,0:T(8,128)(2,1)}, u32[]{:S(2)}) %copy-start.6) | copy-done | bytes 196632
  38.3 0.8 %copy-done.9 = bf16[4,8,768]{2,1,0:T(8,128)(2,1)S(1)} copy-done((bf16[4,8,768]{2,1,0:T(8,128)(2,1)S(1)}, bf16[4,8,768]{2,1,0:T(8,128)(2,1)}, u32[]{:S(2)}) %copy-start.9) | copy-done | bytes 49176
  39.1 0.7 %copy-done.10 = f32[1,768]{1,0:T(1,128)S(1)} copy-done((f32[1,768]{1,0:T(1,128)S(1)}, f32[1,768]{1,0:T(1,128)}, u32[]{:S(2)}) %copy-start.10) | copy-done | bytes 3096
  39.8 0.6 %shard_map.142 = (f32[32,768]{1,0:T(8,128)S(1)}, bf16[32,768]{1,0:T(8,128)(2,1)S(1)}) custom-call(bf16[96,128]{1,0:T(8,128)(2,1)S(1)} %get-tuple-element.19.refs_0_, bf16[4,32,768]{2,1,0:T(8,128)(2,1)S(1)} %constant_dynamic-update-slice_fusion.4.refs_1_, bf16[4,32,768]{2,1,0:T(8,128)(2,1)S(1)} %collective-permute-done.10.refs_2_, ...), custom_call_target="tpu_custom_call" | custom-call | flops 1000000 | bytes 1000000 | tf_op jit(solution)/shard_map/pallas_call | solution.py:206
  40.4 1.6 %collective-permute-start.13 = (bf16[32,768]{1,0:T(8,128)(2,1)S(1)}, bf16[32,768]{1,0:T(8,128)(2,1)S(1)}, u32[]{:S(2)}, u32[]{:S(2)}) collective-permute-start(bf16[32,768]{1,0:T(8,128)(2,1)S(1)} %get-tuple-element.21.refs_0_), channel_id=1, source_target_pairs={{0,16},{16,0},{1,17},{17,1},{2,18},{18,2},{3,19},{19,3},{4,20},{20... | collective-permute-start | bytes 147464 | tf_op jit(solution)/shard_map/ppermute | solution.py:349
  42.0 3.7 %all-to-all-start = ((f32[16,24,128]{2,1,0:T(8,128)}), f32[16,24,128]{2,1,0:T(8,128)S(1)}, u32[]{:S(2)}, u32[]{:S(2)}) async-start(f32[16,24,128]{2,1,0:T(8,128)} %copy-done.7), calls=%async_computation | async-start | bytes 393216 | tf_op jit(solution)/shard_map/all_to_all | solution.py:331
  45.7 0.4 shard_map.143.refs_1_
  46.1 0.6 %collective-permute-start.14 = (bf16[64,1152]{1,0:T(8,128)(2,1)S(1)}, bf16[64,1152]{1,0:T(8,128)(2,1)S(1)}, u32[]{:S(2)}, u32[]{:S(2)}) collective-permute-start(bf16[64,1152]{1,0:T(8,128)(2,1)S(1)} %shard_map.143.refs_1_), channel_id=1, source_target_pairs={{0,16},{16,0},{1,17},{17,1},{2,18},{18,2},{3,19},{19,3},{4,20},{20... | collective-permute-start | bytes 442376 | tf_op jit(solution)/shard_map/ppermute | solution.py:360
  46.7 0.1 fusion.2.own_ref
  47.5 0.1 pad_add_fusion.refs_0_.scalar_ref
  47.5 4.7 %collective-permute-done.14.refs_2_ = bf16[64,1152]{1,0:T(8,128)(2,1)S(1)} collective-permute-done((bf16[64,1152]{1,0:T(8,128)(2,1)S(1)}, bf16[64,1152]{1,0:T(8,128)(2,1)S(1)}, u32[]{:S(2)}, u32[]{:S(2)}) %collective-permute-start.14) | collective-permute-done | bytes 147488 | tf_op jit(solution)/shard_map/ppermute | solution.py:360
  52.2 2.0 %shard_map.144 = bf16[4,8,768]{2,1,0:T(8,128)(2,1)} custom-call(s32[2]{0:T(128)S(1)} %pad_add_fusion.refs_0_.scalar_ref, bf16[64,1152]{1,0:T(8,128)(2,1)S(1)} %shard_map.143.refs_1_, bf16[64,1152]{1,0:T(8,128)(2,1)S(1)} %collective-permute-done.14.refs_2_, f32[32,768]{1,0:T(8,128)S(1)} %get-tuple-element.22.refs_3_, bf16[768,768]{1,0:T(8,128)(2,1)S(1)} %copy-done.2), custom_call_target="tpu_custom_call" | custom-call | flops 1000000 | bytes 1000000 | tf_op jit(solution)/shard_map/pallas_call | solution.py:206
  54.2 0.4 all-to-all-done.pair_ref
  54.6 0.1 scatter.8.factor_ref
  54.7 1.6 %shard_map.145 = f32[8,64]{1,0:T(8,128)} custom-call(s32[2]{0:T(128)S(1)} %pad_add_fusion.refs_0_.scalar_ref, f32[16,24,128]{2,1,0:T(8,128)S(1)} %all-to-all-done.pair_ref, f32[16,128]{1,0:T(8,128)S(1)} %scatter.8.factor_ref, f32[1]{0:T(128)S(6)} %copy.21.offset_ref, f32[8,128]{1,0:T(8,128)S(1)} %fusion.2.own_ref, f32[128,64]{1,0:T(8,128)S(1)} %fusion.1.slab_ref), custom_call_target="tpu_custom_call" | custom-call | flops 1000000 | bytes 1000000 | tf_op jit(solution)/shard_map/pallas_call | solution.py:206
  (36 shorter events, 0.1 us)
Async XLA Ops:
  0.6 35.8 %copy-start.1 = (bf16[768,768]{1,0:T(8,128)(2,1)S(1)}, bf16[768,768]{1,0:T(8,128)(2,1)}, u32[]{:S(2)}) copy-start(bf16[768,768]{1,0:T(8,128)(2,1)} %refs_5_.1) | copy-start | bytes 3538948
  0.6 8.7 %collective-permute-start = (bf16[4,8,768]{2,1,0:T(8,128)(2,1)}, bf16[4,8,768]{2,1,0:T(8,128)(2,1)S(1)}, u32[]{:S(2)}, u32[]{:S(2)}) collective-permute-start(bf16[4,8,768]{2,1,0:T(8,128)(2,1)} %param.17), channel_id=1, source_target_pairs={{0,4},{1,5},{2,6},{3,7},{4,8},{5,9},{6,10},{7,11},{8,12},{9,13},{1... | collective-permute-start | bytes 147464 | tf_op jit(solution)/shard_map/ppermute | solution.py:234
  3.7 6.4 %collective-permute-start.1 = (bf16[4,8,768]{2,1,0:T(8,128)(2,1)}, bf16[4,8,768]{2,1,0:T(8,128)(2,1)S(1)}, u32[]{:S(2)}, u32[]{:S(2)}) collective-permute-start(bf16[4,8,768]{2,1,0:T(8,128)(2,1)} %param.17), channel_id=1, source_target_pairs={{0,8},{1,9},{2,10},{3,11},{4,12},{5,13},{6,14},{7,15},{8,0},{9,1},... | collective-permute-start | bytes 147464 | tf_op jit(solution)/shard_map/ppermute | solution.py:234
  6.3 4.3 %collective-permute-start.2 = (bf16[4,8,768]{2,1,0:T(8,128)(2,1)}, bf16[4,8,768]{2,1,0:T(8,128)(2,1)S(1)}, u32[]{:S(2)}, u32[]{:S(2)}) collective-permute-start(bf16[4,8,768]{2,1,0:T(8,128)(2,1)} %param.17), channel_id=1, source_target_pairs={{0,12},{1,13},{2,14},{3,15},{4,0},{5,1},{6,2},{7,3},{8,4},{9,5},{1... | collective-permute-start | bytes 147464 | tf_op jit(solution)/shard_map/ppermute | solution.py:234
  10.6 11.3 %collective-permute-start.3 = (bf16[4,32,768]{2,1,0:T(8,128)(2,1)S(1)}, bf16[4,32,768]{2,1,0:T(8,128)(2,1)S(1)}, u32[]{:S(2)}, u32[]{:S(2)}) collective-permute-start(bf16[4,32,768]{2,1,0:T(8,128)(2,1)S(1)} %constant_dynamic-update-slice_fusion.refs_1_), channel_id=1, source_target_pairs={{0,2},{1,3},{2,0},{3,1},{4,6},{5,7},{6,4},{7,5},{8,10},{9,11},{10,... | collective-permute-start | bytes 589832 | tf_op jit(solution)/shard_map/ppermute | solution.py:234
  12.3 15.8 %collective-permute-start.4 = (bf16[4,32,768]{2,1,0:T(8,128)(2,1)S(1)}, bf16[4,32,768]{2,1,0:T(8,128)(2,1)S(1)}, u32[]{:S(2)}, u32[]{:S(2)}) collective-permute-start(bf16[4,32,768]{2,1,0:T(8,128)(2,1)S(1)} %constant_dynamic-update-slice_fusion.refs_1_), channel_id=1, source_target_pairs={{0,1},{1,0},{2,3},{3,2},{4,5},{5,4},{6,7},{7,6},{8,9},{9,8},{10,11... | collective-permute-start | bytes 589832 | tf_op jit(solution)/shard_map/ppermute | solution.py:234
  12.3 6.4 %collective-permute-start.7 = (bf16[4,8,768]{2,1,0:T(8,128)(2,1)}, bf16[4,8,768]{2,1,0:T(8,128)(2,1)S(1)}, u32[]{:S(2)}, u32[]{:S(2)}) collective-permute-start(bf16[4,8,768]{2,1,0:T(8,128)(2,1)} %param.18), channel_id=1, source_target_pairs={{0,4},{1,5},{2,6},{3,7},{4,8},{5,9},{6,10},{7,11},{8,12},{9,13},{1... | collective-permute-start | bytes 147464 | tf_op jit(solution)/shard_map/ppermute | solution.py:234
  13.8 6.9 %collective-permute-start.8 = (bf16[4,8,768]{2,1,0:T(8,128)(2,1)}, bf16[4,8,768]{2,1,0:T(8,128)(2,1)S(1)}, u32[]{:S(2)}, u32[]{:S(2)}) collective-permute-start(bf16[4,8,768]{2,1,0:T(8,128)(2,1)} %param.18), channel_id=1, source_target_pairs={{0,8},{1,9},{2,10},{3,11},{4,12},{5,13},{6,14},{7,15},{8,0},{9,1},... | collective-permute-start | bytes 147464 | tf_op jit(solution)/shard_map/ppermute | solution.py:234
  16.7 4.7 %collective-permute-start.9 = (bf16[4,8,768]{2,1,0:T(8,128)(2,1)}, bf16[4,8,768]{2,1,0:T(8,128)(2,1)S(1)}, u32[]{:S(2)}, u32[]{:S(2)}) collective-permute-start(bf16[4,8,768]{2,1,0:T(8,128)(2,1)} %param.18), channel_id=1, source_target_pairs={{0,12},{1,13},{2,14},{3,15},{4,0},{5,1},{6,2},{7,3},{8,4},{9,5},{1... | collective-permute-start | bytes 147464 | tf_op jit(solution)/shard_map/ppermute | solution.py:234
  21.4 6.6 %collective-permute-start.10 = (bf16[4,32,768]{2,1,0:T(8,128)(2,1)S(1)}, bf16[4,32,768]{2,1,0:T(8,128)(2,1)S(1)}, u32[]{:S(2)}, u32[]{:S(2)}) collective-permute-start(bf16[4,32,768]{2,1,0:T(8,128)(2,1)S(1)} %constant_dynamic-update-slice_fusion.4.refs_1_), channel_id=1, source_target_pairs={{0,2},{1,3},{2,0},{3,1},{4,6},{5,7},{6,4},{7,5},{8,10},{9,11},{10,... | collective-permute-start | bytes 589832 | tf_op jit(solution)/shard_map/ppermute | solution.py:234
  21.9 6.2 %collective-permute-start.5 = (bf16[4,32,768]{2,1,0:T(8,128)(2,1)S(1)}, bf16[4,32,768]{2,1,0:T(8,128)(2,1)S(1)}, u32[]{:S(2)}, u32[]{:S(2)}) collective-permute-start(bf16[4,32,768]{2,1,0:T(8,128)(2,1)S(1)} %collective-permute-done.3.refs_2_), channel_id=1, source_target_pairs={{0,1},{1,0},{2,3},{3,2},{4,5},{5,4},{6,7},{7,6},{8,9},{9,8},{10,11... | collective-permute-start | bytes 589832 | tf_op jit(solution)/shard_map/ppermute | solution.py:234
  22.0 13.0 %collective-permute-start.11 = (bf16[4,32,768]{2,1,0:T(8,128)(2,1)S(1)}, bf16[4,32,768]{2,1,0:T(8,128)(2,1)S(1)}, u32[]{:S(2)}, u32[]{:S(2)}) collective-permute-start(bf16[4,32,768]{2,1,0:T(8,128)(2,1)S(1)} %constant_dynamic-update-slice_fusion.4.refs_1_), channel_id=1, source_target_pairs={{0,1},{1,0},{2,3},{3,2},{4,5},{5,4},{6,7},{7,6},{8,9},{9,8},{10,11... | collective-permute-start | bytes 589832 | tf_op jit(solution)/shard_map/ppermute | solution.py:234
  28.1 7.7 %collective-permute-start.12 = (bf16[4,32,768]{2,1,0:T(8,128)(2,1)S(1)}, bf16[4,32,768]{2,1,0:T(8,128)(2,1)S(1)}, u32[]{:S(2)}, u32[]{:S(2)}) collective-permute-start(bf16[4,32,768]{2,1,0:T(8,128)(2,1)S(1)} %collective-permute-done.10.refs_2_), channel_id=1, source_target_pairs={{0,1},{1,0},{2,3},{3,2},{4,5},{5,4},{6,7},{7,6},{8,9},{9,8},{10,11... | collective-permute-start | bytes 589832 | tf_op jit(solution)/shard_map/ppermute | solution.py:234
  28.1 0.8 %copy-start.8 = (bf16[4,8,768]{2,1,0:T(8,128)(2,1)S(1)}, bf16[4,8,768]{2,1,0:T(8,128)(2,1)}, u32[]{:S(2)}) copy-start(bf16[4,8,768]{2,1,0:T(8,128)(2,1)} %refs_0_.1) | copy-start | bytes 147460
  29.2 4.2 %collective-permute-start.6 = (f32[96,128]{1,0:T(8,128)S(1)}, f32[96,128]{1,0:T(8,128)S(1)}, u32[]{:S(2)}, u32[]{:S(2)}) collective-permute-start(f32[96,128]{1,0:T(8,128)S(1)} %shard_map.140.refs_0_), channel_id=1, source_target_pairs={{0,16},{16,0},{1,17},{17,1},{2,18},{18,2},{3,19},{19,3},{4,20},{20... | collective-permute-start | bytes 147464 | tf_op jit(solution)/shard_map/ppermute | solution.py:312
  33.4 0.7 %copy-start.11 = (f32[12]{0:T(128)S(1)}, f32[12]{0:T(128)}, u32[]{:S(2)}) copy-start(f32[12]{0:T(128)} %refs_2_.2) | copy-start | bytes 148
  35.0 0.8 %copy-start.7 = (f32[16,24,128]{2,1,0:T(8,128)}, f32[16,24,128]{2,1,0:T(8,128)S(1)}, u32[]{:S(2)}) copy-start(f32[16,24,128]{2,1,0:T(8,128)S(1)} %get-tuple-element.23) | copy-start | bytes 589828
  35.0 0.7 %copy-start.3 = (bf16[4,32,768]{2,1,0:T(8,128)(2,1)}, bf16[4,32,768]{2,1,0:T(8,128)(2,1)S(1)}, u32[]{:S(2)}) copy-start(bf16[4,32,768]{2,1,0:T(8,128)(2,1)S(1)} %collective-permute-done.11.refs_3_) | copy-start | bytes 589828
  35.8 0.7 %copy-start.5 = (bf16[4,32,768]{2,1,0:T(8,128)(2,1)}, bf16[4,32,768]{2,1,0:T(8,128)(2,1)S(1)}, u32[]{:S(2)}) copy-start(bf16[4,32,768]{2,1,0:T(8,128)(2,1)S(1)} %collective-permute-done.12.refs_4_) | copy-start | bytes 589828
  36.5 0.9 %copy-start.4 = (bf16[4,32,768]{2,1,0:T(8,128)(2,1)S(1)}, bf16[4,32,768]{2,1,0:T(8,128)(2,1)}, u32[]{:S(2)}) copy-start(bf16[4,32,768]{2,1,0:T(8,128)(2,1)} %copy-done.3) | copy-start | bytes 589828
  37.4 0.9 %copy-start.6 = (bf16[4,32,768]{2,1,0:T(8,128)(2,1)S(1)}, bf16[4,32,768]{2,1,0:T(8,128)(2,1)}, u32[]{:S(2)}) copy-start(bf16[4,32,768]{2,1,0:T(8,128)(2,1)} %copy-done.5) | copy-start | bytes 589828
  38.3 0.8 %copy-start.9 = (bf16[4,8,768]{2,1,0:T(8,128)(2,1)S(1)}, bf16[4,8,768]{2,1,0:T(8,128)(2,1)}, u32[]{:S(2)}) copy-start(bf16[4,8,768]{2,1,0:T(8,128)(2,1)} %refs_6_.1) | copy-start | bytes 147460
  39.1 0.7 %copy-start.10 = (f32[1,768]{1,0:T(1,128)S(1)}, f32[1,768]{1,0:T(1,128)}, u32[]{:S(2)}) copy-start(f32[1,768]{1,0:T(1,128)} %reshape.56.refs_7_) | copy-start | bytes 9220
  39.8 5.9 %copy-start = (bf16[768,1152]{1,0:T(8,128)(2,1)S(1)}, bf16[768,1152]{1,0:T(8,128)(2,1)}, u32[]{:S(2)}) copy-start(bf16[768,1152]{1,0:T(8,128)(2,1)} %refs_2_.3) | copy-start | bytes 5308420
  40.4 5.2 %collective-permute-start.13 = (bf16[32,768]{1,0:T(8,128)(2,1)S(1)}, bf16[32,768]{1,0:T(8,128)(2,1)S(1)}, u32[]{:S(2)}, u32[]{:S(2)}) collective-permute-start(bf16[32,768]{1,0:T(8,128)(2,1)S(1)} %get-tuple-element.21.refs_0_), channel_id=1, source_target_pairs={{0,16},{16,0},{1,17},{17,1},{2,18},{18,2},{3,19},{19,3},{4,20},{20... | collective-permute-start | bytes 147464 | tf_op jit(solution)/shard_map/ppermute | solution.py:349
  42.0 4.8 %copy-start.12 = (f32[12]{0:T(128)S(1)}, f32[12]{0:T(128)}, u32[]{:S(2)}) copy-start(f32[12]{0:T(128)} %refs_2_.2) | copy-start | bytes 148
  42.0 10.2 %copy-start.2 = (bf16[768,768]{1,0:T(8,128)(2,1)S(1)}, bf16[768,768]{1,0:T(8,128)(2,1)}, u32[]{:S(2)}) copy-start(bf16[768,768]{1,0:T(8,128)(2,1)} %refs_4_.1) | copy-start | bytes 3538948
  42.0 12.6 %all-to-all-start = ((f32[16,24,128]{2,1,0:T(8,128)}), f32[16,24,128]{2,1,0:T(8,128)S(1)}, u32[]{:S(2)}, u32[]{:S(2)}) async-start(f32[16,24,128]{2,1,0:T(8,128)} %copy-done.7), calls=%async_computation | async-start | bytes 393216 | tf_op jit(solution)/shard_map/all_to_all | solution.py:331
  46.1 6.1 %collective-permute-start.14 = (bf16[64,1152]{1,0:T(8,128)(2,1)S(1)}, bf16[64,1152]{1,0:T(8,128)(2,1)S(1)}, u32[]{:S(2)}, u32[]{:S(2)}) collective-permute-start(bf16[64,1152]{1,0:T(8,128)(2,1)S(1)} %shard_map.143.refs_1_), channel_id=1, source_target_pairs={{0,16},{16,0},{1,17},{17,1},{2,18},{18,2},{3,19},{19,3},{4,20},{20... | collective-permute-start | bytes 442376 | tf_op jit(solution)/shard_map/ppermute | solution.py:360

commit v3 on v2

--- a/solution.py
+++ b/solution.py
@@ -35,30 +35,76 @@
     return LANE_BLOCK if embed % LANE_BLOCK == 0 and LANE_BLOCK % head == 0 else head
 
 
-def logits_kernel(head, part_count, *refs):
-    q_ref, k_refs, out_ref = refs[0], refs[1 : 1 + part_count], refs[-1]
+def arrival_place(index, column, stages, sites):
+    block, place, span = column // sites, column % sites, 1
+    for stride, size in stages:
+        digit = (block // span) % size
+        place = place + ((index // stride) % size + size - digit) % size * (stride * sites)
+        span *= size
+    return place
+
+
+def prepare_kernel(head, stages, scalar_ref, q_ref, skip_ref, gain_ref, factor_ref, *outs):
+    masked_ref, wide_skip_ref, wide_gain_ref, head_ref, order_ref, turn_ref, own_ref, slab_ref = outs
     rows, sites, embed = q_ref.shape
-    width = lane_block(embed, head)
+    heads = embed // head
+    width = masked_ref.shape[2]
     group = width // head
-    lane_head = lax.broadcasted_iota(jnp.int32, (group * sites, width), 1) // head
-    row_head = lax.broadcasted_iota(jnp.int32, (group * sites, width), 0) // sites
+    span = group * sites
+    lane_head = lax.broadcasted_iota(jnp.int32, (span, width), 1) // head
+    row_head = lax.broadcasted_iota(jnp.int32, (span, width), 0) // sites
     own_head = lane_head == row_head
     for block in range(embed // width):
+        for r in range(rows):
+            q = q_ref[r, :, block * width : (block + 1) * width].astype(F32)
+            q = jnp.where(own_head, jnp.concatenate([q] * group, axis=0), 0.0).astype(BF16)
+            masked_ref[r, block * span : (block + 1) * span, :] = q
+    wide_skip_ref[...] = skip_ref[...].astype(F32).reshape(rows * sites, embed)
+    wide_gain_ref[...] = jnp.broadcast_to(gain_ref[...], wide_gain_ref.shape)
+    row = lax.broadcasted_iota(jnp.int32, head_ref.shape, 0)
+    factors = jnp.zeros(head_ref.shape, F32)
+    for h in range(heads):
+        factors = jnp.where(row == h, factor_ref[h], factors)
+    head_ref[...] = factors
+    seq_index, pos_index = scalar_ref[0], scalar_ref[1]
+    length = order_ref.shape[0]
+    row = lax.broadcasted_iota(jnp.int32, (length, length), 0)
+    lane = lax.broadcasted_iota(jnp.int32, (length, length), 1)
+    order_ref[...] = (arrival_place(pos_index, row, stages, sites) == lane).astype(F32)
+    if len(stages) > 1:
+        outer, middle = stages[0][1], stages[1][1]
+        block, inside = row // sites, row % sites
+        first, second, rest = block % outer, (block // outer) % middle, block // (outer * middle)
+        turned = (rest * outer * middle + first * middle + second) * sites + inside
+    else:
+        turned = row
+    turn_ref[...] = (turned == lane).astype(BF16)
+    row = lax.broadcasted_iota(jnp.int32, own_ref.shape, 0)
+    lane = lax.broadcasted_iota(jnp.int32, own_ref.shape, 1)
+    own_ref[...] = (row + pos_index * sites == lane).astype(F32)
+    row = lax.broadcasted_iota(jnp.int32, slab_ref.shape, 0)
+    lane = lax.broadcasted_iota(jnp.int32, slab_ref.shape, 1)
+    slab_ref[...] = (row == lane + seq_index * slab_ref.shape[1]).astype(F32)
+
+
+def logits_kernel(part_count, *refs):
+    q_ref, k_refs, done_refs, out_ref = refs[0], refs[1 : 1 + part_count], refs[1 + part_count : -1], refs[-1]
+    rows, _, width = q_ref.shape
+    blocks = k_refs[0].shape[2] // width
+    span = q_ref.shape[1] // blocks
+    for block in range(blocks):
         cols = slice(block * width, (block + 1) * width)
+        lines = slice(block * span, (block + 1) * span)
         total = None
         for r in range(rows):
-            q = q_ref[r, :, cols].astype(F32)
-            q = jnp.where(own_head, jnp.concatenate([q] * group, axis=0), 0.0).astype(BF16)
             keys = jnp.concatenate([k[r, :, cols] for k in k_refs], axis=0)
-            term = dot_nt(q, keys)
+            term = dot_nt(q_ref[r, lines, :], keys)
             total = term if total is None else total + term
-        out_ref[block * group * sites : (block + 1) * group * sites, :] = total
-
-
-def softmax_kernel(factor, heads, part_count, *refs):
-    parts, (factor_ref, order_ref, w_ref, pair_ref, held) = refs[:part_count], refs[part_count:]
-    rows, length = w_ref.shape
-    sites = rows // heads
+        out_ref[lines, :] = jnp.concatenate([done[lines, :] for done in done_refs] + [total], axis=1)
+
+
+def softmax_kernel(factor, *refs):
+    parts, (turn_ref, w_ref, turned_ref) = refs[:-3], refs[-3:]
     logits = parts[0][...]
     for part in parts[1:]:
         logits = logits + part[...]
@@ -66,7 +112,13 @@
     exponent = jnp.exp(logits - jnp.max(logits, axis=1, keepdims=True))
     shares = (exponent / jnp.sum(exponent, axis=1, keepdims=True)).astype(BF16)
     w_ref[...] = shares
-    shares = shares.astype(F32)
+    turned_ref[...] = dot_nn(shares, turn_ref[...]).astype(BF16)
+
+
+def pair_kernel(heads, w_ref, head_ref, order_ref, pair_ref, held):
+    rows, length = w_ref.shape
+    sites = rows // heads
+    shares = w_ref[...].astype(F32)
     row_sum = jnp.sum(shares, axis=1, keepdims=True)
     lane = lax.broadcasted_iota(jnp.int32, (rows, length), 1)
     row = lax.broadcasted_iota(jnp.int32, (rows, length), 0) % sites
@@ -74,9 +126,10 @@
     head_rows = round_up(heads, 8)
     held[...] = jnp.zeros_like(held)
     held[0:heads, :] = jnp.sum(both, axis=1)
-    merged = shares[0:sites, :] * factor_ref[0]
-    for h in range(1, heads):
-        merged = merged + shares[h * sites : (h + 1) * sites, :] * factor_ref[h]
+    merged = None
+    for h in range(heads):
+        term = shares[h * sites : (h + 1) * sites, :] * head_ref[h : h + 1, 0:1]
+        merged = term if merged is None else merged + term
     held[head_rows : head_rows + sites, :] = merged
     pair_ref[...] = jnp.broadcast_to(
         dot_nn(held[...], order_ref[...], HIGHEST)[None], pair_ref.shape
@@ -86,7 +139,8 @@
 def mix_kernel(head, v_count, *refs):
     w_ref, v_refs = refs[0], refs[1 : 1 + v_count]
     closing_ref, skip_ref, gain_ref, hidden_ref, normed_ref, mixed = refs[1 + v_count :]
-    rows, sites, embed = skip_ref.shape
+    rows, _, embed = v_refs[0].shape
+    sites = skip_ref.shape[0] // rows
     width = lane_block(embed, head)
     group = width // head
     lane_head = lax.broadcasted_iota(jnp.int32, (sites, width), 1) // head
@@ -100,13 +154,11 @@
             for g in range(1, group):
                 own = jnp.where(lane_head == g, product[g * sites : (g + 1) * sites, :], own)
             mixed[r * sites : (r + 1) * sites, cols] = own
-    hidden = skip_ref[...].astype(F32).reshape(rows * sites, embed) + dot_nn(
-        mixed[...].astype(BF16), closing_ref[...]
-    )
+    hidden = skip_ref[...] + dot_nn(mixed[...].astype(BF16), closing_ref[...])
     hidden_ref[...] = hidden
     centered = hidden - jnp.mean(hidden, axis=1, keepdims=True)
     spread = jnp.mean(centered * centered, axis=1, keepdims=True)
-    normed_ref[...] = (centered * lax.rsqrt(spread + 1e-05) * gain_ref[...]).astype(BF16)
+    normed_ref[...] = (centered * lax.rsqrt(spread + 1e-05) * gain_ref[0:1, :]).astype(BF16)
 
 
 def project_kernel(part_count, *refs):
@@ -200,6 +252,9 @@
 
 def call(kernel, out_shape, operands, smem=(), scratch=(), flops=1000000, bytes_accessed=1000000):
     vmem = pl.BlockSpec(memory_space=pltpu.VMEM)
+    held = sum(math.prod(a.shape) * a.dtype.itemsize for a in [*operands, *jax.tree.leaves(out_shape)])
+    held += sum(math.prod(a.shape) * np.dtype(a.dtype).itemsize for a in scratch)
+    limit = 2 * held + 4 * 1024 * 1024
     specs = [
         pl.BlockSpec(memory_space=pltpu.SMEM) if i in smem else vmem for i in range(len(operands))
     ]
@@ -209,7 +264,7 @@
         in_specs=specs,
         out_specs=jax.tree.map(lambda _: vmem, out_shape),
         scratch_shapes=list(scratch),
-        compiler_params=pltpu.CompilerParams(vmem_limit_bytes=24 * 1024 * 1024),
+        compiler_params=pltpu.CompilerParams(vmem_limit_bytes=limit),
         cost_estimate=pl.CostEstimate(
             flops=flops, bytes_accessed=bytes_accessed, transcendentals=0
         ),
@@ -234,28 +289,9 @@
     return lax.ppermute(array, "pos", pairs)
 
 
-def staged_gather(array, axis, count):
-    parts = [array]
-    for at, (stride, size) in enumerate(stages_of(count)):
-        if at == 1:
-            parts = [jnp.concatenate(parts, axis=axis)]
-        parts = parts + [
-            send_pos(part, count, stride, size, delta)
-            for delta in range(1, size)
-            for part in parts
-        ]
-    return parts
-
-
-def arrival_order(index, count):
-    digits = [()]
-    for stage in stages_of(count):
-        digits = [d + (delta,) for delta in range(stage[1]) for d in digits]
-    origin = jnp.zeros((count,), jnp.int32)
-    for at, (stride, size) in enumerate(stages_of(count)):
-        delta = np.array([d[at] for d in digits], np.int32)
-        origin = origin + ((index // stride) % size + size - delta) % size * stride
-    return origin
+def send_all(parts, count, stage):
+    stride, size = stage
+    return [send_pos(part, count, stride, size, delta) for delta in range(1, size) for part in parts]
 
 
 def after(array, *others):
@@ -288,47 +324,78 @@
     columns = upright_threefold_linear.shape[1]
     swapped = seq_count == 2 and columns % 128 == 0
 
-    key_parts = staged_gather(lateral_matched_vectors, 1, pos_count)
-    value_parts = staged_gather(
-        after(lateral_carried_vectors, key_parts[0]), 1, pos_count
-    )
-
-    origin = arrival_order(pos_index, pos_count)
-    place = (origin[:, None] * sites + jnp.arange(sites, dtype=jnp.int32)[None, :]).reshape(length)
-    every = jnp.arange(length, dtype=jnp.int32)
-    slab_at = seq_index * slab_width + jnp.arange(slab_width, dtype=jnp.int32)
-    order = (place[:, None] == every[None, :]).astype(F32)
-    own_rows = pos_index * sites + jnp.arange(sites, dtype=jnp.int32)
-    own_select = (own_rows[:, None] == every[None, :]).astype(F32)
-    slab_select = (every[:, None] == slab_at[None, :]).astype(F32)
+    stages = stages_of(pos_count)
+    outer = stages[0]
+    middle = stages[1] if len(stages) > 1 else None
+
     scalars = jnp.stack([seq_index, pos_index])
-
+    head_rows = round_up(heads, 8)
+    width = lane_block(embed, head)
+    masked, skip, gain, head_factors, order, turn, own_select, slab_select = call(
+        functools.partial(prepare_kernel, head, stages),
+        (
+            jax.ShapeDtypeStruct((rows, heads * sites, width), BF16),
+            jax.ShapeDtypeStruct((cells, embed), F32),
+            jax.ShapeDtypeStruct((8, embed), F32),
+            jax.ShapeDtypeStruct((head_rows, 128), F32),
+            jax.ShapeDtypeStruct((length, length), F32),
+            jax.ShapeDtypeStruct((length, length), BF16),
+            jax.ShapeDtypeStruct((sites, length), F32),
+            jax.ShapeDtypeStruct((length, slab_width), F32),
+        ),
+        [
+            scalars,
+            lateral_asking_vectors,
+            skip_stream_input,
+            upright_normalizer_multiplier.reshape(1, embed),
+            regression_factors,
+        ],
+        smem=(0, 4),
+    )
+
+    value_first = [lateral_carried_vectors]
+    if middle:
+        value_first += send_all(value_first, pos_count, middle)
+    key_first = [lateral_matched_vectors]
+    key_first += send_all(key_first, pos_count, outer)
+    key_first[-1] = after(key_first[-1], value_first[-1], masked)
+    key_parts = [jnp.concatenate(key_first, axis=1)]
+    if middle:
+        key_parts += send_all(key_parts, pos_count, middle)
+    value_parts = [after(jnp.concatenate(value_first, axis=1), key_parts[0])]
+    value_outer = send_all(value_parts, pos_count, outer)
+
+    near = sum(part.shape[1] for part in key_parts)
     partial = call(
-        functools.partial(logits_kernel, head, len(key_parts)),
-        jax.ShapeDtypeStruct((heads * sites, length), F32),
-        [lateral_asking_vectors, *key_parts],
-    )
+        functools.partial(logits_kernel, len(key_parts)),
+        jax.ShapeDtypeStruct((heads * sites, near), F32),
+        [masked, *key_parts],
+        bytes_accessed=20000000,
+    )
+    if len(stages) > 2:
+        far_parts = send_all(key_parts, pos_count, stages[2])
+        partial = call(
+            functools.partial(logits_kernel, len(far_parts)),
+            jax.ShapeDtypeStruct((heads * sites, length), F32),
+            [masked, *far_parts, partial],
+        )
     if seq_count == 2:
         partials = [partial, lax.ppermute(partial, "seq", swap)]
     else:
         partials = [lax.psum(partial, "seq")]
-    head_rows = round_up(heads, 8)
-    shares, pair_local = call(
+    value_parts += [after(part, partials[-1]) for part in value_outer]
+    if len(stages) > 2:
+        value_parts += send_all(value_parts, pos_count, stages[2])
+    shares, shares_turned = call(
         functools.partial(
-            softmax_kernel,
-            1.0 / (math.sqrt(head) * math.sqrt(rows * seq_count)),
-            heads,
-            len(partials),
+            softmax_kernel, 1.0 / (math.sqrt(head) * math.sqrt(rows * seq_count))
         ),
         (
             jax.ShapeDtypeStruct((heads * sites, length), BF16),
-            jax.ShapeDtypeStruct((pos_count, head_rows + sites, length), F32),
+            jax.ShapeDtypeStruct((heads * sites, length), BF16),
         ),
-        [*partials, regression_factors, order],
-        smem=(len(partials),),
-        scratch=[pltpu.VMEM((head_rows + sites, length), F32)],
-    )
-    pair_all = lax.all_to_all(pair_local, "pos", split_axis=0, concat_axis=0, tiled=True)
+        [*partials, turn],
+    )
 
     hidden, normed = call(
         functools.partial(mix_kernel, head, len(value_parts)),
@@ -336,14 +403,22 @@
             jax.ShapeDtypeStruct((cells, embed), F32),
             jax.ShapeDtypeStruct((cells, embed), BF16),
         ),
-        [
-            shares,
-            *value_parts,
-            lateral_closing_linear,
-            skip_stream_input,
-            upright_normalizer_multiplier.reshape(1, embed),
-        ],
+        [shares_turned, *value_parts, lateral_closing_linear, skip, gain],
         scratch=[pltpu.VMEM((cells, embed), F32)],
+    )
+    pair_local = call(
+        functools.partial(pair_kernel, heads),
+        jax.ShapeDtypeStruct((pos_count, head_rows + sites, length), F32),
+        [after(shares, normed), head_factors, order],
+        scratch=[pltpu.VMEM((head_rows + sites, length), F32)],
+    )
+    pair_all = lax.all_to_all(pair_local, "pos", split_axis=0, concat_axis=0, tiled=True)
+    pairing_chances = call(
+        functools.partial(contact_kernel, heads),
+        jax.ShapeDtypeStruct((sites, slab_width), F32),
+        [scalars, pair_all, head_factors, regression_offset, own_select, slab_select],
+        smem=(0, 3),
+        scratch=[pltpu.VMEM((head_rows + sites, length), F32)],
     )
     if swapped:
         normed_all = [normed, lax.ppermute(normed, "seq", swap)]
@@ -370,19 +445,11 @@
     alignment_output = call(
         functools.partial(column_kernel, head, 1.0 / math.sqrt(head), swapped),
         jax.ShapeDtypeStruct((rows, sites, embed), BF16),
-        [*column_inputs, hidden, upright_closing_linear],
+        [*column_inputs, after(hidden, pairing_chances), upright_closing_linear],
         smem=(0,) if swapped else (),
         scratch=scratch,
     )
 
-    factor_column = jnp.zeros((head_rows, 128), F32).at[:heads, :].set(regression_factors[:, None])
-    pairing_chances = call(
-        functools.partial(contact_kernel, heads),
-        jax.ShapeDtypeStruct((sites, slab_width), F32),
-        [scalars, pair_all, factor_column, regression_offset, own_select, slab_select],
-        smem=(0, 3),
-        scratch=[pltpu.VMEM((head_rows + sites, length), F32)],
-    )
     return alignment_output, pairing_chances
 
 

time: 56.9 us -> 53.4 us (0.938)
  local copies, waits for them, and re-layouts: 9.33 us -> 3.77 us
  starting transfers between devices: 21 us -> 22.4 us
  Pallas kernels: 5.98 us -> 7.13 us
    unnamed x32 -> x15, local copies, waits for them, and re-layouts: 7.9 us -> 3.08 us
    ppermute x1, waiting for transfers between devices: 4.69 us -> 0.01 us  [per_device(): column_inputs = [scalars, projected, lax.ppermute(projected, 'seq', swap)]]
    ppermute x1, waiting for transfers between devices: 0.01 us -> 2.6 us  [per_device(): normed_all = [normed, lax.ppermute(normed, 'seq', swap)]]
    all_to_all x1, waiting for transfers between devices: 0.38 us -> 2.16 us  [per_device(): lax.all_to_all(pair_local, 'pos', split_axis=0, concat_axis=0, tiled=True)]
    ppermute x1, waiting for transfers between devices: 1.37 us -> 2.59 us  [per_device(): partials = [partial, lax.ppermute(partial, 'seq', swap)]]
    pallas_call x6 -> x9, Pallas kernels: 5.98 us -> 7.13 us  [call(): pl.pallas_call(kernel, out_shape=out_shape, in_specs=specs, out_specs=jax...]
    ppermute x12 -> x14, waiting for transfers between devices: 11.1 us -> 10 us  [send_pos(): return lax.ppermute(array, 'pos', pairs)]
    ppermute x1, starting transfers between devices: 0.6 us -> 1.55 us  [per_device(): column_inputs = [scalars, projected, lax.ppermute(projected, 'seq', swap)]]
  transfers between devices with their start and end apart: 16 -> 18, of which waited for: 9 -> 7; matrix products, arithmetic and copies ran while one was open for 7% -> 4% of each run, Pallas kernels for 7% -> 7%
where the time goes in v3:
time: 53.4 us; the launch traced here: 53 us
  starting transfers between devices  22.4 us (42%)
  waiting for transfers between devices  17.4 us (33%)
  Pallas kernels  7.13 us (13%)
  local copies, waits for them, and re-layouts  3.77 us (7%)
  between operations  1.43 us (3%)
  other arithmetic  0.88 us (2%)
    ppermute x14, starting transfers between devices, send_pos(): return lax.ppermute(array, 'pos', pairs)  14.2 us
    ppermute x14, waiting for transfers between devices, send_pos(): return lax.ppermute(array, 'pos', pairs)  10 us
    pallas_call x9, Pallas kernels, call(): pl.pallas_call(kernel, out_shape=out_shape, in_specs=specs, out_specs=jax...  7.13 us
    all_to_all x1, starting transfers between devices, per_device(): lax.all_to_all(pair_local, 'pos', split_axis=0, concat_axis=0, tiled=True)  3.52 us
    unnamed x15, local copies, waits for them, and re-layouts  3.08 us
    ppermute x1, waiting for transfers between devices, per_device(): normed_all = [normed, lax.ppermute(normed, 'seq', swap)]  2.6 us
    ppermute x1, waiting for transfers between devices, per_device(): partials = [partial, lax.ppermute(partial, 'seq', swap)]  2.59 us
    all_to_all x1, waiting for transfers between devices, per_device(): lax.all_to_all(pair_local, 'pos', split_axis=0, concat_axis=0, tiled=True)  2.16 us
  transfers between devices with their start and end apart: 18, of which 7 were waited for; matrix products, arithmetic and copies ran while one was open for 4% of the time, Pallas kernels for 7%

profile of v3, /device:TPU:0, one launch (start us, length us, event | category | flops | bytes accessed | tf_op | source)
XLA Modules:
  0.0 53.0 jit_solution(14736617223427361674)
XLA Ops:
  0.6 5.1 %collective-permute-start.2 = (bf16[4,8,768]{2,1,0:T(8,128)(2,1)}, bf16[4,8,768]{2,1,0:T(8,128)(2,1)S(1)}, u32[]{:S(2)}, u32[]{:S(2)}) collective-permute-start(bf16[4,8,768]{2,1,0:T(8,128)(2,1)} %param.12), channel_id=1, source_target_pairs={{0,12},{1,13},{2,14},{3,15},{4,0},{5,1},{6,2},{7,3},{8,4},{9,5},{1... | collective-permute-start | bytes 147464 | tf_op jit(solution)/shard_map/ppermute | solution.py:289
  5.7 1.0 %collective-permute-start.1 = (bf16[4,8,768]{2,1,0:T(8,128)(2,1)}, bf16[4,8,768]{2,1,0:T(8,128)(2,1)S(1)}, u32[]{:S(2)}, u32[]{:S(2)}) collective-permute-start(bf16[4,8,768]{2,1,0:T(8,128)(2,1)} %param.12), channel_id=1, source_target_pairs={{0,8},{1,9},{2,10},{3,11},{4,12},{5,13},{6,14},{7,15},{8,0},{9,1},... | collective-permute-start | bytes 147464 | tf_op jit(solution)/shard_map/ppermute | solution.py:289
  6.8 1.5 %collective-permute-start.3 = (bf16[4,8,768]{2,1,0:T(8,128)(2,1)}, bf16[4,8,768]{2,1,0:T(8,128)(2,1)S(1)}, u32[]{:S(2)}, u32[]{:S(2)}) collective-permute-start(bf16[4,8,768]{2,1,0:T(8,128)(2,1)} %param.13), channel_id=1, source_target_pairs={{0,2},{1,3},{2,0},{3,1},{4,6},{5,7},{6,4},{7,5},{8,10},{9,11},{10,... | collective-permute-start | bytes 147464 | tf_op jit(solution)/shard_map/ppermute | solution.py:289
  8.3 0.8 %constant_dynamic-update-slice_fusion.3 = bf16[4,32,768]{2,1,0:T(8,128)(2,1)S(1)} fusion(bf16[4,8,768]{2,1,0:T(8,128)(2,1)} %param.12), kind=kLoop, calls=%fused_computation.4 | loop fusion | bytes 98304
  9.1 0.1 pad_add_fusion.scalar_ref.refs_0_
  9.2 0.7 %reshape.7.gain_ref = f32[1,768]{1,0:T(1,128)S(1)} reshape(f32[768]{0:T(1024)} %param.15) | data formatting | bytes 6144 | tf_op jit(solution)/shard_map/reshape | solution.py:350
  9.8 0.8 %copy-done.3 = bf16[4,8,768]{2,1,0:T(8,128)(2,1)S(1)} copy-done((bf16[4,8,768]{2,1,0:T(8,128)(2,1)S(1)}, bf16[4,8,768]{2,1,0:T(8,128)(2,1)}, u32[]{:S(2)}) %copy-start.3) | copy-done | bytes 49176
  10.6 0.8 %copy-done.4 = bf16[4,8,768]{2,1,0:T(8,128)(2,1)S(1)} copy-done((bf16[4,8,768]{2,1,0:T(8,128)(2,1)S(1)}, bf16[4,8,768]{2,1,0:T(8,128)(2,1)}, u32[]{:S(2)}) %copy-start.4) | copy-done | bytes 49176
  11.4 0.7 %copy-done.5 = f32[12]{0:T(128)S(1)} copy-done((f32[12]{0:T(128)S(1)}, f32[12]{0:T(128)}, u32[]{:S(2)}) %copy-start.5) | copy-done | bytes 72
  12.1 0.7 %shard_map.113 = (bf16[4,96,256]{2,1,0:T(8,128)(2,1)S(1)}, f32[32,768]{1,0:T(8,128)S(1)}, f32[8,768]{1,0:T(8,128)S(1)}, f32[16,128]{1,0:T(8,128)S(1)}, f32[128,1...) custom-call(s32[2]{0:T(128)S(1)} %pad_add_fusion.scalar_ref.refs_0_, ...), custom_call_target="tpu_custom_call" | custom-call | flops 1000000 | bytes 1000000 | tf_op jit(solution)/shard_map/pallas_call | solution.py:261
  12.8 0.0 collective-permute-done
  12.9 0.0 collective-permute-done.1
  12.9 1.2 %collective-permute-start.5 = (bf16[4,32,768]{2,1,0:T(8,128)(2,1)S(1)}, bf16[4,32,768]{2,1,0:T(8,128)(2,1)S(1)}, u32[]{:S(2)}, u32[]{:S(2)}) collective-permute-start(bf16[4,32,768]{2,1,0:T(8,128)(2,1)S(1)} %constant_dynamic-update-slice_fusion.refs_1_), channel_id=1, source_target_pairs={{0,2},{1,3},{2,0},{3,1},{4,6},{5,7},{6,4},{7,5},{8,10},{9,11},{10,... | collective-permute-start | bytes 589832 | tf_op jit(solution)/shard_map/ppermute | solution.py:289
  14.1 0.0 collective-permute-start.4
  14.1 4.5 %collective-permute-done.5.refs_2_ = bf16[4,32,768]{2,1,0:T(8,128)(2,1)S(1)} collective-permute-done((bf16[4,32,768]{2,1,0:T(8,128)(2,1)S(1)}, bf16[4,32,768]{2,1,0:T(8,128)(2,1)S(1)}, u32[]{:S(2)}, u32[]{:S(2)}) %collective-permute-start.5) | collective-permute-done | bytes 196640 | tf_op jit(solution)/shard_map/ppermute | solution.py:289
  18.7 0.0 collective-permute-start.6
  18.7 0.8 %pad_maximum_fusion.refs_1_ = bf16[4,16,768]{2,1,0:T(8,128)(2,1)S(1)} fusion(bf16[4,8,768]{2,1,0:T(8,128)(2,1)S(1)} %collective-permute-done.3, bf16[4,8,768]{2,1,0:T(8,128)(2,1)} %param.13), kind=kLoop, calls=%fused_computation | loop fusion | flops 196608 | bytes 196608 | tf_op jit(solution)/shard_map/concatenate | solution.py:365
  19.5 2.9 %collective-permute-start.10 = (bf16[4,16,768]{2,1,0:T(8,128)(2,1)S(1)}, bf16[4,16,768]{2,1,0:T(8,128)(2,1)S(1)}, u32[]{:S(2)}, u32[]{:S(2)}) collective-permute-start(bf16[4,16,768]{2,1,0:T(8,128)(2,1)S(1)} %pad_maximum_fusion.refs_1_), channel_id=1, source_target_pairs={{0,12},{1,13},{2,14},{3,15},{4,0},{5,1},{6,2},{7,3},{8,4},{9,5},{1... | collective-permute-start | bytes 294920 | tf_op jit(solution)/shard_map/ppermute | solution.py:289
  22.4 1.9 %collective-permute-start.9 = (bf16[4,16,768]{2,1,0:T(8,128)(2,1)S(1)}, bf16[4,16,768]{2,1,0:T(8,128)(2,1)S(1)}, u32[]{:S(2)}, u32[]{:S(2)}) collective-permute-start(bf16[4,16,768]{2,1,0:T(8,128)(2,1)S(1)} %pad_maximum_fusion.refs_1_), channel_id=1, source_target_pairs={{0,8},{1,9},{2,10},{3,11},{4,12},{5,13},{6,14},{7,15},{8,0},{9,1},... | collective-permute-start | bytes 294920 | tf_op jit(solution)/shard_map/ppermute | solution.py:289
  24.3 0.2 shard_map.114.refs_3_
  24.5 0.0 collective-permute-done.4.refs_1_
  24.5 0.0 collective-permute-done.6.refs_2_
  24.6 0.3 shard_map.115.refs_0_
  24.8 1.6 %collective-permute-start.7 = (f32[96,128]{1,0:T(8,128)S(1)}, f32[96,128]{1,0:T(8,128)S(1)}, u32[]{:S(2)}, u32[]{:S(2)}) collective-permute-start(f32[96,128]{1,0:T(8,128)S(1)} %shard_map.115.refs_0_), channel_id=1, source_target_pairs={{0,16},{16,0},{1,17},{17,1},{2,18},{18,2},{3,19},{19,3},{4,20},{20... | collective-permute-start | bytes 147464 | tf_op jit(solution)/shard_map/ppermute | solution.py:383
  26.4 0.0 collective-permute-start.11
  26.4 0.0 collective-permute-done.10.refs_4_
  26.4 2.6 %collective-permute-done.7.refs_1_ = f32[96,128]{1,0:T(8,128)S(1)} collective-permute-done((f32[96,128]{1,0:T(8,128)S(1)}, f32[96,128]{1,0:T(8,128)S(1)}, u32[]{:S(2)}, u32[]{:S(2)}) %collective-permute-start.7) | collective-permute-done | bytes 49184 | tf_op jit(solution)/shard_map/ppermute | solution.py:383
  29.0 0.0 collective-permute-start.14
  29.0 4.8 %collective-permute-done.9.refs_3_ = bf16[4,16,768]{2,1,0:T(8,128)(2,1)S(1)} collective-permute-done((bf16[4,16,768]{2,1,0:T(8,128)(2,1)S(1)}, bf16[4,16,768]{2,1,0:T(8,128)(2,1)S(1)}, u32[]{:S(2)}, u32[]{:S(2)}) %collective-permute-start.9) | collective-permute-done | bytes 98336 | tf_op jit(solution)/shard_map/ppermute | solution.py:289
  33.8 0.0 collective-permute-done.8.refs_2_
  33.8 0.5 collective-permute-start.12
  34.3 0.3 shard_map.116
  34.6 0.0 collective-permute-done.11.refs_5_
  34.6 0.0 collective-permute-done.14.refs_8_
  34.6 0.5 collective-permute-done.13.refs_7_
  35.1 0.2 collective-permute-done.12.refs_6_
  35.3 0.6 %shard_map.117 = (f32[32,768]{1,0:T(8,128)S(1)}, bf16[32,768]{1,0:T(8,128)(2,1)S(1)}) custom-call(bf16[96,128]{1,0:T(8,128)(2,1)S(1)} %get-tuple-element.24.refs_0_, bf16[4,16,768]{2,1,0:T(8,128)(2,1)S(1)} %pad_maximum_fusion.refs_1_, bf16[4,16,768]{2,1,0:T(8,128)(2,1)S(1)} %collective-permute-done.8.refs_2_, ...), custom_call_target="tpu_custom_call" | custom-call | flops 1000000 | bytes 1000000 | tf_op jit(solution)/shard_map/pallas_call | solution.py:261
  35.9 0.9 %shard_map.119 = f32[16,24,128]{2,1,0:T(8,128)} custom-call(bf16[96,128]{1,0:T(8,128)(2,1)S(1)} %get-tuple-element.34.w_ref, f32[16,128]{1,0:T(8,128)S(1)} %get-tuple-element.35.head_ref.factor_ref, f32[128,128]{1,0:T(8,128)S(1)} %get-tuple-element.36.order_ref), custom_call_target="tpu_custom_call" | custom-call | flops 1000000 | bytes 1000000 | tf_op jit(solution)/shard_map/pallas_call | solution.py:261
  36.8 3.5 %all-to-all-start = ((f32[16,24,128]{2,1,0:T(8,128)}), f32[16,24,128]{2,1,0:T(8,128)S(1)}, u32[]{:S(2)}, u32[]{:S(2)}) async-start(f32[16,24,128]{2,1,0:T(8,128)} %shard_map.119), calls=%async_computation | async-start | bytes 393216 | tf_op jit(solution)/shard_map/all_to_all | solution.py:415
  40.4 0.0 copy-start.1
  40.4 1.6 %collective-permute-start.15 = (bf16[32,768]{1,0:T(8,128)(2,1)S(1)}, bf16[32,768]{1,0:T(8,128)(2,1)S(1)}, u32[]{:S(2)}, u32[]{:S(2)}) collective-permute-start(bf16[32,768]{1,0:T(8,128)(2,1)S(1)} %get-tuple-element.31.refs_0_), channel_id=1, source_target_pairs={{0,16},{16,0},{1,17},{17,1},{2,18},{18,2},{3,19},{19,3},{4,20},{20... | collective-permute-start | bytes 147464 | tf_op jit(solution)/shard_map/ppermute | solution.py:424
  41.9 2.6 %collective-permute-done.15.refs_1_ = bf16[32,768]{1,0:T(8,128)(2,1)S(1)} collective-permute-done((bf16[32,768]{1,0:T(8,128)(2,1)S(1)}, bf16[32,768]{1,0:T(8,128)(2,1)S(1)}, u32[]{:S(2)}, u32[]{:S(2)}) %collective-permute-start.15) | collective-permute-done | bytes 49184 | tf_op jit(solution)/shard_map/ppermute | solution.py:424
  44.5 0.4 shard_map.118.refs_1_
  45.0 1.6 %collective-permute-start.16 = (bf16[64,1152]{1,0:T(8,128)(2,1)S(1)}, bf16[64,1152]{1,0:T(8,128)(2,1)S(1)}, u32[]{:S(2)}, u32[]{:S(2)}) collective-permute-start(bf16[64,1152]{1,0:T(8,128)(2,1)S(1)} %shard_map.118.refs_1_), channel_id=1, source_target_pairs={{0,16},{16,0},{1,17},{17,1},{2,18},{18,2},{3,19},{19,3},{4,20},{20... | collective-permute-start | bytes 442376 | tf_op jit(solution)/shard_map/ppermute | solution.py:435
  47.2 2.2 %all-to-all-done.pair_ref = f32[16,24,128]{2,1,0:T(8,128)S(1)} async-done(((f32[16,24,128]{2,1,0:T(8,128)}), f32[16,24,128]{2,1,0:T(8,128)S(1)}, u32[]{:S(2)}, u32[]{:S(2)}) %all-to-all-start) | async-done | bytes 196640 | tf_op jit(solution)/shard_map/all_to_all | solution.py:415
  49.3 1.6 %shard_map.120 = f32[8,64]{1,0:T(8,128)} custom-call(s32[2]{0:T(128)S(1)} %pad_add_fusion.scalar_ref.refs_0_, f32[16,24,128]{2,1,0:T(8,128)S(1)} %all-to-all-done.pair_ref, f32[16,128]{1,0:T(8,128)S(1)} %get-tuple-element.35.head_ref.factor_ref, f32[1]{0:T(128)S(6)} %copy.15.offset_ref, f32[8,128]{1,0:T(8,128)S(1)} %get-tuple-element.37.own_ref, ...), custom_call_target="tpu_custom_call" | custom-call | flops 1000000 | bytes 1000000 | tf_op jit(solution)/shard_map/pallas_call | solution.py:261
  50.9 0.0 collective-permute-done.16.refs_2_
  50.9 2.0 %shard_map.121 = bf16[4,8,768]{2,1,0:T(8,128)(2,1)} custom-call(s32[2]{0:T(128)S(1)} %pad_add_fusion.scalar_ref.refs_0_, bf16[64,1152]{1,0:T(8,128)(2,1)S(1)} %shard_map.118.refs_1_, bf16[64,1152]{1,0:T(8,128)(2,1)S(1)} %collective-permute-done.16.refs_2_, f32[32,768]{1,0:T(8,128)S(1)} %get-tuple-element.39.refs_3_, bf16[768,768]{1,0:T(8,128)(2,1)S(1)} %copy-done.1), custom_call_target="tpu_custom_call" | custom-call | flops 1000000 | bytes 1000000 | tf_op jit(solution)/shard_map/pallas_call | solution.py:261
  (16 shorter events, 0.0 us)
Async XLA Ops:
  0.6 34.6 %copy-start.2 = (bf16[768,768]{1,0:T(8,128)(2,1)S(1)}, bf16[768,768]{1,0:T(8,128)(2,1)}, u32[]{:S(2)}) copy-start(bf16[768,768]{1,0:T(8,128)(2,1)} %refs_9_.1) | copy-start | bytes 3538948
  0.6 12.2 %collective-permute-start.2 = (bf16[4,8,768]{2,1,0:T(8,128)(2,1)}, bf16[4,8,768]{2,1,0:T(8,128)(2,1)S(1)}, u32[]{:S(2)}, u32[]{:S(2)}) collective-permute-start(bf16[4,8,768]{2,1,0:T(8,128)(2,1)} %param.12), channel_id=1, source_target_pairs={{0,12},{1,13},{2,14},{3,15},{4,0},{5,1},{6,2},{7,3},{8,4},{9,5},{1... | collective-permute-start | bytes 147464 | tf_op jit(solution)/shard_map/ppermute | solution.py:289
  5.7 7.1 %collective-permute-start = (bf16[4,8,768]{2,1,0:T(8,128)(2,1)}, bf16[4,8,768]{2,1,0:T(8,128)(2,1)S(1)}, u32[]{:S(2)}, u32[]{:S(2)}) collective-permute-start(bf16[4,8,768]{2,1,0:T(8,128)(2,1)} %param.12), channel_id=1, source_target_pairs={{0,4},{1,5},{2,6},{3,7},{4,8},{5,9},{6,10},{7,11},{8,12},{9,13},{1... | collective-permute-start | bytes 147464 | tf_op jit(solution)/shard_map/ppermute | solution.py:289
  5.7 7.2 %collective-permute-start.1 = (bf16[4,8,768]{2,1,0:T(8,128)(2,1)}, bf16[4,8,768]{2,1,0:T(8,128)(2,1)S(1)}, u32[]{:S(2)}, u32[]{:S(2)}) collective-permute-start(bf16[4,8,768]{2,1,0:T(8,128)(2,1)} %param.12), channel_id=1, source_target_pairs={{0,8},{1,9},{2,10},{3,11},{4,12},{5,13},{6,14},{7,15},{8,0},{9,1},... | collective-permute-start | bytes 147464 | tf_op jit(solution)/shard_map/ppermute | solution.py:289
  6.8 6.1 %collective-permute-start.3 = (bf16[4,8,768]{2,1,0:T(8,128)(2,1)}, bf16[4,8,768]{2,1,0:T(8,128)(2,1)S(1)}, u32[]{:S(2)}, u32[]{:S(2)}) collective-permute-start(bf16[4,8,768]{2,1,0:T(8,128)(2,1)} %param.13), channel_id=1, source_target_pairs={{0,2},{1,3},{2,0},{3,1},{4,6},{5,7},{6,4},{7,5},{8,10},{9,11},{10,... | collective-permute-start | bytes 147464 | tf_op jit(solution)/shard_map/ppermute | solution.py:289
  9.8 0.8 %copy-start.3 = (bf16[4,8,768]{2,1,0:T(8,128)(2,1)S(1)}, bf16[4,8,768]{2,1,0:T(8,128)(2,1)}, u32[]{:S(2)}) copy-start(bf16[4,8,768]{2,1,0:T(8,128)(2,1)} %q_ref.1) | copy-start | bytes 147460
  10.6 0.8 %copy-start.4 = (bf16[4,8,768]{2,1,0:T(8,128)(2,1)S(1)}, bf16[4,8,768]{2,1,0:T(8,128)(2,1)}, u32[]{:S(2)}) copy-start(bf16[4,8,768]{2,1,0:T(8,128)(2,1)} %skip_ref.1) | copy-start | bytes 147460
  11.4 0.7 %copy-start.5 = (f32[12]{0:T(128)S(1)}, f32[12]{0:T(128)}, u32[]{:S(2)}) copy-start(f32[12]{0:T(128)} %factor_ref.1) | copy-start | bytes 148
  12.9 5.7 %collective-permute-start.5 = (bf16[4,32,768]{2,1,0:T(8,128)(2,1)S(1)}, bf16[4,32,768]{2,1,0:T(8,128)(2,1)S(1)}, u32[]{:S(2)}, u32[]{:S(2)}) collective-permute-start(bf16[4,32,768]{2,1,0:T(8,128)(2,1)S(1)} %constant_dynamic-update-slice_fusion.refs_1_), channel_id=1, source_target_pairs={{0,2},{1,3},{2,0},{3,1},{4,6},{5,7},{6,4},{7,5},{8,10},{9,11},{10,... | collective-permute-start | bytes 589832 | tf_op jit(solution)/shard_map/ppermute | solution.py:289
  14.1 10.4 %collective-permute-start.4 = (bf16[4,32,768]{2,1,0:T(8,128)(2,1)S(1)}, bf16[4,32,768]{2,1,0:T(8,128)(2,1)S(1)}, u32[]{:S(2)}, u32[]{:S(2)}) collective-permute-start(bf16[4,32,768]{2,1,0:T(8,128)(2,1)S(1)} %constant_dynamic-update-slice_fusion.refs_1_), channel_id=1, source_target_pairs={{0,1},{1,0},{2,3},{3,2},{4,5},{5,4},{6,7},{7,6},{8,9},{9,8},{10,11... | collective-permute-start | bytes 589832 | tf_op jit(solution)/shard_map/ppermute | solution.py:289
  18.7 5.9 %collective-permute-start.6 = (bf16[4,32,768]{2,1,0:T(8,128)(2,1)S(1)}, bf16[4,32,768]{2,1,0:T(8,128)(2,1)S(1)}, u32[]{:S(2)}, u32[]{:S(2)}) collective-permute-start(bf16[4,32,768]{2,1,0:T(8,128)(2,1)S(1)} %collective-permute-done.5.refs_2_), channel_id=1, source_target_pairs={{0,1},{1,0},{2,3},{3,2},{4,5},{5,4},{6,7},{7,6},{8,9},{9,8},{10,11... | collective-permute-start | bytes 589832 | tf_op jit(solution)/shard_map/ppermute | solution.py:289
  19.5 6.9 %collective-permute-start.10 = (bf16[4,16,768]{2,1,0:T(8,128)(2,1)S(1)}, bf16[4,16,768]{2,1,0:T(8,128)(2,1)S(1)}, u32[]{:S(2)}, u32[]{:S(2)}) collective-permute-start(bf16[4,16,768]{2,1,0:T(8,128)(2,1)S(1)} %pad_maximum_fusion.refs_1_), channel_id=1, source_target_pairs={{0,12},{1,13},{2,14},{3,15},{4,0},{5,1},{6,2},{7,3},{8,4},{9,5},{1... | collective-permute-start | bytes 294920 | tf_op jit(solution)/shard_map/ppermute | solution.py:289
  22.4 11.4 %collective-permute-start.9 = (bf16[4,16,768]{2,1,0:T(8,128)(2,1)S(1)}, bf16[4,16,768]{2,1,0:T(8,128)(2,1)S(1)}, u32[]{:S(2)}, u32[]{:S(2)}) collective-permute-start(bf16[4,16,768]{2,1,0:T(8,128)(2,1)S(1)} %pad_maximum_fusion.refs_1_), channel_id=1, source_target_pairs={{0,8},{1,9},{2,10},{3,11},{4,12},{5,13},{6,14},{7,15},{8,0},{9,1},... | collective-permute-start | bytes 294920 | tf_op jit(solution)/shard_map/ppermute | solution.py:289
  24.3 9.5 %collective-permute-start.8 = (bf16[4,16,768]{2,1,0:T(8,128)(2,1)S(1)}, bf16[4,16,768]{2,1,0:T(8,128)(2,1)S(1)}, u32[]{:S(2)}, u32[]{:S(2)}) collective-permute-start(bf16[4,16,768]{2,1,0:T(8,128)(2,1)S(1)} %pad_maximum_fusion.refs_1_), channel_id=1, source_target_pairs={{0,4},{1,5},{2,6},{3,7},{4,8},{5,9},{6,10},{7,11},{8,12},{9,13},{1... | collective-permute-start | bytes 294920 | tf_op jit(solution)/shard_map/ppermute | solution.py:289
  24.8 4.2 %collective-permute-start.7 = (f32[96,128]{1,0:T(8,128)S(1)}, f32[96,128]{1,0:T(8,128)S(1)}, u32[]{:S(2)}, u32[]{:S(2)}) collective-permute-start(f32[96,128]{1,0:T(8,128)S(1)} %shard_map.115.refs_0_), channel_id=1, source_target_pairs={{0,16},{16,0},{1,17},{17,1},{2,18},{18,2},{3,19},{19,3},{4,20},{20... | collective-permute-start | bytes 147464 | tf_op jit(solution)/shard_map/ppermute | solution.py:383
  26.4 8.2 %collective-permute-start.11 = (bf16[4,16,768]{2,1,0:T(8,128)(2,1)S(1)}, bf16[4,16,768]{2,1,0:T(8,128)(2,1)S(1)}, u32[]{:S(2)}, u32[]{:S(2)}) collective-permute-start(bf16[4,16,768]{2,1,0:T(8,128)(2,1)S(1)} %pad_maximum_fusion.refs_1_), channel_id=1, source_target_pairs={{0,1},{1,0},{2,3},{3,2},{4,5},{5,4},{6,7},{7,6},{8,9},{9,8},{10,11... | collective-permute-start | bytes 294920 | tf_op jit(solution)/shard_map/ppermute | solution.py:289
  29.0 5.6 %collective-permute-start.14 = (bf16[4,16,768]{2,1,0:T(8,128)(2,1)S(1)}, bf16[4,16,768]{2,1,0:T(8,128)(2,1)S(1)}, u32[]{:S(2)}, u32[]{:S(2)}) collective-permute-start(bf16[4,16,768]{2,1,0:T(8,128)(2,1)S(1)} %collective-permute-done.10.refs_4_), channel_id=1, source_target_pairs={{0,1},{1,0},{2,3},{3,2},{4,5},{5,4},{6,7},{7,6},{8,9},{9,8},{10,11... | collective-permute-start | bytes 294920 | tf_op jit(solution)/shard_map/ppermute | solution.py:289
  33.8 1.3 %collective-permute-start.13 = (bf16[4,16,768]{2,1,0:T(8,128)(2,1)S(1)}, bf16[4,16,768]{2,1,0:T(8,128)(2,1)S(1)}, u32[]{:S(2)}, u32[]{:S(2)}) collective-permute-start(bf16[4,16,768]{2,1,0:T(8,128)(2,1)S(1)} %collective-permute-done.9.refs_3_), channel_id=1, source_target_pairs={{0,1},{1,0},{2,3},{3,2},{4,5},{5,4},{6,7},{7,6},{8,9},{9,8},{10,11... | collective-permute-start | bytes 294920 | tf_op jit(solution)/shard_map/ppermute | solution.py:289
  33.8 1.5 %collective-permute-start.12 = (bf16[4,16,768]{2,1,0:T(8,128)(2,1)S(1)}, bf16[4,16,768]{2,1,0:T(8,128)(2,1)S(1)}, u32[]{:S(2)}, u32[]{:S(2)}) collective-permute-start(bf16[4,16,768]{2,1,0:T(8,128)(2,1)S(1)} %collective-permute-done.8.refs_2_), channel_id=1, source_target_pairs={{0,1},{1,0},{2,3},{3,2},{4,5},{5,4},{6,7},{7,6},{8,9},{9,8},{10,11... | collective-permute-start | bytes 294920 | tf_op jit(solution)/shard_map/ppermute | solution.py:289
  35.3 9.3 %copy-start = (bf16[768,1152]{1,0:T(8,128)(2,1)S(1)}, bf16[768,1152]{1,0:T(8,128)(2,1)}, u32[]{:S(2)}) copy-start(bf16[768,1152]{1,0:T(8,128)(2,1)} %refs_2_.1) | copy-start | bytes 5308420
  36.8 12.5 %all-to-all-start = ((f32[16,24,128]{2,1,0:T(8,128)}), f32[16,24,128]{2,1,0:T(8,128)S(1)}, u32[]{:S(2)}, u32[]{:S(2)}) async-start(f32[16,24,128]{2,1,0:T(8,128)} %shard_map.119), calls=%async_computation | async-start | bytes 393216 | tf_op jit(solution)/shard_map/all_to_all | solution.py:415
  40.4 10.6 %copy-start.1 = (bf16[768,768]{1,0:T(8,128)(2,1)S(1)}, bf16[768,768]{1,0:T(8,128)(2,1)}, u32[]{:S(2)}) copy-start(bf16[768,768]{1,0:T(8,128)(2,1)} %refs_4_.1) | copy-start | bytes 3538948
  40.4 4.2 %collective-permute-start.15 = (bf16[32,768]{1,0:T(8,128)(2,1)S(1)}, bf16[32,768]{1,0:T(8,128)(2,1)S(1)}, u32[]{:S(2)}, u32[]{:S(2)}) collective-permute-start(bf16[32,768]{1,0:T(8,128)(2,1)S(1)} %get-tuple-element.31.refs_0_), channel_id=1, source_target_pairs={{0,16},{16,0},{1,17},{17,1},{2,18},{18,2},{3,19},{19,3},{4,20},{20... | collective-permute-start | bytes 147464 | tf_op jit(solution)/shard_map/ppermute | solution.py:424
  45.0 6.0 %collective-permute-start.16 = (bf16[64,1152]{1,0:T(8,128)(2,1)S(1)}, bf16[64,1152]{1,0:T(8,128)(2,1)S(1)}, u32[]{:S(2)}, u32[]{:S(2)}) collective-permute-start(bf16[64,1152]{1,0:T(8,128)(2,1)S(1)} %shard_map.118.refs_1_), channel_id=1, source_target_pairs={{0,16},{16,0},{1,17},{17,1},{2,18},{18,2},{3,19},{19,3},{4,20},{20... | collective-permute-start | bytes 442376 | tf_op jit(solution)/shard_map/ppermute | solution.py:435

commit v4 on v3

--- a/solution.py
+++ b/solution.py
@@ -44,13 +44,20 @@
     return place
 
 
-def prepare_kernel(head, stages, scalar_ref, q_ref, skip_ref, gain_ref, factor_ref, *outs):
-    masked_ref, wide_skip_ref, wide_gain_ref, head_ref, order_ref, turn_ref, own_ref, slab_ref = outs
+def fetch(pairs, sems):
+    copies = [pltpu.make_async_copy(src, dst, sems.at[i]) for i, (src, dst) in enumerate(pairs)]
+    for copy in copies:
+        copy.start()
+    for copy in copies:
+        copy.wait()
+
+
+def query_kernel(head, q_hbm, masked_ref, q_ref, sems):
     rows, sites, embed = q_ref.shape
-    heads = embed // head
     width = masked_ref.shape[2]
     group = width // head
     span = group * sites
+    fetch([(q_hbm, q_ref)], sems)
     lane_head = lax.broadcasted_iota(jnp.int32, (span, width), 1) // head
     row_head = lax.broadcasted_iota(jnp.int32, (span, width), 0) // sites
     own_head = lane_head == row_head
@@ -59,8 +66,14 @@
             q = q_ref[r, :, block * width : (block + 1) * width].astype(F32)
             q = jnp.where(own_head, jnp.concatenate([q] * group, axis=0), 0.0).astype(BF16)
             masked_ref[r, block * span : (block + 1) * span, :] = q
-    wide_skip_ref[...] = skip_ref[...].astype(F32).reshape(rows * sites, embed)
-    wide_gain_ref[...] = jnp.broadcast_to(gain_ref[...], wide_gain_ref.shape)
+
+
+def prepare_kernel(heads, stages, scalar_ref, skip_hbm, gain_ref, factor_ref, *refs):
+    wide_skip_ref, wide_gain_ref, head_ref, order_ref, own_ref, slab_ref, skip_ref, sems = refs
+    _, sites, embed = skip_ref.shape
+    copy = pltpu.make_async_copy(skip_hbm, skip_ref, sems.at[0])
+    copy.start()
+    wide_gain_ref[...] = jnp.broadcast_to(gain_ref[...].reshape(1, embed), wide_gain_ref.shape)
     row = lax.broadcasted_iota(jnp.int32, head_ref.shape, 0)
     factors = jnp.zeros(head_ref.shape, F32)
     for h in range(heads):
@@ -71,20 +84,14 @@
     row = lax.broadcasted_iota(jnp.int32, (length, length), 0)
     lane = lax.broadcasted_iota(jnp.int32, (length, length), 1)
     order_ref[...] = (arrival_place(pos_index, row, stages, sites) == lane).astype(F32)
-    if len(stages) > 1:
-        outer, middle = stages[0][1], stages[1][1]
-        block, inside = row // sites, row % sites
-        first, second, rest = block % outer, (block // outer) % middle, block // (outer * middle)
-        turned = (rest * outer * middle + first * middle + second) * sites + inside
-    else:
-        turned = row
-    turn_ref[...] = (turned == lane).astype(BF16)
     row = lax.broadcasted_iota(jnp.int32, own_ref.shape, 0)
     lane = lax.broadcasted_iota(jnp.int32, own_ref.shape, 1)
     own_ref[...] = (row + pos_index * sites == lane).astype(F32)
     row = lax.broadcasted_iota(jnp.int32, slab_ref.shape, 0)
     lane = lax.broadcasted_iota(jnp.int32, slab_ref.shape, 1)
     slab_ref[...] = (row == lane + seq_index * slab_ref.shape[1]).astype(F32)
+    copy.wait()
+    wide_skip_ref[...] = skip_ref[...].astype(F32).reshape(wide_skip_ref.shape)
 
 
 def logits_kernel(part_count, *refs):
@@ -104,7 +111,7 @@
 
 
 def softmax_kernel(factor, *refs):
-    parts, (turn_ref, w_ref, turned_ref) = refs[:-3], refs[-3:]
+    parts, w_ref = refs[:-1], refs[-1]
     logits = parts[0][...]
     for part in parts[1:]:
         logits = logits + part[...]
@@ -112,7 +119,6 @@
     exponent = jnp.exp(logits - jnp.max(logits, axis=1, keepdims=True))
     shares = (exponent / jnp.sum(exponent, axis=1, keepdims=True)).astype(BF16)
     w_ref[...] = shares
-    turned_ref[...] = dot_nn(shares, turn_ref[...]).astype(BF16)
 
 
 def pair_kernel(heads, w_ref, head_ref, order_ref, pair_ref, held):
@@ -167,24 +173,9 @@
     out_ref[...] = dot_nn(normed, weight_ref[...]).astype(BF16)
 
 
-def column_kernel(head, factor, swapped, *refs):
-    if swapped:
-        scalar_ref, own_ref, other_ref = refs[:3]
-        full = refs[-1]
-        hidden_ref, closing_ref, out_ref, products, mixed = refs[3:-1]
-        cells, columns = own_ref.shape
-        own_at = pl.multiple_of(scalar_ref[0] * columns, 128)
-        other_at = pl.multiple_of((1 - scalar_ref[0]) * columns, 128)
-        full[:, pl.ds(own_at, columns)] = own_ref[...]
-        full[0 : cells // 2, pl.ds(other_at, columns)] = other_ref[cells // 2 :, :]
-        full[cells // 2 :, pl.ds(other_at, columns)] = other_ref[0 : cells // 2, :]
-    else:
-        query_ref, full = refs[:2]
-        hidden_ref, closing_ref, out_ref, products, mixed = refs[2:]
+def column_attend(head, factor, query, keys, values, hidden_ref, closing_ref, out_ref, products, mixed):
     rows, sites, embed = out_ref.shape
-    own_rows = rows * sites
-    heads = embed // head
-    padded = round_up(heads, 128)
+    padded = round_up(embed // head, 128)
     pick = (
         lax.broadcasted_iota(jnp.int32, (embed, padded), 0) // head
         == lax.broadcasted_iota(jnp.int32, (embed, padded), 1)
@@ -193,15 +184,7 @@
         lax.broadcasted_iota(jnp.int32, (padded, embed), 1) // head
         == lax.broadcasted_iota(jnp.int32, (padded, embed), 0)
     ).astype(BF16)
-    if swapped:
-        query = full[0:own_rows, 0:embed].astype(F32)
-        key, value = full[:, embed : 2 * embed].astype(F32), full[:, 2 * embed :].astype(F32)
-    else:
-        query = query_ref[...].astype(F32)
-        key, value = full[:, 0:embed].astype(F32), full[:, embed:].astype(F32)
-    seqs = key.shape[0] // sites
-    keys = [key[t * sites : (t + 1) * sites, :] for t in range(seqs)]
-    values = [value[t * sites : (t + 1) * sites, :] for t in range(seqs)]
+    seqs = len(keys)
     for s in range(rows):
         for t in range(seqs):
             at = (s * seqs + t) * sites
@@ -224,6 +207,48 @@
     out_ref[...] = out.reshape(rows, sites, embed).astype(BF16)
 
 
+def column_kernel(head, factor, query_ref, kv_ref, *refs):
+    rows, sites, embed = refs[2].shape
+    kv = kv_ref[...].astype(F32)
+    seqs = kv.shape[0] // sites
+    keys = [kv[t * sites : (t + 1) * sites, 0:embed] for t in range(seqs)]
+    values = [kv[t * sites : (t + 1) * sites, embed:] for t in range(seqs)]
+    column_attend(head, factor, query_ref[...].astype(F32), keys, values, *refs)
+
+
+def swapped_column_kernel(head, factor, scalar_ref, own_ref, other_ref, *refs):
+    rows, sites, embed = refs[2].shape
+    cells, columns = own_ref.shape
+    half = cells // 2
+
+    def piece(first_is_own, start, stop, at, size):
+        found = []
+        for block in range(2):
+            lo, hi = max(start, block * columns), min(stop, (block + 1) * columns)
+            if lo < hi:
+                cols = slice(lo - block * columns, hi - block * columns)
+                if (block == 0) == first_is_own:
+                    found.append(own_ref[at : at + size, cols])
+                else:
+                    turned = (at + half) % cells
+                    found.append(other_ref[turned : turned + size, cols])
+        return jnp.concatenate(found, axis=1).astype(F32)
+
+    def attend(first_is_own):
+        query = piece(first_is_own, 0, embed, 0, half)
+        keys, values = [], []
+        for at in (0, half):
+            key = piece(first_is_own, embed, 2 * embed, at, half)
+            value = piece(first_is_own, 2 * embed, 3 * embed, at, half)
+            for t in range(half // sites):
+                keys.append(key[t * sites : (t + 1) * sites, :])
+                values.append(value[t * sites : (t + 1) * sites, :])
+        column_attend(head, factor, query, keys, values, *refs)
+
+    pl.when(scalar_ref[0] == 0)(functools.partial(attend, True))
+    pl.when(scalar_ref[0] == 1)(functools.partial(attend, False))
+
+
 def contact_kernel(heads, scalar_ref, pair_ref, factor_ref, offset_ref, own_ref, slab_ref, out_ref, held):
     count, step, length = pair_ref.shape
     head_rows = round_up(heads, 8)
@@ -250,13 +275,18 @@
     )
 
 
-def call(kernel, out_shape, operands, smem=(), scratch=(), flops=1000000, bytes_accessed=1000000):
+def call(kernel, out_shape, operands, smem=(), hbm=(), scratch=(), bytes_accessed=1000000):
     vmem = pl.BlockSpec(memory_space=pltpu.VMEM)
     held = sum(math.prod(a.shape) * a.dtype.itemsize for a in [*operands, *jax.tree.leaves(out_shape)])
-    held += sum(math.prod(a.shape) * np.dtype(a.dtype).itemsize for a in scratch)
+    held += sum(
+        math.prod(a.shape) * np.dtype(a.dtype).itemsize
+        for a in scratch
+        if a.memory_space == pltpu.VMEM
+    )
     limit = 2 * held + 4 * 1024 * 1024
     specs = [
-        pl.BlockSpec(memory_space=pltpu.SMEM) if i in smem else vmem for i in range(len(operands))
+        pl.BlockSpec(memory_space=pltpu.SMEM if i in smem else pl.ANY if i in hbm else pltpu.VMEM)
+        for i in range(len(operands))
     ]
     return pl.pallas_call(
         kernel,
@@ -266,7 +296,7 @@
         scratch_shapes=list(scratch),
         compiler_params=pltpu.CompilerParams(vmem_limit_bytes=limit),
         cost_estimate=pl.CostEstimate(
-            flops=flops, bytes_accessed=bytes_accessed, transcendentals=0
+            flops=1000000, bytes_accessed=bytes_accessed, transcendentals=0
         ),
     )(*operands)
 
@@ -331,47 +361,32 @@
     scalars = jnp.stack([seq_index, pos_index])
     head_rows = round_up(heads, 8)
     width = lane_block(embed, head)
-    masked, skip, gain, head_factors, order, turn, own_select, slab_select = call(
-        functools.partial(prepare_kernel, head, stages),
-        (
-            jax.ShapeDtypeStruct((rows, heads * sites, width), BF16),
-            jax.ShapeDtypeStruct((cells, embed), F32),
-            jax.ShapeDtypeStruct((8, embed), F32),
-            jax.ShapeDtypeStruct((head_rows, 128), F32),
-            jax.ShapeDtypeStruct((length, length), F32),
-            jax.ShapeDtypeStruct((length, length), BF16),
-            jax.ShapeDtypeStruct((sites, length), F32),
-            jax.ShapeDtypeStruct((length, slab_width), F32),
-        ),
-        [
-            scalars,
-            lateral_asking_vectors,
-            skip_stream_input,
-            upright_normalizer_multiplier.reshape(1, embed),
-            regression_factors,
-        ],
-        smem=(0, 4),
-    )
-
-    value_first = [lateral_carried_vectors]
-    if middle:
-        value_first += send_all(value_first, pos_count, middle)
+    masked = call(
+        functools.partial(query_kernel, head),
+        jax.ShapeDtypeStruct((rows, heads * sites, width), BF16),
+        [lateral_asking_vectors],
+        hbm=(0,),
+        scratch=[pltpu.VMEM((rows, sites, embed), BF16), pltpu.SemaphoreType.DMA((1,))],
+    )
+
     key_first = [lateral_matched_vectors]
     key_first += send_all(key_first, pos_count, outer)
-    key_first[-1] = after(key_first[-1], value_first[-1], masked)
+    key_first[-1] = after(key_first[-1], masked)
     key_parts = [jnp.concatenate(key_first, axis=1)]
     if middle:
         key_parts += send_all(key_parts, pos_count, middle)
-    value_parts = [after(jnp.concatenate(value_first, axis=1), key_parts[0])]
-    value_outer = send_all(value_parts, pos_count, outer)
-
+    value_first = [after(lateral_carried_vectors, key_parts[0])]
+    value_first += send_all(value_first, pos_count, outer)
     near = sum(part.shape[1] for part in key_parts)
     partial = call(
         functools.partial(logits_kernel, len(key_parts)),
         jax.ShapeDtypeStruct((heads * sites, near), F32),
         [masked, *key_parts],
-        bytes_accessed=20000000,
-    )
+    )
+    value_first = [value_first[0]] + [after(part, partial) for part in value_first[1:]]
+    value_parts = [jnp.concatenate(value_first, axis=1)]
+    if middle:
+        value_parts += send_all(value_parts, pos_count, middle)
     if len(stages) > 2:
         far_parts = send_all(key_parts, pos_count, stages[2])
         partial = call(
@@ -379,22 +394,39 @@
             jax.ShapeDtypeStruct((heads * sites, length), F32),
             [masked, *far_parts, partial],
         )
+    skip, gain, head_factors, order, own_select, slab_select = call(
+        functools.partial(prepare_kernel, heads, stages),
+        (
+            jax.ShapeDtypeStruct((cells, embed), F32),
+            jax.ShapeDtypeStruct((8, embed), F32),
+            jax.ShapeDtypeStruct((head_rows, 128), F32),
+            jax.ShapeDtypeStruct((length, length), F32),
+            jax.ShapeDtypeStruct((sites, length), F32),
+            jax.ShapeDtypeStruct((length, slab_width), F32),
+        ),
+        [
+            after(scalars, partial),
+            skip_stream_input,
+            upright_normalizer_multiplier,
+            regression_factors,
+        ],
+        smem=(0, 3),
+        hbm=(1,),
+        scratch=[pltpu.VMEM((rows, sites, embed), BF16), pltpu.SemaphoreType.DMA((1,))],
+    )
+    if len(stages) > 2:
+        value_parts = value_parts[:1] + [after(part, skip) for part in value_parts[1:]]
+        value_parts += send_all(value_parts, pos_count, stages[2])
     if seq_count == 2:
-        partials = [partial, lax.ppermute(partial, "seq", swap)]
+        partials = [partial, after(lax.ppermute(partial, "seq", swap), skip)]
     else:
         partials = [lax.psum(partial, "seq")]
-    value_parts += [after(part, partials[-1]) for part in value_outer]
-    if len(stages) > 2:
-        value_parts += send_all(value_parts, pos_count, stages[2])
-    shares, shares_turned = call(
+    shares = call(
         functools.partial(
             softmax_kernel, 1.0 / (math.sqrt(head) * math.sqrt(rows * seq_count))
         ),
-        (
-            jax.ShapeDtypeStruct((heads * sites, length), BF16),
-            jax.ShapeDtypeStruct((heads * sites, length), BF16),
-        ),
-        [*partials, turn],
+        jax.ShapeDtypeStruct((heads * sites, length), BF16),
+        partials,
     )
 
     hidden, normed = call(
@@ -403,13 +435,14 @@
             jax.ShapeDtypeStruct((cells, embed), F32),
             jax.ShapeDtypeStruct((cells, embed), BF16),
         ),
-        [shares_turned, *value_parts, lateral_closing_linear, skip, gain],
+        [shares, *value_parts, lateral_closing_linear, skip, gain],
         scratch=[pltpu.VMEM((cells, embed), F32)],
     )
     pair_local = call(
         functools.partial(pair_kernel, heads),
         jax.ShapeDtypeStruct((pos_count, head_rows + sites, length), F32),
         [after(shares, normed), head_factors, order],
+        bytes_accessed=10000000,
         scratch=[pltpu.VMEM((head_rows + sites, length), F32)],
     )
     pair_all = lax.all_to_all(pair_local, "pos", split_axis=0, concat_axis=0, tiled=True)
@@ -432,24 +465,24 @@
         [*normed_all, weight],
     )
     if swapped:
-        column_inputs = [scalars, projected, lax.ppermute(projected, "seq", swap)]
+        column, column_inputs = swapped_column_kernel, [
+            scalars,
+            projected,
+            lax.ppermute(projected, "seq", swap),
+        ]
     else:
         key_value = lax.all_gather(projected[:, embed:], "seq", axis=0, tiled=True)
-        column_inputs = [projected[:, :embed], key_value]
-    scratch = [
-        pltpu.VMEM((cells * rows * seq_count, embed), F32),
-        pltpu.VMEM((cells, embed), F32),
-    ]
-    if swapped:
-        scratch.append(pltpu.VMEM((cells * 2, columns * 2), BF16))
+        column, column_inputs = column_kernel, [projected[:, :embed], key_value]
     alignment_output = call(
-        functools.partial(column_kernel, head, 1.0 / math.sqrt(head), swapped),
+        functools.partial(column, head, 1.0 / math.sqrt(head)),
         jax.ShapeDtypeStruct((rows, sites, embed), BF16),
         [*column_inputs, after(hidden, pairing_chances), upright_closing_linear],
         smem=(0,) if swapped else (),
-        scratch=scratch,
-    )
-
+        scratch=[
+            pltpu.VMEM((cells * rows * seq_count, embed), F32),
+            pltpu.VMEM((cells, embed), F32),
+        ],
+    )
     return alignment_output, pairing_chances
 
 

time: 53.4 us -> 51.4 us (0.963)
  local copies, waits for them, and re-layouts: 3.77 us -> 2.57 us
  other arithmetic: 0.88 us -> 0.07 us
    concatenate x1 -> x0, other arithmetic: 0.81 us -> none  [per_device(): value_parts = [after(jnp.concatenate(value_first, axis=1), key_parts[0])]]
    ppermute x14 -> x12, starting transfers between devices: 14.2 us -> 13.4 us  [send_pos(): return lax.ppermute(array, 'pos', pairs)]
    reshape x1 -> x0, local copies, waits for them, and re-layouts: 0.69 us -> none  [per_device(): upright_normalizer_multiplier.reshape(1, embed)]
    all_to_all x1, starting transfers between devices: 3.52 us -> 4.13 us  [per_device(): lax.all_to_all(pair_local, 'pos', split_axis=0, concat_axis=0, tiled=True)]
    unnamed x15 -> x32, local copies, waits for them, and re-layouts: 3.08 us -> 2.56 us
    ppermute x14 -> x12, waiting for transfers between devices: 10 us -> 10.1 us  [send_pos(): return lax.ppermute(array, 'pos', pairs)]
    pallas_call x9 -> x10, Pallas kernels: 7.13 us -> 7.11 us  [call(): pl.pallas_call(kernel, out_shape=out_shape, in_specs=specs, out_specs=jax...]
  transfers between devices with their start and end apart: 18 -> 16, of which waited for: 7 -> 9; matrix products, arithmetic and copies ran while one was open for 4% -> 3% of each run, Pallas kernels for 7% -> 7%
where the time goes in v4:
time: 51.4 us; the launch traced here: 51 us
  starting transfers between devices  22.2 us (43%)
  waiting for transfers between devices  17.5 us (34%)
  Pallas kernels  7.11 us (14%)
  local copies, waits for them, and re-layouts  2.57 us (5%)
  between operations  1.53 us (3%)
    ppermute x12, starting transfers between devices, send_pos(): return lax.ppermute(array, 'pos', pairs)  13.4 us
    ppermute x12, waiting for transfers between devices, send_pos(): return lax.ppermute(array, 'pos', pairs)  10.1 us
    pallas_call x10, Pallas kernels, call(): pl.pallas_call(kernel, out_shape=out_shape, in_specs=specs, out_specs=jax...  7.11 us
    all_to_all x1, starting transfers between devices, per_device(): lax.all_to_all(pair_local, 'pos', split_axis=0, concat_axis=0, tiled=True)  4.13 us
    ppermute x1, waiting for transfers between devices, per_device(): partials = [partial, after(lax.ppermute(partial, 'seq', swap), skip)]  2.66 us
    ppermute x1, waiting for transfers between devices, per_device(): normed_all = [normed, lax.ppermute(normed, 'seq', swap)]  2.6 us
    unnamed x32, local copies, waits for them, and re-layouts  2.56 us
    all_to_all x1, waiting for transfers between devices, per_device(): lax.all_to_all(pair_local, 'pos', split_axis=0, concat_axis=0, tiled=True)  2.19 us
  transfers between devices with their start and end apart: 16, of which 9 were waited for; matrix products, arithmetic and copies ran while one was open for 3% of the time, Pallas kernels for 7%

profile of v4, /device:TPU:0, one launch (start us, length us, event | category | flops | bytes accessed | tf_op | source)
XLA Modules:
  0.0 51.0 jit_solution(15484466875353625592)
XLA Ops:
  0.7 3.1 %collective-permute-start = (bf16[4,8,768]{2,1,0:T(8,128)(2,1)}, bf16[4,8,768]{2,1,0:T(8,128)(2,1)S(1)}, u32[]{:S(2)}, u32[]{:S(2)}) collective-permute-start(bf16[4,8,768]{2,1,0:T(8,128)(2,1)} %param.12), channel_id=1, source_target_pairs={{0,4},{1,5},{2,6},{3,7},{4,8},{5,9},{6,10},{7,11},{8,12},{9,13},{1... | collective-permute-start | bytes 147464 | tf_op jit(solution)/shard_map/ppermute | solution.py:319
  3.7 2.6 %collective-permute-start.1 = (bf16[4,8,768]{2,1,0:T(8,128)(2,1)}, bf16[4,8,768]{2,1,0:T(8,128)(2,1)S(1)}, u32[]{:S(2)}, u32[]{:S(2)}) collective-permute-start(bf16[4,8,768]{2,1,0:T(8,128)(2,1)} %param.12), channel_id=1, source_target_pairs={{0,8},{1,9},{2,10},{3,11},{4,12},{5,13},{6,14},{7,15},{8,0},{9,1},... | collective-permute-start | bytes 147464 | tf_op jit(solution)/shard_map/ppermute | solution.py:319
  6.3 1.3 %collective-permute-start.2 = (bf16[4,8,768]{2,1,0:T(8,128)(2,1)}, bf16[4,8,768]{2,1,0:T(8,128)(2,1)S(1)}, u32[]{:S(2)}, u32[]{:S(2)}) collective-permute-start(bf16[4,8,768]{2,1,0:T(8,128)(2,1)} %param.12), channel_id=1, source_target_pairs={{0,12},{1,13},{2,14},{3,15},{4,0},{5,1},{6,2},{7,3},{8,4},{9,5},{1... | collective-permute-start | bytes 147464 | tf_op jit(solution)/shard_map/ppermute | solution.py:319
  7.7 0.8 %constant_dynamic-update-slice_fusion.3 = bf16[4,32,768]{2,1,0:T(8,128)(2,1)S(1)} fusion(bf16[4,8,768]{2,1,0:T(8,128)(2,1)} %param.12), kind=kLoop, calls=%fused_computation.3 | loop fusion | bytes 98304
  8.5 0.8 %copy-done.4 = bf16[4,8,768]{2,1,0:T(8,128)(2,1)S(1)} copy-done((bf16[4,8,768]{2,1,0:T(8,128)(2,1)S(1)}, bf16[4,8,768]{2,1,0:T(8,128)(2,1)}, u32[]{:S(2)}) %copy-start.4) | copy-done | bytes 49176
  9.3 0.1 shard_map.113.refs_0_
  9.4 0.0 collective-permute-done
  9.4 1.2 %collective-permute-done.2 = bf16[4,8,768]{2,1,0:T(8,128)(2,1)S(1)} collective-permute-done((bf16[4,8,768]{2,1,0:T(8,128)(2,1)}, bf16[4,8,768]{2,1,0:T(8,128)(2,1)S(1)}, u32[]{:S(2)}, u32[]{:S(2)}) %collective-permute-start.2) | collective-permute-done | bytes 49184 | tf_op jit(solution)/shard_map/ppermute | solution.py:319
  10.6 0.0 collective-permute-done.1
  10.7 1.7 %collective-permute-start.4 = (bf16[4,32,768]{2,1,0:T(8,128)(2,1)S(1)}, bf16[4,32,768]{2,1,0:T(8,128)(2,1)S(1)}, u32[]{:S(2)}, u32[]{:S(2)}) collective-permute-start(bf16[4,32,768]{2,1,0:T(8,128)(2,1)S(1)} %constant_dynamic-update-slice_fusion.refs_1_), channel_id=1, source_target_pairs={{0,2},{1,3},{2,0},{3,1},{4,6},{5,7},{6,4},{7,5},{8,10},{9,11},{10,... | collective-permute-start | bytes 589832 | tf_op jit(solution)/shard_map/ppermute | solution.py:319
  12.4 0.0 collective-permute-start.3
  12.4 0.7 %collective-permute-start.7 = (bf16[4,8,768]{2,1,0:T(8,128)(2,1)}, bf16[4,8,768]{2,1,0:T(8,128)(2,1)S(1)}, u32[]{:S(2)}, u32[]{:S(2)}) collective-permute-start(bf16[4,8,768]{2,1,0:T(8,128)(2,1)} %param.13), channel_id=1, source_target_pairs={{0,4},{1,5},{2,6},{3,7},{4,8},{5,9},{6,10},{7,11},{8,12},{9,13},{1... | collective-permute-start | bytes 147464 | tf_op jit(solution)/shard_map/ppermute | solution.py:319
  13.1 2.9 %collective-permute-start.8 = (bf16[4,8,768]{2,1,0:T(8,128)(2,1)}, bf16[4,8,768]{2,1,0:T(8,128)(2,1)S(1)}, u32[]{:S(2)}, u32[]{:S(2)}) collective-permute-start(bf16[4,8,768]{2,1,0:T(8,128)(2,1)} %param.13), channel_id=1, source_target_pairs={{0,8},{1,9},{2,10},{3,11},{4,12},{5,13},{6,14},{7,15},{8,0},{9,1},... | collective-permute-start | bytes 147464 | tf_op jit(solution)/shard_map/ppermute | solution.py:319
  16.0 0.3 collective-permute-start.9
  16.2 0.8 %constant_dynamic-update-slice_fusion.7 = bf16[4,32,768]{2,1,0:T(8,128)(2,1)S(1)} fusion(bf16[4,8,768]{2,1,0:T(8,128)(2,1)} %param.13), kind=kLoop, calls=%fused_computation.7 | loop fusion | bytes 98304
  17.1 0.0 collective-permute-done.4.refs_2_
  17.1 0.2 shard_map.114.refs_3_
  17.3 1.7 %collective-permute-done.7 = bf16[4,8,768]{2,1,0:T(8,128)(2,1)S(1)} collective-permute-done((bf16[4,8,768]{2,1,0:T(8,128)(2,1)}, bf16[4,8,768]{2,1,0:T(8,128)(2,1)S(1)}, u32[]{:S(2)}, u32[]{:S(2)}) %collective-permute-start.7) | collective-permute-done | bytes 49184 | tf_op jit(solution)/shard_map/ppermute | solution.py:319
  19.0 1.7 %collective-permute-done.8 = bf16[4,8,768]{2,1,0:T(8,128)(2,1)S(1)} collective-permute-done((bf16[4,8,768]{2,1,0:T(8,128)(2,1)}, bf16[4,8,768]{2,1,0:T(8,128)(2,1)S(1)}, u32[]{:S(2)}, u32[]{:S(2)}) %collective-permute-start.8) | collective-permute-done | bytes 49184 | tf_op jit(solution)/shard_map/ppermute | solution.py:319
  20.7 0.1 collective-permute-done.9
  20.8 0.1 collective-permute-start.5
  20.9 0.6 %collective-permute-start.10 = (bf16[4,32,768]{2,1,0:T(8,128)(2,1)S(1)}, bf16[4,32,768]{2,1,0:T(8,128)(2,1)S(1)}, u32[]{:S(2)}, u32[]{:S(2)}) collective-permute-start(bf16[4,32,768]{2,1,0:T(8,128)(2,1)S(1)} %constant_dynamic-update-slice_fusion.4.refs_1_), channel_id=1, source_target_pairs={{0,2},{1,3},{2,0},{3,1},{4,6},{5,7},{6,4},{7,5},{8,10},{9,11},{10,... | collective-permute-start | bytes 589832 | tf_op jit(solution)/shard_map/ppermute | solution.py:319
  21.5 0.1 pad_add_fusion.scalar_ref
  21.6 0.2 collective-permute-start.11
  21.8 0.5 %collective-permute-done.5.refs_2_ = bf16[4,32,768]{2,1,0:T(8,128)(2,1)S(1)} collective-permute-done((bf16[4,32,768]{2,1,0:T(8,128)(2,1)S(1)}, bf16[4,32,768]{2,1,0:T(8,128)(2,1)S(1)}, u32[]{:S(2)}, u32[]{:S(2)}) %collective-permute-start.5) | collective-permute-done | bytes 196640 | tf_op jit(solution)/shard_map/ppermute | solution.py:319
  22.3 0.3 shard_map.115.refs_0_
  22.6 0.0 copy-done.3
  22.7 0.8 %shard_map.116 = (f32[32,768]{1,0:T(8,128)S(1)}, f32[8,768]{1,0:T(8,128)S(1)}, f32[16,128]{1,0:T(8,128)S(1)}, f32[128,128]{1,0:T(8,128)S(1)}, f32[8,128]{1,0:T(8,128)S(1)}, /*index=5*/f32[128,64]{1,0:T(8,128)S(1)}) custom-call(s32[2]{0:T(128)S(1)} %pad_add_fusion.scalar_ref, bf16[4,8,768]{2,1,0:T(8,128)(2,1)S(1)} %copy-done.3, f32[768]{0:T(1024)S(1)} %copy-done.11, ...), custom_call_target="tpu_custom_call" | custom-call | flops 1000000 | bytes 1000000 | tf_op jit(solution)/shard_map/pallas_call | solution.py:291
  23.4 0.0 copy-start.5
  23.5 0.0 copy-start.9
  23.5 4.8 %collective-permute-done.10.refs_2_ = bf16[4,32,768]{2,1,0:T(8,128)(2,1)S(1)} collective-permute-done((bf16[4,32,768]{2,1,0:T(8,128)(2,1)S(1)}, bf16[4,32,768]{2,1,0:T(8,128)(2,1)S(1)}, u32[]{:S(2)}, u32[]{:S(2)}) %collective-permute-start.10) | collective-permute-done | bytes 196640 | tf_op jit(solution)/shard_map/ppermute | solution.py:319
  28.2 0.0 collective-permute-start.12
  28.2 1.5 %collective-permute-start.6 = (f32[96,128]{1,0:T(8,128)S(1)}, f32[96,128]{1,0:T(8,128)S(1)}, u32[]{:S(2)}, u32[]{:S(2)}) collective-permute-start(f32[96,128]{1,0:T(8,128)S(1)} %shard_map.115.refs_0_), channel_id=1, source_target_pairs={{0,16},{16,0},{1,17},{17,1},{2,18},{18,2},{3,19},{19,3},{4,20},{20... | collective-permute-start | bytes 147464 | tf_op jit(solution)/shard_map/ppermute | solution.py:421
  29.7 2.7 %collective-permute-done.6.refs_1_ = f32[96,128]{1,0:T(8,128)S(1)} collective-permute-done((f32[96,128]{1,0:T(8,128)S(1)}, f32[96,128]{1,0:T(8,128)S(1)}, u32[]{:S(2)}, u32[]{:S(2)}) %collective-permute-start.6) | collective-permute-done | bytes 49184 | tf_op jit(solution)/shard_map/ppermute | solution.py:421
  32.4 0.2 shard_map.117.refs_0_.w_ref
  32.6 0.0 collective-permute-done.11.refs_3_
  32.6 0.0 copy-start
  32.6 0.6 %shard_map.118 = (f32[32,768]{1,0:T(8,128)S(1)}, bf16[32,768]{1,0:T(8,128)(2,1)S(1)}) custom-call(bf16[96,128]{1,0:T(8,128)(2,1)S(1)} %shard_map.117.refs_0_.w_ref, bf16[4,32,768]{2,1,0:T(8,128)(2,1)S(1)} %constant_dynamic-update-slice_fusion.4.refs_1_, bf16[4,32,768]{2,1,0:T(8,128)(2,1)S(1)} %collective-permute-done.10.refs_2_, ...), custom_call_target="tpu_custom_call" | custom-call | flops 1000000 | bytes 1000000 | tf_op jit(solution)/shard_map/pallas_call | solution.py:291
  33.3 0.9 %shard_map.120 = f32[16,24,128]{2,1,0:T(8,128)} custom-call(bf16[96,128]{1,0:T(8,128)(2,1)S(1)} %shard_map.117.refs_0_.w_ref, f32[16,128]{1,0:T(8,128)S(1)} %get-tuple-element.33.head_ref.factor_ref, f32[128,128]{1,0:T(8,128)S(1)} %get-tuple-element.34.order_ref), custom_call_target="tpu_custom_call" | custom-call | flops 1000000 | bytes 10000000 | tf_op jit(solution)/shard_map/pallas_call | solution.py:291
  34.2 4.1 %all-to-all-start = ((f32[16,24,128]{2,1,0:T(8,128)}), f32[16,24,128]{2,1,0:T(8,128)S(1)}, u32[]{:S(2)}, u32[]{:S(2)}) async-start(f32[16,24,128]{2,1,0:T(8,128)} %shard_map.120), calls=%async_computation | async-start | bytes 393216 | tf_op jit(solution)/shard_map/all_to_all | solution.py:448
  38.4 0.0 copy-start.1
  38.4 1.6 %collective-permute-start.13 = (bf16[32,768]{1,0:T(8,128)(2,1)S(1)}, bf16[32,768]{1,0:T(8,128)(2,1)S(1)}, u32[]{:S(2)}, u32[]{:S(2)}) collective-permute-start(bf16[32,768]{1,0:T(8,128)(2,1)S(1)} %get-tuple-element.30.refs_0_), channel_id=1, source_target_pairs={{0,16},{16,0},{1,17},{17,1},{2,18},{18,2},{3,19},{19,3},{4,20},{20... | collective-permute-start | bytes 147464 | tf_op jit(solution)/shard_map/ppermute | solution.py:457
  39.9 2.6 %collective-permute-done.13.refs_1_ = bf16[32,768]{1,0:T(8,128)(2,1)S(1)} collective-permute-done((bf16[32,768]{1,0:T(8,128)(2,1)S(1)}, bf16[32,768]{1,0:T(8,128)(2,1)S(1)}, u32[]{:S(2)}, u32[]{:S(2)}) %collective-permute-start.13) | collective-permute-done | bytes 49184 | tf_op jit(solution)/shard_map/ppermute | solution.py:457
  42.5 0.4 shard_map.119.own_ref
  43.0 1.6 %collective-permute-start.14 = (bf16[64,1152]{1,0:T(8,128)(2,1)S(1)}, bf16[64,1152]{1,0:T(8,128)(2,1)S(1)}, u32[]{:S(2)}, u32[]{:S(2)}) collective-permute-start(bf16[64,1152]{1,0:T(8,128)(2,1)S(1)} %shard_map.119.own_ref), channel_id=1, source_target_pairs={{0,16},{16,0},{1,17},{17,1},{2,18},{18,2},{3,19},{19,3},{4,20},{20... | collective-permute-start | bytes 442376 | tf_op jit(solution)/shard_map/ppermute | solution.py:471
  45.2 2.2 %all-to-all-done.pair_ref = f32[16,24,128]{2,1,0:T(8,128)S(1)} async-done(((f32[16,24,128]{2,1,0:T(8,128)}), f32[16,24,128]{2,1,0:T(8,128)S(1)}, u32[]{:S(2)}, u32[]{:S(2)}) %all-to-all-start) | async-done | bytes 196640 | tf_op jit(solution)/shard_map/all_to_all | solution.py:448
  47.4 1.6 %shard_map.121 = f32[8,64]{1,0:T(8,128)} custom-call(s32[2]{0:T(128)S(1)} %copy-done.8, f32[16,24,128]{2,1,0:T(8,128)S(1)} %all-to-all-done.pair_ref, f32[16,128]{1,0:T(8,128)S(1)} %copy-done.6, f32[1]{0:T(128)S(6)} %copy.18.offset_ref, f32[8,128]{1,0:T(8,128)S(1)} %copy-done.10, f32[128,64]{1,0:T(8,128)S(1)} %get-tuple-element.36.slab_ref), custom_call_target="tpu_custom_call" | custom-call | flops 1000000 | bytes 1000000 | tf_op jit(solution)/shard_map/pallas_call | solution.py:291
  49.0 2.0 %shard_map.122 = bf16[4,8,768]{2,1,0:T(8,128)(2,1)} custom-call(s32[2]{0:T(128)S(1)} %copy-done.8, bf16[64,1152]{1,0:T(8,128)(2,1)S(1)} %shard_map.119.own_ref, bf16[64,1152]{1,0:T(8,128)(2,1)S(1)} %collective-permute-done.14.other_ref, f32[32,768]{1,0:T(8,128)S(1)} %get-tuple-element.37.refs_0_, bf16[768,768]{1,0:T(8,128)(2,1)S(1)} %copy-done.1), custom_call_target="tpu_custom_call" | custom-call | flops 1000000 | bytes 1000000 | tf_op jit(solution)/shard_map/pallas_call | solution.py:291
  (29 shorter events, 0.1 us)
Async XLA Ops:
  0.6 22.0 %copy-start.3 = (bf16[4,8,768]{2,1,0:T(8,128)(2,1)S(1)}, bf16[4,8,768]{2,1,0:T(8,128)(2,1)}, u32[]{:S(2)}) copy-start(bf16[4,8,768]{2,1,0:T(8,128)(2,1)} %skip_hbm.1) | copy-start | bytes 147460
  0.6 22.0 %copy-start.11 = (f32[768]{0:T(1024)S(1)}, f32[768]{0:T(1024)}, u32[]{:S(2)}) copy-start(f32[768]{0:T(1024)} %gain_ref.1) | copy-start | bytes 9220
  0.7 22.0 %copy-start.12 = (f32[12]{0:T(128)S(1)}, f32[12]{0:T(128)}, u32[]{:S(2)}) copy-start(f32[12]{0:T(128)} %factor_ref.1) | copy-start | bytes 148
  0.7 8.7 %collective-permute-start = (bf16[4,8,768]{2,1,0:T(8,128)(2,1)}, bf16[4,8,768]{2,1,0:T(8,128)(2,1)S(1)}, u32[]{:S(2)}, u32[]{:S(2)}) collective-permute-start(bf16[4,8,768]{2,1,0:T(8,128)(2,1)} %param.12), channel_id=1, source_target_pairs={{0,4},{1,5},{2,6},{3,7},{4,8},{5,9},{6,10},{7,11},{8,12},{9,13},{1... | collective-permute-start | bytes 147464 | tf_op jit(solution)/shard_map/ppermute | solution.py:319
  3.7 6.9 %collective-permute-start.1 = (bf16[4,8,768]{2,1,0:T(8,128)(2,1)}, bf16[4,8,768]{2,1,0:T(8,128)(2,1)S(1)}, u32[]{:S(2)}, u32[]{:S(2)}) collective-permute-start(bf16[4,8,768]{2,1,0:T(8,128)(2,1)} %param.12), channel_id=1, source_target_pairs={{0,8},{1,9},{2,10},{3,11},{4,12},{5,13},{6,14},{7,15},{8,0},{9,1},... | collective-permute-start | bytes 147464 | tf_op jit(solution)/shard_map/ppermute | solution.py:319
  6.3 4.3 %collective-permute-start.2 = (bf16[4,8,768]{2,1,0:T(8,128)(2,1)}, bf16[4,8,768]{2,1,0:T(8,128)(2,1)S(1)}, u32[]{:S(2)}, u32[]{:S(2)}) collective-permute-start(bf16[4,8,768]{2,1,0:T(8,128)(2,1)} %param.12), channel_id=1, source_target_pairs={{0,12},{1,13},{2,14},{3,15},{4,0},{5,1},{6,2},{7,3},{8,4},{9,5},{1... | collective-permute-start | bytes 147464 | tf_op jit(solution)/shard_map/ppermute | solution.py:319
  8.5 0.8 %copy-start.4 = (bf16[4,8,768]{2,1,0:T(8,128)(2,1)S(1)}, bf16[4,8,768]{2,1,0:T(8,128)(2,1)}, u32[]{:S(2)}) copy-start(bf16[4,8,768]{2,1,0:T(8,128)(2,1)} %q_hbm.1) | copy-start | bytes 147460
  9.3 23.3 %copy-start.2 = (bf16[768,768]{1,0:T(8,128)(2,1)S(1)}, bf16[768,768]{1,0:T(8,128)(2,1)}, u32[]{:S(2)}) copy-start(bf16[768,768]{1,0:T(8,128)(2,1)} %refs_5_.1) | copy-start | bytes 3538948
  10.7 6.4 %collective-permute-start.4 = (bf16[4,32,768]{2,1,0:T(8,128)(2,1)S(1)}, bf16[4,32,768]{2,1,0:T(8,128)(2,1)S(1)}, u32[]{:S(2)}, u32[]{:S(2)}) collective-permute-start(bf16[4,32,768]{2,1,0:T(8,128)(2,1)S(1)} %constant_dynamic-update-slice_fusion.refs_1_), channel_id=1, source_target_pairs={{0,2},{1,3},{2,0},{3,1},{4,6},{5,7},{6,4},{7,5},{8,10},{9,11},{10,... | collective-permute-start | bytes 589832 | tf_op jit(solution)/shard_map/ppermute | solution.py:319
  12.4 9.4 %collective-permute-start.3 = (bf16[4,32,768]{2,1,0:T(8,128)(2,1)S(1)}, bf16[4,32,768]{2,1,0:T(8,128)(2,1)S(1)}, u32[]{:S(2)}, u32[]{:S(2)}) collective-permute-start(bf16[4,32,768]{2,1,0:T(8,128)(2,1)S(1)} %constant_dynamic-update-slice_fusion.refs_1_), channel_id=1, source_target_pairs={{0,1},{1,0},{2,3},{3,2},{4,5},{5,4},{6,7},{7,6},{8,9},{9,8},{10,11... | collective-permute-start | bytes 589832 | tf_op jit(solution)/shard_map/ppermute | solution.py:319
  12.4 6.7 %collective-permute-start.7 = (bf16[4,8,768]{2,1,0:T(8,128)(2,1)}, bf16[4,8,768]{2,1,0:T(8,128)(2,1)S(1)}, u32[]{:S(2)}, u32[]{:S(2)}) collective-permute-start(bf16[4,8,768]{2,1,0:T(8,128)(2,1)} %param.13), channel_id=1, source_target_pairs={{0,4},{1,5},{2,6},{3,7},{4,8},{5,9},{6,10},{7,11},{8,12},{9,13},{1... | collective-permute-start | bytes 147464 | tf_op jit(solution)/shard_map/ppermute | solution.py:319
  13.1 7.7 %collective-permute-start.8 = (bf16[4,8,768]{2,1,0:T(8,128)(2,1)}, bf16[4,8,768]{2,1,0:T(8,128)(2,1)S(1)}, u32[]{:S(2)}, u32[]{:S(2)}) collective-permute-start(bf16[4,8,768]{2,1,0:T(8,128)(2,1)} %param.13), channel_id=1, source_target_pairs={{0,8},{1,9},{2,10},{3,11},{4,12},{5,13},{6,14},{7,15},{8,0},{9,1},... | collective-permute-start | bytes 147464 | tf_op jit(solution)/shard_map/ppermute | solution.py:319
  16.0 4.9 %collective-permute-start.9 = (bf16[4,8,768]{2,1,0:T(8,128)(2,1)}, bf16[4,8,768]{2,1,0:T(8,128)(2,1)S(1)}, u32[]{:S(2)}, u32[]{:S(2)}) collective-permute-start(bf16[4,8,768]{2,1,0:T(8,128)(2,1)} %param.13), channel_id=1, source_target_pairs={{0,12},{1,13},{2,14},{3,15},{4,0},{5,1},{6,2},{7,3},{8,4},{9,5},{1... | collective-permute-start | bytes 147464 | tf_op jit(solution)/shard_map/ppermute | solution.py:319
  20.8 1.5 %collective-permute-start.5 = (bf16[4,32,768]{2,1,0:T(8,128)(2,1)S(1)}, bf16[4,32,768]{2,1,0:T(8,128)(2,1)S(1)}, u32[]{:S(2)}, u32[]{:S(2)}) collective-permute-start(bf16[4,32,768]{2,1,0:T(8,128)(2,1)S(1)} %collective-permute-done.4.refs_2_), channel_id=1, source_target_pairs={{0,1},{1,0},{2,3},{3,2},{4,5},{5,4},{6,7},{7,6},{8,9},{9,8},{10,11... | collective-permute-start | bytes 589832 | tf_op jit(solution)/shard_map/ppermute | solution.py:319
  20.9 7.3 %collective-permute-start.10 = (bf16[4,32,768]{2,1,0:T(8,128)(2,1)S(1)}, bf16[4,32,768]{2,1,0:T(8,128)(2,1)S(1)}, u32[]{:S(2)}, u32[]{:S(2)}) collective-permute-start(bf16[4,32,768]{2,1,0:T(8,128)(2,1)S(1)} %constant_dynamic-update-slice_fusion.4.refs_1_), channel_id=1, source_target_pairs={{0,2},{1,3},{2,0},{3,1},{4,6},{5,7},{6,4},{7,5},{8,10},{9,11},{10,... | collective-permute-start | bytes 589832 | tf_op jit(solution)/shard_map/ppermute | solution.py:319
  21.6 11.0 %copy-start.7 = (s32[2]{0:T(128)}, s32[2]{0:T(128)S(1)}, u32[]{:S(2)}) copy-start(s32[2]{0:T(128)S(1)} %pad_add_fusion.scalar_ref) | copy-start | bytes 28
  21.6 10.9 %collective-permute-start.11 = (bf16[4,32,768]{2,1,0:T(8,128)(2,1)S(1)}, bf16[4,32,768]{2,1,0:T(8,128)(2,1)S(1)}, u32[]{:S(2)}, u32[]{:S(2)}) collective-permute-start(bf16[4,32,768]{2,1,0:T(8,128)(2,1)S(1)} %constant_dynamic-update-slice_fusion.4.refs_1_), channel_id=1, source_target_pairs={{0,1},{1,0},{2,3},{3,2},{4,5},{5,4},{6,7},{7,6},{8,9},{9,8},{10,11... | collective-permute-start | bytes 589832 | tf_op jit(solution)/shard_map/ppermute | solution.py:319
  23.4 9.8 %copy-start.5 = (f32[16,128]{1,0:T(8,128)}, f32[16,128]{1,0:T(8,128)S(1)}, u32[]{:S(2)}) copy-start(f32[16,128]{1,0:T(8,128)S(1)} %get-tuple-element.33.head_ref.factor_ref) | copy-start | bytes 24580
  23.5 9.8 %copy-start.9 = (f32[8,128]{1,0:T(8,128)}, f32[8,128]{1,0:T(8,128)S(1)}, u32[]{:S(2)}) copy-start(f32[8,128]{1,0:T(8,128)S(1)} %get-tuple-element.35.own_ref) | copy-start | bytes 12292
  28.2 4.4 %collective-permute-start.12 = (bf16[4,32,768]{2,1,0:T(8,128)(2,1)S(1)}, bf16[4,32,768]{2,1,0:T(8,128)(2,1)S(1)}, u32[]{:S(2)}, u32[]{:S(2)}) collective-permute-start(bf16[4,32,768]{2,1,0:T(8,128)(2,1)S(1)} %collective-permute-done.10.refs_2_), channel_id=1, source_target_pairs={{0,1},{1,0},{2,3},{3,2},{4,5},{5,4},{6,7},{7,6},{8,9},{9,8},{10,11... | collective-permute-start | bytes 589832 | tf_op jit(solution)/shard_map/ppermute | solution.py:319
  28.2 4.2 %collective-permute-start.6 = (f32[96,128]{1,0:T(8,128)S(1)}, f32[96,128]{1,0:T(8,128)S(1)}, u32[]{:S(2)}, u32[]{:S(2)}) collective-permute-start(f32[96,128]{1,0:T(8,128)S(1)} %shard_map.115.refs_0_), channel_id=1, source_target_pairs={{0,16},{16,0},{1,17},{17,1},{2,18},{18,2},{3,19},{19,3},{4,20},{20... | collective-permute-start | bytes 147464 | tf_op jit(solution)/shard_map/ppermute | solution.py:421
  32.6 9.9 %copy-start = (bf16[768,1152]{1,0:T(8,128)(2,1)S(1)}, bf16[768,1152]{1,0:T(8,128)(2,1)}, u32[]{:S(2)}) copy-start(bf16[768,1152]{1,0:T(8,128)(2,1)} %refs_2_.1) | copy-start | bytes 5308420
  34.2 13.1 %copy-start.6 = (f32[16,128]{1,0:T(8,128)S(1)}, f32[16,128]{1,0:T(8,128)}, u32[]{:S(2)}) copy-start(f32[16,128]{1,0:T(8,128)} %copy-done.5) | copy-start | bytes 24580
  34.2 13.1 %copy-start.8 = (s32[2]{0:T(128)S(1)}, s32[2]{0:T(128)}, u32[]{:S(2)}) copy-start(s32[2]{0:T(128)} %copy-done.7) | copy-start | bytes 28
  34.2 13.1 %copy-start.10 = (f32[8,128]{1,0:T(8,128)S(1)}, f32[8,128]{1,0:T(8,128)}, u32[]{:S(2)}) copy-start(f32[8,128]{1,0:T(8,128)} %copy-done.9) | copy-start | bytes 12292
  34.2 13.1 %all-to-all-start = ((f32[16,24,128]{2,1,0:T(8,128)}), f32[16,24,128]{2,1,0:T(8,128)S(1)}, u32[]{:S(2)}, u32[]{:S(2)}) async-start(f32[16,24,128]{2,1,0:T(8,128)} %shard_map.120), calls=%async_computation | async-start | bytes 393216 | tf_op jit(solution)/shard_map/all_to_all | solution.py:448
  38.4 10.6 %copy-start.1 = (bf16[768,768]{1,0:T(8,128)(2,1)S(1)}, bf16[768,768]{1,0:T(8,128)(2,1)}, u32[]{:S(2)}) copy-start(bf16[768,768]{1,0:T(8,128)(2,1)} %refs_1_.1) | copy-start | bytes 3538948
  38.4 4.2 %collective-permute-start.13 = (bf16[32,768]{1,0:T(8,128)(2,1)S(1)}, bf16[32,768]{1,0:T(8,128)(2,1)S(1)}, u32[]{:S(2)}, u32[]{:S(2)}) collective-permute-start(bf16[32,768]{1,0:T(8,128)(2,1)S(1)} %get-tuple-element.30.refs_0_), channel_id=1, source_target_pairs={{0,16},{16,0},{1,17},{17,1},{2,18},{18,2},{3,19},{19,3},{4,20},{20... | collective-permute-start | bytes 147464 | tf_op jit(solution)/shard_map/ppermute | solution.py:457
  43.0 6.0 %collective-permute-start.14 = (bf16[64,1152]{1,0:T(8,128)(2,1)S(1)}, bf16[64,1152]{1,0:T(8,128)(2,1)S(1)}, u32[]{:S(2)}, u32[]{:S(2)}) collective-permute-start(bf16[64,1152]{1,0:T(8,128)(2,1)S(1)} %shard_map.119.own_ref), channel_id=1, source_target_pairs={{0,16},{16,0},{1,17},{17,1},{2,18},{18,2},{3,19},{19,3},{4,20},{20... | collective-permute-start | bytes 442376 | tf_op jit(solution)/shard_map/ppermute | solution.py:471

commit v5 on v4

--- a/solution.py
+++ b/solution.py
@@ -68,7 +68,7 @@
             masked_ref[r, block * span : (block + 1) * span, :] = q
 
 
-def prepare_kernel(heads, stages, scalar_ref, skip_hbm, gain_ref, factor_ref, *refs):
+def prepare_kernel(heads, stages, scalar_ref, skip_hbm, gain_ref, factor_ref, offset_ref, *refs):
     wide_skip_ref, wide_gain_ref, head_ref, order_ref, own_ref, slab_ref, skip_ref, sems = refs
     _, sites, embed = skip_ref.shape
     copy = pltpu.make_async_copy(skip_hbm, skip_ref, sems.at[0])
@@ -78,7 +78,7 @@
     factors = jnp.zeros(head_ref.shape, F32)
     for h in range(heads):
         factors = jnp.where(row == h, factor_ref[h], factors)
-    head_ref[...] = factors
+    head_ref[...] = jnp.where(row == round_up(heads, 8), offset_ref[0], factors)
     seq_index, pos_index = scalar_ref[0], scalar_ref[1]
     length = order_ref.shape[0]
     row = lax.broadcasted_iota(jnp.int32, (length, length), 0)
@@ -216,7 +216,7 @@
     column_attend(head, factor, query_ref[...].astype(F32), keys, values, *refs)
 
 
-def swapped_column_kernel(head, factor, scalar_ref, own_ref, other_ref, *refs):
+def swapped_column_kernel(head, factor, own_ref, other_ref, *refs):
     rows, sites, embed = refs[2].shape
     cells, columns = own_ref.shape
     half = cells // 2
@@ -245,11 +245,12 @@
                 values.append(value[t * sites : (t + 1) * sites, :])
         column_attend(head, factor, query, keys, values, *refs)
 
-    pl.when(scalar_ref[0] == 0)(functools.partial(attend, True))
-    pl.when(scalar_ref[0] == 1)(functools.partial(attend, False))
-
-
-def contact_kernel(heads, scalar_ref, pair_ref, factor_ref, offset_ref, own_ref, slab_ref, out_ref, held):
+    seq_index = lax.axis_index("seq")
+    pl.when(seq_index == 0)(functools.partial(attend, True))
+    pl.when(seq_index == 1)(functools.partial(attend, False))
+
+
+def contact_kernel(heads, pair_ref, factor_ref, own_ref, slab_ref, out_ref, held):
     count, step, length = pair_ref.shape
     head_rows = round_up(heads, 8)
     sites = step - head_rows
@@ -258,20 +259,20 @@
     for n in range(1, count):
         total = total + pair_ref[n, 0:head_rows, :]
     held[0:head_rows, :] = total
-    held[head_rows:step, :] = pair_ref[scalar_ref[1], head_rows:step, :]
-    first = scalar_ref[0] * blocks
+    held[head_rows:step, :] = pair_ref[lax.axis_index("pos"), head_rows:step, :]
+    first = lax.axis_index("seq") * blocks
     table = jnp.concatenate(
         [pair_ref[first + n, head_rows:step, :] for n in range(blocks)], axis=0
     )
     amount = jnp.sum(total, axis=1, keepdims=True)
     real = lax.broadcasted_iota(jnp.int32, (head_rows, 1), 0) < heads
-    share = jnp.where(real, factor_ref[:, 0:1] / jnp.where(real, amount, 1.0), 0.0)
+    share = jnp.where(real, factor_ref[0:head_rows, 0:1] / jnp.where(real, amount, 1.0), 0.0)
     slab = dot_nn(held[...], slab_ref[...], HIGHEST)
     own = dot_nt(own_ref[...], total * share, HIGHEST)
     mirrored = dot_nt(own_ref[...], table, HIGHEST)
     adjuster = dot_nn(own, slab[0:head_rows, :], HIGHEST)
     out_ref[...] = jax.nn.sigmoid(
-        slab[head_rows:step, :] + mirrored - adjuster + offset_ref[0]
+        slab[head_rows:step, :] + mirrored - adjuster + factor_ref[head_rows : head_rows + 1, 0:1]
     )
 
 
@@ -369,24 +370,24 @@
         scratch=[pltpu.VMEM((rows, sites, embed), BF16), pltpu.SemaphoreType.DMA((1,))],
     )
 
-    key_first = [lateral_matched_vectors]
-    key_first += send_all(key_first, pos_count, outer)
-    key_first[-1] = after(key_first[-1], masked)
+    both = jnp.concatenate([lateral_matched_vectors, lateral_carried_vectors], axis=0)
+    arrived = send_all([both], pos_count, outer)
+    arrived[-1] = after(arrived[-1], masked)
+    key_first = [lateral_matched_vectors] + [part[:rows] for part in arrived]
     key_parts = [jnp.concatenate(key_first, axis=1)]
     if middle:
         key_parts += send_all(key_parts, pos_count, middle)
-    value_first = [after(lateral_carried_vectors, key_parts[0])]
-    value_first += send_all(value_first, pos_count, outer)
+    arrived[-1] = after(arrived[-1], key_parts[0])
+    value_first = [lateral_carried_vectors] + [part[rows:] for part in arrived]
+    value_parts = [jnp.concatenate(value_first, axis=1)]
+    if middle:
+        value_parts += send_all(value_parts, pos_count, middle)
     near = sum(part.shape[1] for part in key_parts)
     partial = call(
         functools.partial(logits_kernel, len(key_parts)),
         jax.ShapeDtypeStruct((heads * sites, near), F32),
         [masked, *key_parts],
     )
-    value_first = [value_first[0]] + [after(part, partial) for part in value_first[1:]]
-    value_parts = [jnp.concatenate(value_first, axis=1)]
-    if middle:
-        value_parts += send_all(value_parts, pos_count, middle)
     if len(stages) > 2:
         far_parts = send_all(key_parts, pos_count, stages[2])
         partial = call(
@@ -399,7 +400,7 @@
         (
             jax.ShapeDtypeStruct((cells, embed), F32),
             jax.ShapeDtypeStruct((8, embed), F32),
-            jax.ShapeDtypeStruct((head_rows, 128), F32),
+            jax.ShapeDtypeStruct((head_rows + 8, 128), F32),
             jax.ShapeDtypeStruct((length, length), F32),
             jax.ShapeDtypeStruct((sites, length), F32),
             jax.ShapeDtypeStruct((length, slab_width), F32),
@@ -409,18 +410,19 @@
             skip_stream_input,
             upright_normalizer_multiplier,
             regression_factors,
+            regression_offset,
         ],
-        smem=(0, 3),
+        smem=(0, 3, 4),
         hbm=(1,),
         scratch=[pltpu.VMEM((rows, sites, embed), BF16), pltpu.SemaphoreType.DMA((1,))],
     )
-    if len(stages) > 2:
-        value_parts = value_parts[:1] + [after(part, skip) for part in value_parts[1:]]
-        value_parts += send_all(value_parts, pos_count, stages[2])
     if seq_count == 2:
         partials = [partial, after(lax.ppermute(partial, "seq", swap), skip)]
     else:
         partials = [lax.psum(partial, "seq")]
+    if len(stages) > 2:
+        value_parts = value_parts[:1] + [after(part, partials[-1]) for part in value_parts[1:]]
+        value_parts += send_all(value_parts, pos_count, stages[2])
     shares = call(
         functools.partial(
             softmax_kernel, 1.0 / (math.sqrt(head) * math.sqrt(rows * seq_count))
@@ -449,8 +451,7 @@
     pairing_chances = call(
         functools.partial(contact_kernel, heads),
         jax.ShapeDtypeStruct((sites, slab_width), F32),
-        [scalars, pair_all, head_factors, regression_offset, own_select, slab_select],
-        smem=(0, 3),
+        [pair_all, head_factors, own_select, slab_select],
         scratch=[pltpu.VMEM((head_rows + sites, length), F32)],
     )
     if swapped:
@@ -463,10 +464,10 @@
         functools.partial(project_kernel, len(normed_all)),
         jax.ShapeDtypeStruct((cells * len(normed_all), weight.shape[1]), BF16),
         [*normed_all, weight],
+        bytes_accessed=10000000,
     )
     if swapped:
         column, column_inputs = swapped_column_kernel, [
-            scalars,
             projected,
             lax.ppermute(projected, "seq", swap),
         ]
@@ -477,7 +478,6 @@
         functools.partial(column, head, 1.0 / math.sqrt(head)),
         jax.ShapeDtypeStruct((rows, sites, embed), BF16),
         [*column_inputs, after(hidden, pairing_chances), upright_closing_linear],
-        smem=(0,) if swapped else (),
         scratch=[
             pltpu.VMEM((cells * rows * seq_count, embed), F32),
             pltpu.VMEM((cells, embed), F32),

time: 51.4 us -> 52.3 us (1.018)
  starting transfers between devices: 22.2 us -> 18.2 us
  waiting for transfers between devices: 17.5 us -> 21.3 us
  local copies, waits for them, and re-layouts: 2.57 us -> 3.89 us
  Pallas kernels: 7.11 us -> 6.01 us
  other arithmetic: 0.07 us -> 1 us
    ppermute x12 -> x9, waiting for transfers between devices: 10.1 us -> 14.8 us  [send_pos(): return lax.ppermute(array, 'pos', pairs)]
    ppermute x12 -> x9, starting transfers between devices: 13.4 us -> 9.27 us  [send_pos(): return lax.ppermute(array, 'pos', pairs)]
    ppermute x1, waiting for transfers between devices: 2.66 us -> 0.98 us  [per_device(): partials = [partial, after(lax.ppermute(partial, 'seq', swap), skip)]]
    pallas_call x10, Pallas kernels: 7.11 us -> 6.01 us  [call(): pl.pallas_call(kernel, out_shape=out_shape, in_specs=specs, out_specs=jax...]
    concatenate x0 -> x2, other arithmetic: none -> 0.92 us  [the longest x1 0.91 us: per_device(): key_parts = [jnp.concatenate(key_first, axis=1)]]
    ppermute x1, waiting for transfers between devices: 0.01 us -> 0.92 us  [per_device(): lax.ppermute(projected, 'seq', swap)]
    concatenate x2 -> x1, local copies, waits for them, and re-layouts: 0.01 us -> 0.8 us  [per_device(): jnp.concatenate([lateral_matched_vectors, lateral_carried_vectors], axis=0)]
    unnamed x32 -> x21, local copies, waits for them, and re-layouts: 2.56 us -> 3.06 us
  transfers between devices with their start and end apart: 16 -> 13, of which waited for: 9 -> 10; matrix products, arithmetic and copies ran while one was open for 3% -> 0% of each run, Pallas kernels for 7% -> 6%
where the time goes in v5:
time: 52.3 us; the launch traced here: 51.8 us
  waiting for transfers between devices  21.3 us (41%)
  starting transfers between devices  18.2 us (35%)
  Pallas kernels  6.01 us (11%)
  local copies, waits for them, and re-layouts  3.89 us (7%)
  between operations  1.45 us (3%)
  other arithmetic  1 us (2%)
    ppermute x9, waiting for transfers between devices, send_pos(): return lax.ppermute(array, 'pos', pairs)  14.8 us
    ppermute x9, starting transfers between devices, send_pos(): return lax.ppermute(array, 'pos', pairs)  9.27 us
    pallas_call x10, Pallas kernels, call(): pl.pallas_call(kernel, out_shape=out_shape, in_specs=specs, out_specs=jax...  6.01 us
    all_to_all x1, starting transfers between devices, per_device(): lax.all_to_all(pair_local, 'pos', split_axis=0, concat_axis=0, tiled=True)  4.23 us
    unnamed x21, local copies, waits for them, and re-layouts  3.06 us
    ppermute x1, waiting for transfers between devices, per_device(): normed_all = [normed, lax.ppermute(normed, 'seq', swap)]  2.81 us
    all_to_all x1, waiting for transfers between devices, per_device(): lax.all_to_all(pair_local, 'pos', split_axis=0, concat_axis=0, tiled=True)  1.83 us
    ppermute x1, starting transfers between devices, per_device(): partials = [partial, after(lax.ppermute(partial, 'seq', swap), skip)]  1.56 us
  transfers between devices with their start and end apart: 13, of which 10 were waited for; matrix products, arithmetic and copies ran while one was open for 0% of the time, Pallas kernels for 6%

profile of v5, /device:TPU:0, one launch (start us, length us, event | category | flops | bytes accessed | tf_op | source)
XLA Modules:
  0.0 51.8 jit_solution(13902359079330452411)
XLA Ops:
  0.6 0.0 copy-start.9
  0.6 0.8 %constant_dynamic-update-slice_fusion.1 = bf16[8,8,768]{2,1,0:T(8,128)(2,1)S(1)} fusion(bf16[4,8,768]{2,1,0:T(8,128)(2,1)} %param.12), kind=kLoop, calls=%fused_computation.3 | loop fusion | bytes 98304
  1.5 0.8 %constant_dynamic-update-slice_fusion = bf16[8,8,768]{2,1,0:T(8,128)(2,1)S(1)} fusion(bf16[8,8,768]{2,1,0:T(8,128)(2,1)S(1)} %constant_dynamic-update-slice_fusion.1, bf16[4,8,768]{2,1,0:T(8,128)(2,1)} %param.13), kind=kLoop, calls=%fused_computation.2 | loop fusion | bytes 98304 | tf_op jit(solution)/shard_map/concatenate | solution.py:373
  2.3 3.0 %collective-permute-start = (bf16[8,8,768]{2,1,0:T(8,128)(2,1)S(1)}, bf16[8,8,768]{2,1,0:T(8,128)(2,1)S(1)}, u32[]{:S(2)}, u32[]{:S(2)}) collective-permute-start(bf16[8,8,768]{2,1,0:T(8,128)(2,1)S(1)} %constant_dynamic-update-slice_fusion), channel_id=1, source_target_pairs={{0,4},{1,5},{2,6},{3,7},{4,8},{5,9},{6,10},{7,11},{8,12},{9,13},{1... | collective-permute-start | bytes 294920 | tf_op jit(solution)/shard_map/ppermute | solution.py:320
  5.3 2.0 %collective-permute-start.2 = (bf16[8,8,768]{2,1,0:T(8,128)(2,1)S(1)}, bf16[8,8,768]{2,1,0:T(8,128)(2,1)S(1)}, u32[]{:S(2)}, u32[]{:S(2)}) collective-permute-start(bf16[8,8,768]{2,1,0:T(8,128)(2,1)S(1)} %constant_dynamic-update-slice_fusion), channel_id=1, source_target_pairs={{0,12},{1,13},{2,14},{3,15},{4,0},{5,1},{6,2},{7,3},{8,4},{9,5},{1... | collective-permute-start | bytes 294920 | tf_op jit(solution)/shard_map/ppermute | solution.py:320
  7.3 1.0 %collective-permute-start.1 = (bf16[8,8,768]{2,1,0:T(8,128)(2,1)S(1)}, bf16[8,8,768]{2,1,0:T(8,128)(2,1)S(1)}, u32[]{:S(2)}, u32[]{:S(2)}) collective-permute-start(bf16[8,8,768]{2,1,0:T(8,128)(2,1)S(1)} %constant_dynamic-update-slice_fusion), channel_id=1, source_target_pairs={{0,8},{1,9},{2,10},{3,11},{4,12},{5,13},{6,14},{7,15},{8,0},{9,1},... | collective-permute-start | bytes 294920 | tf_op jit(solution)/shard_map/ppermute | solution.py:320
  8.3 0.8 %copy-done.4 = bf16[4,8,768]{2,1,0:T(8,128)(2,1)S(1)} copy-done((bf16[4,8,768]{2,1,0:T(8,128)(2,1)S(1)}, bf16[4,8,768]{2,1,0:T(8,128)(2,1)}, u32[]{:S(2)}) %copy-start.4) | copy-done | bytes 49176
  9.1 0.1 shard_map.113.refs_0_
  9.2 1.6 %collective-permute-done = bf16[8,8,768]{2,1,0:T(8,128)(2,1)S(1)} collective-permute-done((bf16[8,8,768]{2,1,0:T(8,128)(2,1)S(1)}, bf16[8,8,768]{2,1,0:T(8,128)(2,1)S(1)}, u32[]{:S(2)}, u32[]{:S(2)}) %collective-permute-start) | collective-permute-done | bytes 98336 | tf_op jit(solution)/shard_map/ppermute | solution.py:320
  10.8 0.8 %collective-permute-done.2 = bf16[8,8,768]{2,1,0:T(8,128)(2,1)S(1)} collective-permute-done((bf16[8,8,768]{2,1,0:T(8,128)(2,1)S(1)}, bf16[8,8,768]{2,1,0:T(8,128)(2,1)S(1)}, u32[]{:S(2)}, u32[]{:S(2)}) %collective-permute-start.2) | collective-permute-done | bytes 98336 | tf_op jit(solution)/shard_map/ppermute | solution.py:320
  11.7 0.0 copy-start.8
  11.7 4.7 %collective-permute-done.1 = bf16[8,8,768]{2,1,0:T(8,128)(2,1)S(1)} collective-permute-done((bf16[8,8,768]{2,1,0:T(8,128)(2,1)S(1)}, bf16[8,8,768]{2,1,0:T(8,128)(2,1)S(1)}, u32[]{:S(2)}, u32[]{:S(2)}) %collective-permute-start.1) | collective-permute-done | bytes 98336 | tf_op jit(solution)/shard_map/ppermute | solution.py:320
  16.4 0.0 copy-start.2
  16.4 0.9 %pad_maximum_fusion.refs_1_ = bf16[4,32,768]{2,1,0:T(8,128)(2,1)S(1)} fusion(bf16[4,8,768]{2,1,0:T(8,128)(2,1)S(1)} %slice.20, bf16[4,8,768]{2,1,0:T(8,128)(2,1)S(1)} %get-tuple-element.35, bf16[4,8,768]{2,1,0:T(8,128)(2,1)S(1)} %get-tuple-element.33, bf16[4,8,768]{2,1,0:T(8,128)(2,1)} %param.12), kind=kLoop, calls=%fused_computation | loop fusion | flops 786432 | bytes 393216 | tf_op jit(solution)/shard_map/concatenate | solution.py:377
  17.4 1.6 %collective-permute-start.4 = (bf16[4,32,768]{2,1,0:T(8,128)(2,1)S(1)}, bf16[4,32,768]{2,1,0:T(8,128)(2,1)S(1)}, u32[]{:S(2)}, u32[]{:S(2)}) collective-permute-start(bf16[4,32,768]{2,1,0:T(8,128)(2,1)S(1)} %pad_maximum_fusion.refs_1_), channel_id=1, source_target_pairs={{0,2},{1,3},{2,0},{3,1},{4,6},{5,7},{6,4},{7,5},{8,10},{9,11},{10,... | collective-permute-start | bytes 589832 | tf_op jit(solution)/shard_map/ppermute | solution.py:320
  18.9 0.0 collective-permute-start.3
  18.9 5.2 %collective-permute-done.4.refs_2_ = bf16[4,32,768]{2,1,0:T(8,128)(2,1)S(1)} collective-permute-done((bf16[4,32,768]{2,1,0:T(8,128)(2,1)S(1)}, bf16[4,32,768]{2,1,0:T(8,128)(2,1)S(1)}, u32[]{:S(2)}, u32[]{:S(2)}) %collective-permute-start.4) | collective-permute-done | bytes 196640 | tf_op jit(solution)/shard_map/ppermute | solution.py:320
  24.1 0.0 collective-permute-start.5
  24.1 1.5 %collective-permute-start.7 = (bf16[4,32,768]{2,1,0:T(8,128)(2,1)S(1)}, bf16[4,32,768]{2,1,0:T(8,128)(2,1)S(1)}, u32[]{:S(2)}, u32[]{:S(2)}) collective-permute-start(bf16[4,32,768]{2,1,0:T(8,128)(2,1)S(1)} %pad_maximum_fusion.1.refs_1_), channel_id=1, source_target_pairs={{0,2},{1,3},{2,0},{3,1},{4,6},{5,7},{6,4},{7,5},{8,10},{9,11},{10,... | collective-permute-start | bytes 589832 | tf_op jit(solution)/shard_map/ppermute | solution.py:320
  25.7 0.2 shard_map.114.refs_3_
  25.9 0.0 collective-permute-done.3.refs_1_
  25.9 0.0 collective-permute-done.5.refs_2_
  25.9 0.3 shard_map.115.refs_0_
  26.2 1.6 %collective-permute-start.6 = (f32[96,128]{1,0:T(8,128)S(1)}, f32[96,128]{1,0:T(8,128)S(1)}, u32[]{:S(2)}, u32[]{:S(2)}) collective-permute-start(f32[96,128]{1,0:T(8,128)S(1)} %shard_map.115.refs_0_), channel_id=1, source_target_pairs={{0,16},{16,0},{1,17},{17,1},{2,18},{18,2},{3,19},{19,3},{4,20},{20... | collective-permute-start | bytes 147464 | tf_op jit(solution)/shard_map/ppermute | solution.py:420
  27.8 0.1 pad_add_fusion.scalar_ref
  28.5 0.1 collective-permute-start.8
  28.6 0.8 %shard_map.116 = (f32[32,768]{1,0:T(8,128)S(1)}, f32[8,768]{1,0:T(8,128)S(1)}, f32[24,128]{1,0:T(8,128)S(1)}, f32[128,128]{1,0:T(8,128)S(1)}, f32[8,128]{1,0:T(8,128)S(1)}, /*index=5*/f32[128,64]{1,0:T(8,128)S(1)}) custom-call(s32[2]{0:T(128)S(1)} %pad_add_fusion.scalar_ref, bf16[4,8,768]{2,1,0:T(8,128)(2,1)S(1)} %copy-done.3, f32[768]{0:T(1024)S(1)} %copy-done.7, ...), custom_call_target="tpu_custom_call" | custom-call | flops 1000000 | bytes 1000000 | tf_op jit(solution)/shard_map/pallas_call | solution.py:292
  29.4 1.0 %collective-permute-done.6.refs_1_ = f32[96,128]{1,0:T(8,128)S(1)} collective-permute-done((f32[96,128]{1,0:T(8,128)S(1)}, f32[96,128]{1,0:T(8,128)S(1)}, u32[]{:S(2)}, u32[]{:S(2)}) %collective-permute-start.6) | collective-permute-done | bytes 49184 | tf_op jit(solution)/shard_map/ppermute | solution.py:420
  30.4 1.1 %collective-permute-done.7.refs_2_ = bf16[4,32,768]{2,1,0:T(8,128)(2,1)S(1)} collective-permute-done((bf16[4,32,768]{2,1,0:T(8,128)(2,1)S(1)}, bf16[4,32,768]{2,1,0:T(8,128)(2,1)S(1)}, u32[]{:S(2)}, u32[]{:S(2)}) %collective-permute-start.7) | collective-permute-done | bytes 196640 | tf_op jit(solution)/shard_map/ppermute | solution.py:320
  31.5 0.0 collective-permute-start.9
  31.5 0.2 shard_map.117.refs_0_.w_ref
  31.7 0.0 collective-permute-done.8.refs_3_
  31.7 1.2 %collective-permute-done.9.refs_4_ = bf16[4,32,768]{2,1,0:T(8,128)(2,1)S(1)} collective-permute-done((bf16[4,32,768]{2,1,0:T(8,128)(2,1)S(1)}, bf16[4,32,768]{2,1,0:T(8,128)(2,1)S(1)}, u32[]{:S(2)}, u32[]{:S(2)}) %collective-permute-start.9) | collective-permute-done | bytes 196640 | tf_op jit(solution)/shard_map/ppermute | solution.py:320
  33.0 0.6 %shard_map.118 = (f32[32,768]{1,0:T(8,128)S(1)}, bf16[32,768]{1,0:T(8,128)(2,1)S(1)}) custom-call(bf16[96,128]{1,0:T(8,128)(2,1)S(1)} %shard_map.117.refs_0_.w_ref, bf16[4,32,768]{2,1,0:T(8,128)(2,1)S(1)} %pad_maximum_fusion.1.refs_1_, bf16[4,32,768]{2,1,0:T(8,128)(2,1)S(1)} %collective-permute-done.7.refs_2_, ...), custom_call_target="tpu_custom_call" | custom-call | flops 1000000 | bytes 1000000 | tf_op jit(solution)/shard_map/pallas_call | solution.py:292
  33.6 0.0 copy-start.5
  33.6 0.6 %copy-done.5 = bf16[32,768]{1,0:T(8,128)(2,1)} copy-done((bf16[32,768]{1,0:T(8,128)(2,1)}, bf16[32,768]{1,0:T(8,128)(2,1)S(1)}, u32[]{:S(2)}) %copy-start.5) | copy-done | bytes 49176
  34.2 0.9 %shard_map.120 = f32[16,24,128]{2,1,0:T(8,128)} custom-call(bf16[96,128]{1,0:T(8,128)(2,1)S(1)} %shard_map.117.refs_0_.w_ref, f32[24,128]{1,0:T(8,128)S(1)} %get-tuple-element.27.head_ref.factor_ref, f32[128,128]{1,0:T(8,128)S(1)} %get-tuple-element.28.order_ref), custom_call_target="tpu_custom_call" | custom-call | flops 1000000 | bytes 10000000 | tf_op jit(solution)/shard_map/pallas_call | solution.py:292
  35.2 4.2 %all-to-all-start = ((f32[16,24,128]{2,1,0:T(8,128)}), f32[16,24,128]{2,1,0:T(8,128)S(1)}, u32[]{:S(2)}, u32[]{:S(2)}) async-start(f32[16,24,128]{2,1,0:T(8,128)} %shard_map.120), calls=%async_computation | async-start | bytes 393216 | tf_op jit(solution)/shard_map/all_to_all | solution.py:450
  39.4 0.0 copy-start.1
  39.4 1.6 %collective-permute-start.10 = (bf16[32,768]{1,0:T(8,128)(2,1)}, bf16[32,768]{1,0:T(8,128)(2,1)S(1)}, u32[]{:S(2)}, u32[]{:S(2)}) collective-permute-start(bf16[32,768]{1,0:T(8,128)(2,1)} %copy-done.5), channel_id=1, source_target_pairs={{0,16},{16,0},{1,17},{17,1},{2,18},{18,2},{3,19},{19,3},{4,20},{20... | collective-permute-start | bytes 147464 | tf_op jit(solution)/shard_map/ppermute | solution.py:458
  41.0 2.8 %collective-permute-done.10.refs_1_ = bf16[32,768]{1,0:T(8,128)(2,1)S(1)} collective-permute-done((bf16[32,768]{1,0:T(8,128)(2,1)}, bf16[32,768]{1,0:T(8,128)(2,1)S(1)}, u32[]{:S(2)}, u32[]{:S(2)}) %collective-permute-start.10) | collective-permute-done | bytes 49184 | tf_op jit(solution)/shard_map/ppermute | solution.py:458
  43.8 0.8 %copy-done.6 = bf16[32,768]{1,0:T(8,128)(2,1)S(1)} copy-done((bf16[32,768]{1,0:T(8,128)(2,1)S(1)}, bf16[32,768]{1,0:T(8,128)(2,1)}, u32[]{:S(2)}) %copy-start.6) | copy-done | bytes 49176
  44.6 0.4 shard_map.119.own_ref
  45.0 1.6 %collective-permute-start.11 = (bf16[64,1152]{1,0:T(8,128)(2,1)S(1)}, bf16[64,1152]{1,0:T(8,128)(2,1)S(1)}, u32[]{:S(2)}, u32[]{:S(2)}) collective-permute-start(bf16[64,1152]{1,0:T(8,128)(2,1)S(1)} %shard_map.119.own_ref), channel_id=1, source_target_pairs={{0,16},{16,0},{1,17},{17,1},{2,18},{18,2},{3,19},{19,3},{4,20},{20... | collective-permute-start | bytes 442376 | tf_op jit(solution)/shard_map/ppermute | solution.py:472
  46.6 1.8 %all-to-all-done.pair_ref = f32[16,24,128]{2,1,0:T(8,128)S(1)} async-done(((f32[16,24,128]{2,1,0:T(8,128)}), f32[16,24,128]{2,1,0:T(8,128)S(1)}, u32[]{:S(2)}, u32[]{:S(2)}) %all-to-all-start) | async-done | bytes 196640 | tf_op jit(solution)/shard_map/all_to_all | solution.py:450
  48.4 1.0 %shard_map.121 = f32[8,64]{1,0:T(8,128)} custom-call(f32[16,24,128]{2,1,0:T(8,128)S(1)} %all-to-all-done.pair_ref, f32[24,128]{1,0:T(8,128)S(1)} %get-tuple-element.27.head_ref.factor_ref, f32[8,128]{1,0:T(8,128)S(1)} %get-tuple-element.29.own_ref, f32[128,64]{1,0:T(8,128)S(1)} %get-tuple-element.30.slab_ref), custom_call_target="tpu_custom_call" | custom-call | flops 1000000 | bytes 1000000 | tf_op jit(solution)/shard_map/pallas_call | solution.py:292
  49.4 0.9 %collective-permute-done.11.other_ref = bf16[64,1152]{1,0:T(8,128)(2,1)S(1)} collective-permute-done((bf16[64,1152]{1,0:T(8,128)(2,1)S(1)}, bf16[64,1152]{1,0:T(8,128)(2,1)S(1)}, u32[]{:S(2)}, u32[]{:S(2)}) %collective-permute-start.11) | collective-permute-done | bytes 147488 | tf_op jit(solution)/shard_map/ppermute | solution.py:472
  50.4 1.5 %shard_map.122 = bf16[4,8,768]{2,1,0:T(8,128)(2,1)} custom-call(bf16[64,1152]{1,0:T(8,128)(2,1)S(1)} %shard_map.119.own_ref, bf16[64,1152]{1,0:T(8,128)(2,1)S(1)} %collective-permute-done.11.other_ref, f32[32,768]{1,0:T(8,128)S(1)} %get-tuple-element.31.refs_0_, bf16[768,768]{1,0:T(8,128)(2,1)S(1)} %copy-done.1), custom_call_target="tpu_custom_call" | custom-call | flops 1000000 | bytes 1000000 | tf_op jit(solution)/shard_map/pallas_call | solution.py:292
  (17 shorter events, 0.1 us)
Async XLA Ops:
  0.6 23.5 %copy-start.9 = (bf16[4,8,768]{2,1,0:T(8,128)(2,1)S(1)}, bf16[4,8,768]{2,1,0:T(8,128)(2,1)}, u32[]{:S(2)}) copy-start(bf16[4,8,768]{2,1,0:T(8,128)(2,1)} %param.13) | copy-start | bytes 147460
  2.3 8.5 %collective-permute-start = (bf16[8,8,768]{2,1,0:T(8,128)(2,1)S(1)}, bf16[8,8,768]{2,1,0:T(8,128)(2,1)S(1)}, u32[]{:S(2)}, u32[]{:S(2)}) collective-permute-start(bf16[8,8,768]{2,1,0:T(8,128)(2,1)S(1)} %constant_dynamic-update-slice_fusion), channel_id=1, source_target_pairs={{0,4},{1,5},{2,6},{3,7},{4,8},{5,9},{6,10},{7,11},{8,12},{9,13},{1... | collective-permute-start | bytes 294920 | tf_op jit(solution)/shard_map/ppermute | solution.py:320
  5.3 6.4 %collective-permute-start.2 = (bf16[8,8,768]{2,1,0:T(8,128)(2,1)S(1)}, bf16[8,8,768]{2,1,0:T(8,128)(2,1)S(1)}, u32[]{:S(2)}, u32[]{:S(2)}) collective-permute-start(bf16[8,8,768]{2,1,0:T(8,128)(2,1)S(1)} %constant_dynamic-update-slice_fusion), channel_id=1, source_target_pairs={{0,12},{1,13},{2,14},{3,15},{4,0},{5,1},{6,2},{7,3},{8,4},{9,5},{1... | collective-permute-start | bytes 294920 | tf_op jit(solution)/shard_map/ppermute | solution.py:320
  7.3 9.1 %collective-permute-start.1 = (bf16[8,8,768]{2,1,0:T(8,128)(2,1)S(1)}, bf16[8,8,768]{2,1,0:T(8,128)(2,1)S(1)}, u32[]{:S(2)}, u32[]{:S(2)}) collective-permute-start(bf16[8,8,768]{2,1,0:T(8,128)(2,1)S(1)} %constant_dynamic-update-slice_fusion), channel_id=1, source_target_pairs={{0,8},{1,9},{2,10},{3,11},{4,12},{5,13},{6,14},{7,15},{8,0},{9,1},... | collective-permute-start | bytes 294920 | tf_op jit(solution)/shard_map/ppermute | solution.py:320
  8.3 0.8 %copy-start.4 = (bf16[4,8,768]{2,1,0:T(8,128)(2,1)S(1)}, bf16[4,8,768]{2,1,0:T(8,128)(2,1)}, u32[]{:S(2)}) copy-start(bf16[4,8,768]{2,1,0:T(8,128)(2,1)} %q_hbm.1) | copy-start | bytes 147460
  11.7 16.9 %copy-start.3 = (bf16[4,8,768]{2,1,0:T(8,128)(2,1)S(1)}, bf16[4,8,768]{2,1,0:T(8,128)(2,1)}, u32[]{:S(2)}) copy-start(bf16[4,8,768]{2,1,0:T(8,128)(2,1)} %skip_hbm.1) | copy-start | bytes 147460
  11.7 16.9 %copy-start.7 = (f32[768]{0:T(1024)S(1)}, f32[768]{0:T(1024)}, u32[]{:S(2)}) copy-start(f32[768]{0:T(1024)} %gain_ref.1) | copy-start | bytes 9220
  11.7 16.9 %copy-start.8 = (f32[12]{0:T(128)S(1)}, f32[12]{0:T(128)}, u32[]{:S(2)}) copy-start(f32[12]{0:T(128)} %factor_ref.1) | copy-start | bytes 148
  16.4 16.5 %copy-start.2 = (bf16[768,768]{1,0:T(8,128)(2,1)S(1)}, bf16[768,768]{1,0:T(8,128)(2,1)}, u32[]{:S(2)}) copy-start(bf16[768,768]{1,0:T(8,128)(2,1)} %refs_5_.1) | copy-start | bytes 3538948
  17.4 6.8 %collective-permute-start.4 = (bf16[4,32,768]{2,1,0:T(8,128)(2,1)S(1)}, bf16[4,32,768]{2,1,0:T(8,128)(2,1)S(1)}, u32[]{:S(2)}, u32[]{:S(2)}) collective-permute-start(bf16[4,32,768]{2,1,0:T(8,128)(2,1)S(1)} %pad_maximum_fusion.refs_1_), channel_id=1, source_target_pairs={{0,2},{1,3},{2,0},{3,1},{4,6},{5,7},{6,4},{7,5},{8,10},{9,11},{10,... | collective-permute-start | bytes 589832 | tf_op jit(solution)/shard_map/ppermute | solution.py:320
  18.9 7.0 %collective-permute-start.3 = (bf16[4,32,768]{2,1,0:T(8,128)(2,1)S(1)}, bf16[4,32,768]{2,1,0:T(8,128)(2,1)S(1)}, u32[]{:S(2)}, u32[]{:S(2)}) collective-permute-start(bf16[4,32,768]{2,1,0:T(8,128)(2,1)S(1)} %pad_maximum_fusion.refs_1_), channel_id=1, source_target_pairs={{0,1},{1,0},{2,3},{3,2},{4,5},{5,4},{6,7},{7,6},{8,9},{9,8},{10,11... | collective-permute-start | bytes 589832 | tf_op jit(solution)/shard_map/ppermute | solution.py:320
  24.1 1.8 %collective-permute-start.5 = (bf16[4,32,768]{2,1,0:T(8,128)(2,1)S(1)}, bf16[4,32,768]{2,1,0:T(8,128)(2,1)S(1)}, u32[]{:S(2)}, u32[]{:S(2)}) collective-permute-start(bf16[4,32,768]{2,1,0:T(8,128)(2,1)S(1)} %collective-permute-done.4.refs_2_), channel_id=1, source_target_pairs={{0,1},{1,0},{2,3},{3,2},{4,5},{5,4},{6,7},{7,6},{8,9},{9,8},{10,11... | collective-permute-start | bytes 589832 | tf_op jit(solution)/shard_map/ppermute | solution.py:320
  24.1 7.4 %collective-permute-start.7 = (bf16[4,32,768]{2,1,0:T(8,128)(2,1)S(1)}, bf16[4,32,768]{2,1,0:T(8,128)(2,1)S(1)}, u32[]{:S(2)}, u32[]{:S(2)}) collective-permute-start(bf16[4,32,768]{2,1,0:T(8,128)(2,1)S(1)} %pad_maximum_fusion.1.refs_1_), channel_id=1, source_target_pairs={{0,2},{1,3},{2,0},{3,1},{4,6},{5,7},{6,4},{7,5},{8,10},{9,11},{10,... | collective-permute-start | bytes 589832 | tf_op jit(solution)/shard_map/ppermute | solution.py:320
  26.2 4.2 %collective-permute-start.6 = (f32[96,128]{1,0:T(8,128)S(1)}, f32[96,128]{1,0:T(8,128)S(1)}, u32[]{:S(2)}, u32[]{:S(2)}) collective-permute-start(f32[96,128]{1,0:T(8,128)S(1)} %shard_map.115.refs_0_), channel_id=1, source_target_pairs={{0,16},{16,0},{1,17},{17,1},{2,18},{18,2},{3,19},{19,3},{4,20},{20... | collective-permute-start | bytes 147464 | tf_op jit(solution)/shard_map/ppermute | solution.py:420
  28.5 3.2 %collective-permute-start.8 = (bf16[4,32,768]{2,1,0:T(8,128)(2,1)S(1)}, bf16[4,32,768]{2,1,0:T(8,128)(2,1)S(1)}, u32[]{:S(2)}, u32[]{:S(2)}) collective-permute-start(bf16[4,32,768]{2,1,0:T(8,128)(2,1)S(1)} %pad_maximum_fusion.1.refs_1_), channel_id=1, source_target_pairs={{0,1},{1,0},{2,3},{3,2},{4,5},{5,4},{6,7},{7,6},{8,9},{9,8},{10,11... | collective-permute-start | bytes 589832 | tf_op jit(solution)/shard_map/ppermute | solution.py:320
  31.5 1.4 %collective-permute-start.9 = (bf16[4,32,768]{2,1,0:T(8,128)(2,1)S(1)}, bf16[4,32,768]{2,1,0:T(8,128)(2,1)S(1)}, u32[]{:S(2)}, u32[]{:S(2)}) collective-permute-start(bf16[4,32,768]{2,1,0:T(8,128)(2,1)S(1)} %collective-permute-done.7.refs_2_), channel_id=1, source_target_pairs={{0,1},{1,0},{2,3},{3,2},{4,5},{5,4},{6,7},{7,6},{8,9},{9,8},{10,11... | collective-permute-start | bytes 589832 | tf_op jit(solution)/shard_map/ppermute | solution.py:320
  33.0 10.8 %copy-start = (bf16[768,1152]{1,0:T(8,128)(2,1)S(1)}, bf16[768,1152]{1,0:T(8,128)(2,1)}, u32[]{:S(2)}) copy-start(bf16[768,1152]{1,0:T(8,128)(2,1)} %refs_2_.1) | copy-start | bytes 5308420
  33.6 0.6 %copy-start.5 = (bf16[32,768]{1,0:T(8,128)(2,1)}, bf16[32,768]{1,0:T(8,128)(2,1)S(1)}, u32[]{:S(2)}) copy-start(bf16[32,768]{1,0:T(8,128)(2,1)S(1)} %get-tuple-element.24.refs_0_) | copy-start | bytes 147460
  35.2 13.2 %all-to-all-start = ((f32[16,24,128]{2,1,0:T(8,128)}), f32[16,24,128]{2,1,0:T(8,128)S(1)}, u32[]{:S(2)}, u32[]{:S(2)}) async-start(f32[16,24,128]{2,1,0:T(8,128)} %shard_map.120), calls=%async_computation | async-start | bytes 393216 | tf_op jit(solution)/shard_map/all_to_all | solution.py:450
  39.4 11.0 %copy-start.1 = (bf16[768,768]{1,0:T(8,128)(2,1)S(1)}, bf16[768,768]{1,0:T(8,128)(2,1)}, u32[]{:S(2)}) copy-start(bf16[768,768]{1,0:T(8,128)(2,1)} %refs_1_.1) | copy-start | bytes 3538948
  39.4 4.4 %collective-permute-start.10 = (bf16[32,768]{1,0:T(8,128)(2,1)}, bf16[32,768]{1,0:T(8,128)(2,1)S(1)}, u32[]{:S(2)}, u32[]{:S(2)}) collective-permute-start(bf16[32,768]{1,0:T(8,128)(2,1)} %copy-done.5), channel_id=1, source_target_pairs={{0,16},{16,0},{1,17},{17,1},{2,18},{18,2},{3,19},{19,3},{4,20},{20... | collective-permute-start | bytes 147464 | tf_op jit(solution)/shard_map/ppermute | solution.py:458
  43.8 0.8 %copy-start.6 = (bf16[32,768]{1,0:T(8,128)(2,1)S(1)}, bf16[32,768]{1,0:T(8,128)(2,1)}, u32[]{:S(2)}) copy-start(bf16[32,768]{1,0:T(8,128)(2,1)} %copy-done.5) | copy-start | bytes 147460
  45.0 5.4 %collective-permute-start.11 = (bf16[64,1152]{1,0:T(8,128)(2,1)S(1)}, bf16[64,1152]{1,0:T(8,128)(2,1)S(1)}, u32[]{:S(2)}, u32[]{:S(2)}) collective-permute-start(bf16[64,1152]{1,0:T(8,128)(2,1)S(1)} %shard_map.119.own_ref), channel_id=1, source_target_pairs={{0,16},{16,0},{1,17},{17,1},{2,18},{18,2},{3,19},{19,3},{4,20},{20... | collective-permute-start | bytes 442376 | tf_op jit(solution)/shard_map/ppermute | solution.py:472

commit v6 on v5

--- a/solution.py
+++ b/solution.py
@@ -362,32 +362,28 @@
     scalars = jnp.stack([seq_index, pos_index])
     head_rows = round_up(heads, 8)
     width = lane_block(embed, head)
+    value_first = [lateral_carried_vectors] + send_all([lateral_carried_vectors], pos_count, outer)
+    key_first = [lateral_matched_vectors] + send_all([lateral_matched_vectors], pos_count, outer)
+    key_parts = [jnp.concatenate(key_first, axis=1)]
     masked = call(
         functools.partial(query_kernel, head),
         jax.ShapeDtypeStruct((rows, heads * sites, width), BF16),
-        [lateral_asking_vectors],
+        [after(lateral_asking_vectors, key_parts[0])],
         hbm=(0,),
         scratch=[pltpu.VMEM((rows, sites, embed), BF16), pltpu.SemaphoreType.DMA((1,))],
     )
-
-    both = jnp.concatenate([lateral_matched_vectors, lateral_carried_vectors], axis=0)
-    arrived = send_all([both], pos_count, outer)
-    arrived[-1] = after(arrived[-1], masked)
-    key_first = [lateral_matched_vectors] + [part[:rows] for part in arrived]
-    key_parts = [jnp.concatenate(key_first, axis=1)]
     if middle:
         key_parts += send_all(key_parts, pos_count, middle)
-    arrived[-1] = after(arrived[-1], key_parts[0])
-    value_first = [lateral_carried_vectors] + [part[rows:] for part in arrived]
-    value_parts = [jnp.concatenate(value_first, axis=1)]
-    if middle:
-        value_parts += send_all(value_parts, pos_count, middle)
     near = sum(part.shape[1] for part in key_parts)
     partial = call(
         functools.partial(logits_kernel, len(key_parts)),
         jax.ShapeDtypeStruct((heads * sites, near), F32),
         [masked, *key_parts],
     )
+    value_first[1] = after(value_first[1], masked)
+    value_parts = [jnp.concatenate(value_first, axis=1)]
+    if middle:
+        value_parts += send_all(value_parts, pos_count, middle)
     if len(stages) > 2:
         far_parts = send_all(key_parts, pos_count, stages[2])
         partial = call(

time: 52.3 us -> 47.2 us (0.902)
  waiting for transfers between devices: 21.3 us -> 12.1 us
  starting transfers between devices: 18.2 us -> 23.2 us
  other arithmetic: 1 us -> 0.07 us
    ppermute x9 -> x12, waiting for transfers between devices: 14.8 us -> 5.61 us  [send_pos(): return lax.ppermute(array, 'pos', pairs)]
    ppermute x9 -> x12, starting transfers between devices: 9.27 us -> 14.1 us  [send_pos(): return lax.ppermute(array, 'pos', pairs)]
    concatenate x2 -> x0, other arithmetic: 0.92 us -> none  [the longest x1 0.91 us: per_device(): key_parts = [jnp.concatenate(key_first, axis=1)]]
    unnamed x21 -> x24, local copies, waits for them, and re-layouts: 3.06 us -> 3.86 us
    concatenate x1 -> x2, local copies, waits for them, and re-layouts: 0.8 us -> 0.01 us  [the longest x1 0.01 us: per_device(): key_parts = [jnp.concatenate(key_first, axis=1)]]
  transfers between devices with their start and end apart: 13 -> 16, of which waited for: 10 -> 7; matrix products, arithmetic and copies ran while one was open for 0% -> 4% of each run, Pallas kernels for 6% -> 6%
where the time goes in v6:
time: 47.2 us; the launch traced here: 46.8 us
  starting transfers between devices  23.2 us (49%)
  waiting for transfers between devices  12.1 us (26%)
  Pallas kernels  6.01 us (13%)
  local copies, waits for them, and re-layouts  3.87 us (8%)
  between operations  1.49 us (3%)
    ppermute x12, starting transfers between devices, send_pos(): return lax.ppermute(array, 'pos', pairs)  14.1 us
    pallas_call x10, Pallas kernels, call(): pl.pallas_call(kernel, out_shape=out_shape, in_specs=specs, out_specs=jax...  6.01 us
    ppermute x12, waiting for transfers between devices, send_pos(): return lax.ppermute(array, 'pos', pairs)  5.61 us
    all_to_all x1, starting transfers between devices, per_device(): lax.all_to_all(pair_local, 'pos', split_axis=0, concat_axis=0, tiled=True)  4.36 us
    unnamed x24, local copies, waits for them, and re-layouts  3.86 us
    ppermute x1, waiting for transfers between devices, per_device(): normed_all = [normed, lax.ppermute(normed, 'seq', swap)]  2.81 us
    all_to_all x1, waiting for transfers between devices, per_device(): lax.all_to_all(pair_local, 'pos', split_axis=0, concat_axis=0, tiled=True)  1.83 us
    ppermute x1, starting transfers between devices, per_device(): partials = [partial, after(lax.ppermute(partial, 'seq', swap), skip)]  1.56 us
  transfers between devices with their start and end apart: 16, of which 7 were waited for; matrix products, arithmetic and copies ran while one was open for 4% of the time, Pallas kernels for 6%

profile of v6, /device:TPU:0, one launch (start us, length us, event | category | flops | bytes accessed | tf_op | source)
XLA Modules:
  0.0 46.8 jit_solution(17933170063700485972)
XLA Ops:
  0.7 3.1 %collective-permute-start = (bf16[4,8,768]{2,1,0:T(8,128)(2,1)}, bf16[4,8,768]{2,1,0:T(8,128)(2,1)S(1)}, u32[]{:S(2)}, u32[]{:S(2)}) collective-permute-start(bf16[4,8,768]{2,1,0:T(8,128)(2,1)} %param.12), channel_id=1, source_target_pairs={{0,4},{1,5},{2,6},{3,7},{4,8},{5,9},{6,10},{7,11},{8,12},{9,13},{1... | collective-permute-start | bytes 147464 | tf_op jit(solution)/shard_map/ppermute | solution.py:320
  3.7 2.6 %collective-permute-start.1 = (bf16[4,8,768]{2,1,0:T(8,128)(2,1)}, bf16[4,8,768]{2,1,0:T(8,128)(2,1)S(1)}, u32[]{:S(2)}, u32[]{:S(2)}) collective-permute-start(bf16[4,8,768]{2,1,0:T(8,128)(2,1)} %param.12), channel_id=1, source_target_pairs={{0,8},{1,9},{2,10},{3,11},{4,12},{5,13},{6,14},{7,15},{8,0},{9,1},... | collective-permute-start | bytes 147464 | tf_op jit(solution)/shard_map/ppermute | solution.py:320
  6.3 1.3 %collective-permute-start.2 = (bf16[4,8,768]{2,1,0:T(8,128)(2,1)}, bf16[4,8,768]{2,1,0:T(8,128)(2,1)S(1)}, u32[]{:S(2)}, u32[]{:S(2)}) collective-permute-start(bf16[4,8,768]{2,1,0:T(8,128)(2,1)} %param.12), channel_id=1, source_target_pairs={{0,12},{1,13},{2,14},{3,15},{4,0},{5,1},{6,2},{7,3},{8,4},{9,5},{1... | collective-permute-start | bytes 147464 | tf_op jit(solution)/shard_map/ppermute | solution.py:320
  7.7 0.7 %collective-permute-start.7 = (bf16[4,8,768]{2,1,0:T(8,128)(2,1)}, bf16[4,8,768]{2,1,0:T(8,128)(2,1)S(1)}, u32[]{:S(2)}, u32[]{:S(2)}) collective-permute-start(bf16[4,8,768]{2,1,0:T(8,128)(2,1)} %param.13), channel_id=1, source_target_pairs={{0,4},{1,5},{2,6},{3,7},{4,8},{5,9},{6,10},{7,11},{8,12},{9,13},{1... | collective-permute-start | bytes 147464 | tf_op jit(solution)/shard_map/ppermute | solution.py:320
  8.4 0.3 collective-permute-start.8
  8.7 0.8 %constant_dynamic-update-slice_fusion.3 = bf16[4,32,768]{2,1,0:T(8,128)(2,1)S(1)} fusion(bf16[4,8,768]{2,1,0:T(8,128)(2,1)} %param.12), kind=kLoop, calls=%fused_computation.3 | loop fusion | bytes 98304
  9.5 0.8 %constant_dynamic-update-slice_fusion.7 = bf16[4,32,768]{2,1,0:T(8,128)(2,1)S(1)} fusion(bf16[4,8,768]{2,1,0:T(8,128)(2,1)} %param.13), kind=kLoop, calls=%fused_computation.7 | loop fusion | bytes 98304
  10.3 0.0 collective-permute-done
  10.3 2.9 %collective-permute-start.9 = (bf16[4,8,768]{2,1,0:T(8,128)(2,1)}, bf16[4,8,768]{2,1,0:T(8,128)(2,1)S(1)}, u32[]{:S(2)}, u32[]{:S(2)}) collective-permute-start(bf16[4,8,768]{2,1,0:T(8,128)(2,1)} %param.13), channel_id=1, source_target_pairs={{0,12},{1,13},{2,14},{3,15},{4,0},{5,1},{6,2},{7,3},{8,4},{9,5},{1... | collective-permute-start | bytes 147464 | tf_op jit(solution)/shard_map/ppermute | solution.py:320
  13.2 0.0 collective-permute-done.1
  13.2 0.0 collective-permute-done.2
  13.2 1.6 %collective-permute-start.4 = (bf16[4,32,768]{2,1,0:T(8,128)(2,1)S(1)}, bf16[4,32,768]{2,1,0:T(8,128)(2,1)S(1)}, u32[]{:S(2)}, u32[]{:S(2)}) collective-permute-start(bf16[4,32,768]{2,1,0:T(8,128)(2,1)S(1)} %constant_dynamic-update-slice_fusion.refs_1_), channel_id=1, source_target_pairs={{0,2},{1,3},{2,0},{3,1},{4,6},{5,7},{6,4},{7,5},{8,10},{9,11},{10,... | collective-permute-start | bytes 589832 | tf_op jit(solution)/shard_map/ppermute | solution.py:320
  14.8 0.0 collective-permute-start.3
  14.8 0.8 %copy-done.4 = bf16[4,8,768]{2,1,0:T(8,128)(2,1)S(1)} copy-done((bf16[4,8,768]{2,1,0:T(8,128)(2,1)S(1)}, bf16[4,8,768]{2,1,0:T(8,128)(2,1)}, u32[]{:S(2)}) %copy-start.4) | copy-done | bytes 49176
  15.6 0.1 shard_map.113.refs_0_
  15.7 0.0 collective-permute-done.7
  15.7 0.0 collective-permute-done.8
  15.7 3.2 %collective-permute-done.4.refs_2_ = bf16[4,32,768]{2,1,0:T(8,128)(2,1)S(1)} collective-permute-done((bf16[4,32,768]{2,1,0:T(8,128)(2,1)S(1)}, bf16[4,32,768]{2,1,0:T(8,128)(2,1)S(1)}, u32[]{:S(2)}, u32[]{:S(2)}) %collective-permute-start.4) | collective-permute-done | bytes 196640 | tf_op jit(solution)/shard_map/ppermute | solution.py:320
  18.9 0.0 collective-permute-start.5
  18.9 0.0 collective-permute-done.9
  19.0 1.6 %collective-permute-start.10 = (bf16[4,32,768]{2,1,0:T(8,128)(2,1)S(1)}, bf16[4,32,768]{2,1,0:T(8,128)(2,1)S(1)}, u32[]{:S(2)}, u32[]{:S(2)}) collective-permute-start(bf16[4,32,768]{2,1,0:T(8,128)(2,1)S(1)} %constant_dynamic-update-slice_fusion.4.refs_1_), channel_id=1, source_target_pairs={{0,2},{1,3},{2,0},{3,1},{4,6},{5,7},{6,4},{7,5},{8,10},{9,11},{10,... | collective-permute-start | bytes 589832 | tf_op jit(solution)/shard_map/ppermute | solution.py:320
  20.5 0.2 shard_map.114.refs_3_
  20.8 0.0 collective-permute-done.3.refs_1_
  20.8 0.0 collective-permute-done.5.refs_2_
  20.8 0.3 shard_map.115.refs_0_
  21.1 1.6 %collective-permute-start.6 = (f32[96,128]{1,0:T(8,128)S(1)}, f32[96,128]{1,0:T(8,128)S(1)}, u32[]{:S(2)}, u32[]{:S(2)}) collective-permute-start(f32[96,128]{1,0:T(8,128)S(1)} %shard_map.115.refs_0_), channel_id=1, source_target_pairs={{0,16},{16,0},{1,17},{17,1},{2,18},{18,2},{3,19},{19,3},{4,20},{20... | collective-permute-start | bytes 147464 | tf_op jit(solution)/shard_map/ppermute | solution.py:416
  22.6 0.1 pad_add_fusion.scalar_ref
  23.4 0.1 collective-permute-start.11
  23.5 0.8 %shard_map.116 = (f32[32,768]{1,0:T(8,128)S(1)}, f32[8,768]{1,0:T(8,128)S(1)}, f32[24,128]{1,0:T(8,128)S(1)}, f32[128,128]{1,0:T(8,128)S(1)}, f32[8,128]{1,0:T(8,128)S(1)}, /*index=5*/f32[128,64]{1,0:T(8,128)S(1)}) custom-call(s32[2]{0:T(128)S(1)} %pad_add_fusion.scalar_ref, bf16[4,8,768]{2,1,0:T(8,128)(2,1)S(1)} %copy-done.3, f32[768]{0:T(1024)S(1)} %copy-done.7, ...), custom_call_target="tpu_custom_call" | custom-call | flops 1000000 | bytes 1000000 | tf_op jit(solution)/shard_map/pallas_call | solution.py:292
  24.3 1.0 %collective-permute-done.6.refs_1_ = f32[96,128]{1,0:T(8,128)S(1)} collective-permute-done((f32[96,128]{1,0:T(8,128)S(1)}, f32[96,128]{1,0:T(8,128)S(1)}, u32[]{:S(2)}, u32[]{:S(2)}) %collective-permute-start.6) | collective-permute-done | bytes 49184 | tf_op jit(solution)/shard_map/ppermute | solution.py:416
  25.2 1.1 %collective-permute-done.10.refs_2_ = bf16[4,32,768]{2,1,0:T(8,128)(2,1)S(1)} collective-permute-done((bf16[4,32,768]{2,1,0:T(8,128)(2,1)S(1)}, bf16[4,32,768]{2,1,0:T(8,128)(2,1)S(1)}, u32[]{:S(2)}, u32[]{:S(2)}) %collective-permute-start.10) | collective-permute-done | bytes 196640 | tf_op jit(solution)/shard_map/ppermute | solution.py:320
  26.3 0.2 shard_map.117.refs_0_.w_ref
  26.5 1.2 %collective-permute-done.12.refs_4_ = bf16[4,32,768]{2,1,0:T(8,128)(2,1)S(1)} collective-permute-done((bf16[4,32,768]{2,1,0:T(8,128)(2,1)S(1)}, bf16[4,32,768]{2,1,0:T(8,128)(2,1)S(1)}, u32[]{:S(2)}, u32[]{:S(2)}) %collective-permute-start.12) | collective-permute-done | bytes 196640 | tf_op jit(solution)/shard_map/ppermute | solution.py:320
  27.8 0.6 %shard_map.118 = (f32[32,768]{1,0:T(8,128)S(1)}, bf16[32,768]{1,0:T(8,128)(2,1)S(1)}) custom-call(bf16[96,128]{1,0:T(8,128)(2,1)S(1)} %shard_map.117.refs_0_.w_ref, bf16[4,32,768]{2,1,0:T(8,128)(2,1)S(1)} %constant_dynamic-update-slice_fusion.4.refs_1_, bf16[4,32,768]{2,1,0:T(8,128)(2,1)S(1)} %collective-permute-done.10.refs_2_, ...), custom_call_target="tpu_custom_call" | custom-call | flops 1000000 | bytes 1000000 | tf_op jit(solution)/shard_map/pallas_call | solution.py:292
  28.4 0.0 copy-start.5
  28.4 0.6 %copy-done.5 = bf16[32,768]{1,0:T(8,128)(2,1)} copy-done((bf16[32,768]{1,0:T(8,128)(2,1)}, bf16[32,768]{1,0:T(8,128)(2,1)S(1)}, u32[]{:S(2)}) %copy-start.5) | copy-done | bytes 49176
  29.0 0.9 %shard_map.120 = f32[16,24,128]{2,1,0:T(8,128)} custom-call(bf16[96,128]{1,0:T(8,128)(2,1)S(1)} %shard_map.117.refs_0_.w_ref, f32[24,128]{1,0:T(8,128)S(1)} %get-tuple-element.27.head_ref.factor_ref, f32[128,128]{1,0:T(8,128)S(1)} %get-tuple-element.28.order_ref), custom_call_target="tpu_custom_call" | custom-call | flops 1000000 | bytes 10000000 | tf_op jit(solution)/shard_map/pallas_call | solution.py:292
  30.0 4.4 %all-to-all-start = ((f32[16,24,128]{2,1,0:T(8,128)}), f32[16,24,128]{2,1,0:T(8,128)S(1)}, u32[]{:S(2)}, u32[]{:S(2)}) async-start(f32[16,24,128]{2,1,0:T(8,128)} %shard_map.120), calls=%async_computation | async-start | bytes 393216 | tf_op jit(solution)/shard_map/all_to_all | solution.py:446
  34.3 0.0 copy-start.1
  34.3 1.6 %collective-permute-start.13 = (bf16[32,768]{1,0:T(8,128)(2,1)}, bf16[32,768]{1,0:T(8,128)(2,1)S(1)}, u32[]{:S(2)}, u32[]{:S(2)}) collective-permute-start(bf16[32,768]{1,0:T(8,128)(2,1)} %copy-done.5), channel_id=1, source_target_pairs={{0,16},{16,0},{1,17},{17,1},{2,18},{18,2},{3,19},{19,3},{4,20},{20... | collective-permute-start | bytes 147464 | tf_op jit(solution)/shard_map/ppermute | solution.py:454
  35.9 2.8 %collective-permute-done.13.refs_1_ = bf16[32,768]{1,0:T(8,128)(2,1)S(1)} collective-permute-done((bf16[32,768]{1,0:T(8,128)(2,1)}, bf16[32,768]{1,0:T(8,128)(2,1)S(1)}, u32[]{:S(2)}, u32[]{:S(2)}) %collective-permute-start.13) | collective-permute-done | bytes 49184 | tf_op jit(solution)/shard_map/ppermute | solution.py:454
  38.7 0.8 %copy-done.6 = bf16[32,768]{1,0:T(8,128)(2,1)S(1)} copy-done((bf16[32,768]{1,0:T(8,128)(2,1)S(1)}, bf16[32,768]{1,0:T(8,128)(2,1)}, u32[]{:S(2)}) %copy-start.6) | copy-done | bytes 49176
  39.5 0.4 shard_map.119.own_ref
  39.9 1.6 %collective-permute-start.14 = (bf16[64,1152]{1,0:T(8,128)(2,1)S(1)}, bf16[64,1152]{1,0:T(8,128)(2,1)S(1)}, u32[]{:S(2)}, u32[]{:S(2)}) collective-permute-start(bf16[64,1152]{1,0:T(8,128)(2,1)S(1)} %shard_map.119.own_ref), channel_id=1, source_target_pairs={{0,16},{16,0},{1,17},{17,1},{2,18},{18,2},{3,19},{19,3},{4,20},{20... | collective-permute-start | bytes 442376 | tf_op jit(solution)/shard_map/ppermute | solution.py:468
  41.5 1.8 %all-to-all-done.pair_ref = f32[16,24,128]{2,1,0:T(8,128)S(1)} async-done(((f32[16,24,128]{2,1,0:T(8,128)}), f32[16,24,128]{2,1,0:T(8,128)S(1)}, u32[]{:S(2)}, u32[]{:S(2)}) %all-to-all-start) | async-done | bytes 196640 | tf_op jit(solution)/shard_map/all_to_all | solution.py:446
  43.3 1.0 %shard_map.121 = f32[8,64]{1,0:T(8,128)} custom-call(f32[16,24,128]{2,1,0:T(8,128)S(1)} %all-to-all-done.pair_ref, f32[24,128]{1,0:T(8,128)S(1)} %get-tuple-element.27.head_ref.factor_ref, f32[8,128]{1,0:T(8,128)S(1)} %get-tuple-element.29.own_ref, f32[128,64]{1,0:T(8,128)S(1)} %get-tuple-element.30.slab_ref), custom_call_target="tpu_custom_call" | custom-call | flops 1000000 | bytes 1000000 | tf_op jit(solution)/shard_map/pallas_call | solution.py:292
  44.4 0.9 %collective-permute-done.14.other_ref = bf16[64,1152]{1,0:T(8,128)(2,1)S(1)} collective-permute-done((bf16[64,1152]{1,0:T(8,128)(2,1)S(1)}, bf16[64,1152]{1,0:T(8,128)(2,1)S(1)}, u32[]{:S(2)}, u32[]{:S(2)}) %collective-permute-start.14) | collective-permute-done | bytes 147488 | tf_op jit(solution)/shard_map/ppermute | solution.py:468
  45.3 1.5 %shard_map.122 = bf16[4,8,768]{2,1,0:T(8,128)(2,1)} custom-call(bf16[64,1152]{1,0:T(8,128)(2,1)S(1)} %shard_map.119.own_ref, bf16[64,1152]{1,0:T(8,128)(2,1)S(1)} %collective-permute-done.14.other_ref, f32[32,768]{1,0:T(8,128)S(1)} %get-tuple-element.31.refs_0_, bf16[768,768]{1,0:T(8,128)(2,1)S(1)} %copy-done.1), custom_call_target="tpu_custom_call" | custom-call | flops 1000000 | bytes 1000000 | tf_op jit(solution)/shard_map/pallas_call | solution.py:292
  (21 shorter events, 0.1 us)
Async XLA Ops:
  0.6 22.8 %copy-start.3 = (bf16[4,8,768]{2,1,0:T(8,128)(2,1)S(1)}, bf16[4,8,768]{2,1,0:T(8,128)(2,1)}, u32[]{:S(2)}) copy-start(bf16[4,8,768]{2,1,0:T(8,128)(2,1)} %skip_hbm.1) | copy-start | bytes 147460
  0.6 22.8 %copy-start.7 = (f32[768]{0:T(1024)S(1)}, f32[768]{0:T(1024)}, u32[]{:S(2)}) copy-start(f32[768]{0:T(1024)} %gain_ref.1) | copy-start | bytes 9220
  0.7 22.8 %copy-start.8 = (f32[12]{0:T(128)S(1)}, f32[12]{0:T(128)}, u32[]{:S(2)}) copy-start(f32[12]{0:T(128)} %factor_ref.1) | copy-start | bytes 148
  0.7 9.6 %collective-permute-start = (bf16[4,8,768]{2,1,0:T(8,128)(2,1)}, bf16[4,8,768]{2,1,0:T(8,128)(2,1)S(1)}, u32[]{:S(2)}, u32[]{:S(2)}) collective-permute-start(bf16[4,8,768]{2,1,0:T(8,128)(2,1)} %param.12), channel_id=1, source_target_pairs={{0,4},{1,5},{2,6},{3,7},{4,8},{5,9},{6,10},{7,11},{8,12},{9,13},{1... | collective-permute-start | bytes 147464 | tf_op jit(solution)/shard_map/ppermute | solution.py:320
  3.7 9.4 %collective-permute-start.1 = (bf16[4,8,768]{2,1,0:T(8,128)(2,1)}, bf16[4,8,768]{2,1,0:T(8,128)(2,1)S(1)}, u32[]{:S(2)}, u32[]{:S(2)}) collective-permute-start(bf16[4,8,768]{2,1,0:T(8,128)(2,1)} %param.12), channel_id=1, source_target_pairs={{0,8},{1,9},{2,10},{3,11},{4,12},{5,13},{6,14},{7,15},{8,0},{9,1},... | collective-permute-start | bytes 147464 | tf_op jit(solution)/shard_map/ppermute | solution.py:320
  6.3 6.9 %collective-permute-start.2 = (bf16[4,8,768]{2,1,0:T(8,128)(2,1)}, bf16[4,8,768]{2,1,0:T(8,128)(2,1)S(1)}, u32[]{:S(2)}, u32[]{:S(2)}) collective-permute-start(bf16[4,8,768]{2,1,0:T(8,128)(2,1)} %param.12), channel_id=1, source_target_pairs={{0,12},{1,13},{2,14},{3,15},{4,0},{5,1},{6,2},{7,3},{8,4},{9,5},{1... | collective-permute-start | bytes 147464 | tf_op jit(solution)/shard_map/ppermute | solution.py:320
  7.7 8.0 %collective-permute-start.7 = (bf16[4,8,768]{2,1,0:T(8,128)(2,1)}, bf16[4,8,768]{2,1,0:T(8,128)(2,1)S(1)}, u32[]{:S(2)}, u32[]{:S(2)}) collective-permute-start(bf16[4,8,768]{2,1,0:T(8,128)(2,1)} %param.13), channel_id=1, source_target_pairs={{0,4},{1,5},{2,6},{3,7},{4,8},{5,9},{6,10},{7,11},{8,12},{9,13},{1... | collective-permute-start | bytes 147464 | tf_op jit(solution)/shard_map/ppermute | solution.py:320
  8.4 7.3 %collective-permute-start.8 = (bf16[4,8,768]{2,1,0:T(8,128)(2,1)}, bf16[4,8,768]{2,1,0:T(8,128)(2,1)S(1)}, u32[]{:S(2)}, u32[]{:S(2)}) collective-permute-start(bf16[4,8,768]{2,1,0:T(8,128)(2,1)} %param.13), channel_id=1, source_target_pairs={{0,8},{1,9},{2,10},{3,11},{4,12},{5,13},{6,14},{7,15},{8,0},{9,1},... | collective-permute-start | bytes 147464 | tf_op jit(solution)/shard_map/ppermute | solution.py:320
  10.3 17.5 %copy-start.2 = (bf16[768,768]{1,0:T(8,128)(2,1)S(1)}, bf16[768,768]{1,0:T(8,128)(2,1)}, u32[]{:S(2)}) copy-start(bf16[768,768]{1,0:T(8,128)(2,1)} %refs_5_.1) | copy-start | bytes 3538948
  10.3 8.6 %collective-permute-start.9 = (bf16[4,8,768]{2,1,0:T(8,128)(2,1)}, bf16[4,8,768]{2,1,0:T(8,128)(2,1)S(1)}, u32[]{:S(2)}, u32[]{:S(2)}) collective-permute-start(bf16[4,8,768]{2,1,0:T(8,128)(2,1)} %param.13), channel_id=1, source_target_pairs={{0,12},{1,13},{2,14},{3,15},{4,0},{5,1},{6,2},{7,3},{8,4},{9,5},{1... | collective-permute-start | bytes 147464 | tf_op jit(solution)/shard_map/ppermute | solution.py:320
  13.2 5.7 %collective-permute-start.4 = (bf16[4,32,768]{2,1,0:T(8,128)(2,1)S(1)}, bf16[4,32,768]{2,1,0:T(8,128)(2,1)S(1)}, u32[]{:S(2)}, u32[]{:S(2)}) collective-permute-start(bf16[4,32,768]{2,1,0:T(8,128)(2,1)S(1)} %constant_dynamic-update-slice_fusion.refs_1_), channel_id=1, source_target_pairs={{0,2},{1,3},{2,0},{3,1},{4,6},{5,7},{6,4},{7,5},{8,10},{9,11},{10,... | collective-permute-start | bytes 589832 | tf_op jit(solution)/shard_map/ppermute | solution.py:320
  14.8 6.0 %collective-permute-start.3 = (bf16[4,32,768]{2,1,0:T(8,128)(2,1)S(1)}, bf16[4,32,768]{2,1,0:T(8,128)(2,1)S(1)}, u32[]{:S(2)}, u32[]{:S(2)}) collective-permute-start(bf16[4,32,768]{2,1,0:T(8,128)(2,1)S(1)} %constant_dynamic-update-slice_fusion.refs_1_), channel_id=1, source_target_pairs={{0,1},{1,0},{2,3},{3,2},{4,5},{5,4},{6,7},{7,6},{8,9},{9,8},{10,11... | collective-permute-start | bytes 589832 | tf_op jit(solution)/shard_map/ppermute | solution.py:320
  14.8 0.8 %copy-start.4 = (bf16[4,8,768]{2,1,0:T(8,128)(2,1)S(1)}, bf16[4,8,768]{2,1,0:T(8,128)(2,1)}, u32[]{:S(2)}) copy-start(bf16[4,8,768]{2,1,0:T(8,128)(2,1)} %q_hbm) | copy-start | bytes 147460
  18.9 1.8 %collective-permute-start.5 = (bf16[4,32,768]{2,1,0:T(8,128)(2,1)S(1)}, bf16[4,32,768]{2,1,0:T(8,128)(2,1)S(1)}, u32[]{:S(2)}, u32[]{:S(2)}) collective-permute-start(bf16[4,32,768]{2,1,0:T(8,128)(2,1)S(1)} %collective-permute-done.4.refs_2_), channel_id=1, source_target_pairs={{0,1},{1,0},{2,3},{3,2},{4,5},{5,4},{6,7},{7,6},{8,9},{9,8},{10,11... | collective-permute-start | bytes 589832 | tf_op jit(solution)/shard_map/ppermute | solution.py:320
  19.0 7.4 %collective-permute-start.10 = (bf16[4,32,768]{2,1,0:T(8,128)(2,1)S(1)}, bf16[4,32,768]{2,1,0:T(8,128)(2,1)S(1)}, u32[]{:S(2)}, u32[]{:S(2)}) collective-permute-start(bf16[4,32,768]{2,1,0:T(8,128)(2,1)S(1)} %constant_dynamic-update-slice_fusion.4.refs_1_), channel_id=1, source_target_pairs={{0,2},{1,3},{2,0},{3,1},{4,6},{5,7},{6,4},{7,5},{8,10},{9,11},{10,... | collective-permute-start | bytes 589832 | tf_op jit(solution)/shard_map/ppermute | solution.py:320
  21.1 4.2 %collective-permute-start.6 = (f32[96,128]{1,0:T(8,128)S(1)}, f32[96,128]{1,0:T(8,128)S(1)}, u32[]{:S(2)}, u32[]{:S(2)}) collective-permute-start(f32[96,128]{1,0:T(8,128)S(1)} %shard_map.115.refs_0_), channel_id=1, source_target_pairs={{0,16},{16,0},{1,17},{17,1},{2,18},{18,2},{3,19},{19,3},{4,20},{20... | collective-permute-start | bytes 147464 | tf_op jit(solution)/shard_map/ppermute | solution.py:416
  23.4 3.2 %collective-permute-start.11 = (bf16[4,32,768]{2,1,0:T(8,128)(2,1)S(1)}, bf16[4,32,768]{2,1,0:T(8,128)(2,1)S(1)}, u32[]{:S(2)}, u32[]{:S(2)}) collective-permute-start(bf16[4,32,768]{2,1,0:T(8,128)(2,1)S(1)} %constant_dynamic-update-slice_fusion.4.refs_1_), channel_id=1, source_target_pairs={{0,1},{1,0},{2,3},{3,2},{4,5},{5,4},{6,7},{7,6},{8,9},{9,8},{10,11... | collective-permute-start | bytes 589832 | tf_op jit(solution)/shard_map/ppermute | solution.py:320
  26.3 1.4 %collective-permute-start.12 = (bf16[4,32,768]{2,1,0:T(8,128)(2,1)S(1)}, bf16[4,32,768]{2,1,0:T(8,128)(2,1)S(1)}, u32[]{:S(2)}, u32[]{:S(2)}) collective-permute-start(bf16[4,32,768]{2,1,0:T(8,128)(2,1)S(1)} %collective-permute-done.10.refs_2_), channel_id=1, source_target_pairs={{0,1},{1,0},{2,3},{3,2},{4,5},{5,4},{6,7},{7,6},{8,9},{9,8},{10,11... | collective-permute-start | bytes 589832 | tf_op jit(solution)/shard_map/ppermute | solution.py:320
  27.8 10.9 %copy-start = (bf16[768,1152]{1,0:T(8,128)(2,1)S(1)}, bf16[768,1152]{1,0:T(8,128)(2,1)}, u32[]{:S(2)}) copy-start(bf16[768,1152]{1,0:T(8,128)(2,1)} %refs_2_.1) | copy-start | bytes 5308420
  28.4 0.6 %copy-start.5 = (bf16[32,768]{1,0:T(8,128)(2,1)}, bf16[32,768]{1,0:T(8,128)(2,1)S(1)}, u32[]{:S(2)}) copy-start(bf16[32,768]{1,0:T(8,128)(2,1)S(1)} %get-tuple-element.24.refs_0_) | copy-start | bytes 147460
  30.0 13.4 %all-to-all-start = ((f32[16,24,128]{2,1,0:T(8,128)}), f32[16,24,128]{2,1,0:T(8,128)S(1)}, u32[]{:S(2)}, u32[]{:S(2)}) async-start(f32[16,24,128]{2,1,0:T(8,128)} %shard_map.120), calls=%async_computation | async-start | bytes 393216 | tf_op jit(solution)/shard_map/all_to_all | solution.py:446
  34.3 11.0 %copy-start.1 = (bf16[768,768]{1,0:T(8,128)(2,1)S(1)}, bf16[768,768]{1,0:T(8,128)(2,1)}, u32[]{:S(2)}) copy-start(bf16[768,768]{1,0:T(8,128)(2,1)} %refs_1_.1) | copy-start | bytes 3538948
  34.3 4.4 %collective-permute-start.13 = (bf16[32,768]{1,0:T(8,128)(2,1)}, bf16[32,768]{1,0:T(8,128)(2,1)S(1)}, u32[]{:S(2)}, u32[]{:S(2)}) collective-permute-start(bf16[32,768]{1,0:T(8,128)(2,1)} %copy-done.5), channel_id=1, source_target_pairs={{0,16},{16,0},{1,17},{17,1},{2,18},{18,2},{3,19},{19,3},{4,20},{20... | collective-permute-start | bytes 147464 | tf_op jit(solution)/shard_map/ppermute | solution.py:454
  38.7 0.8 %copy-start.6 = (bf16[32,768]{1,0:T(8,128)(2,1)S(1)}, bf16[32,768]{1,0:T(8,128)(2,1)}, u32[]{:S(2)}) copy-start(bf16[32,768]{1,0:T(8,128)(2,1)} %copy-done.5) | copy-start | bytes 147460
  39.9 5.4 %collective-permute-start.14 = (bf16[64,1152]{1,0:T(8,128)(2,1)S(1)}, bf16[64,1152]{1,0:T(8,128)(2,1)S(1)}, u32[]{:S(2)}, u32[]{:S(2)}) collective-permute-start(bf16[64,1152]{1,0:T(8,128)(2,1)S(1)} %shard_map.119.own_ref), channel_id=1, source_target_pairs={{0,16},{16,0},{1,17},{17,1},{2,18},{18,2},{3,19},{19,3},{4,20},{20... | collective-permute-start | bytes 442376 | tf_op jit(solution)/shard_map/ppermute | solution.py:468

commit v7 on v6

--- a/solution.py
+++ b/solution.py
@@ -362,9 +362,13 @@
     scalars = jnp.stack([seq_index, pos_index])
     head_rows = round_up(heads, 8)
     width = lane_block(embed, head)
-    value_first = [lateral_carried_vectors] + send_all([lateral_carried_vectors], pos_count, outer)
     key_first = [lateral_matched_vectors] + send_all([lateral_matched_vectors], pos_count, outer)
     key_parts = [jnp.concatenate(key_first, axis=1)]
+    later_value = after(lateral_carried_vectors, key_parts[0])
+    value_first = [later_value]
+    for delta in range(1, outer[1]):
+        sent = lateral_carried_vectors if delta in (1, outer[1] - 1) else later_value
+        value_first.append(send_pos(sent, pos_count, *outer, delta))
     masked = call(
         functools.partial(query_kernel, head),
         jax.ShapeDtypeStruct((rows, heads * sites, width), BF16),
@@ -416,9 +420,6 @@
         partials = [partial, after(lax.ppermute(partial, "seq", swap), skip)]
     else:
         partials = [lax.psum(partial, "seq")]
-    if len(stages) > 2:
-        value_parts = value_parts[:1] + [after(part, partials[-1]) for part in value_parts[1:]]
-        value_parts += send_all(value_parts, pos_count, stages[2])
     shares = call(
         functools.partial(
             softmax_kernel, 1.0 / (math.sqrt(head) * math.sqrt(rows * seq_count))
@@ -427,6 +428,16 @@
         partials,
     )
 
+    pair_local = call(
+        functools.partial(pair_kernel, heads),
+        jax.ShapeDtypeStruct((pos_count, head_rows + sites, length), F32),
+        [shares, head_factors, order],
+        bytes_accessed=10000000,
+        scratch=[pltpu.VMEM((head_rows + sites, length), F32)],
+    )
+    if len(stages) > 2:
+        value_parts = value_parts[:1] + [after(part, pair_local) for part in value_parts[1:]]
+        value_parts += send_all(value_parts, pos_count, stages[2])
     hidden, normed = call(
         functools.partial(mix_kernel, head, len(value_parts)),
         (
@@ -435,13 +446,6 @@
         ),
         [shares, *value_parts, lateral_closing_linear, skip, gain],
         scratch=[pltpu.VMEM((cells, embed), F32)],
-    )
-    pair_local = call(
-        functools.partial(pair_kernel, heads),
-        jax.ShapeDtypeStruct((pos_count, head_rows + sites, length), F32),
-        [after(shares, normed), head_factors, order],
-        bytes_accessed=10000000,
-        scratch=[pltpu.VMEM((head_rows + sites, length), F32)],
     )
     pair_all = lax.all_to_all(pair_local, "pos", split_axis=0, concat_axis=0, tiled=True)
     pairing_chances = call(
@@ -460,7 +464,7 @@
         functools.partial(project_kernel, len(normed_all)),
         jax.ShapeDtypeStruct((cells * len(normed_all), weight.shape[1]), BF16),
         [*normed_all, weight],
-        bytes_accessed=10000000,
+        bytes_accessed=30000000,
     )
     if swapped:
         column, column_inputs = swapped_column_kernel, [

time: 47.2 us -> 46.8 us (level)
  starting transfers between devices: 23.2 us -> 21.3 us
  Pallas kernels: 6.01 us -> 7.14 us
  local copies, waits for them, and re-layouts: 3.87 us -> 4.72 us
  waiting for transfers between devices: 12.1 us -> 11.6 us
    ppermute x1, waiting for transfers between devices: 0.93 us -> 2.49 us  [per_device(): lax.ppermute(projected, 'seq', swap)]
    all_to_all x1, waiting for transfers between devices: 1.83 us -> 0.39 us  [per_device(): lax.all_to_all(pair_local, 'pos', split_axis=0, concat_axis=0, tiled=True)]
    ppermute x12, starting transfers between devices: 14.1 us -> 12.7 us  [send_pos(): return lax.ppermute(array, 'pos', pairs)]
    pallas_call x10, Pallas kernels: 6.01 us -> 7.14 us  [call(): pl.pallas_call(kernel, out_shape=out_shape, in_specs=specs, out_specs=jax...]
    ppermute x1, waiting for transfers between devices: 0.98 us -> 0.01 us  [per_device(): partials = [partial, after(lax.ppermute(partial, 'seq', swap), skip)]]
    unnamed x24 -> x28, local copies, waits for them, and re-layouts: 3.86 us -> 4.71 us
    all_to_all x1, starting transfers between devices: 4.36 us -> 3.61 us  [per_device(): lax.all_to_all(pair_local, 'pos', split_axis=0, concat_axis=0, tiled=True)]
  transfers between devices with their start and end apart: 16 -> 16, of which waited for: 7 -> 6; matrix products, arithmetic and copies ran while one was open for 4% -> 4% of each run, Pallas kernels for 6% -> 12%
where the time goes in v7:
time: 46.8 us; the launch traced here: 46.3 us
  starting transfers between devices  21.3 us (46%)
  waiting for transfers between devices  11.6 us (25%)
  Pallas kernels  7.14 us (15%)
  local copies, waits for them, and re-layouts  4.72 us (10%)
  between operations  1.54 us (3%)
    ppermute x12, starting transfers between devices, send_pos(): return lax.ppermute(array, 'pos', pairs)  12.7 us
    pallas_call x10, Pallas kernels, call(): pl.pallas_call(kernel, out_shape=out_shape, in_specs=specs, out_specs=jax...  7.14 us
    ppermute x12, waiting for transfers between devices, send_pos(): return lax.ppermute(array, 'pos', pairs)  6.05 us
    unnamed x28, local copies, waits for them, and re-layouts  4.71 us
    all_to_all x1, starting transfers between devices, per_device(): lax.all_to_all(pair_local, 'pos', split_axis=0, concat_axis=0, tiled=True)  3.61 us
    ppermute x1, waiting for transfers between devices, per_device(): normed_all = [normed, lax.ppermute(normed, 'seq', swap)]  2.69 us
    ppermute x1, waiting for transfers between devices, per_device(): lax.ppermute(projected, 'seq', swap)  2.49 us
    ppermute x1, starting transfers between devices, per_device(): partials = [partial, after(lax.ppermute(partial, 'seq', swap), skip)]  1.99 us
  transfers between devices with their start and end apart: 16, of which 6 were waited for; matrix products, arithmetic and copies ran while one was open for 4% of the time, Pallas kernels for 12%

profile of v7, /device:TPU:0, one launch (start us, length us, event | category | flops | bytes accessed | tf_op | source)
XLA Modules:
  0.0 46.3 jit_solution(17865396816433937928)
XLA Ops:
  0.7 3.1 %collective-permute-start = (bf16[4,8,768]{2,1,0:T(8,128)(2,1)}, bf16[4,8,768]{2,1,0:T(8,128)(2,1)S(1)}, u32[]{:S(2)}, u32[]{:S(2)}) collective-permute-start(bf16[4,8,768]{2,1,0:T(8,128)(2,1)} %param.12), channel_id=1, source_target_pairs={{0,4},{1,5},{2,6},{3,7},{4,8},{5,9},{6,10},{7,11},{8,12},{9,13},{1... | collective-permute-start | bytes 147464 | tf_op jit(solution)/shard_map/ppermute | solution.py:320
  3.7 2.6 %collective-permute-start.1 = (bf16[4,8,768]{2,1,0:T(8,128)(2,1)}, bf16[4,8,768]{2,1,0:T(8,128)(2,1)S(1)}, u32[]{:S(2)}, u32[]{:S(2)}) collective-permute-start(bf16[4,8,768]{2,1,0:T(8,128)(2,1)} %param.12), channel_id=1, source_target_pairs={{0,8},{1,9},{2,10},{3,11},{4,12},{5,13},{6,14},{7,15},{8,0},{9,1},... | collective-permute-start | bytes 147464 | tf_op jit(solution)/shard_map/ppermute | solution.py:320
  6.3 1.3 %collective-permute-start.2 = (bf16[4,8,768]{2,1,0:T(8,128)(2,1)}, bf16[4,8,768]{2,1,0:T(8,128)(2,1)S(1)}, u32[]{:S(2)}, u32[]{:S(2)}) collective-permute-start(bf16[4,8,768]{2,1,0:T(8,128)(2,1)} %param.12), channel_id=1, source_target_pairs={{0,12},{1,13},{2,14},{3,15},{4,0},{5,1},{6,2},{7,3},{8,4},{9,5},{1... | collective-permute-start | bytes 147464 | tf_op jit(solution)/shard_map/ppermute | solution.py:320
  7.7 0.7 %collective-permute-start.7 = (bf16[4,8,768]{2,1,0:T(8,128)(2,1)}, bf16[4,8,768]{2,1,0:T(8,128)(2,1)S(1)}, u32[]{:S(2)}, u32[]{:S(2)}) collective-permute-start(bf16[4,8,768]{2,1,0:T(8,128)(2,1)} %param.13), channel_id=1, source_target_pairs={{0,4},{1,5},{2,6},{3,7},{4,8},{5,9},{6,10},{7,11},{8,12},{9,13},{1... | collective-permute-start | bytes 147464 | tf_op jit(solution)/shard_map/ppermute | solution.py:320
  8.4 3.1 %collective-permute-start.9 = (bf16[4,8,768]{2,1,0:T(8,128)(2,1)}, bf16[4,8,768]{2,1,0:T(8,128)(2,1)S(1)}, u32[]{:S(2)}, u32[]{:S(2)}) collective-permute-start(bf16[4,8,768]{2,1,0:T(8,128)(2,1)} %param.13), channel_id=1, source_target_pairs={{0,12},{1,13},{2,14},{3,15},{4,0},{5,1},{6,2},{7,3},{8,4},{9,5},{1... | collective-permute-start | bytes 147464 | tf_op jit(solution)/shard_map/ppermute | solution.py:320
  11.5 0.8 %constant_dynamic-update-slice_fusion.3 = bf16[4,32,768]{2,1,0:T(8,128)(2,1)S(1)} fusion(bf16[4,8,768]{2,1,0:T(8,128)(2,1)} %param.12), kind=kLoop, calls=%fused_computation.3 | loop fusion | bytes 98304
  12.3 0.0 collective-permute-done
  12.3 0.0 collective-permute-done.1
  12.3 0.0 collective-permute-done.2
  12.4 1.6 %collective-permute-start.4 = (bf16[4,32,768]{2,1,0:T(8,128)(2,1)S(1)}, bf16[4,32,768]{2,1,0:T(8,128)(2,1)S(1)}, u32[]{:S(2)}, u32[]{:S(2)}) collective-permute-start(bf16[4,32,768]{2,1,0:T(8,128)(2,1)S(1)} %constant_dynamic-update-slice_fusion.refs_1_), channel_id=1, source_target_pairs={{0,2},{1,3},{2,0},{3,1},{4,6},{5,7},{6,4},{7,5},{8,10},{9,11},{10,... | collective-permute-start | bytes 589832 | tf_op jit(solution)/shard_map/ppermute | solution.py:320
  13.9 0.0 collective-permute-start.3
  14.0 0.8 %copy-done.6 = bf16[4,8,768]{2,1,0:T(8,128)(2,1)S(1)} copy-done((bf16[4,8,768]{2,1,0:T(8,128)(2,1)S(1)}, bf16[4,8,768]{2,1,0:T(8,128)(2,1)}, u32[]{:S(2)}) %copy-start.6) | copy-done | bytes 49176
  14.7 0.1 shard_map.113.refs_0_
  14.8 0.1 collective-permute-start.8
  14.9 0.8 %constant_dynamic-update-slice_fusion.7 = bf16[4,32,768]{2,1,0:T(8,128)(2,1)S(1)} fusion(bf16[4,8,768]{2,1,0:T(8,128)(2,1)} %param.13), kind=kLoop, calls=%fused_computation.7 | loop fusion | bytes 98304
  15.7 2.3 %collective-permute-done.4.refs_2_ = bf16[4,32,768]{2,1,0:T(8,128)(2,1)S(1)} collective-permute-done((bf16[4,32,768]{2,1,0:T(8,128)(2,1)S(1)}, bf16[4,32,768]{2,1,0:T(8,128)(2,1)S(1)}, u32[]{:S(2)}, u32[]{:S(2)}) %collective-permute-start.4) | collective-permute-done | bytes 196640 | tf_op jit(solution)/shard_map/ppermute | solution.py:320
  18.1 0.0 collective-permute-start.5
  18.1 2.6 %collective-permute-done.8 = bf16[4,8,768]{2,1,0:T(8,128)(2,1)S(1)} collective-permute-done((bf16[4,8,768]{2,1,0:T(8,128)(2,1)}, bf16[4,8,768]{2,1,0:T(8,128)(2,1)S(1)}, u32[]{:S(2)}, u32[]{:S(2)}) %collective-permute-start.8) | collective-permute-done | bytes 49184 | tf_op jit(solution)/shard_map/ppermute | solution.py:320
  20.8 0.1 collective-permute-start.10
  20.9 0.2 shard_map.114.refs_3_
  21.1 0.0 collective-permute-done.3.refs_1_
  21.1 0.0 collective-permute-done.5.refs_2_
  21.1 0.3 shard_map.115.refs_0_
  21.4 2.0 %collective-permute-start.6 = (f32[96,128]{1,0:T(8,128)S(1)}, f32[96,128]{1,0:T(8,128)S(1)}, u32[]{:S(2)}, u32[]{:S(2)}) collective-permute-start(f32[96,128]{1,0:T(8,128)S(1)} %shard_map.115.refs_0_), channel_id=1, source_target_pairs={{0,16},{16,0},{1,17},{17,1},{2,18},{18,2},{3,19},{19,3},{4,20},{20... | collective-permute-start | bytes 147464 | tf_op jit(solution)/shard_map/ppermute | solution.py:420
  23.4 0.1 pad_add_fusion.scalar_ref
  24.2 0.1 collective-permute-start.11
  24.3 0.8 %shard_map.116 = (f32[32,768]{1,0:T(8,128)S(1)}, f32[8,768]{1,0:T(8,128)S(1)}, f32[24,128]{1,0:T(8,128)S(1)}, f32[128,128]{1,0:T(8,128)S(1)}, f32[8,128]{1,0:T(8,128)S(1)}, /*index=5*/f32[128,64]{1,0:T(8,128)S(1)}) custom-call(s32[2]{0:T(128)S(1)} %pad_add_fusion.scalar_ref, bf16[4,8,768]{2,1,0:T(8,128)(2,1)S(1)} %copy-done.5, f32[768]{0:T(1024)S(1)} %copy-done.9, ...), custom_call_target="tpu_custom_call" | custom-call | flops 1000000 | bytes 1000000 | tf_op jit(solution)/shard_map/pallas_call | solution.py:292
  25.0 0.0 copy-start.7
  25.1 0.6 %copy-done.7 = f32[8,768]{1,0:T(8,128)} copy-done((f32[8,768]{1,0:T(8,128)}, f32[8,768]{1,0:T(8,128)S(1)}, u32[]{:S(2)}) %copy-start.7) | copy-done | bytes 24600
  25.7 0.0 collective-permute-done.6.refs_1_
  25.7 0.2 shard_map.117.w_ref.refs_0_
  25.8 0.9 %shard_map.118 = f32[16,24,128]{2,1,0:T(8,128)} custom-call(bf16[96,128]{1,0:T(8,128)(2,1)S(1)} %shard_map.117.w_ref.refs_0_, f32[24,128]{1,0:T(8,128)S(1)} %get-tuple-element.23.head_ref.factor_ref, f32[128,128]{1,0:T(8,128)S(1)} %get-tuple-element.24.order_ref), custom_call_target="tpu_custom_call" | custom-call | flops 1000000 | bytes 10000000 | tf_op jit(solution)/shard_map/pallas_call | solution.py:292
  26.8 1.0 %collective-permute-done.10.refs_2_ = bf16[4,32,768]{2,1,0:T(8,128)(2,1)} collective-permute-done((bf16[4,32,768]{2,1,0:T(8,128)(2,1)S(1)}, bf16[4,32,768]{2,1,0:T(8,128)(2,1)}, u32[]{:S(2)}, u32[]{:S(2)}) %collective-permute-start.10) | collective-permute-done | bytes 196640 | tf_op jit(solution)/shard_map/ppermute | solution.py:320
  27.8 3.6 %all-to-all-start = ((f32[16,24,128]{2,1,0:T(8,128)}), f32[16,24,128]{2,1,0:T(8,128)S(1)}, u32[]{:S(2)}, u32[]{:S(2)}) async-start(f32[16,24,128]{2,1,0:T(8,128)} %shard_map.118), calls=%async_computation | async-start | bytes 393216 | tf_op jit(solution)/shard_map/all_to_all | solution.py:450
  31.4 0.0 collective-permute-done.11.refs_3_
  31.5 0.0 copy-start.8
  31.5 0.7 %copy-done.8 = f32[8,768]{1,0:T(8,128)S(1)} copy-done((f32[8,768]{1,0:T(8,128)S(1)}, f32[8,768]{1,0:T(8,128)}, u32[]{:S(2)}) %copy-start.8) | copy-done | bytes 24600
  32.2 1.7 %shard_map.119 = (f32[32,768]{1,0:T(8,128)S(1)}, bf16[32,768]{1,0:T(8,128)(2,1)S(1)}) custom-call(bf16[96,128]{1,0:T(8,128)(2,1)S(1)} %shard_map.117.w_ref.refs_0_, bf16[4,32,768]{2,1,0:T(8,128)(2,1)S(1)} %constant_dynamic-update-slice_fusion.4.refs_1_, bf16[4,32,768]{2,1,0:T(8,128)(2,1)} %collective-permute-done.10.refs_2_, ...), custom_call_target="tpu_custom_call" | custom-call | flops 1000000 | bytes 1000000 | tf_op jit(solution)/shard_map/pallas_call | solution.py:292
  34.0 0.0 copy-start.1
  34.0 1.5 %collective-permute-start.13 = (bf16[32,768]{1,0:T(8,128)(2,1)S(1)}, bf16[32,768]{1,0:T(8,128)(2,1)S(1)}, u32[]{:S(2)}, u32[]{:S(2)}) collective-permute-start(bf16[32,768]{1,0:T(8,128)(2,1)S(1)} %get-tuple-element.27.refs_0_), channel_id=1, source_target_pairs={{0,16},{16,0},{1,17},{17,1},{2,18},{18,2},{3,19},{19,3},{4,20},{20... | collective-permute-start | bytes 147464 | tf_op jit(solution)/shard_map/ppermute | solution.py:458
  35.4 2.7 %collective-permute-done.13.refs_1_ = bf16[32,768]{1,0:T(8,128)(2,1)S(1)} collective-permute-done((bf16[32,768]{1,0:T(8,128)(2,1)S(1)}, bf16[32,768]{1,0:T(8,128)(2,1)S(1)}, u32[]{:S(2)}, u32[]{:S(2)}) %collective-permute-start.13) | collective-permute-done | bytes 49184 | tf_op jit(solution)/shard_map/ppermute | solution.py:458
  38.1 0.4 shard_map.120.own_ref
  38.6 1.5 %collective-permute-start.14 = (bf16[64,1152]{1,0:T(8,128)(2,1)S(1)}, bf16[64,1152]{1,0:T(8,128)(2,1)S(1)}, u32[]{:S(2)}, u32[]{:S(2)}) collective-permute-start(bf16[64,1152]{1,0:T(8,128)(2,1)S(1)} %shard_map.120.own_ref), channel_id=1, source_target_pairs={{0,16},{16,0},{1,17},{17,1},{2,18},{18,2},{3,19},{19,3},{4,20},{20... | collective-permute-start | bytes 442376 | tf_op jit(solution)/shard_map/ppermute | solution.py:472
  40.0 0.4 all-to-all-done.pair_ref
  40.4 1.1 %shard_map.121 = f32[8,64]{1,0:T(8,128)} custom-call(f32[16,24,128]{2,1,0:T(8,128)S(1)} %all-to-all-done.pair_ref, f32[24,128]{1,0:T(8,128)S(1)} %get-tuple-element.23.head_ref.factor_ref, f32[8,128]{1,0:T(8,128)S(1)} %get-tuple-element.29.own_ref, f32[128,64]{1,0:T(8,128)S(1)} %get-tuple-element.30.slab_ref), custom_call_target="tpu_custom_call" | custom-call | flops 1000000 | bytes 1000000 | tf_op jit(solution)/shard_map/pallas_call | solution.py:292
  41.5 2.5 %collective-permute-done.14.other_ref = bf16[64,1152]{1,0:T(8,128)(2,1)S(1)} collective-permute-done((bf16[64,1152]{1,0:T(8,128)(2,1)S(1)}, bf16[64,1152]{1,0:T(8,128)(2,1)S(1)}, u32[]{:S(2)}, u32[]{:S(2)}) %collective-permute-start.14) | collective-permute-done | bytes 147488 | tf_op jit(solution)/shard_map/ppermute | solution.py:472
  44.0 0.9 %copy-done.4 = f32[32,768]{1,0:T(8,128)S(1)} copy-done((f32[32,768]{1,0:T(8,128)S(1)}, f32[32,768]{1,0:T(8,128)}, u32[]{:S(2)}) %copy-start.4) | copy-done | bytes 98328
  44.9 1.5 %shard_map.122 = bf16[4,8,768]{2,1,0:T(8,128)(2,1)} custom-call(bf16[64,1152]{1,0:T(8,128)(2,1)S(1)} %shard_map.120.own_ref, bf16[64,1152]{1,0:T(8,128)(2,1)S(1)} %collective-permute-done.14.other_ref, f32[32,768]{1,0:T(8,128)S(1)} %copy-done.4, bf16[768,768]{1,0:T(8,128)(2,1)S(1)} %copy-done.1), custom_call_target="tpu_custom_call" | custom-call | flops 1000000 | bytes 1000000 | tf_op jit(solution)/shard_map/pallas_call | solution.py:292
  (25 shorter events, 0.1 us)
Async XLA Ops:
  0.6 23.6 %copy-start.5 = (bf16[4,8,768]{2,1,0:T(8,128)(2,1)S(1)}, bf16[4,8,768]{2,1,0:T(8,128)(2,1)}, u32[]{:S(2)}) copy-start(bf16[4,8,768]{2,1,0:T(8,128)(2,1)} %skip_hbm.1) | copy-start | bytes 147460
  0.6 23.6 %copy-start.9 = (f32[768]{0:T(1024)S(1)}, f32[768]{0:T(1024)}, u32[]{:S(2)}) copy-start(f32[768]{0:T(1024)} %gain_ref.1) | copy-start | bytes 9220
  0.7 23.6 %copy-start.10 = (f32[12]{0:T(128)S(1)}, f32[12]{0:T(128)}, u32[]{:S(2)}) copy-start(f32[12]{0:T(128)} %factor_ref.1) | copy-start | bytes 148
  0.7 11.6 %collective-permute-start = (bf16[4,8,768]{2,1,0:T(8,128)(2,1)}, bf16[4,8,768]{2,1,0:T(8,128)(2,1)S(1)}, u32[]{:S(2)}, u32[]{:S(2)}) collective-permute-start(bf16[4,8,768]{2,1,0:T(8,128)(2,1)} %param.12), channel_id=1, source_target_pairs={{0,4},{1,5},{2,6},{3,7},{4,8},{5,9},{6,10},{7,11},{8,12},{9,13},{1... | collective-permute-start | bytes 147464 | tf_op jit(solution)/shard_map/ppermute | solution.py:320
  3.7 8.6 %collective-permute-start.1 = (bf16[4,8,768]{2,1,0:T(8,128)(2,1)}, bf16[4,8,768]{2,1,0:T(8,128)(2,1)S(1)}, u32[]{:S(2)}, u32[]{:S(2)}) collective-permute-start(bf16[4,8,768]{2,1,0:T(8,128)(2,1)} %param.12), channel_id=1, source_target_pairs={{0,8},{1,9},{2,10},{3,11},{4,12},{5,13},{6,14},{7,15},{8,0},{9,1},... | collective-permute-start | bytes 147464 | tf_op jit(solution)/shard_map/ppermute | solution.py:320
  6.3 6.0 %collective-permute-start.2 = (bf16[4,8,768]{2,1,0:T(8,128)(2,1)}, bf16[4,8,768]{2,1,0:T(8,128)(2,1)S(1)}, u32[]{:S(2)}, u32[]{:S(2)}) collective-permute-start(bf16[4,8,768]{2,1,0:T(8,128)(2,1)} %param.12), channel_id=1, source_target_pairs={{0,12},{1,13},{2,14},{3,15},{4,0},{5,1},{6,2},{7,3},{8,4},{9,5},{1... | collective-permute-start | bytes 147464 | tf_op jit(solution)/shard_map/ppermute | solution.py:320
  7.7 7.2 %collective-permute-start.7 = (bf16[4,8,768]{2,1,0:T(8,128)(2,1)}, bf16[4,8,768]{2,1,0:T(8,128)(2,1)S(1)}, u32[]{:S(2)}, u32[]{:S(2)}) collective-permute-start(bf16[4,8,768]{2,1,0:T(8,128)(2,1)} %param.13), channel_id=1, source_target_pairs={{0,4},{1,5},{2,6},{3,7},{4,8},{5,9},{6,10},{7,11},{8,12},{9,13},{1... | collective-permute-start | bytes 147464 | tf_op jit(solution)/shard_map/ppermute | solution.py:320
  8.4 12.4 %collective-permute-start.9 = (bf16[4,8,768]{2,1,0:T(8,128)(2,1)}, bf16[4,8,768]{2,1,0:T(8,128)(2,1)S(1)}, u32[]{:S(2)}, u32[]{:S(2)}) collective-permute-start(bf16[4,8,768]{2,1,0:T(8,128)(2,1)} %param.13), channel_id=1, source_target_pairs={{0,12},{1,13},{2,14},{3,15},{4,0},{5,1},{6,2},{7,3},{8,4},{9,5},{1... | collective-permute-start | bytes 147464 | tf_op jit(solution)/shard_map/ppermute | solution.py:320
  12.4 5.7 %collective-permute-start.4 = (bf16[4,32,768]{2,1,0:T(8,128)(2,1)S(1)}, bf16[4,32,768]{2,1,0:T(8,128)(2,1)S(1)}, u32[]{:S(2)}, u32[]{:S(2)}) collective-permute-start(bf16[4,32,768]{2,1,0:T(8,128)(2,1)S(1)} %constant_dynamic-update-slice_fusion.refs_1_), channel_id=1, source_target_pairs={{0,2},{1,3},{2,0},{3,1},{4,6},{5,7},{6,4},{7,5},{8,10},{9,11},{10,... | collective-permute-start | bytes 589832 | tf_op jit(solution)/shard_map/ppermute | solution.py:320
  13.9 7.2 %collective-permute-start.3 = (bf16[4,32,768]{2,1,0:T(8,128)(2,1)S(1)}, bf16[4,32,768]{2,1,0:T(8,128)(2,1)S(1)}, u32[]{:S(2)}, u32[]{:S(2)}) collective-permute-start(bf16[4,32,768]{2,1,0:T(8,128)(2,1)S(1)} %constant_dynamic-update-slice_fusion.refs_1_), channel_id=1, source_target_pairs={{0,1},{1,0},{2,3},{3,2},{4,5},{5,4},{6,7},{7,6},{8,9},{9,8},{10,11... | collective-permute-start | bytes 589832 | tf_op jit(solution)/shard_map/ppermute | solution.py:320
  13.9 0.8 %copy-start.6 = (bf16[4,8,768]{2,1,0:T(8,128)(2,1)S(1)}, bf16[4,8,768]{2,1,0:T(8,128)(2,1)}, u32[]{:S(2)}) copy-start(bf16[4,8,768]{2,1,0:T(8,128)(2,1)} %q_hbm) | copy-start | bytes 147460
  14.8 5.9 %collective-permute-start.8 = (bf16[4,8,768]{2,1,0:T(8,128)(2,1)}, bf16[4,8,768]{2,1,0:T(8,128)(2,1)S(1)}, u32[]{:S(2)}, u32[]{:S(2)}) collective-permute-start(bf16[4,8,768]{2,1,0:T(8,128)(2,1)} %param.13), channel_id=1, source_target_pairs={{0,8},{1,9},{2,10},{3,11},{4,12},{5,13},{6,14},{7,15},{8,0},{9,1},... | collective-permute-start | bytes 147464 | tf_op jit(solution)/shard_map/ppermute | solution.py:320
  18.1 3.0 %collective-permute-start.5 = (bf16[4,32,768]{2,1,0:T(8,128)(2,1)S(1)}, bf16[4,32,768]{2,1,0:T(8,128)(2,1)S(1)}, u32[]{:S(2)}, u32[]{:S(2)}) collective-permute-start(bf16[4,32,768]{2,1,0:T(8,128)(2,1)S(1)} %collective-permute-done.4.refs_2_), channel_id=1, source_target_pairs={{0,1},{1,0},{2,3},{3,2},{4,5},{5,4},{6,7},{7,6},{8,9},{9,8},{10,11... | collective-permute-start | bytes 589832 | tf_op jit(solution)/shard_map/ppermute | solution.py:320
  20.7 10.7 %copy-start.2 = (bf16[768,768]{1,0:T(8,128)(2,1)S(1)}, bf16[768,768]{1,0:T(8,128)(2,1)}, u32[]{:S(2)}) copy-start(bf16[768,768]{1,0:T(8,128)(2,1)} %refs_5_.1) | copy-start | bytes 3538948
  20.8 7.0 %collective-permute-start.10 = (bf16[4,32,768]{2,1,0:T(8,128)(2,1)S(1)}, bf16[4,32,768]{2,1,0:T(8,128)(2,1)}, u32[]{:S(2)}, u32[]{:S(2)}) collective-permute-start(bf16[4,32,768]{2,1,0:T(8,128)(2,1)S(1)} %constant_dynamic-update-slice_fusion.4.refs_1_), channel_id=1, source_target_pairs={{0,2},{1,3},{2,0},{3,1},{4,6},{5,7},{6,4},{7,5},{8,10},{9,11},{10,... | collective-permute-start | bytes 589832 | tf_op jit(solution)/shard_map/ppermute | solution.py:320
  21.4 4.2 %collective-permute-start.6 = (f32[96,128]{1,0:T(8,128)S(1)}, f32[96,128]{1,0:T(8,128)S(1)}, u32[]{:S(2)}, u32[]{:S(2)}) collective-permute-start(f32[96,128]{1,0:T(8,128)S(1)} %shard_map.115.refs_0_), channel_id=1, source_target_pairs={{0,16},{16,0},{1,17},{17,1},{2,18},{18,2},{3,19},{19,3},{4,20},{20... | collective-permute-start | bytes 147464 | tf_op jit(solution)/shard_map/ppermute | solution.py:420
  24.2 7.3 %collective-permute-start.11 = (bf16[4,32,768]{2,1,0:T(8,128)(2,1)S(1)}, bf16[4,32,768]{2,1,0:T(8,128)(2,1)}, u32[]{:S(2)}, u32[]{:S(2)}) collective-permute-start(bf16[4,32,768]{2,1,0:T(8,128)(2,1)S(1)} %constant_dynamic-update-slice_fusion.4.refs_1_), channel_id=1, source_target_pairs={{0,1},{1,0},{2,3},{3,2},{4,5},{5,4},{6,7},{7,6},{8,9},{9,8},{10,11... | collective-permute-start | bytes 589832 | tf_op jit(solution)/shard_map/ppermute | solution.py:320
  25.0 0.6 %copy-start.7 = (f32[8,768]{1,0:T(8,128)}, f32[8,768]{1,0:T(8,128)S(1)}, u32[]{:S(2)}) copy-start(f32[8,768]{1,0:T(8,128)S(1)} %get-tuple-element.26.refs_7_) | copy-start | bytes 73732
  26.8 11.3 %copy-start = (bf16[768,1152]{1,0:T(8,128)(2,1)S(1)}, bf16[768,1152]{1,0:T(8,128)(2,1)}, u32[]{:S(2)}) copy-start(bf16[768,1152]{1,0:T(8,128)(2,1)} %refs_2_.1) | copy-start | bytes 5308420
  27.8 3.6 %collective-permute-start.12 = (bf16[4,32,768]{2,1,0:T(8,128)(2,1)}, bf16[4,32,768]{2,1,0:T(8,128)(2,1)}, u32[]{:S(2)}, u32[]{:S(2)}) collective-permute-start(bf16[4,32,768]{2,1,0:T(8,128)(2,1)} %collective-permute-done.10.refs_2_), channel_id=1, source_target_pairs={{0,1},{1,0},{2,3},{3,2},{4,5},{5,4},{6,7},{7,6},{8,9},{9,8},{10,11... | collective-permute-start | bytes 589832 | tf_op jit(solution)/shard_map/ppermute | solution.py:320
  27.8 12.6 %all-to-all-start = ((f32[16,24,128]{2,1,0:T(8,128)}), f32[16,24,128]{2,1,0:T(8,128)S(1)}, u32[]{:S(2)}, u32[]{:S(2)}) async-start(f32[16,24,128]{2,1,0:T(8,128)} %shard_map.118), calls=%async_computation | async-start | bytes 393216 | tf_op jit(solution)/shard_map/all_to_all | solution.py:450
  31.5 0.7 %copy-start.8 = (f32[8,768]{1,0:T(8,128)S(1)}, f32[8,768]{1,0:T(8,128)}, u32[]{:S(2)}) copy-start(f32[8,768]{1,0:T(8,128)} %copy-done.7) | copy-start | bytes 73732
  34.0 4.6 %copy-start.3 = (f32[32,768]{1,0:T(8,128)}, f32[32,768]{1,0:T(8,128)S(1)}, u32[]{:S(2)}) copy-start(f32[32,768]{1,0:T(8,128)S(1)} %get-tuple-element.31.refs_0_) | copy-start | bytes 294916
  34.0 10.0 %copy-start.1 = (bf16[768,768]{1,0:T(8,128)(2,1)S(1)}, bf16[768,768]{1,0:T(8,128)(2,1)}, u32[]{:S(2)}) copy-start(bf16[768,768]{1,0:T(8,128)(2,1)} %refs_1_.1) | copy-start | bytes 3538948
  34.0 4.2 %collective-permute-start.13 = (bf16[32,768]{1,0:T(8,128)(2,1)S(1)}, bf16[32,768]{1,0:T(8,128)(2,1)S(1)}, u32[]{:S(2)}, u32[]{:S(2)}) collective-permute-start(bf16[32,768]{1,0:T(8,128)(2,1)S(1)} %get-tuple-element.27.refs_0_), channel_id=1, source_target_pairs={{0,16},{16,0},{1,17},{17,1},{2,18},{18,2},{3,19},{19,3},{4,20},{20... | collective-permute-start | bytes 147464 | tf_op jit(solution)/shard_map/ppermute | solution.py:458
  38.6 5.4 %collective-permute-start.14 = (bf16[64,1152]{1,0:T(8,128)(2,1)S(1)}, bf16[64,1152]{1,0:T(8,128)(2,1)S(1)}, u32[]{:S(2)}, u32[]{:S(2)}) collective-permute-start(bf16[64,1152]{1,0:T(8,128)(2,1)S(1)} %shard_map.120.own_ref), channel_id=1, source_target_pairs={{0,16},{16,0},{1,17},{17,1},{2,18},{18,2},{3,19},{19,3},{4,20},{20... | collective-permute-start | bytes 442376 | tf_op jit(solution)/shard_map/ppermute | solution.py:472
  44.0 0.9 %copy-start.4 = (f32[32,768]{1,0:T(8,128)S(1)}, f32[32,768]{1,0:T(8,128)}, u32[]{:S(2)}) copy-start(f32[32,768]{1,0:T(8,128)} %copy-done.3) | copy-start | bytes 294916

commit v8 on v7

--- a/solution.py
+++ b/solution.py
@@ -432,7 +432,6 @@
         functools.partial(pair_kernel, heads),
         jax.ShapeDtypeStruct((pos_count, head_rows + sites, length), F32),
         [shares, head_factors, order],
-        bytes_accessed=10000000,
         scratch=[pltpu.VMEM((head_rows + sites, length), F32)],
     )
     if len(stages) > 2:
@@ -464,7 +463,6 @@
         functools.partial(project_kernel, len(normed_all)),
         jax.ShapeDtypeStruct((cells * len(normed_all), weight.shape[1]), BF16),
         [*normed_all, weight],
-        bytes_accessed=30000000,
     )
     if swapped:
         column, column_inputs = swapped_column_kernel, [

time: 46.8 us -> 46.8 us (level)
  no operation moved by 1% of the time
where the time goes in v8:
time: 46.8 us; the launch traced here: 46.3 us
  starting transfers between devices  21.3 us (46%)
  waiting for transfers between devices  11.6 us (25%)
  Pallas kernels  7.14 us (15%)
  local copies, waits for them, and re-layouts  4.72 us (10%)
  between operations  1.54 us (3%)
    ppermute x12, starting transfers between devices, send_pos(): return lax.ppermute(array, 'pos', pairs)  12.7 us
    pallas_call x10, Pallas kernels, call(): pl.pallas_call(kernel, out_shape=out_shape, in_specs=specs, out_specs=jax...  7.14 us
    ppermute x12, waiting for transfers between devices, send_pos(): return lax.ppermute(array, 'pos', pairs)  6.05 us
    unnamed x28, local copies, waits for them, and re-layouts  4.71 us
    all_to_all x1, starting transfers between devices, per_device(): lax.all_to_all(pair_local, 'pos', split_axis=0, concat_axis=0, tiled=True)  3.61 us
    ppermute x1, waiting for transfers between devices, per_device(): normed_all = [normed, lax.ppermute(normed, 'seq', swap)]  2.69 us
    ppermute x1, waiting for transfers between devices, per_device(): lax.ppermute(projected, 'seq', swap)  2.49 us
    ppermute x1, starting transfers between devices, per_device(): partials = [partial, after(lax.ppermute(partial, 'seq', swap), skip)]  1.99 us
  transfers between devices with their start and end apart: 16, of which 6 were waited for; matrix products, arithmetic and copies ran while one was open for 4% of the time, Pallas kernels for 12%

profile of v8, /device:TPU:0, one launch (start us, length us, event | category | flops | bytes accessed | tf_op | source)
XLA Modules:
  0.0 46.3 jit_solution(17865396816433937928)
XLA Ops:
  0.7 3.1 %collective-permute-start = (bf16[4,8,768]{2,1,0:T(8,128)(2,1)}, bf16[4,8,768]{2,1,0:T(8,128)(2,1)S(1)}, u32[]{:S(2)}, u32[]{:S(2)}) collective-permute-start(bf16[4,8,768]{2,1,0:T(8,128)(2,1)} %param.12), channel_id=1, source_target_pairs={{0,4},{1,5},{2,6},{3,7},{4,8},{5,9},{6,10},{7,11},{8,12},{9,13},{1... | collective-permute-start | bytes 147464 | tf_op jit(solution)/shard_map/ppermute | solution.py:320
  3.7 2.6 %collective-permute-start.1 = (bf16[4,8,768]{2,1,0:T(8,128)(2,1)}, bf16[4,8,768]{2,1,0:T(8,128)(2,1)S(1)}, u32[]{:S(2)}, u32[]{:S(2)}) collective-permute-start(bf16[4,8,768]{2,1,0:T(8,128)(2,1)} %param.12), channel_id=1, source_target_pairs={{0,8},{1,9},{2,10},{3,11},{4,12},{5,13},{6,14},{7,15},{8,0},{9,1},... | collective-permute-start | bytes 147464 | tf_op jit(solution)/shard_map/ppermute | solution.py:320
  6.3 1.3 %collective-permute-start.2 = (bf16[4,8,768]{2,1,0:T(8,128)(2,1)}, bf16[4,8,768]{2,1,0:T(8,128)(2,1)S(1)}, u32[]{:S(2)}, u32[]{:S(2)}) collective-permute-start(bf16[4,8,768]{2,1,0:T(8,128)(2,1)} %param.12), channel_id=1, source_target_pairs={{0,12},{1,13},{2,14},{3,15},{4,0},{5,1},{6,2},{7,3},{8,4},{9,5},{1... | collective-permute-start | bytes 147464 | tf_op jit(solution)/shard_map/ppermute | solution.py:320
  7.7 0.7 %collective-permute-start.7 = (bf16[4,8,768]{2,1,0:T(8,128)(2,1)}, bf16[4,8,768]{2,1,0:T(8,128)(2,1)S(1)}, u32[]{:S(2)}, u32[]{:S(2)}) collective-permute-start(bf16[4,8,768]{2,1,0:T(8,128)(2,1)} %param.13), channel_id=1, source_target_pairs={{0,4},{1,5},{2,6},{3,7},{4,8},{5,9},{6,10},{7,11},{8,12},{9,13},{1... | collective-permute-start | bytes 147464 | tf_op jit(solution)/shard_map/ppermute | solution.py:320
  8.4 3.1 %collective-permute-start.9 = (bf16[4,8,768]{2,1,0:T(8,128)(2,1)}, bf16[4,8,768]{2,1,0:T(8,128)(2,1)S(1)}, u32[]{:S(2)}, u32[]{:S(2)}) collective-permute-start(bf16[4,8,768]{2,1,0:T(8,128)(2,1)} %param.13), channel_id=1, source_target_pairs={{0,12},{1,13},{2,14},{3,15},{4,0},{5,1},{6,2},{7,3},{8,4},{9,5},{1... | collective-permute-start | bytes 147464 | tf_op jit(solution)/shard_map/ppermute | solution.py:320
  11.5 0.8 %constant_dynamic-update-slice_fusion.3 = bf16[4,32,768]{2,1,0:T(8,128)(2,1)S(1)} fusion(bf16[4,8,768]{2,1,0:T(8,128)(2,1)} %param.12), kind=kLoop, calls=%fused_computation.3 | loop fusion | bytes 98304
  12.3 0.0 collective-permute-done
  12.3 0.0 collective-permute-done.1
  12.3 0.0 collective-permute-done.2
  12.4 1.6 %collective-permute-start.4 = (bf16[4,32,768]{2,1,0:T(8,128)(2,1)S(1)}, bf16[4,32,768]{2,1,0:T(8,128)(2,1)S(1)}, u32[]{:S(2)}, u32[]{:S(2)}) collective-permute-start(bf16[4,32,768]{2,1,0:T(8,128)(2,1)S(1)} %constant_dynamic-update-slice_fusion.refs_1_), channel_id=1, source_target_pairs={{0,2},{1,3},{2,0},{3,1},{4,6},{5,7},{6,4},{7,5},{8,10},{9,11},{10,... | collective-permute-start | bytes 589832 | tf_op jit(solution)/shard_map/ppermute | solution.py:320
  13.9 0.0 collective-permute-start.3
  14.0 0.8 %copy-done.6 = bf16[4,8,768]{2,1,0:T(8,128)(2,1)S(1)} copy-done((bf16[4,8,768]{2,1,0:T(8,128)(2,1)S(1)}, bf16[4,8,768]{2,1,0:T(8,128)(2,1)}, u32[]{:S(2)}) %copy-start.6) | copy-done | bytes 49176
  14.7 0.1 shard_map.113.refs_0_
  14.8 0.1 collective-permute-start.8
  14.9 0.8 %constant_dynamic-update-slice_fusion.7 = bf16[4,32,768]{2,1,0:T(8,128)(2,1)S(1)} fusion(bf16[4,8,768]{2,1,0:T(8,128)(2,1)} %param.13), kind=kLoop, calls=%fused_computation.7 | loop fusion | bytes 98304
  15.7 2.3 %collective-permute-done.4.refs_2_ = bf16[4,32,768]{2,1,0:T(8,128)(2,1)S(1)} collective-permute-done((bf16[4,32,768]{2,1,0:T(8,128)(2,1)S(1)}, bf16[4,32,768]{2,1,0:T(8,128)(2,1)S(1)}, u32[]{:S(2)}, u32[]{:S(2)}) %collective-permute-start.4) | collective-permute-done | bytes 196640 | tf_op jit(solution)/shard_map/ppermute | solution.py:320
  18.1 0.0 collective-permute-start.5
  18.1 2.6 %collective-permute-done.8 = bf16[4,8,768]{2,1,0:T(8,128)(2,1)S(1)} collective-permute-done((bf16[4,8,768]{2,1,0:T(8,128)(2,1)}, bf16[4,8,768]{2,1,0:T(8,128)(2,1)S(1)}, u32[]{:S(2)}, u32[]{:S(2)}) %collective-permute-start.8) | collective-permute-done | bytes 49184 | tf_op jit(solution)/shard_map/ppermute | solution.py:320
  20.8 0.1 collective-permute-start.10
  20.9 0.2 shard_map.114.refs_3_
  21.1 0.0 collective-permute-done.3.refs_1_
  21.1 0.0 collective-permute-done.5.refs_2_
  21.1 0.3 shard_map.115.refs_0_
  21.4 2.0 %collective-permute-start.6 = (f32[96,128]{1,0:T(8,128)S(1)}, f32[96,128]{1,0:T(8,128)S(1)}, u32[]{:S(2)}, u32[]{:S(2)}) collective-permute-start(f32[96,128]{1,0:T(8,128)S(1)} %shard_map.115.refs_0_), channel_id=1, source_target_pairs={{0,16},{16,0},{1,17},{17,1},{2,18},{18,2},{3,19},{19,3},{4,20},{20... | collective-permute-start | bytes 147464 | tf_op jit(solution)/shard_map/ppermute | solution.py:420
  23.4 0.1 pad_add_fusion.scalar_ref
  24.2 0.1 collective-permute-start.11
  24.3 0.8 %shard_map.116 = (f32[32,768]{1,0:T(8,128)S(1)}, f32[8,768]{1,0:T(8,128)S(1)}, f32[24,128]{1,0:T(8,128)S(1)}, f32[128,128]{1,0:T(8,128)S(1)}, f32[8,128]{1,0:T(8,128)S(1)}, /*index=5*/f32[128,64]{1,0:T(8,128)S(1)}) custom-call(s32[2]{0:T(128)S(1)} %pad_add_fusion.scalar_ref, bf16[4,8,768]{2,1,0:T(8,128)(2,1)S(1)} %copy-done.5, f32[768]{0:T(1024)S(1)} %copy-done.9, ...), custom_call_target="tpu_custom_call" | custom-call | flops 1000000 | bytes 1000000 | tf_op jit(solution)/shard_map/pallas_call | solution.py:292
  25.0 0.0 copy-start.7
  25.1 0.6 %copy-done.7 = f32[8,768]{1,0:T(8,128)} copy-done((f32[8,768]{1,0:T(8,128)}, f32[8,768]{1,0:T(8,128)S(1)}, u32[]{:S(2)}) %copy-start.7) | copy-done | bytes 24600
  25.7 0.0 collective-permute-done.6.refs_1_
  25.7 0.2 shard_map.117.w_ref.refs_0_
  25.8 0.9 %shard_map.118 = f32[16,24,128]{2,1,0:T(8,128)} custom-call(bf16[96,128]{1,0:T(8,128)(2,1)S(1)} %shard_map.117.w_ref.refs_0_, f32[24,128]{1,0:T(8,128)S(1)} %get-tuple-element.23.head_ref.factor_ref, f32[128,128]{1,0:T(8,128)S(1)} %get-tuple-element.24.order_ref), custom_call_target="tpu_custom_call" | custom-call | flops 1000000 | bytes 1000000 | tf_op jit(solution)/shard_map/pallas_call | solution.py:292
  26.8 1.0 %collective-permute-done.10.refs_2_ = bf16[4,32,768]{2,1,0:T(8,128)(2,1)} collective-permute-done((bf16[4,32,768]{2,1,0:T(8,128)(2,1)S(1)}, bf16[4,32,768]{2,1,0:T(8,128)(2,1)}, u32[]{:S(2)}, u32[]{:S(2)}) %collective-permute-start.10) | collective-permute-done | bytes 196640 | tf_op jit(solution)/shard_map/ppermute | solution.py:320
  27.8 3.6 %all-to-all-start = ((f32[16,24,128]{2,1,0:T(8,128)}), f32[16,24,128]{2,1,0:T(8,128)S(1)}, u32[]{:S(2)}, u32[]{:S(2)}) async-start(f32[16,24,128]{2,1,0:T(8,128)} %shard_map.118), calls=%async_computation | async-start | bytes 393216 | tf_op jit(solution)/shard_map/all_to_all | solution.py:449
  31.4 0.0 collective-permute-done.11.refs_3_
  31.5 0.0 copy-start.8
  31.5 0.7 %copy-done.8 = f32[8,768]{1,0:T(8,128)S(1)} copy-done((f32[8,768]{1,0:T(8,128)S(1)}, f32[8,768]{1,0:T(8,128)}, u32[]{:S(2)}) %copy-start.8) | copy-done | bytes 24600
  32.2 1.7 %shard_map.119 = (f32[32,768]{1,0:T(8,128)S(1)}, bf16[32,768]{1,0:T(8,128)(2,1)S(1)}) custom-call(bf16[96,128]{1,0:T(8,128)(2,1)S(1)} %shard_map.117.w_ref.refs_0_, bf16[4,32,768]{2,1,0:T(8,128)(2,1)S(1)} %constant_dynamic-update-slice_fusion.4.refs_1_, bf16[4,32,768]{2,1,0:T(8,128)(2,1)} %collective-permute-done.10.refs_2_, ...), custom_call_target="tpu_custom_call" | custom-call | flops 1000000 | bytes 1000000 | tf_op jit(solution)/shard_map/pallas_call | solution.py:292
  34.0 0.0 copy-start.1
  34.0 1.5 %collective-permute-start.13 = (bf16[32,768]{1,0:T(8,128)(2,1)S(1)}, bf16[32,768]{1,0:T(8,128)(2,1)S(1)}, u32[]{:S(2)}, u32[]{:S(2)}) collective-permute-start(bf16[32,768]{1,0:T(8,128)(2,1)S(1)} %get-tuple-element.27.refs_0_), channel_id=1, source_target_pairs={{0,16},{16,0},{1,17},{17,1},{2,18},{18,2},{3,19},{19,3},{4,20},{20... | collective-permute-start | bytes 147464 | tf_op jit(solution)/shard_map/ppermute | solution.py:457
  35.4 2.7 %collective-permute-done.13.refs_1_ = bf16[32,768]{1,0:T(8,128)(2,1)S(1)} collective-permute-done((bf16[32,768]{1,0:T(8,128)(2,1)S(1)}, bf16[32,768]{1,0:T(8,128)(2,1)S(1)}, u32[]{:S(2)}, u32[]{:S(2)}) %collective-permute-start.13) | collective-permute-done | bytes 49184 | tf_op jit(solution)/shard_map/ppermute | solution.py:457
  38.1 0.4 shard_map.120.own_ref
  38.6 1.5 %collective-permute-start.14 = (bf16[64,1152]{1,0:T(8,128)(2,1)S(1)}, bf16[64,1152]{1,0:T(8,128)(2,1)S(1)}, u32[]{:S(2)}, u32[]{:S(2)}) collective-permute-start(bf16[64,1152]{1,0:T(8,128)(2,1)S(1)} %shard_map.120.own_ref), channel_id=1, source_target_pairs={{0,16},{16,0},{1,17},{17,1},{2,18},{18,2},{3,19},{19,3},{4,20},{20... | collective-permute-start | bytes 442376 | tf_op jit(solution)/shard_map/ppermute | solution.py:470
  40.0 0.4 all-to-all-done.pair_ref
  40.4 1.1 %shard_map.121 = f32[8,64]{1,0:T(8,128)} custom-call(f32[16,24,128]{2,1,0:T(8,128)S(1)} %all-to-all-done.pair_ref, f32[24,128]{1,0:T(8,128)S(1)} %get-tuple-element.23.head_ref.factor_ref, f32[8,128]{1,0:T(8,128)S(1)} %get-tuple-element.29.own_ref, f32[128,64]{1,0:T(8,128)S(1)} %get-tuple-element.30.slab_ref), custom_call_target="tpu_custom_call" | custom-call | flops 1000000 | bytes 1000000 | tf_op jit(solution)/shard_map/pallas_call | solution.py:292
  41.5 2.5 %collective-permute-done.14.other_ref = bf16[64,1152]{1,0:T(8,128)(2,1)S(1)} collective-permute-done((bf16[64,1152]{1,0:T(8,128)(2,1)S(1)}, bf16[64,1152]{1,0:T(8,128)(2,1)S(1)}, u32[]{:S(2)}, u32[]{:S(2)}) %collective-permute-start.14) | collective-permute-done | bytes 147488 | tf_op jit(solution)/shard_map/ppermute | solution.py:470
  44.0 0.9 %copy-done.4 = f32[32,768]{1,0:T(8,128)S(1)} copy-done((f32[32,768]{1,0:T(8,128)S(1)}, f32[32,768]{1,0:T(8,128)}, u32[]{:S(2)}) %copy-start.4) | copy-done | bytes 98328
  44.9 1.5 %shard_map.122 = bf16[4,8,768]{2,1,0:T(8,128)(2,1)} custom-call(bf16[64,1152]{1,0:T(8,128)(2,1)S(1)} %shard_map.120.own_ref, bf16[64,1152]{1,0:T(8,128)(2,1)S(1)} %collective-permute-done.14.other_ref, f32[32,768]{1,0:T(8,128)S(1)} %copy-done.4, bf16[768,768]{1,0:T(8,128)(2,1)S(1)} %copy-done.1), custom_call_target="tpu_custom_call" | custom-call | flops 1000000 | bytes 1000000 | tf_op jit(solution)/shard_map/pallas_call | solution.py:292
  (25 shorter events, 0.1 us)
Async XLA Ops:
  0.6 23.6 %copy-start.5 = (bf16[4,8,768]{2,1,0:T(8,128)(2,1)S(1)}, bf16[4,8,768]{2,1,0:T(8,128)(2,1)}, u32[]{:S(2)}) copy-start(bf16[4,8,768]{2,1,0:T(8,128)(2,1)} %skip_hbm.1) | copy-start | bytes 147460
  0.6 23.6 %copy-start.9 = (f32[768]{0:T(1024)S(1)}, f32[768]{0:T(1024)}, u32[]{:S(2)}) copy-start(f32[768]{0:T(1024)} %gain_ref.1) | copy-start | bytes 9220
  0.7 23.6 %copy-start.10 = (f32[12]{0:T(128)S(1)}, f32[12]{0:T(128)}, u32[]{:S(2)}) copy-start(f32[12]{0:T(128)} %factor_ref.1) | copy-start | bytes 148
  0.7 11.6 %collective-permute-start = (bf16[4,8,768]{2,1,0:T(8,128)(2,1)}, bf16[4,8,768]{2,1,0:T(8,128)(2,1)S(1)}, u32[]{:S(2)}, u32[]{:S(2)}) collective-permute-start(bf16[4,8,768]{2,1,0:T(8,128)(2,1)} %param.12), channel_id=1, source_target_pairs={{0,4},{1,5},{2,6},{3,7},{4,8},{5,9},{6,10},{7,11},{8,12},{9,13},{1... | collective-permute-start | bytes 147464 | tf_op jit(solution)/shard_map/ppermute | solution.py:320
  3.7 8.6 %collective-permute-start.1 = (bf16[4,8,768]{2,1,0:T(8,128)(2,1)}, bf16[4,8,768]{2,1,0:T(8,128)(2,1)S(1)}, u32[]{:S(2)}, u32[]{:S(2)}) collective-permute-start(bf16[4,8,768]{2,1,0:T(8,128)(2,1)} %param.12), channel_id=1, source_target_pairs={{0,8},{1,9},{2,10},{3,11},{4,12},{5,13},{6,14},{7,15},{8,0},{9,1},... | collective-permute-start | bytes 147464 | tf_op jit(solution)/shard_map/ppermute | solution.py:320
  6.3 6.0 %collective-permute-start.2 = (bf16[4,8,768]{2,1,0:T(8,128)(2,1)}, bf16[4,8,768]{2,1,0:T(8,128)(2,1)S(1)}, u32[]{:S(2)}, u32[]{:S(2)}) collective-permute-start(bf16[4,8,768]{2,1,0:T(8,128)(2,1)} %param.12), channel_id=1, source_target_pairs={{0,12},{1,13},{2,14},{3,15},{4,0},{5,1},{6,2},{7,3},{8,4},{9,5},{1... | collective-permute-start | bytes 147464 | tf_op jit(solution)/shard_map/ppermute | solution.py:320
  7.7 7.2 %collective-permute-start.7 = (bf16[4,8,768]{2,1,0:T(8,128)(2,1)}, bf16[4,8,768]{2,1,0:T(8,128)(2,1)S(1)}, u32[]{:S(2)}, u32[]{:S(2)}) collective-permute-start(bf16[4,8,768]{2,1,0:T(8,128)(2,1)} %param.13), channel_id=1, source_target_pairs={{0,4},{1,5},{2,6},{3,7},{4,8},{5,9},{6,10},{7,11},{8,12},{9,13},{1... | collective-permute-start | bytes 147464 | tf_op jit(solution)/shard_map/ppermute | solution.py:320
  8.4 12.4 %collective-permute-start.9 = (bf16[4,8,768]{2,1,0:T(8,128)(2,1)}, bf16[4,8,768]{2,1,0:T(8,128)(2,1)S(1)}, u32[]{:S(2)}, u32[]{:S(2)}) collective-permute-start(bf16[4,8,768]{2,1,0:T(8,128)(2,1)} %param.13), channel_id=1, source_target_pairs={{0,12},{1,13},{2,14},{3,15},{4,0},{5,1},{6,2},{7,3},{8,4},{9,5},{1... | collective-permute-start | bytes 147464 | tf_op jit(solution)/shard_map/ppermute | solution.py:320
  12.4 5.7 %collective-permute-start.4 = (bf16[4,32,768]{2,1,0:T(8,128)(2,1)S(1)}, bf16[4,32,768]{2,1,0:T(8,128)(2,1)S(1)}, u32[]{:S(2)}, u32[]{:S(2)}) collective-permute-start(bf16[4,32,768]{2,1,0:T(8,128)(2,1)S(1)} %constant_dynamic-update-slice_fusion.refs_1_), channel_id=1, source_target_pairs={{0,2},{1,3},{2,0},{3,1},{4,6},{5,7},{6,4},{7,5},{8,10},{9,11},{10,... | collective-permute-start | bytes 589832 | tf_op jit(solution)/shard_map/ppermute | solution.py:320
  13.9 7.2 %collective-permute-start.3 = (bf16[4,32,768]{2,1,0:T(8,128)(2,1)S(1)}, bf16[4,32,768]{2,1,0:T(8,128)(2,1)S(1)}, u32[]{:S(2)}, u32[]{:S(2)}) collective-permute-start(bf16[4,32,768]{2,1,0:T(8,128)(2,1)S(1)} %constant_dynamic-update-slice_fusion.refs_1_), channel_id=1, source_target_pairs={{0,1},{1,0},{2,3},{3,2},{4,5},{5,4},{6,7},{7,6},{8,9},{9,8},{10,11... | collective-permute-start | bytes 589832 | tf_op jit(solution)/shard_map/ppermute | solution.py:320
  13.9 0.8 %copy-start.6 = (bf16[4,8,768]{2,1,0:T(8,128)(2,1)S(1)}, bf16[4,8,768]{2,1,0:T(8,128)(2,1)}, u32[]{:S(2)}) copy-start(bf16[4,8,768]{2,1,0:T(8,128)(2,1)} %q_hbm) | copy-start | bytes 147460
  14.8 5.9 %collective-permute-start.8 = (bf16[4,8,768]{2,1,0:T(8,128)(2,1)}, bf16[4,8,768]{2,1,0:T(8,128)(2,1)S(1)}, u32[]{:S(2)}, u32[]{:S(2)}) collective-permute-start(bf16[4,8,768]{2,1,0:T(8,128)(2,1)} %param.13), channel_id=1, source_target_pairs={{0,8},{1,9},{2,10},{3,11},{4,12},{5,13},{6,14},{7,15},{8,0},{9,1},... | collective-permute-start | bytes 147464 | tf_op jit(solution)/shard_map/ppermute | solution.py:320
  18.1 3.0 %collective-permute-start.5 = (bf16[4,32,768]{2,1,0:T(8,128)(2,1)S(1)}, bf16[4,32,768]{2,1,0:T(8,128)(2,1)S(1)}, u32[]{:S(2)}, u32[]{:S(2)}) collective-permute-start(bf16[4,32,768]{2,1,0:T(8,128)(2,1)S(1)} %collective-permute-done.4.refs_2_), channel_id=1, source_target_pairs={{0,1},{1,0},{2,3},{3,2},{4,5},{5,4},{6,7},{7,6},{8,9},{9,8},{10,11... | collective-permute-start | bytes 589832 | tf_op jit(solution)/shard_map/ppermute | solution.py:320
  20.7 10.7 %copy-start.2 = (bf16[768,768]{1,0:T(8,128)(2,1)S(1)}, bf16[768,768]{1,0:T(8,128)(2,1)}, u32[]{:S(2)}) copy-start(bf16[768,768]{1,0:T(8,128)(2,1)} %refs_5_.1) | copy-start | bytes 3538948
  20.8 7.0 %collective-permute-start.10 = (bf16[4,32,768]{2,1,0:T(8,128)(2,1)S(1)}, bf16[4,32,768]{2,1,0:T(8,128)(2,1)}, u32[]{:S(2)}, u32[]{:S(2)}) collective-permute-start(bf16[4,32,768]{2,1,0:T(8,128)(2,1)S(1)} %constant_dynamic-update-slice_fusion.4.refs_1_), channel_id=1, source_target_pairs={{0,2},{1,3},{2,0},{3,1},{4,6},{5,7},{6,4},{7,5},{8,10},{9,11},{10,... | collective-permute-start | bytes 589832 | tf_op jit(solution)/shard_map/ppermute | solution.py:320
  21.4 4.2 %collective-permute-start.6 = (f32[96,128]{1,0:T(8,128)S(1)}, f32[96,128]{1,0:T(8,128)S(1)}, u32[]{:S(2)}, u32[]{:S(2)}) collective-permute-start(f32[96,128]{1,0:T(8,128)S(1)} %shard_map.115.refs_0_), channel_id=1, source_target_pairs={{0,16},{16,0},{1,17},{17,1},{2,18},{18,2},{3,19},{19,3},{4,20},{20... | collective-permute-start | bytes 147464 | tf_op jit(solution)/shard_map/ppermute | solution.py:420
  24.2 7.3 %collective-permute-start.11 = (bf16[4,32,768]{2,1,0:T(8,128)(2,1)S(1)}, bf16[4,32,768]{2,1,0:T(8,128)(2,1)}, u32[]{:S(2)}, u32[]{:S(2)}) collective-permute-start(bf16[4,32,768]{2,1,0:T(8,128)(2,1)S(1)} %constant_dynamic-update-slice_fusion.4.refs_1_), channel_id=1, source_target_pairs={{0,1},{1,0},{2,3},{3,2},{4,5},{5,4},{6,7},{7,6},{8,9},{9,8},{10,11... | collective-permute-start | bytes 589832 | tf_op jit(solution)/shard_map/ppermute | solution.py:320
  25.0 0.6 %copy-start.7 = (f32[8,768]{1,0:T(8,128)}, f32[8,768]{1,0:T(8,128)S(1)}, u32[]{:S(2)}) copy-start(f32[8,768]{1,0:T(8,128)S(1)} %get-tuple-element.26.refs_7_) | copy-start | bytes 73732
  26.8 11.3 %copy-start = (bf16[768,1152]{1,0:T(8,128)(2,1)S(1)}, bf16[768,1152]{1,0:T(8,128)(2,1)}, u32[]{:S(2)}) copy-start(bf16[768,1152]{1,0:T(8,128)(2,1)} %refs_2_.1) | copy-start | bytes 5308420
  27.8 3.6 %collective-permute-start.12 = (bf16[4,32,768]{2,1,0:T(8,128)(2,1)}, bf16[4,32,768]{2,1,0:T(8,128)(2,1)}, u32[]{:S(2)}, u32[]{:S(2)}) collective-permute-start(bf16[4,32,768]{2,1,0:T(8,128)(2,1)} %collective-permute-done.10.refs_2_), channel_id=1, source_target_pairs={{0,1},{1,0},{2,3},{3,2},{4,5},{5,4},{6,7},{7,6},{8,9},{9,8},{10,11... | collective-permute-start | bytes 589832 | tf_op jit(solution)/shard_map/ppermute | solution.py:320
  27.8 12.6 %all-to-all-start = ((f32[16,24,128]{2,1,0:T(8,128)}), f32[16,24,128]{2,1,0:T(8,128)S(1)}, u32[]{:S(2)}, u32[]{:S(2)}) async-start(f32[16,24,128]{2,1,0:T(8,128)} %shard_map.118), calls=%async_computation | async-start | bytes 393216 | tf_op jit(solution)/shard_map/all_to_all | solution.py:449
  31.5 0.7 %copy-start.8 = (f32[8,768]{1,0:T(8,128)S(1)}, f32[8,768]{1,0:T(8,128)}, u32[]{:S(2)}) copy-start(f32[8,768]{1,0:T(8,128)} %copy-done.7) | copy-start | bytes 73732
  34.0 4.6 %copy-start.3 = (f32[32,768]{1,0:T(8,128)}, f32[32,768]{1,0:T(8,128)S(1)}, u32[]{:S(2)}) copy-start(f32[32,768]{1,0:T(8,128)S(1)} %get-tuple-element.31.refs_0_) | copy-start | bytes 294916
  34.0 10.0 %copy-start.1 = (bf16[768,768]{1,0:T(8,128)(2,1)S(1)}, bf16[768,768]{1,0:T(8,128)(2,1)}, u32[]{:S(2)}) copy-start(bf16[768,768]{1,0:T(8,128)(2,1)} %refs_1_.1) | copy-start | bytes 3538948
  34.0 4.2 %collective-permute-start.13 = (bf16[32,768]{1,0:T(8,128)(2,1)S(1)}, bf16[32,768]{1,0:T(8,128)(2,1)S(1)}, u32[]{:S(2)}, u32[]{:S(2)}) collective-permute-start(bf16[32,768]{1,0:T(8,128)(2,1)S(1)} %get-tuple-element.27.refs_0_), channel_id=1, source_target_pairs={{0,16},{16,0},{1,17},{17,1},{2,18},{18,2},{3,19},{19,3},{4,20},{20... | collective-permute-start | bytes 147464 | tf_op jit(solution)/shard_map/ppermute | solution.py:457
  38.6 5.4 %collective-permute-start.14 = (bf16[64,1152]{1,0:T(8,128)(2,1)S(1)}, bf16[64,1152]{1,0:T(8,128)(2,1)S(1)}, u32[]{:S(2)}, u32[]{:S(2)}) collective-permute-start(bf16[64,1152]{1,0:T(8,128)(2,1)S(1)} %shard_map.120.own_ref), channel_id=1, source_target_pairs={{0,16},{16,0},{1,17},{17,1},{2,18},{18,2},{3,19},{19,3},{4,20},{20... | collective-permute-start | bytes 442376 | tf_op jit(solution)/shard_map/ppermute | solution.py:470
  44.0 0.9 %copy-start.4 = (f32[32,768]{1,0:T(8,128)S(1)}, f32[32,768]{1,0:T(8,128)}, u32[]{:S(2)}) copy-start(f32[32,768]{1,0:T(8,128)} %copy-done.3) | copy-start | bytes 294916

commit v9 on v8

--- a/solution.py
+++ b/solution.py
@@ -68,12 +68,8 @@
             masked_ref[r, block * span : (block + 1) * span, :] = q
 
 
-def prepare_kernel(heads, stages, scalar_ref, skip_hbm, gain_ref, factor_ref, offset_ref, *refs):
-    wide_skip_ref, wide_gain_ref, head_ref, order_ref, own_ref, slab_ref, skip_ref, sems = refs
-    _, sites, embed = skip_ref.shape
-    copy = pltpu.make_async_copy(skip_hbm, skip_ref, sems.at[0])
-    copy.start()
-    wide_gain_ref[...] = jnp.broadcast_to(gain_ref[...].reshape(1, embed), wide_gain_ref.shape)
+def prepare_kernel(heads, sites, stages, scalar_ref, factor_ref, offset_ref, *refs):
+    head_ref, order_ref, own_ref, slab_ref = refs
     row = lax.broadcasted_iota(jnp.int32, head_ref.shape, 0)
     factors = jnp.zeros(head_ref.shape, F32)
     for h in range(heads):
@@ -90,8 +86,6 @@
     row = lax.broadcasted_iota(jnp.int32, slab_ref.shape, 0)
     lane = lax.broadcasted_iota(jnp.int32, slab_ref.shape, 1)
     slab_ref[...] = (row == lane + seq_index * slab_ref.shape[1]).astype(F32)
-    copy.wait()
-    wide_skip_ref[...] = skip_ref[...].astype(F32).reshape(wide_skip_ref.shape)
 
 
 def logits_kernel(part_count, *refs):
@@ -145,8 +139,7 @@
 def mix_kernel(head, v_count, *refs):
     w_ref, v_refs = refs[0], refs[1 : 1 + v_count]
     closing_ref, skip_ref, gain_ref, hidden_ref, normed_ref, mixed = refs[1 + v_count :]
-    rows, _, embed = v_refs[0].shape
-    sites = skip_ref.shape[0] // rows
+    rows, sites, embed = skip_ref.shape
     width = lane_block(embed, head)
     group = width // head
     lane_head = lax.broadcasted_iota(jnp.int32, (sites, width), 1) // head
@@ -160,11 +153,11 @@
             for g in range(1, group):
                 own = jnp.where(lane_head == g, product[g * sites : (g + 1) * sites, :], own)
             mixed[r * sites : (r + 1) * sites, cols] = own
-    hidden = skip_ref[...] + dot_nn(mixed[...].astype(BF16), closing_ref[...])
+    hidden = skip_ref[...].astype(F32).reshape(rows * sites, embed) + dot_nn(mixed[...].astype(BF16), closing_ref[...])
     hidden_ref[...] = hidden
     centered = hidden - jnp.mean(hidden, axis=1, keepdims=True)
     spread = jnp.mean(centered * centered, axis=1, keepdims=True)
-    normed_ref[...] = (centered * lax.rsqrt(spread + 1e-05) * gain_ref[0:1, :]).astype(BF16)
+    normed_ref[...] = (centered * lax.rsqrt(spread + 1e-05) * gain_ref[...].reshape(1, embed)).astype(BF16)
 
 
 def project_kernel(part_count, *refs):
@@ -364,11 +357,8 @@
     width = lane_block(embed, head)
     key_first = [lateral_matched_vectors] + send_all([lateral_matched_vectors], pos_count, outer)
     key_parts = [jnp.concatenate(key_first, axis=1)]
-    later_value = after(lateral_carried_vectors, key_parts[0])
-    value_first = [later_value]
-    for delta in range(1, outer[1]):
-        sent = lateral_carried_vectors if delta in (1, outer[1] - 1) else later_value
-        value_first.append(send_pos(sent, pos_count, *outer, delta))
+    value_first = [after(lateral_carried_vectors, key_parts[0])]
+    value_first += send_all([lateral_carried_vectors], pos_count, outer)
     masked = call(
         functools.partial(query_kernel, head),
         jax.ShapeDtypeStruct((rows, heads * sites, width), BF16),
@@ -395,29 +385,19 @@
             jax.ShapeDtypeStruct((heads * sites, length), F32),
             [masked, *far_parts, partial],
         )
-    skip, gain, head_factors, order, own_select, slab_select = call(
-        functools.partial(prepare_kernel, heads, stages),
+    head_factors, order, own_select, slab_select = call(
+        functools.partial(prepare_kernel, heads, sites, stages),
         (
-            jax.ShapeDtypeStruct((cells, embed), F32),
-            jax.ShapeDtypeStruct((8, embed), F32),
             jax.ShapeDtypeStruct((head_rows + 8, 128), F32),
             jax.ShapeDtypeStruct((length, length), F32),
             jax.ShapeDtypeStruct((sites, length), F32),
             jax.ShapeDtypeStruct((length, slab_width), F32),
         ),
-        [
-            after(scalars, partial),
-            skip_stream_input,
-            upright_normalizer_multiplier,
-            regression_factors,
-            regression_offset,
-        ],
-        smem=(0, 3, 4),
-        hbm=(1,),
-        scratch=[pltpu.VMEM((rows, sites, embed), BF16), pltpu.SemaphoreType.DMA((1,))],
+        [after(scalars, partial), regression_factors, regression_offset],
+        smem=(0, 1, 2),
     )
     if seq_count == 2:
-        partials = [partial, after(lax.ppermute(partial, "seq", swap), skip)]
+        partials = [partial, after(lax.ppermute(partial, "seq", swap), order)]
     else:
         partials = [lax.psum(partial, "seq")]
     shares = call(
@@ -443,7 +423,13 @@
             jax.ShapeDtypeStruct((cells, embed), F32),
             jax.ShapeDtypeStruct((cells, embed), BF16),
         ),
-        [shares, *value_parts, lateral_closing_linear, skip, gain],
+        [
+            shares,
+            *value_parts,
+            lateral_closing_linear,
+            skip_stream_input,
+            upright_normalizer_multiplier,
+        ],
         scratch=[pltpu.VMEM((cells, embed), F32)],
     )
     pair_all = lax.all_to_all(pair_local, "pos", split_axis=0, concat_axis=0, tiled=True)
@@ -455,7 +441,7 @@
     )
     if swapped:
         normed_all = [normed, lax.ppermute(normed, "seq", swap)]
-        weight = upright_threefold_linear
+        weight = after(upright_threefold_linear, normed)
     else:
         normed_all = [normed]
         weight = lax.all_gather(upright_threefold_linear, "seq", axis=1, tiled=True)
@@ -475,7 +461,11 @@
     alignment_output = call(
         functools.partial(column, head, 1.0 / math.sqrt(head)),
         jax.ShapeDtypeStruct((rows, sites, embed), BF16),
-        [*column_inputs, after(hidden, pairing_chances), upright_closing_linear],
+        [
+            *column_inputs,
+            after(hidden, pairing_chances),
+            after(upright_closing_linear, projected),
+        ],
         scratch=[
             pltpu.VMEM((cells * rows * seq_count, embed), F32),
             pltpu.VMEM((cells, embed), F32),

time: 46.8 us -> 44.6 us (0.953)
  waiting for transfers between devices: 11.6 us -> 8.99 us
  starting transfers between devices: 21.3 us -> 23.3 us
  local copies, waits for them, and re-layouts: 4.72 us -> 3.25 us
    ppermute x12, waiting for transfers between devices: 6.05 us -> 2.53 us  [send_pos(): return lax.ppermute(array, 'pos', pairs)]
    unnamed x28 -> x20, local copies, waits for them, and re-layouts: 4.71 us -> 3.24 us
    ppermute x12, starting transfers between devices: 12.7 us -> 14.1 us  [send_pos(): return lax.ppermute(array, 'pos', pairs)]
    ppermute x1, waiting for transfers between devices: 0.01 us -> 1.08 us  [per_device(): partials = [partial, after(lax.ppermute(partial, 'seq', swap), order)]]
    all_to_all x1, starting transfers between devices: 3.61 us -> 4.51 us  [per_device(): lax.all_to_all(pair_local, 'pos', split_axis=0, concat_axis=0, tiled=True)]
  transfers between devices with their start and end apart: 16 -> 16, of which waited for: 6 -> 6; matrix products, arithmetic and copies ran while one was open for 4% -> 4% of each run, Pallas kernels for 12% -> 13%
where the time goes in v9:
time: 44.6 us; the launch traced here: 44.1 us
  starting transfers between devices  23.3 us (52%)
  waiting for transfers between devices  8.99 us (20%)
  Pallas kernels  7.05 us (16%)
  local copies, waits for them, and re-layouts  3.25 us (7%)
  between operations  1.48 us (3%)
    ppermute x12, starting transfers between devices, send_pos(): return lax.ppermute(array, 'pos', pairs)  14.1 us
    pallas_call x10, Pallas kernels, call(): pl.pallas_call(kernel, out_shape=out_shape, in_specs=specs, out_specs=jax...  7.05 us
    all_to_all x1, starting transfers between devices, per_device(): lax.all_to_all(pair_local, 'pos', split_axis=0, concat_axis=0, tiled=True)  4.51 us
    unnamed x20, local copies, waits for them, and re-layouts  3.24 us
    ppermute x1, waiting for transfers between devices, per_device(): normed_all = [normed, lax.ppermute(normed, 'seq', swap)]  2.6 us
    ppermute x1, waiting for transfers between devices, per_device(): lax.ppermute(projected, 'seq', swap)  2.54 us
    ppermute x12, waiting for transfers between devices, send_pos(): return lax.ppermute(array, 'pos', pairs)  2.53 us
    ppermute x1, starting transfers between devices, per_device(): partials = [partial, after(lax.ppermute(partial, 'seq', swap), order)]  1.56 us
  transfers between devices with their start and end apart: 16, of which 6 were waited for; matrix products, arithmetic and copies ran while one was open for 4% of the time, Pallas kernels for 13%

profile of v9, /device:TPU:0, one launch (start us, length us, event | category | flops | bytes accessed | tf_op | source)
XLA Modules:
  0.0 44.1 jit_solution(5606303648644304254)
XLA Ops:
  0.6 3.1 %collective-permute-start = (bf16[4,8,768]{2,1,0:T(8,128)(2,1)}, bf16[4,8,768]{2,1,0:T(8,128)(2,1)S(1)}, u32[]{:S(2)}, u32[]{:S(2)}) collective-permute-start(bf16[4,8,768]{2,1,0:T(8,128)(2,1)} %param.12), channel_id=1, source_target_pairs={{0,4},{1,5},{2,6},{3,7},{4,8},{5,9},{6,10},{7,11},{8,12},{9,13},{1... | collective-permute-start | bytes 147464 | tf_op jit(solution)/shard_map/ppermute | solution.py:313
  3.7 2.6 %collective-permute-start.1 = (bf16[4,8,768]{2,1,0:T(8,128)(2,1)}, bf16[4,8,768]{2,1,0:T(8,128)(2,1)S(1)}, u32[]{:S(2)}, u32[]{:S(2)}) collective-permute-start(bf16[4,8,768]{2,1,0:T(8,128)(2,1)} %param.12), channel_id=1, source_target_pairs={{0,8},{1,9},{2,10},{3,11},{4,12},{5,13},{6,14},{7,15},{8,0},{9,1},... | collective-permute-start | bytes 147464 | tf_op jit(solution)/shard_map/ppermute | solution.py:313
  6.3 1.3 %collective-permute-start.2 = (bf16[4,8,768]{2,1,0:T(8,128)(2,1)}, bf16[4,8,768]{2,1,0:T(8,128)(2,1)S(1)}, u32[]{:S(2)}, u32[]{:S(2)}) collective-permute-start(bf16[4,8,768]{2,1,0:T(8,128)(2,1)} %param.12), channel_id=1, source_target_pairs={{0,12},{1,13},{2,14},{3,15},{4,0},{5,1},{6,2},{7,3},{8,4},{9,5},{1... | collective-permute-start | bytes 147464 | tf_op jit(solution)/shard_map/ppermute | solution.py:313
  7.7 0.7 %collective-permute-start.7 = (bf16[4,8,768]{2,1,0:T(8,128)(2,1)}, bf16[4,8,768]{2,1,0:T(8,128)(2,1)S(1)}, u32[]{:S(2)}, u32[]{:S(2)}) collective-permute-start(bf16[4,8,768]{2,1,0:T(8,128)(2,1)} %param.13), channel_id=1, source_target_pairs={{0,4},{1,5},{2,6},{3,7},{4,8},{5,9},{6,10},{7,11},{8,12},{9,13},{1... | collective-permute-start | bytes 147464 | tf_op jit(solution)/shard_map/ppermute | solution.py:313
  8.3 0.3 collective-permute-start.8
  8.7 0.8 %constant_dynamic-update-slice_fusion.3 = bf16[4,32,768]{2,1,0:T(8,128)(2,1)S(1)} fusion(bf16[4,8,768]{2,1,0:T(8,128)(2,1)} %param.12), kind=kLoop, calls=%fused_computation.3 | loop fusion | bytes 98304
  9.5 0.0 collective-permute-done
  9.5 2.8 %collective-permute-start.9 = (bf16[4,8,768]{2,1,0:T(8,128)(2,1)}, bf16[4,8,768]{2,1,0:T(8,128)(2,1)S(1)}, u32[]{:S(2)}, u32[]{:S(2)}) collective-permute-start(bf16[4,8,768]{2,1,0:T(8,128)(2,1)} %param.13), channel_id=1, source_target_pairs={{0,12},{1,13},{2,14},{3,15},{4,0},{5,1},{6,2},{7,3},{8,4},{9,5},{1... | collective-permute-start | bytes 147464 | tf_op jit(solution)/shard_map/ppermute | solution.py:313
  12.3 0.0 collective-permute-done.1
  12.3 0.0 collective-permute-done.2
  12.3 1.6 %collective-permute-start.4 = (bf16[4,32,768]{2,1,0:T(8,128)(2,1)S(1)}, bf16[4,32,768]{2,1,0:T(8,128)(2,1)S(1)}, u32[]{:S(2)}, u32[]{:S(2)}) collective-permute-start(bf16[4,32,768]{2,1,0:T(8,128)(2,1)S(1)} %constant_dynamic-update-slice_fusion.refs_1_), channel_id=1, source_target_pairs={{0,2},{1,3},{2,0},{3,1},{4,6},{5,7},{6,4},{7,5},{8,10},{9,11},{10,... | collective-permute-start | bytes 589832 | tf_op jit(solution)/shard_map/ppermute | solution.py:313
  13.9 0.0 collective-permute-start.3
  13.9 0.8 %copy-done.3 = bf16[4,8,768]{2,1,0:T(8,128)(2,1)S(1)} copy-done((bf16[4,8,768]{2,1,0:T(8,128)(2,1)S(1)}, bf16[4,8,768]{2,1,0:T(8,128)(2,1)}, u32[]{:S(2)}) %copy-start.3) | copy-done | bytes 49176
  14.7 0.1 shard_map.113.refs_0_
  14.8 0.0 collective-permute-done.7
  14.8 0.8 %constant_dynamic-update-slice_fusion.7 = bf16[4,32,768]{2,1,0:T(8,128)(2,1)S(1)} fusion(bf16[4,8,768]{2,1,0:T(8,128)(2,1)} %param.13), kind=kLoop, calls=%fused_computation.7 | loop fusion | bytes 98304
  15.6 0.0 copy-start.5
  15.7 2.4 %collective-permute-done.4.refs_2_ = bf16[4,32,768]{2,1,0:T(8,128)(2,1)S(1)} collective-permute-done((bf16[4,32,768]{2,1,0:T(8,128)(2,1)S(1)}, bf16[4,32,768]{2,1,0:T(8,128)(2,1)S(1)}, u32[]{:S(2)}, u32[]{:S(2)}) %collective-permute-start.4) | collective-permute-done | bytes 196640 | tf_op jit(solution)/shard_map/ppermute | solution.py:313
  18.1 0.0 collective-permute-start.5
  18.1 0.0 collective-permute-done.9
  18.1 1.6 %collective-permute-start.10 = (bf16[4,32,768]{2,1,0:T(8,128)(2,1)S(1)}, bf16[4,32,768]{2,1,0:T(8,128)(2,1)}, u32[]{:S(2)}, u32[]{:S(2)}) collective-permute-start(bf16[4,32,768]{2,1,0:T(8,128)(2,1)S(1)} %constant_dynamic-update-slice_fusion.4.refs_1_), channel_id=1, source_target_pairs={{0,2},{1,3},{2,0},{3,1},{4,6},{5,7},{6,4},{7,5},{8,10},{9,11},{10,... | collective-permute-start | bytes 589832 | tf_op jit(solution)/shard_map/ppermute | solution.py:313
  19.7 0.2 shard_map.114.refs_3_
  19.9 0.0 collective-permute-done.5.refs_2_
  19.9 0.3 shard_map.115.refs_0_
  20.2 1.6 %collective-permute-start.6 = (f32[96,128]{1,0:T(8,128)S(1)}, f32[96,128]{1,0:T(8,128)S(1)}, u32[]{:S(2)}, u32[]{:S(2)}) collective-permute-start(f32[96,128]{1,0:T(8,128)S(1)} %shard_map.115.refs_0_), channel_id=1, source_target_pairs={{0,16},{16,0},{1,17},{17,1},{2,18},{18,2},{3,19},{19,3},{4,20},{20... | collective-permute-start | bytes 147464 | tf_op jit(solution)/shard_map/ppermute | solution.py:400
  21.7 0.1 pad_add_fusion.scalar_ref
  22.5 0.1 collective-permute-start.11
  22.6 0.7 %shard_map.116 = (f32[24,128]{1,0:T(8,128)S(1)}, f32[128,128]{1,0:T(8,128)S(1)}, f32[8,128]{1,0:T(8,128)S(1)}, f32[128,64]{1,0:T(8,128)S(1)}) custom-call(s32[2]{0:T(128)S(1)} %pad_add_fusion.scalar_ref, f32[12]{0:T(128)S(1)} %copy-done.6, f32[1]{0:T(128)S(6)} %copy.18.offset_ref), custom_call_target="tpu_custom_call" | custom-call | flops 1000000 | bytes 1000000 | tf_op jit(solution)/shard_map/pallas_call | solution.py:285
  23.3 1.1 %collective-permute-done.6.refs_1_ = f32[96,128]{1,0:T(8,128)S(1)} collective-permute-done((f32[96,128]{1,0:T(8,128)S(1)}, f32[96,128]{1,0:T(8,128)S(1)}, u32[]{:S(2)}, u32[]{:S(2)}) %collective-permute-start.6) | collective-permute-done | bytes 49184 | tf_op jit(solution)/shard_map/ppermute | solution.py:400
  24.4 0.2 shard_map.117.w_ref.refs_0_
  24.5 0.9 %shard_map.118 = f32[16,24,128]{2,1,0:T(8,128)} custom-call(bf16[96,128]{1,0:T(8,128)(2,1)S(1)} %shard_map.117.w_ref.refs_0_, f32[24,128]{1,0:T(8,128)S(1)} %get-tuple-element.23.head_ref.factor_ref, f32[128,128]{1,0:T(8,128)S(1)} %get-tuple-element.19.order_ref), custom_call_target="tpu_custom_call" | custom-call | flops 1000000 | bytes 1000000 | tf_op jit(solution)/shard_map/pallas_call | solution.py:285
  25.5 0.1 collective-permute-done.10.refs_2_
  25.6 0.0 collective-permute-start.12
  25.6 4.5 %all-to-all-start = ((f32[16,24,128]{2,1,0:T(8,128)}), f32[16,24,128]{2,1,0:T(8,128)S(1)}, u32[]{:S(2)}, u32[]{:S(2)}) async-start(f32[16,24,128]{2,1,0:T(8,128)} %shard_map.118), calls=%async_computation | async-start | bytes 393216 | tf_op jit(solution)/shard_map/all_to_all | solution.py:435
  30.1 0.0 collective-permute-done.11.refs_3_
  30.1 0.0 collective-permute-done.12.refs_4_
  30.1 0.0 copy-start.4
  30.1 0.8 %copy-done.4 = bf16[4,8,768]{2,1,0:T(8,128)(2,1)S(1)} copy-done((bf16[4,8,768]{2,1,0:T(8,128)(2,1)S(1)}, bf16[4,8,768]{2,1,0:T(8,128)(2,1)}, u32[]{:S(2)}) %copy-start.4) | copy-done | bytes 49176
  30.9 1.7 %shard_map.119 = (f32[32,768]{1,0:T(8,128)S(1)}, bf16[32,768]{1,0:T(8,128)(2,1)S(1)}) custom-call(bf16[96,128]{1,0:T(8,128)(2,1)S(1)} %shard_map.117.w_ref.refs_0_, bf16[4,32,768]{2,1,0:T(8,128)(2,1)S(1)} %constant_dynamic-update-slice_fusion.4.refs_1_, bf16[4,32,768]{2,1,0:T(8,128)(2,1)} %collective-permute-done.10.refs_2_, ...), custom_call_target="tpu_custom_call" | custom-call | flops 1000000 | bytes 1000000 | tf_op jit(solution)/shard_map/pallas_call | solution.py:285
  32.7 0.0 copy-start.2
  32.7 1.6 %collective-permute-start.13 = (bf16[32,768]{1,0:T(8,128)(2,1)S(1)}, bf16[32,768]{1,0:T(8,128)(2,1)S(1)}, u32[]{:S(2)}, u32[]{:S(2)}) collective-permute-start(bf16[32,768]{1,0:T(8,128)(2,1)S(1)} %get-tuple-element.25.refs_0_), channel_id=1, source_target_pairs={{0,16},{16,0},{1,17},{17,1},{2,18},{18,2},{3,19},{19,3},{4,20},{20... | collective-permute-start | bytes 147464 | tf_op jit(solution)/shard_map/ppermute | solution.py:443
  34.2 2.6 %collective-permute-done.13.refs_1_ = bf16[32,768]{1,0:T(8,128)(2,1)S(1)} collective-permute-done((bf16[32,768]{1,0:T(8,128)(2,1)S(1)}, bf16[32,768]{1,0:T(8,128)(2,1)S(1)}, u32[]{:S(2)}, u32[]{:S(2)}) %collective-permute-start.13) | collective-permute-done | bytes 49184 | tf_op jit(solution)/shard_map/ppermute | solution.py:443
  36.8 0.4 shard_map.120.own_ref
  37.3 1.6 %collective-permute-start.14 = (bf16[64,1152]{1,0:T(8,128)(2,1)S(1)}, bf16[64,1152]{1,0:T(8,128)(2,1)S(1)}, u32[]{:S(2)}, u32[]{:S(2)}) collective-permute-start(bf16[64,1152]{1,0:T(8,128)(2,1)S(1)} %shard_map.120.own_ref), channel_id=1, source_target_pairs={{0,16},{16,0},{1,17},{17,1},{2,18},{18,2},{3,19},{19,3},{4,20},{20... | collective-permute-start | bytes 442376 | tf_op jit(solution)/shard_map/ppermute | solution.py:456
  38.8 0.2 all-to-all-done.pair_ref
  39.1 1.1 %shard_map.121 = f32[8,64]{1,0:T(8,128)} custom-call(f32[16,24,128]{2,1,0:T(8,128)S(1)} %all-to-all-done.pair_ref, f32[24,128]{1,0:T(8,128)S(1)} %get-tuple-element.23.head_ref.factor_ref, f32[8,128]{1,0:T(8,128)S(1)} %get-tuple-element.28.own_ref, f32[128,64]{1,0:T(8,128)S(1)} %get-tuple-element.29.slab_ref), custom_call_target="tpu_custom_call" | custom-call | flops 1000000 | bytes 1000000 | tf_op jit(solution)/shard_map/pallas_call | solution.py:285
  40.1 2.5 %collective-permute-done.14.other_ref = bf16[64,1152]{1,0:T(8,128)(2,1)S(1)} collective-permute-done((bf16[64,1152]{1,0:T(8,128)(2,1)S(1)}, bf16[64,1152]{1,0:T(8,128)(2,1)S(1)}, u32[]{:S(2)}, u32[]{:S(2)}) %collective-permute-start.14) | collective-permute-done | bytes 147488 | tf_op jit(solution)/shard_map/ppermute | solution.py:456
  42.7 1.5 %shard_map.122 = bf16[4,8,768]{2,1,0:T(8,128)(2,1)} custom-call(bf16[64,1152]{1,0:T(8,128)(2,1)S(1)} %shard_map.120.own_ref, bf16[64,1152]{1,0:T(8,128)(2,1)S(1)} %collective-permute-done.14.other_ref, f32[32,768]{1,0:T(8,128)S(1)} %get-tuple-element.30.refs_0_, bf16[768,768]{1,0:T(8,128)(2,1)S(1)} %copy-done.2), custom_call_target="tpu_custom_call" | custom-call | flops 1000000 | bytes 1000000 | tf_op jit(solution)/shard_map/pallas_call | solution.py:285
  (17 shorter events, 0.1 us)
Async XLA Ops:
  0.6 21.9 %copy-start.6 = (f32[12]{0:T(128)S(1)}, f32[12]{0:T(128)}, u32[]{:S(2)}) copy-start(f32[12]{0:T(128)} %factor_ref.1) | copy-start | bytes 148
  0.6 8.8 %collective-permute-start = (bf16[4,8,768]{2,1,0:T(8,128)(2,1)}, bf16[4,8,768]{2,1,0:T(8,128)(2,1)S(1)}, u32[]{:S(2)}, u32[]{:S(2)}) collective-permute-start(bf16[4,8,768]{2,1,0:T(8,128)(2,1)} %param.12), channel_id=1, source_target_pairs={{0,4},{1,5},{2,6},{3,7},{4,8},{5,9},{6,10},{7,11},{8,12},{9,13},{1... | collective-permute-start | bytes 147464 | tf_op jit(solution)/shard_map/ppermute | solution.py:313
  3.7 8.6 %collective-permute-start.1 = (bf16[4,8,768]{2,1,0:T(8,128)(2,1)}, bf16[4,8,768]{2,1,0:T(8,128)(2,1)S(1)}, u32[]{:S(2)}, u32[]{:S(2)}) collective-permute-start(bf16[4,8,768]{2,1,0:T(8,128)(2,1)} %param.12), channel_id=1, source_target_pairs={{0,8},{1,9},{2,10},{3,11},{4,12},{5,13},{6,14},{7,15},{8,0},{9,1},... | collective-permute-start | bytes 147464 | tf_op jit(solution)/shard_map/ppermute | solution.py:313
  6.3 6.0 %collective-permute-start.2 = (bf16[4,8,768]{2,1,0:T(8,128)(2,1)}, bf16[4,8,768]{2,1,0:T(8,128)(2,1)S(1)}, u32[]{:S(2)}, u32[]{:S(2)}) collective-permute-start(bf16[4,8,768]{2,1,0:T(8,128)(2,1)} %param.12), channel_id=1, source_target_pairs={{0,12},{1,13},{2,14},{3,15},{4,0},{5,1},{6,2},{7,3},{8,4},{9,5},{1... | collective-permute-start | bytes 147464 | tf_op jit(solution)/shard_map/ppermute | solution.py:313
  7.7 7.1 %collective-permute-start.7 = (bf16[4,8,768]{2,1,0:T(8,128)(2,1)}, bf16[4,8,768]{2,1,0:T(8,128)(2,1)S(1)}, u32[]{:S(2)}, u32[]{:S(2)}) collective-permute-start(bf16[4,8,768]{2,1,0:T(8,128)(2,1)} %param.13), channel_id=1, source_target_pairs={{0,4},{1,5},{2,6},{3,7},{4,8},{5,9},{6,10},{7,11},{8,12},{9,13},{1... | collective-permute-start | bytes 147464 | tf_op jit(solution)/shard_map/ppermute | solution.py:313
  8.3 7.3 %collective-permute-start.8 = (bf16[4,8,768]{2,1,0:T(8,128)(2,1)}, bf16[4,8,768]{2,1,0:T(8,128)(2,1)S(1)}, u32[]{:S(2)}, u32[]{:S(2)}) collective-permute-start(bf16[4,8,768]{2,1,0:T(8,128)(2,1)} %param.13), channel_id=1, source_target_pairs={{0,8},{1,9},{2,10},{3,11},{4,12},{5,13},{6,14},{7,15},{8,0},{9,1},... | collective-permute-start | bytes 147464 | tf_op jit(solution)/shard_map/ppermute | solution.py:313
  9.5 8.6 %collective-permute-start.9 = (bf16[4,8,768]{2,1,0:T(8,128)(2,1)}, bf16[4,8,768]{2,1,0:T(8,128)(2,1)S(1)}, u32[]{:S(2)}, u32[]{:S(2)}) collective-permute-start(bf16[4,8,768]{2,1,0:T(8,128)(2,1)} %param.13), channel_id=1, source_target_pairs={{0,12},{1,13},{2,14},{3,15},{4,0},{5,1},{6,2},{7,3},{8,4},{9,5},{1... | collective-permute-start | bytes 147464 | tf_op jit(solution)/shard_map/ppermute | solution.py:313
  12.3 5.7 %collective-permute-start.4 = (bf16[4,32,768]{2,1,0:T(8,128)(2,1)S(1)}, bf16[4,32,768]{2,1,0:T(8,128)(2,1)S(1)}, u32[]{:S(2)}, u32[]{:S(2)}) collective-permute-start(bf16[4,32,768]{2,1,0:T(8,128)(2,1)S(1)} %constant_dynamic-update-slice_fusion.refs_1_), channel_id=1, source_target_pairs={{0,2},{1,3},{2,0},{3,1},{4,6},{5,7},{6,4},{7,5},{8,10},{9,11},{10,... | collective-permute-start | bytes 589832 | tf_op jit(solution)/shard_map/ppermute | solution.py:313
  13.9 6.0 %collective-permute-start.3 = (bf16[4,32,768]{2,1,0:T(8,128)(2,1)S(1)}, bf16[4,32,768]{2,1,0:T(8,128)(2,1)S(1)}, u32[]{:S(2)}, u32[]{:S(2)}) collective-permute-start(bf16[4,32,768]{2,1,0:T(8,128)(2,1)S(1)} %constant_dynamic-update-slice_fusion.refs_1_), channel_id=1, source_target_pairs={{0,1},{1,0},{2,3},{3,2},{4,5},{5,4},{6,7},{7,6},{8,9},{9,8},{10,11... | collective-permute-start | bytes 589832 | tf_op jit(solution)/shard_map/ppermute | solution.py:313
  13.9 0.8 %copy-start.3 = (bf16[4,8,768]{2,1,0:T(8,128)(2,1)S(1)}, bf16[4,8,768]{2,1,0:T(8,128)(2,1)}, u32[]{:S(2)}) copy-start(bf16[4,8,768]{2,1,0:T(8,128)(2,1)} %q_hbm) | copy-start | bytes 147460
  15.6 14.5 %copy-start.1 = (bf16[768,768]{1,0:T(8,128)(2,1)S(1)}, bf16[768,768]{1,0:T(8,128)(2,1)}, u32[]{:S(2)}) copy-start(bf16[768,768]{1,0:T(8,128)(2,1)} %refs_5_.1) | copy-start | bytes 3538948
  15.6 14.5 %copy-start.5 = (f32[768]{0:T(1024)S(1)}, f32[768]{0:T(1024)}, u32[]{:S(2)}) copy-start(f32[768]{0:T(1024)} %refs_7_.1) | copy-start | bytes 9220
  18.1 1.8 %collective-permute-start.5 = (bf16[4,32,768]{2,1,0:T(8,128)(2,1)S(1)}, bf16[4,32,768]{2,1,0:T(8,128)(2,1)S(1)}, u32[]{:S(2)}, u32[]{:S(2)}) collective-permute-start(bf16[4,32,768]{2,1,0:T(8,128)(2,1)S(1)} %collective-permute-done.4.refs_2_), channel_id=1, source_target_pairs={{0,1},{1,0},{2,3},{3,2},{4,5},{5,4},{6,7},{7,6},{8,9},{9,8},{10,11... | collective-permute-start | bytes 589832 | tf_op jit(solution)/shard_map/ppermute | solution.py:313
  18.1 7.5 %collective-permute-start.10 = (bf16[4,32,768]{2,1,0:T(8,128)(2,1)S(1)}, bf16[4,32,768]{2,1,0:T(8,128)(2,1)}, u32[]{:S(2)}, u32[]{:S(2)}) collective-permute-start(bf16[4,32,768]{2,1,0:T(8,128)(2,1)S(1)} %constant_dynamic-update-slice_fusion.4.refs_1_), channel_id=1, source_target_pairs={{0,2},{1,3},{2,0},{3,1},{4,6},{5,7},{6,4},{7,5},{8,10},{9,11},{10,... | collective-permute-start | bytes 589832 | tf_op jit(solution)/shard_map/ppermute | solution.py:313
  20.2 4.2 %collective-permute-start.6 = (f32[96,128]{1,0:T(8,128)S(1)}, f32[96,128]{1,0:T(8,128)S(1)}, u32[]{:S(2)}, u32[]{:S(2)}) collective-permute-start(f32[96,128]{1,0:T(8,128)S(1)} %shard_map.115.refs_0_), channel_id=1, source_target_pairs={{0,16},{16,0},{1,17},{17,1},{2,18},{18,2},{3,19},{19,3},{4,20},{20... | collective-permute-start | bytes 147464 | tf_op jit(solution)/shard_map/ppermute | solution.py:400
  22.5 7.6 %collective-permute-start.11 = (bf16[4,32,768]{2,1,0:T(8,128)(2,1)S(1)}, bf16[4,32,768]{2,1,0:T(8,128)(2,1)}, u32[]{:S(2)}, u32[]{:S(2)}) collective-permute-start(bf16[4,32,768]{2,1,0:T(8,128)(2,1)S(1)} %constant_dynamic-update-slice_fusion.4.refs_1_), channel_id=1, source_target_pairs={{0,1},{1,0},{2,3},{3,2},{4,5},{5,4},{6,7},{7,6},{8,9},{9,8},{10,11... | collective-permute-start | bytes 589832 | tf_op jit(solution)/shard_map/ppermute | solution.py:313
  25.5 11.4 %copy-start = (bf16[768,1152]{1,0:T(8,128)(2,1)S(1)}, bf16[768,1152]{1,0:T(8,128)(2,1)}, u32[]{:S(2)}) copy-start(bf16[768,1152]{1,0:T(8,128)(2,1)} %refs_2_) | copy-start | bytes 5308420
  25.6 4.5 %collective-permute-start.12 = (bf16[4,32,768]{2,1,0:T(8,128)(2,1)}, bf16[4,32,768]{2,1,0:T(8,128)(2,1)}, u32[]{:S(2)}, u32[]{:S(2)}) collective-permute-start(bf16[4,32,768]{2,1,0:T(8,128)(2,1)} %collective-permute-done.10.refs_2_), channel_id=1, source_target_pairs={{0,1},{1,0},{2,3},{3,2},{4,5},{5,4},{6,7},{7,6},{8,9},{9,8},{10,11... | collective-permute-start | bytes 589832 | tf_op jit(solution)/shard_map/ppermute | solution.py:313
  25.6 13.5 %all-to-all-start = ((f32[16,24,128]{2,1,0:T(8,128)}), f32[16,24,128]{2,1,0:T(8,128)S(1)}, u32[]{:S(2)}, u32[]{:S(2)}) async-start(f32[16,24,128]{2,1,0:T(8,128)} %shard_map.118), calls=%async_computation | async-start | bytes 393216 | tf_op jit(solution)/shard_map/all_to_all | solution.py:435
  30.1 0.8 %copy-start.4 = (bf16[4,8,768]{2,1,0:T(8,128)(2,1)S(1)}, bf16[4,8,768]{2,1,0:T(8,128)(2,1)}, u32[]{:S(2)}) copy-start(bf16[4,8,768]{2,1,0:T(8,128)(2,1)} %refs_6_.1) | copy-start | bytes 147460
  32.7 10.0 %copy-start.2 = (bf16[768,768]{1,0:T(8,128)(2,1)S(1)}, bf16[768,768]{1,0:T(8,128)(2,1)}, u32[]{:S(2)}) copy-start(bf16[768,768]{1,0:T(8,128)(2,1)} %refs_1_) | copy-start | bytes 3538948
  32.7 4.2 %collective-permute-start.13 = (bf16[32,768]{1,0:T(8,128)(2,1)S(1)}, bf16[32,768]{1,0:T(8,128)(2,1)S(1)}, u32[]{:S(2)}, u32[]{:S(2)}) collective-permute-start(bf16[32,768]{1,0:T(8,128)(2,1)S(1)} %get-tuple-element.25.refs_0_), channel_id=1, source_target_pairs={{0,16},{16,0},{1,17},{17,1},{2,18},{18,2},{3,19},{19,3},{4,20},{20... | collective-permute-start | bytes 147464 | tf_op jit(solution)/shard_map/ppermute | solution.py:443
  37.3 5.4 %collective-permute-start.14 = (bf16[64,1152]{1,0:T(8,128)(2,1)S(1)}, bf16[64,1152]{1,0:T(8,128)(2,1)S(1)}, u32[]{:S(2)}, u32[]{:S(2)}) collective-permute-start(bf16[64,1152]{1,0:T(8,128)(2,1)S(1)} %shard_map.120.own_ref), channel_id=1, source_target_pairs={{0,16},{16,0},{1,17},{17,1},{2,18},{18,2},{3,19},{19,3},{4,20},{20... | collective-permute-start | bytes 442376 | tf_op jit(solution)/shard_map/ppermute | solution.py:456

commit v10 on v9

--- a/solution.py
+++ b/solution.py
@@ -463,7 +463,7 @@
         jax.ShapeDtypeStruct((rows, sites, embed), BF16),
         [
             *column_inputs,
-            after(hidden, pairing_chances),
+            hidden,
             after(upright_closing_linear, projected),
         ],
         scratch=[

time: 44.6 us -> 44.6 us (level)
  no operation moved by 1% of the time
where the time goes in v10:
time: 44.6 us; the launch traced here: 44.1 us
  starting transfers between devices  23.3 us (52%)
  waiting for transfers between devices  8.99 us (20%)
  Pallas kernels  7.05 us (16%)
  local copies, waits for them, and re-layouts  3.25 us (7%)
  between operations  1.48 us (3%)
    ppermute x12, starting transfers between devices, send_pos(): return lax.ppermute(array, 'pos', pairs)  14.1 us
    pallas_call x10, Pallas kernels, call(): pl.pallas_call(kernel, out_shape=out_shape, in_specs=specs, out_specs=jax...  7.05 us
    all_to_all x1, starting transfers between devices, per_device(): lax.all_to_all(pair_local, 'pos', split_axis=0, concat_axis=0, tiled=True)  4.51 us
    unnamed x20, local copies, waits for them, and re-layouts  3.24 us
    ppermute x1, waiting for transfers between devices, per_device(): normed_all = [normed, lax.ppermute(normed, 'seq', swap)]  2.6 us
    ppermute x1, waiting for transfers between devices, per_device(): lax.ppermute(projected, 'seq', swap)  2.54 us
    ppermute x12, waiting for transfers between devices, send_pos(): return lax.ppermute(array, 'pos', pairs)  2.53 us
    ppermute x1, starting transfers between devices, per_device(): partials = [partial, after(lax.ppermute(partial, 'seq', swap), order)]  1.56 us
  transfers between devices with their start and end apart: 16, of which 6 were waited for; matrix products, arithmetic and copies ran while one was open for 4% of the time, Pallas kernels for 13%

profile of v10, /device:TPU:0, one launch (start us, length us, event | category | flops | bytes accessed | tf_op | source)
XLA Modules:
  0.0 44.1 jit_solution(15349420125863379313)
XLA Ops:
  0.6 3.1 %collective-permute-start = (bf16[4,8,768]{2,1,0:T(8,128)(2,1)}, bf16[4,8,768]{2,1,0:T(8,128)(2,1)S(1)}, u32[]{:S(2)}, u32[]{:S(2)}) collective-permute-start(bf16[4,8,768]{2,1,0:T(8,128)(2,1)} %param.12), channel_id=1, source_target_pairs={{0,4},{1,5},{2,6},{3,7},{4,8},{5,9},{6,10},{7,11},{8,12},{9,13},{1... | collective-permute-start | bytes 147464 | tf_op jit(solution)/shard_map/ppermute | solution.py:313
  3.7 2.6 %collective-permute-start.1 = (bf16[4,8,768]{2,1,0:T(8,128)(2,1)}, bf16[4,8,768]{2,1,0:T(8,128)(2,1)S(1)}, u32[]{:S(2)}, u32[]{:S(2)}) collective-permute-start(bf16[4,8,768]{2,1,0:T(8,128)(2,1)} %param.12), channel_id=1, source_target_pairs={{0,8},{1,9},{2,10},{3,11},{4,12},{5,13},{6,14},{7,15},{8,0},{9,1},... | collective-permute-start | bytes 147464 | tf_op jit(solution)/shard_map/ppermute | solution.py:313
  6.3 1.3 %collective-permute-start.2 = (bf16[4,8,768]{2,1,0:T(8,128)(2,1)}, bf16[4,8,768]{2,1,0:T(8,128)(2,1)S(1)}, u32[]{:S(2)}, u32[]{:S(2)}) collective-permute-start(bf16[4,8,768]{2,1,0:T(8,128)(2,1)} %param.12), channel_id=1, source_target_pairs={{0,12},{1,13},{2,14},{3,15},{4,0},{5,1},{6,2},{7,3},{8,4},{9,5},{1... | collective-permute-start | bytes 147464 | tf_op jit(solution)/shard_map/ppermute | solution.py:313
  7.7 0.7 %collective-permute-start.7 = (bf16[4,8,768]{2,1,0:T(8,128)(2,1)}, bf16[4,8,768]{2,1,0:T(8,128)(2,1)S(1)}, u32[]{:S(2)}, u32[]{:S(2)}) collective-permute-start(bf16[4,8,768]{2,1,0:T(8,128)(2,1)} %param.13), channel_id=1, source_target_pairs={{0,4},{1,5},{2,6},{3,7},{4,8},{5,9},{6,10},{7,11},{8,12},{9,13},{1... | collective-permute-start | bytes 147464 | tf_op jit(solution)/shard_map/ppermute | solution.py:313
  8.3 0.3 collective-permute-start.8
  8.7 0.8 %constant_dynamic-update-slice_fusion.3 = bf16[4,32,768]{2,1,0:T(8,128)(2,1)S(1)} fusion(bf16[4,8,768]{2,1,0:T(8,128)(2,1)} %param.12), kind=kLoop, calls=%fused_computation.3 | loop fusion | bytes 98304
  9.5 0.0 collective-permute-done
  9.5 2.8 %collective-permute-start.9 = (bf16[4,8,768]{2,1,0:T(8,128)(2,1)}, bf16[4,8,768]{2,1,0:T(8,128)(2,1)S(1)}, u32[]{:S(2)}, u32[]{:S(2)}) collective-permute-start(bf16[4,8,768]{2,1,0:T(8,128)(2,1)} %param.13), channel_id=1, source_target_pairs={{0,12},{1,13},{2,14},{3,15},{4,0},{5,1},{6,2},{7,3},{8,4},{9,5},{1... | collective-permute-start | bytes 147464 | tf_op jit(solution)/shard_map/ppermute | solution.py:313
  12.3 0.0 collective-permute-done.1
  12.3 0.0 collective-permute-done.2
  12.3 1.6 %collective-permute-start.4 = (bf16[4,32,768]{2,1,0:T(8,128)(2,1)S(1)}, bf16[4,32,768]{2,1,0:T(8,128)(2,1)S(1)}, u32[]{:S(2)}, u32[]{:S(2)}) collective-permute-start(bf16[4,32,768]{2,1,0:T(8,128)(2,1)S(1)} %constant_dynamic-update-slice_fusion.refs_1_), channel_id=1, source_target_pairs={{0,2},{1,3},{2,0},{3,1},{4,6},{5,7},{6,4},{7,5},{8,10},{9,11},{10,... | collective-permute-start | bytes 589832 | tf_op jit(solution)/shard_map/ppermute | solution.py:313
  13.9 0.0 collective-permute-start.3
  13.9 0.8 %copy-done.3 = bf16[4,8,768]{2,1,0:T(8,128)(2,1)S(1)} copy-done((bf16[4,8,768]{2,1,0:T(8,128)(2,1)S(1)}, bf16[4,8,768]{2,1,0:T(8,128)(2,1)}, u32[]{:S(2)}) %copy-start.3) | copy-done | bytes 49176
  14.7 0.1 shard_map.113.refs_0_
  14.8 0.0 collective-permute-done.7
  14.8 0.8 %constant_dynamic-update-slice_fusion.7 = bf16[4,32,768]{2,1,0:T(8,128)(2,1)S(1)} fusion(bf16[4,8,768]{2,1,0:T(8,128)(2,1)} %param.13), kind=kLoop, calls=%fused_computation.7 | loop fusion | bytes 98304
  15.6 0.0 copy-start.5
  15.7 2.4 %collective-permute-done.4.refs_2_ = bf16[4,32,768]{2,1,0:T(8,128)(2,1)S(1)} collective-permute-done((bf16[4,32,768]{2,1,0:T(8,128)(2,1)S(1)}, bf16[4,32,768]{2,1,0:T(8,128)(2,1)S(1)}, u32[]{:S(2)}, u32[]{:S(2)}) %collective-permute-start.4) | collective-permute-done | bytes 196640 | tf_op jit(solution)/shard_map/ppermute | solution.py:313
  18.1 0.0 collective-permute-start.5
  18.1 0.0 collective-permute-done.9
  18.1 1.6 %collective-permute-start.10 = (bf16[4,32,768]{2,1,0:T(8,128)(2,1)S(1)}, bf16[4,32,768]{2,1,0:T(8,128)(2,1)}, u32[]{:S(2)}, u32[]{:S(2)}) collective-permute-start(bf16[4,32,768]{2,1,0:T(8,128)(2,1)S(1)} %constant_dynamic-update-slice_fusion.4.refs_1_), channel_id=1, source_target_pairs={{0,2},{1,3},{2,0},{3,1},{4,6},{5,7},{6,4},{7,5},{8,10},{9,11},{10,... | collective-permute-start | bytes 589832 | tf_op jit(solution)/shard_map/ppermute | solution.py:313
  19.7 0.2 shard_map.114.refs_3_
  19.9 0.0 collective-permute-done.5.refs_2_
  19.9 0.3 shard_map.115.refs_0_
  20.2 1.6 %collective-permute-start.6 = (f32[96,128]{1,0:T(8,128)S(1)}, f32[96,128]{1,0:T(8,128)S(1)}, u32[]{:S(2)}, u32[]{:S(2)}) collective-permute-start(f32[96,128]{1,0:T(8,128)S(1)} %shard_map.115.refs_0_), channel_id=1, source_target_pairs={{0,16},{16,0},{1,17},{17,1},{2,18},{18,2},{3,19},{19,3},{4,20},{20... | collective-permute-start | bytes 147464 | tf_op jit(solution)/shard_map/ppermute | solution.py:400
  21.7 0.1 pad_add_fusion.scalar_ref
  22.5 0.1 collective-permute-start.11
  22.6 0.7 %shard_map.116 = (f32[24,128]{1,0:T(8,128)S(1)}, f32[128,128]{1,0:T(8,128)S(1)}, f32[8,128]{1,0:T(8,128)S(1)}, f32[128,64]{1,0:T(8,128)S(1)}) custom-call(s32[2]{0:T(128)S(1)} %pad_add_fusion.scalar_ref, f32[12]{0:T(128)S(1)} %copy-done.6, f32[1]{0:T(128)S(6)} %copy.18.offset_ref), custom_call_target="tpu_custom_call" | custom-call | flops 1000000 | bytes 1000000 | tf_op jit(solution)/shard_map/pallas_call | solution.py:285
  23.3 1.1 %collective-permute-done.6.refs_1_ = f32[96,128]{1,0:T(8,128)S(1)} collective-permute-done((f32[96,128]{1,0:T(8,128)S(1)}, f32[96,128]{1,0:T(8,128)S(1)}, u32[]{:S(2)}, u32[]{:S(2)}) %collective-permute-start.6) | collective-permute-done | bytes 49184 | tf_op jit(solution)/shard_map/ppermute | solution.py:400
  24.4 0.2 shard_map.117.w_ref.refs_0_
  24.5 0.9 %shard_map.118 = f32[16,24,128]{2,1,0:T(8,128)} custom-call(bf16[96,128]{1,0:T(8,128)(2,1)S(1)} %shard_map.117.w_ref.refs_0_, f32[24,128]{1,0:T(8,128)S(1)} %get-tuple-element.22.head_ref.factor_ref, f32[128,128]{1,0:T(8,128)S(1)} %get-tuple-element.18.order_ref), custom_call_target="tpu_custom_call" | custom-call | flops 1000000 | bytes 1000000 | tf_op jit(solution)/shard_map/pallas_call | solution.py:285
  25.5 0.1 collective-permute-done.10.refs_2_
  25.6 0.0 collective-permute-start.12
  25.6 4.5 %all-to-all-start = ((f32[16,24,128]{2,1,0:T(8,128)}), f32[16,24,128]{2,1,0:T(8,128)S(1)}, u32[]{:S(2)}, u32[]{:S(2)}) async-start(f32[16,24,128]{2,1,0:T(8,128)} %shard_map.118), calls=%async_computation | async-start | bytes 393216 | tf_op jit(solution)/shard_map/all_to_all | solution.py:435
  30.1 0.0 collective-permute-done.11.refs_3_
  30.1 0.0 collective-permute-done.12.refs_4_
  30.1 0.0 copy-start.4
  30.1 0.8 %copy-done.4 = bf16[4,8,768]{2,1,0:T(8,128)(2,1)S(1)} copy-done((bf16[4,8,768]{2,1,0:T(8,128)(2,1)S(1)}, bf16[4,8,768]{2,1,0:T(8,128)(2,1)}, u32[]{:S(2)}) %copy-start.4) | copy-done | bytes 49176
  30.9 1.7 %shard_map.119 = (f32[32,768]{1,0:T(8,128)S(1)}, bf16[32,768]{1,0:T(8,128)(2,1)S(1)}) custom-call(bf16[96,128]{1,0:T(8,128)(2,1)S(1)} %shard_map.117.w_ref.refs_0_, bf16[4,32,768]{2,1,0:T(8,128)(2,1)S(1)} %constant_dynamic-update-slice_fusion.4.refs_1_, bf16[4,32,768]{2,1,0:T(8,128)(2,1)} %collective-permute-done.10.refs_2_, ...), custom_call_target="tpu_custom_call" | custom-call | flops 1000000 | bytes 1000000 | tf_op jit(solution)/shard_map/pallas_call | solution.py:285
  32.7 0.0 copy-start.2
  32.7 1.6 %collective-permute-start.13 = (bf16[32,768]{1,0:T(8,128)(2,1)S(1)}, bf16[32,768]{1,0:T(8,128)(2,1)S(1)}, u32[]{:S(2)}, u32[]{:S(2)}) collective-permute-start(bf16[32,768]{1,0:T(8,128)(2,1)S(1)} %get-tuple-element.24.refs_0_), channel_id=1, source_target_pairs={{0,16},{16,0},{1,17},{17,1},{2,18},{18,2},{3,19},{19,3},{4,20},{20... | collective-permute-start | bytes 147464 | tf_op jit(solution)/shard_map/ppermute | solution.py:443
  34.2 2.6 %collective-permute-done.13.refs_1_ = bf16[32,768]{1,0:T(8,128)(2,1)S(1)} collective-permute-done((bf16[32,768]{1,0:T(8,128)(2,1)S(1)}, bf16[32,768]{1,0:T(8,128)(2,1)S(1)}, u32[]{:S(2)}, u32[]{:S(2)}) %collective-permute-start.13) | collective-permute-done | bytes 49184 | tf_op jit(solution)/shard_map/ppermute | solution.py:443
  36.8 0.4 shard_map.120.own_ref
  37.3 1.6 %collective-permute-start.14 = (bf16[64,1152]{1,0:T(8,128)(2,1)S(1)}, bf16[64,1152]{1,0:T(8,128)(2,1)S(1)}, u32[]{:S(2)}, u32[]{:S(2)}) collective-permute-start(bf16[64,1152]{1,0:T(8,128)(2,1)S(1)} %shard_map.120.own_ref), channel_id=1, source_target_pairs={{0,16},{16,0},{1,17},{17,1},{2,18},{18,2},{3,19},{19,3},{4,20},{20... | collective-permute-start | bytes 442376 | tf_op jit(solution)/shard_map/ppermute | solution.py:456
  38.8 0.2 all-to-all-done.pair_ref
  39.1 1.1 %shard_map.122 = f32[8,64]{1,0:T(8,128)} custom-call(f32[16,24,128]{2,1,0:T(8,128)S(1)} %all-to-all-done.pair_ref, f32[24,128]{1,0:T(8,128)S(1)} %get-tuple-element.22.head_ref.factor_ref, f32[8,128]{1,0:T(8,128)S(1)} %get-tuple-element.28.own_ref, f32[128,64]{1,0:T(8,128)S(1)} %get-tuple-element.29.slab_ref), custom_call_target="tpu_custom_call" | custom-call | flops 1000000 | bytes 1000000 | tf_op jit(solution)/shard_map/pallas_call | solution.py:285
  40.1 2.5 %collective-permute-done.14.other_ref = bf16[64,1152]{1,0:T(8,128)(2,1)S(1)} collective-permute-done((bf16[64,1152]{1,0:T(8,128)(2,1)S(1)}, bf16[64,1152]{1,0:T(8,128)(2,1)S(1)}, u32[]{:S(2)}, u32[]{:S(2)}) %collective-permute-start.14) | collective-permute-done | bytes 147488 | tf_op jit(solution)/shard_map/ppermute | solution.py:456
  42.7 1.5 %shard_map.121 = bf16[4,8,768]{2,1,0:T(8,128)(2,1)} custom-call(bf16[64,1152]{1,0:T(8,128)(2,1)S(1)} %shard_map.120.own_ref, bf16[64,1152]{1,0:T(8,128)(2,1)S(1)} %collective-permute-done.14.other_ref, f32[32,768]{1,0:T(8,128)S(1)} %get-tuple-element.26.refs_0_, bf16[768,768]{1,0:T(8,128)(2,1)S(1)} %copy-done.2), custom_call_target="tpu_custom_call" | custom-call | flops 1000000 | bytes 1000000 | tf_op jit(solution)/shard_map/pallas_call | solution.py:285
  (17 shorter events, 0.1 us)
Async XLA Ops:
  0.6 21.9 %copy-start.6 = (f32[12]{0:T(128)S(1)}, f32[12]{0:T(128)}, u32[]{:S(2)}) copy-start(f32[12]{0:T(128)} %factor_ref.1) | copy-start | bytes 148
  0.6 8.8 %collective-permute-start = (bf16[4,8,768]{2,1,0:T(8,128)(2,1)}, bf16[4,8,768]{2,1,0:T(8,128)(2,1)S(1)}, u32[]{:S(2)}, u32[]{:S(2)}) collective-permute-start(bf16[4,8,768]{2,1,0:T(8,128)(2,1)} %param.12), channel_id=1, source_target_pairs={{0,4},{1,5},{2,6},{3,7},{4,8},{5,9},{6,10},{7,11},{8,12},{9,13},{1... | collective-permute-start | bytes 147464 | tf_op jit(solution)/shard_map/ppermute | solution.py:313
  3.7 8.6 %collective-permute-start.1 = (bf16[4,8,768]{2,1,0:T(8,128)(2,1)}, bf16[4,8,768]{2,1,0:T(8,128)(2,1)S(1)}, u32[]{:S(2)}, u32[]{:S(2)}) collective-permute-start(bf16[4,8,768]{2,1,0:T(8,128)(2,1)} %param.12), channel_id=1, source_target_pairs={{0,8},{1,9},{2,10},{3,11},{4,12},{5,13},{6,14},{7,15},{8,0},{9,1},... | collective-permute-start | bytes 147464 | tf_op jit(solution)/shard_map/ppermute | solution.py:313
  6.3 6.0 %collective-permute-start.2 = (bf16[4,8,768]{2,1,0:T(8,128)(2,1)}, bf16[4,8,768]{2,1,0:T(8,128)(2,1)S(1)}, u32[]{:S(2)}, u32[]{:S(2)}) collective-permute-start(bf16[4,8,768]{2,1,0:T(8,128)(2,1)} %param.12), channel_id=1, source_target_pairs={{0,12},{1,13},{2,14},{3,15},{4,0},{5,1},{6,2},{7,3},{8,4},{9,5},{1... | collective-permute-start | bytes 147464 | tf_op jit(solution)/shard_map/ppermute | solution.py:313
  7.7 7.1 %collective-permute-start.7 = (bf16[4,8,768]{2,1,0:T(8,128)(2,1)}, bf16[4,8,768]{2,1,0:T(8,128)(2,1)S(1)}, u32[]{:S(2)}, u32[]{:S(2)}) collective-permute-start(bf16[4,8,768]{2,1,0:T(8,128)(2,1)} %param.13), channel_id=1, source_target_pairs={{0,4},{1,5},{2,6},{3,7},{4,8},{5,9},{6,10},{7,11},{8,12},{9,13},{1... | collective-permute-start | bytes 147464 | tf_op jit(solution)/shard_map/ppermute | solution.py:313
  8.3 7.3 %collective-permute-start.8 = (bf16[4,8,768]{2,1,0:T(8,128)(2,1)}, bf16[4,8,768]{2,1,0:T(8,128)(2,1)S(1)}, u32[]{:S(2)}, u32[]{:S(2)}) collective-permute-start(bf16[4,8,768]{2,1,0:T(8,128)(2,1)} %param.13), channel_id=1, source_target_pairs={{0,8},{1,9},{2,10},{3,11},{4,12},{5,13},{6,14},{7,15},{8,0},{9,1},... | collective-permute-start | bytes 147464 | tf_op jit(solution)/shard_map/ppermute | solution.py:313
  9.5 8.6 %collective-permute-start.9 = (bf16[4,8,768]{2,1,0:T(8,128)(2,1)}, bf16[4,8,768]{2,1,0:T(8,128)(2,1)S(1)}, u32[]{:S(2)}, u32[]{:S(2)}) collective-permute-start(bf16[4,8,768]{2,1,0:T(8,128)(2,1)} %param.13), channel_id=1, source_target_pairs={{0,12},{1,13},{2,14},{3,15},{4,0},{5,1},{6,2},{7,3},{8,4},{9,5},{1... | collective-permute-start | bytes 147464 | tf_op jit(solution)/shard_map/ppermute | solution.py:313
  12.3 5.7 %collective-permute-start.4 = (bf16[4,32,768]{2,1,0:T(8,128)(2,1)S(1)}, bf16[4,32,768]{2,1,0:T(8,128)(2,1)S(1)}, u32[]{:S(2)}, u32[]{:S(2)}) collective-permute-start(bf16[4,32,768]{2,1,0:T(8,128)(2,1)S(1)} %constant_dynamic-update-slice_fusion.refs_1_), channel_id=1, source_target_pairs={{0,2},{1,3},{2,0},{3,1},{4,6},{5,7},{6,4},{7,5},{8,10},{9,11},{10,... | collective-permute-start | bytes 589832 | tf_op jit(solution)/shard_map/ppermute | solution.py:313
  13.9 6.0 %collective-permute-start.3 = (bf16[4,32,768]{2,1,0:T(8,128)(2,1)S(1)}, bf16[4,32,768]{2,1,0:T(8,128)(2,1)S(1)}, u32[]{:S(2)}, u32[]{:S(2)}) collective-permute-start(bf16[4,32,768]{2,1,0:T(8,128)(2,1)S(1)} %constant_dynamic-update-slice_fusion.refs_1_), channel_id=1, source_target_pairs={{0,1},{1,0},{2,3},{3,2},{4,5},{5,4},{6,7},{7,6},{8,9},{9,8},{10,11... | collective-permute-start | bytes 589832 | tf_op jit(solution)/shard_map/ppermute | solution.py:313
  13.9 0.8 %copy-start.3 = (bf16[4,8,768]{2,1,0:T(8,128)(2,1)S(1)}, bf16[4,8,768]{2,1,0:T(8,128)(2,1)}, u32[]{:S(2)}) copy-start(bf16[4,8,768]{2,1,0:T(8,128)(2,1)} %q_hbm) | copy-start | bytes 147460
  15.6 14.5 %copy-start.1 = (bf16[768,768]{1,0:T(8,128)(2,1)S(1)}, bf16[768,768]{1,0:T(8,128)(2,1)}, u32[]{:S(2)}) copy-start(bf16[768,768]{1,0:T(8,128)(2,1)} %refs_5_.1) | copy-start | bytes 3538948
  15.6 14.5 %copy-start.5 = (f32[768]{0:T(1024)S(1)}, f32[768]{0:T(1024)}, u32[]{:S(2)}) copy-start(f32[768]{0:T(1024)} %refs_7_.1) | copy-start | bytes 9220
  18.1 1.8 %collective-permute-start.5 = (bf16[4,32,768]{2,1,0:T(8,128)(2,1)S(1)}, bf16[4,32,768]{2,1,0:T(8,128)(2,1)S(1)}, u32[]{:S(2)}, u32[]{:S(2)}) collective-permute-start(bf16[4,32,768]{2,1,0:T(8,128)(2,1)S(1)} %collective-permute-done.4.refs_2_), channel_id=1, source_target_pairs={{0,1},{1,0},{2,3},{3,2},{4,5},{5,4},{6,7},{7,6},{8,9},{9,8},{10,11... | collective-permute-start | bytes 589832 | tf_op jit(solution)/shard_map/ppermute | solution.py:313
  18.1 7.5 %collective-permute-start.10 = (bf16[4,32,768]{2,1,0:T(8,128)(2,1)S(1)}, bf16[4,32,768]{2,1,0:T(8,128)(2,1)}, u32[]{:S(2)}, u32[]{:S(2)}) collective-permute-start(bf16[4,32,768]{2,1,0:T(8,128)(2,1)S(1)} %constant_dynamic-update-slice_fusion.4.refs_1_), channel_id=1, source_target_pairs={{0,2},{1,3},{2,0},{3,1},{4,6},{5,7},{6,4},{7,5},{8,10},{9,11},{10,... | collective-permute-start | bytes 589832 | tf_op jit(solution)/shard_map/ppermute | solution.py:313
  20.2 4.2 %collective-permute-start.6 = (f32[96,128]{1,0:T(8,128)S(1)}, f32[96,128]{1,0:T(8,128)S(1)}, u32[]{:S(2)}, u32[]{:S(2)}) collective-permute-start(f32[96,128]{1,0:T(8,128)S(1)} %shard_map.115.refs_0_), channel_id=1, source_target_pairs={{0,16},{16,0},{1,17},{17,1},{2,18},{18,2},{3,19},{19,3},{4,20},{20... | collective-permute-start | bytes 147464 | tf_op jit(solution)/shard_map/ppermute | solution.py:400
  22.5 7.6 %collective-permute-start.11 = (bf16[4,32,768]{2,1,0:T(8,128)(2,1)S(1)}, bf16[4,32,768]{2,1,0:T(8,128)(2,1)}, u32[]{:S(2)}, u32[]{:S(2)}) collective-permute-start(bf16[4,32,768]{2,1,0:T(8,128)(2,1)S(1)} %constant_dynamic-update-slice_fusion.4.refs_1_), channel_id=1, source_target_pairs={{0,1},{1,0},{2,3},{3,2},{4,5},{5,4},{6,7},{7,6},{8,9},{9,8},{10,11... | collective-permute-start | bytes 589832 | tf_op jit(solution)/shard_map/ppermute | solution.py:313
  25.5 11.4 %copy-start = (bf16[768,1152]{1,0:T(8,128)(2,1)S(1)}, bf16[768,1152]{1,0:T(8,128)(2,1)}, u32[]{:S(2)}) copy-start(bf16[768,1152]{1,0:T(8,128)(2,1)} %refs_2_) | copy-start | bytes 5308420
  25.6 4.5 %collective-permute-start.12 = (bf16[4,32,768]{2,1,0:T(8,128)(2,1)}, bf16[4,32,768]{2,1,0:T(8,128)(2,1)}, u32[]{:S(2)}, u32[]{:S(2)}) collective-permute-start(bf16[4,32,768]{2,1,0:T(8,128)(2,1)} %collective-permute-done.10.refs_2_), channel_id=1, source_target_pairs={{0,1},{1,0},{2,3},{3,2},{4,5},{5,4},{6,7},{7,6},{8,9},{9,8},{10,11... | collective-permute-start | bytes 589832 | tf_op jit(solution)/shard_map/ppermute | solution.py:313
  25.6 13.5 %all-to-all-start = ((f32[16,24,128]{2,1,0:T(8,128)}), f32[16,24,128]{2,1,0:T(8,128)S(1)}, u32[]{:S(2)}, u32[]{:S(2)}) async-start(f32[16,24,128]{2,1,0:T(8,128)} %shard_map.118), calls=%async_computation | async-start | bytes 393216 | tf_op jit(solution)/shard_map/all_to_all | solution.py:435
  30.1 0.8 %copy-start.4 = (bf16[4,8,768]{2,1,0:T(8,128)(2,1)S(1)}, bf16[4,8,768]{2,1,0:T(8,128)(2,1)}, u32[]{:S(2)}) copy-start(bf16[4,8,768]{2,1,0:T(8,128)(2,1)} %refs_6_.1) | copy-start | bytes 147460
  32.7 10.0 %copy-start.2 = (bf16[768,768]{1,0:T(8,128)(2,1)S(1)}, bf16[768,768]{1,0:T(8,128)(2,1)}, u32[]{:S(2)}) copy-start(bf16[768,768]{1,0:T(8,128)(2,1)} %refs_1_) | copy-start | bytes 3538948
  32.7 4.2 %collective-permute-start.13 = (bf16[32,768]{1,0:T(8,128)(2,1)S(1)}, bf16[32,768]{1,0:T(8,128)(2,1)S(1)}, u32[]{:S(2)}, u32[]{:S(2)}) collective-permute-start(bf16[32,768]{1,0:T(8,128)(2,1)S(1)} %get-tuple-element.24.refs_0_), channel_id=1, source_target_pairs={{0,16},{16,0},{1,17},{17,1},{2,18},{18,2},{3,19},{19,3},{4,20},{20... | collective-permute-start | bytes 147464 | tf_op jit(solution)/shard_map/ppermute | solution.py:443
  37.3 5.4 %collective-permute-start.14 = (bf16[64,1152]{1,0:T(8,128)(2,1)S(1)}, bf16[64,1152]{1,0:T(8,128)(2,1)S(1)}, u32[]{:S(2)}, u32[]{:S(2)}) collective-permute-start(bf16[64,1152]{1,0:T(8,128)(2,1)S(1)} %shard_map.120.own_ref), channel_id=1, source_target_pairs={{0,16},{16,0},{1,17},{17,1},{2,18},{18,2},{3,19},{19,3},{4,20},{20... | collective-permute-start | bytes 442376 | tf_op jit(solution)/shard_map/ppermute | solution.py:456

commit v11 on v10

--- a/solution.py
+++ b/solution.py
@@ -433,12 +433,6 @@
         scratch=[pltpu.VMEM((cells, embed), F32)],
     )
     pair_all = lax.all_to_all(pair_local, "pos", split_axis=0, concat_axis=0, tiled=True)
-    pairing_chances = call(
-        functools.partial(contact_kernel, heads),
-        jax.ShapeDtypeStruct((sites, slab_width), F32),
-        [pair_all, head_factors, own_select, slab_select],
-        scratch=[pltpu.VMEM((head_rows + sites, length), F32)],
-    )
     if swapped:
         normed_all = [normed, lax.ppermute(normed, "seq", swap)]
         weight = after(upright_threefold_linear, normed)
@@ -471,6 +465,12 @@
             pltpu.VMEM((cells, embed), F32),
         ],
     )
+    pairing_chances = call(
+        functools.partial(contact_kernel, heads),
+        jax.ShapeDtypeStruct((sites, slab_width), F32),
+        [pair_all, after(head_factors, alignment_output), own_select, slab_select],
+        scratch=[pltpu.VMEM((head_rows + sites, length), F32)],
+    )
     return alignment_output, pairing_chances
 
 

time: 44.6 us -> 44.8 us (level)
  waiting for transfers between devices: 8.99 us -> 10 us
  local copies, waits for them, and re-layouts: 3.25 us -> 2.46 us
    ppermute x1, waiting for transfers between devices: 2.54 us -> 3.84 us  [per_device(): lax.ppermute(projected, 'seq', swap)]
    unnamed x20, local copies, waits for them, and re-layouts: 3.24 us -> 2.45 us
  transfers between devices with their start and end apart: 16 -> 16, of which waited for: 6 -> 5; matrix products, arithmetic and copies ran while one was open for 4% -> 4% of each run, Pallas kernels for 13% -> 14%
where the time goes in v11:
time: 44.8 us; the launch traced here: 44.4 us
  starting transfers between devices  23.3 us (52%)
  waiting for transfers between devices  10 us (22%)
  Pallas kernels  7.06 us (16%)
  local copies, waits for them, and re-layouts  2.46 us (5%)
  between operations  1.49 us (3%)
    ppermute x12, starting transfers between devices, send_pos(): return lax.ppermute(array, 'pos', pairs)  14.1 us
    pallas_call x10, Pallas kernels, call(): pl.pallas_call(kernel, out_shape=out_shape, in_specs=specs, out_specs=jax...  7.06 us
    all_to_all x1, starting transfers between devices, per_device(): lax.all_to_all(pair_local, 'pos', split_axis=0, concat_axis=0, tiled=True)  4.51 us
    ppermute x1, waiting for transfers between devices, per_device(): lax.ppermute(projected, 'seq', swap)  3.84 us
    ppermute x1, waiting for transfers between devices, per_device(): normed_all = [normed, lax.ppermute(normed, 'seq', swap)]  2.6 us
    ppermute x12, waiting for transfers between devices, send_pos(): return lax.ppermute(array, 'pos', pairs)  2.52 us
    unnamed x20, local copies, waits for them, and re-layouts  2.45 us
    ppermute x1, starting transfers between devices, per_device(): partials = [partial, after(lax.ppermute(partial, 'seq', swap), order)]  1.56 us
  transfers between devices with their start and end apart: 16, of which 5 were waited for; matrix products, arithmetic and copies ran while one was open for 4% of the time, Pallas kernels for 14%

profile of v11, /device:TPU:0, one launch (start us, length us, event | category | flops | bytes accessed | tf_op | source)
XLA Modules:
  0.0 44.4 jit_solution(8377987510710075434)
XLA Ops:
  0.6 3.1 %collective-permute-start = (bf16[4,8,768]{2,1,0:T(8,128)(2,1)}, bf16[4,8,768]{2,1,0:T(8,128)(2,1)S(1)}, u32[]{:S(2)}, u32[]{:S(2)}) collective-permute-start(bf16[4,8,768]{2,1,0:T(8,128)(2,1)} %param.12), channel_id=1, source_target_pairs={{0,4},{1,5},{2,6},{3,7},{4,8},{5,9},{6,10},{7,11},{8,12},{9,13},{1... | collective-permute-start | bytes 147464 | tf_op jit(solution)/shard_map/ppermute | solution.py:313
  3.7 2.6 %collective-permute-start.1 = (bf16[4,8,768]{2,1,0:T(8,128)(2,1)}, bf16[4,8,768]{2,1,0:T(8,128)(2,1)S(1)}, u32[]{:S(2)}, u32[]{:S(2)}) collective-permute-start(bf16[4,8,768]{2,1,0:T(8,128)(2,1)} %param.12), channel_id=1, source_target_pairs={{0,8},{1,9},{2,10},{3,11},{4,12},{5,13},{6,14},{7,15},{8,0},{9,1},... | collective-permute-start | bytes 147464 | tf_op jit(solution)/shard_map/ppermute | solution.py:313
  6.3 1.3 %collective-permute-start.2 = (bf16[4,8,768]{2,1,0:T(8,128)(2,1)}, bf16[4,8,768]{2,1,0:T(8,128)(2,1)S(1)}, u32[]{:S(2)}, u32[]{:S(2)}) collective-permute-start(bf16[4,8,768]{2,1,0:T(8,128)(2,1)} %param.12), channel_id=1, source_target_pairs={{0,12},{1,13},{2,14},{3,15},{4,0},{5,1},{6,2},{7,3},{8,4},{9,5},{1... | collective-permute-start | bytes 147464 | tf_op jit(solution)/shard_map/ppermute | solution.py:313
  7.7 0.7 %collective-permute-start.7 = (bf16[4,8,768]{2,1,0:T(8,128)(2,1)}, bf16[4,8,768]{2,1,0:T(8,128)(2,1)S(1)}, u32[]{:S(2)}, u32[]{:S(2)}) collective-permute-start(bf16[4,8,768]{2,1,0:T(8,128)(2,1)} %param.13), channel_id=1, source_target_pairs={{0,4},{1,5},{2,6},{3,7},{4,8},{5,9},{6,10},{7,11},{8,12},{9,13},{1... | collective-permute-start | bytes 147464 | tf_op jit(solution)/shard_map/ppermute | solution.py:313
  8.3 0.3 collective-permute-start.8
  8.7 0.8 %constant_dynamic-update-slice_fusion.3 = bf16[4,32,768]{2,1,0:T(8,128)(2,1)S(1)} fusion(bf16[4,8,768]{2,1,0:T(8,128)(2,1)} %param.12), kind=kLoop, calls=%fused_computation.3 | loop fusion | bytes 98304
  9.5 0.0 collective-permute-done
  9.5 2.8 %collective-permute-start.9 = (bf16[4,8,768]{2,1,0:T(8,128)(2,1)}, bf16[4,8,768]{2,1,0:T(8,128)(2,1)S(1)}, u32[]{:S(2)}, u32[]{:S(2)}) collective-permute-start(bf16[4,8,768]{2,1,0:T(8,128)(2,1)} %param.13), channel_id=1, source_target_pairs={{0,12},{1,13},{2,14},{3,15},{4,0},{5,1},{6,2},{7,3},{8,4},{9,5},{1... | collective-permute-start | bytes 147464 | tf_op jit(solution)/shard_map/ppermute | solution.py:313
  12.3 0.0 collective-permute-done.1
  12.3 0.0 collective-permute-done.2
  12.3 1.6 %collective-permute-start.4 = (bf16[4,32,768]{2,1,0:T(8,128)(2,1)S(1)}, bf16[4,32,768]{2,1,0:T(8,128)(2,1)S(1)}, u32[]{:S(2)}, u32[]{:S(2)}) collective-permute-start(bf16[4,32,768]{2,1,0:T(8,128)(2,1)S(1)} %constant_dynamic-update-slice_fusion.refs_1_), channel_id=1, source_target_pairs={{0,2},{1,3},{2,0},{3,1},{4,6},{5,7},{6,4},{7,5},{8,10},{9,11},{10,... | collective-permute-start | bytes 589832 | tf_op jit(solution)/shard_map/ppermute | solution.py:313
  13.9 0.0 collective-permute-start.3
  13.9 0.8 %copy-done.3 = bf16[4,8,768]{2,1,0:T(8,128)(2,1)S(1)} copy-done((bf16[4,8,768]{2,1,0:T(8,128)(2,1)S(1)}, bf16[4,8,768]{2,1,0:T(8,128)(2,1)}, u32[]{:S(2)}) %copy-start.3) | copy-done | bytes 49176
  14.7 0.1 shard_map.113.refs_0_
  14.8 0.0 collective-permute-done.7
  14.8 0.8 %constant_dynamic-update-slice_fusion.7 = bf16[4,32,768]{2,1,0:T(8,128)(2,1)S(1)} fusion(bf16[4,8,768]{2,1,0:T(8,128)(2,1)} %param.13), kind=kLoop, calls=%fused_computation.7 | loop fusion | bytes 98304
  15.6 0.0 copy-start.4
  15.6 0.0 copy-start.5
  15.6 0.0 collective-permute-done.8
  15.7 2.4 %collective-permute-done.4.refs_2_ = bf16[4,32,768]{2,1,0:T(8,128)(2,1)S(1)} collective-permute-done((bf16[4,32,768]{2,1,0:T(8,128)(2,1)S(1)}, bf16[4,32,768]{2,1,0:T(8,128)(2,1)S(1)}, u32[]{:S(2)}, u32[]{:S(2)}) %collective-permute-start.4) | collective-permute-done | bytes 196640 | tf_op jit(solution)/shard_map/ppermute | solution.py:313
  18.1 0.0 collective-permute-start.5
  18.1 0.0 collective-permute-done.9
  18.1 1.6 %collective-permute-start.10 = (bf16[4,32,768]{2,1,0:T(8,128)(2,1)S(1)}, bf16[4,32,768]{2,1,0:T(8,128)(2,1)}, u32[]{:S(2)}, u32[]{:S(2)}) collective-permute-start(bf16[4,32,768]{2,1,0:T(8,128)(2,1)S(1)} %constant_dynamic-update-slice_fusion.4.refs_1_), channel_id=1, source_target_pairs={{0,2},{1,3},{2,0},{3,1},{4,6},{5,7},{6,4},{7,5},{8,10},{9,11},{10,... | collective-permute-start | bytes 589832 | tf_op jit(solution)/shard_map/ppermute | solution.py:313
  19.7 0.2 shard_map.114.refs_3_
  19.9 0.0 collective-permute-done.3.refs_1_
  19.9 0.0 collective-permute-done.5.refs_2_
  19.9 0.3 shard_map.115.refs_0_
  20.2 1.6 %collective-permute-start.6 = (f32[96,128]{1,0:T(8,128)S(1)}, f32[96,128]{1,0:T(8,128)S(1)}, u32[]{:S(2)}, u32[]{:S(2)}) collective-permute-start(f32[96,128]{1,0:T(8,128)S(1)} %shard_map.115.refs_0_), channel_id=1, source_target_pairs={{0,16},{16,0},{1,17},{17,1},{2,18},{18,2},{3,19},{19,3},{4,20},{20... | collective-permute-start | bytes 147464 | tf_op jit(solution)/shard_map/ppermute | solution.py:400
  21.7 0.1 pad_add_fusion.scalar_ref
  22.5 0.1 collective-permute-start.11
  22.6 0.7 %shard_map.116 = (f32[24,128]{1,0:T(8,128)S(1)}, f32[128,128]{1,0:T(8,128)S(1)}, f32[8,128]{1,0:T(8,128)S(1)}, f32[128,64]{1,0:T(8,128)S(1)}) custom-call(s32[2]{0:T(128)S(1)} %pad_add_fusion.scalar_ref, f32[12]{0:T(128)S(1)} %copy-done.6, f32[1]{0:T(128)S(6)} %copy.18.offset_ref), custom_call_target="tpu_custom_call" | custom-call | flops 1000000 | bytes 1000000 | tf_op jit(solution)/shard_map/pallas_call | solution.py:285
  23.3 1.1 %collective-permute-done.6.refs_1_ = f32[96,128]{1,0:T(8,128)S(1)} collective-permute-done((f32[96,128]{1,0:T(8,128)S(1)}, f32[96,128]{1,0:T(8,128)S(1)}, u32[]{:S(2)}, u32[]{:S(2)}) %collective-permute-start.6) | collective-permute-done | bytes 49184 | tf_op jit(solution)/shard_map/ppermute | solution.py:400
  24.4 0.2 shard_map.117.w_ref.refs_0_
  24.5 0.9 %shard_map.118 = f32[16,24,128]{2,1,0:T(8,128)} custom-call(bf16[96,128]{1,0:T(8,128)(2,1)S(1)} %shard_map.117.w_ref.refs_0_, f32[24,128]{1,0:T(8,128)S(1)} %get-tuple-element.29.head_ref.factor_ref, f32[128,128]{1,0:T(8,128)S(1)} %get-tuple-element.19.order_ref), custom_call_target="tpu_custom_call" | custom-call | flops 1000000 | bytes 1000000 | tf_op jit(solution)/shard_map/pallas_call | solution.py:285
  25.5 0.1 collective-permute-done.10.refs_2_
  25.6 0.0 collective-permute-start.12
  25.6 4.5 %all-to-all-start = ((f32[16,24,128]{2,1,0:T(8,128)}), f32[16,24,128]{2,1,0:T(8,128)S(1)}, u32[]{:S(2)}, u32[]{:S(2)}) async-start(f32[16,24,128]{2,1,0:T(8,128)} %shard_map.118), calls=%async_computation | async-start | bytes 393216 | tf_op jit(solution)/shard_map/all_to_all | solution.py:435
  30.1 0.0 collective-permute-done.11.refs_3_
  30.1 1.7 %shard_map.119 = (f32[32,768]{1,0:T(8,128)S(1)}, bf16[32,768]{1,0:T(8,128)(2,1)S(1)}) custom-call(bf16[96,128]{1,0:T(8,128)(2,1)S(1)} %shard_map.117.w_ref.refs_0_, bf16[4,32,768]{2,1,0:T(8,128)(2,1)S(1)} %constant_dynamic-update-slice_fusion.4.refs_1_, bf16[4,32,768]{2,1,0:T(8,128)(2,1)} %collective-permute-done.10.refs_2_, ...), custom_call_target="tpu_custom_call" | custom-call | flops 1000000 | bytes 1000000 | tf_op jit(solution)/shard_map/pallas_call | solution.py:285
  31.9 0.0 copy-start.2
  31.9 1.6 %collective-permute-start.13 = (bf16[32,768]{1,0:T(8,128)(2,1)S(1)}, bf16[32,768]{1,0:T(8,128)(2,1)S(1)}, u32[]{:S(2)}, u32[]{:S(2)}) collective-permute-start(bf16[32,768]{1,0:T(8,128)(2,1)S(1)} %get-tuple-element.25.refs_0_), channel_id=1, source_target_pairs={{0,16},{16,0},{1,17},{17,1},{2,18},{18,2},{3,19},{19,3},{4,20},{20... | collective-permute-start | bytes 147464 | tf_op jit(solution)/shard_map/ppermute | solution.py:437
  33.4 2.6 %collective-permute-done.13.refs_1_ = bf16[32,768]{1,0:T(8,128)(2,1)S(1)} collective-permute-done((bf16[32,768]{1,0:T(8,128)(2,1)S(1)}, bf16[32,768]{1,0:T(8,128)(2,1)S(1)}, u32[]{:S(2)}, u32[]{:S(2)}) %collective-permute-start.13) | collective-permute-done | bytes 49184 | tf_op jit(solution)/shard_map/ppermute | solution.py:437
  36.0 0.4 shard_map.120.own_ref
  36.5 1.6 %collective-permute-start.14 = (bf16[64,1152]{1,0:T(8,128)(2,1)S(1)}, bf16[64,1152]{1,0:T(8,128)(2,1)S(1)}, u32[]{:S(2)}, u32[]{:S(2)}) collective-permute-start(bf16[64,1152]{1,0:T(8,128)(2,1)S(1)} %shard_map.120.own_ref), channel_id=1, source_target_pairs={{0,16},{16,0},{1,17},{17,1},{2,18},{18,2},{3,19},{19,3},{4,20},{20... | collective-permute-start | bytes 442376 | tf_op jit(solution)/shard_map/ppermute | solution.py:450
  38.0 3.8 %collective-permute-done.14.other_ref = bf16[64,1152]{1,0:T(8,128)(2,1)S(1)} collective-permute-done((bf16[64,1152]{1,0:T(8,128)(2,1)S(1)}, bf16[64,1152]{1,0:T(8,128)(2,1)S(1)}, u32[]{:S(2)}, u32[]{:S(2)}) %collective-permute-start.14) | collective-permute-done | bytes 147488 | tf_op jit(solution)/shard_map/ppermute | solution.py:450
  41.9 1.5 %shard_map.121 = bf16[4,8,768]{2,1,0:T(8,128)(2,1)} custom-call(bf16[64,1152]{1,0:T(8,128)(2,1)S(1)} %shard_map.120.own_ref, bf16[64,1152]{1,0:T(8,128)(2,1)S(1)} %collective-permute-done.14.other_ref, f32[32,768]{1,0:T(8,128)S(1)} %get-tuple-element.27.refs_0_, bf16[768,768]{1,0:T(8,128)(2,1)S(1)} %copy-done.2), custom_call_target="tpu_custom_call" | custom-call | flops 1000000 | bytes 1000000 | tf_op jit(solution)/shard_map/pallas_call | solution.py:285
  43.3 0.0 all-to-all-done.pair_ref
  43.3 1.1 %shard_map.122 = f32[8,64]{1,0:T(8,128)} custom-call(f32[16,24,128]{2,1,0:T(8,128)S(1)} %all-to-all-done.pair_ref, f32[24,128]{1,0:T(8,128)S(1)} %get-tuple-element.29.head_ref.factor_ref, f32[8,128]{1,0:T(8,128)S(1)} %get-tuple-element.30.own_ref, f32[128,64]{1,0:T(8,128)S(1)} %get-tuple-element.31.slab_ref), custom_call_target="tpu_custom_call" | custom-call | flops 1000000 | bytes 1000000 | tf_op jit(solution)/shard_map/pallas_call | solution.py:285
  (17 shorter events, 0.1 us)
Async XLA Ops:
  0.6 21.9 %copy-start.6 = (f32[12]{0:T(128)S(1)}, f32[12]{0:T(128)}, u32[]{:S(2)}) copy-start(f32[12]{0:T(128)} %factor_ref.1) | copy-start | bytes 148
  0.6 8.8 %collective-permute-start = (bf16[4,8,768]{2,1,0:T(8,128)(2,1)}, bf16[4,8,768]{2,1,0:T(8,128)(2,1)S(1)}, u32[]{:S(2)}, u32[]{:S(2)}) collective-permute-start(bf16[4,8,768]{2,1,0:T(8,128)(2,1)} %param.12), channel_id=1, source_target_pairs={{0,4},{1,5},{2,6},{3,7},{4,8},{5,9},{6,10},{7,11},{8,12},{9,13},{1... | collective-permute-start | bytes 147464 | tf_op jit(solution)/shard_map/ppermute | solution.py:313
  3.7 8.6 %collective-permute-start.1 = (bf16[4,8,768]{2,1,0:T(8,128)(2,1)}, bf16[4,8,768]{2,1,0:T(8,128)(2,1)S(1)}, u32[]{:S(2)}, u32[]{:S(2)}) collective-permute-start(bf16[4,8,768]{2,1,0:T(8,128)(2,1)} %param.12), channel_id=1, source_target_pairs={{0,8},{1,9},{2,10},{3,11},{4,12},{5,13},{6,14},{7,15},{8,0},{9,1},... | collective-permute-start | bytes 147464 | tf_op jit(solution)/shard_map/ppermute | solution.py:313
  6.3 6.0 %collective-permute-start.2 = (bf16[4,8,768]{2,1,0:T(8,128)(2,1)}, bf16[4,8,768]{2,1,0:T(8,128)(2,1)S(1)}, u32[]{:S(2)}, u32[]{:S(2)}) collective-permute-start(bf16[4,8,768]{2,1,0:T(8,128)(2,1)} %param.12), channel_id=1, source_target_pairs={{0,12},{1,13},{2,14},{3,15},{4,0},{5,1},{6,2},{7,3},{8,4},{9,5},{1... | collective-permute-start | bytes 147464 | tf_op jit(solution)/shard_map/ppermute | solution.py:313
  7.7 7.1 %collective-permute-start.7 = (bf16[4,8,768]{2,1,0:T(8,128)(2,1)}, bf16[4,8,768]{2,1,0:T(8,128)(2,1)S(1)}, u32[]{:S(2)}, u32[]{:S(2)}) collective-permute-start(bf16[4,8,768]{2,1,0:T(8,128)(2,1)} %param.13), channel_id=1, source_target_pairs={{0,4},{1,5},{2,6},{3,7},{4,8},{5,9},{6,10},{7,11},{8,12},{9,13},{1... | collective-permute-start | bytes 147464 | tf_op jit(solution)/shard_map/ppermute | solution.py:313
  8.3 7.3 %collective-permute-start.8 = (bf16[4,8,768]{2,1,0:T(8,128)(2,1)}, bf16[4,8,768]{2,1,0:T(8,128)(2,1)S(1)}, u32[]{:S(2)}, u32[]{:S(2)}) collective-permute-start(bf16[4,8,768]{2,1,0:T(8,128)(2,1)} %param.13), channel_id=1, source_target_pairs={{0,8},{1,9},{2,10},{3,11},{4,12},{5,13},{6,14},{7,15},{8,0},{9,1},... | collective-permute-start | bytes 147464 | tf_op jit(solution)/shard_map/ppermute | solution.py:313
  9.5 8.6 %collective-permute-start.9 = (bf16[4,8,768]{2,1,0:T(8,128)(2,1)}, bf16[4,8,768]{2,1,0:T(8,128)(2,1)S(1)}, u32[]{:S(2)}, u32[]{:S(2)}) collective-permute-start(bf16[4,8,768]{2,1,0:T(8,128)(2,1)} %param.13), channel_id=1, source_target_pairs={{0,12},{1,13},{2,14},{3,15},{4,0},{5,1},{6,2},{7,3},{8,4},{9,5},{1... | collective-permute-start | bytes 147464 | tf_op jit(solution)/shard_map/ppermute | solution.py:313
  12.3 5.7 %collective-permute-start.4 = (bf16[4,32,768]{2,1,0:T(8,128)(2,1)S(1)}, bf16[4,32,768]{2,1,0:T(8,128)(2,1)S(1)}, u32[]{:S(2)}, u32[]{:S(2)}) collective-permute-start(bf16[4,32,768]{2,1,0:T(8,128)(2,1)S(1)} %constant_dynamic-update-slice_fusion.refs_1_), channel_id=1, source_target_pairs={{0,2},{1,3},{2,0},{3,1},{4,6},{5,7},{6,4},{7,5},{8,10},{9,11},{10,... | collective-permute-start | bytes 589832 | tf_op jit(solution)/shard_map/ppermute | solution.py:313
  13.9 6.0 %collective-permute-start.3 = (bf16[4,32,768]{2,1,0:T(8,128)(2,1)S(1)}, bf16[4,32,768]{2,1,0:T(8,128)(2,1)S(1)}, u32[]{:S(2)}, u32[]{:S(2)}) collective-permute-start(bf16[4,32,768]{2,1,0:T(8,128)(2,1)S(1)} %constant_dynamic-update-slice_fusion.refs_1_), channel_id=1, source_target_pairs={{0,1},{1,0},{2,3},{3,2},{4,5},{5,4},{6,7},{7,6},{8,9},{9,8},{10,11... | collective-permute-start | bytes 589832 | tf_op jit(solution)/shard_map/ppermute | solution.py:313
  13.9 0.8 %copy-start.3 = (bf16[4,8,768]{2,1,0:T(8,128)(2,1)S(1)}, bf16[4,8,768]{2,1,0:T(8,128)(2,1)}, u32[]{:S(2)}) copy-start(bf16[4,8,768]{2,1,0:T(8,128)(2,1)} %q_hbm) | copy-start | bytes 147460
  15.6 14.5 %copy-start.1 = (bf16[768,768]{1,0:T(8,128)(2,1)S(1)}, bf16[768,768]{1,0:T(8,128)(2,1)}, u32[]{:S(2)}) copy-start(bf16[768,768]{1,0:T(8,128)(2,1)} %refs_5_.1) | copy-start | bytes 3538948
  15.6 14.5 %copy-start.4 = (bf16[4,8,768]{2,1,0:T(8,128)(2,1)S(1)}, bf16[4,8,768]{2,1,0:T(8,128)(2,1)}, u32[]{:S(2)}) copy-start(bf16[4,8,768]{2,1,0:T(8,128)(2,1)} %refs_6_.1) | copy-start | bytes 147460
  15.6 14.5 %copy-start.5 = (f32[768]{0:T(1024)S(1)}, f32[768]{0:T(1024)}, u32[]{:S(2)}) copy-start(f32[768]{0:T(1024)} %refs_7_.1) | copy-start | bytes 9220
  18.1 1.8 %collective-permute-start.5 = (bf16[4,32,768]{2,1,0:T(8,128)(2,1)S(1)}, bf16[4,32,768]{2,1,0:T(8,128)(2,1)S(1)}, u32[]{:S(2)}, u32[]{:S(2)}) collective-permute-start(bf16[4,32,768]{2,1,0:T(8,128)(2,1)S(1)} %collective-permute-done.4.refs_2_), channel_id=1, source_target_pairs={{0,1},{1,0},{2,3},{3,2},{4,5},{5,4},{6,7},{7,6},{8,9},{9,8},{10,11... | collective-permute-start | bytes 589832 | tf_op jit(solution)/shard_map/ppermute | solution.py:313
  18.1 7.5 %collective-permute-start.10 = (bf16[4,32,768]{2,1,0:T(8,128)(2,1)S(1)}, bf16[4,32,768]{2,1,0:T(8,128)(2,1)}, u32[]{:S(2)}, u32[]{:S(2)}) collective-permute-start(bf16[4,32,768]{2,1,0:T(8,128)(2,1)S(1)} %constant_dynamic-update-slice_fusion.4.refs_1_), channel_id=1, source_target_pairs={{0,2},{1,3},{2,0},{3,1},{4,6},{5,7},{6,4},{7,5},{8,10},{9,11},{10,... | collective-permute-start | bytes 589832 | tf_op jit(solution)/shard_map/ppermute | solution.py:313
  20.2 4.2 %collective-permute-start.6 = (f32[96,128]{1,0:T(8,128)S(1)}, f32[96,128]{1,0:T(8,128)S(1)}, u32[]{:S(2)}, u32[]{:S(2)}) collective-permute-start(f32[96,128]{1,0:T(8,128)S(1)} %shard_map.115.refs_0_), channel_id=1, source_target_pairs={{0,16},{16,0},{1,17},{17,1},{2,18},{18,2},{3,19},{19,3},{4,20},{20... | collective-permute-start | bytes 147464 | tf_op jit(solution)/shard_map/ppermute | solution.py:400
  22.5 7.6 %collective-permute-start.11 = (bf16[4,32,768]{2,1,0:T(8,128)(2,1)S(1)}, bf16[4,32,768]{2,1,0:T(8,128)(2,1)}, u32[]{:S(2)}, u32[]{:S(2)}) collective-permute-start(bf16[4,32,768]{2,1,0:T(8,128)(2,1)S(1)} %constant_dynamic-update-slice_fusion.4.refs_1_), channel_id=1, source_target_pairs={{0,1},{1,0},{2,3},{3,2},{4,5},{5,4},{6,7},{7,6},{8,9},{9,8},{10,11... | collective-permute-start | bytes 589832 | tf_op jit(solution)/shard_map/ppermute | solution.py:313
  25.5 10.6 %copy-start = (bf16[768,1152]{1,0:T(8,128)(2,1)S(1)}, bf16[768,1152]{1,0:T(8,128)(2,1)}, u32[]{:S(2)}) copy-start(bf16[768,1152]{1,0:T(8,128)(2,1)} %refs_2_) | copy-start | bytes 5308420
  25.6 4.5 %collective-permute-start.12 = (bf16[4,32,768]{2,1,0:T(8,128)(2,1)}, bf16[4,32,768]{2,1,0:T(8,128)(2,1)}, u32[]{:S(2)}, u32[]{:S(2)}) collective-permute-start(bf16[4,32,768]{2,1,0:T(8,128)(2,1)} %collective-permute-done.10.refs_2_), channel_id=1, source_target_pairs={{0,1},{1,0},{2,3},{3,2},{4,5},{5,4},{6,7},{7,6},{8,9},{9,8},{10,11... | collective-permute-start | bytes 589832 | tf_op jit(solution)/shard_map/ppermute | solution.py:313
  25.6 17.8 %all-to-all-start = ((f32[16,24,128]{2,1,0:T(8,128)}), f32[16,24,128]{2,1,0:T(8,128)S(1)}, u32[]{:S(2)}, u32[]{:S(2)}) async-start(f32[16,24,128]{2,1,0:T(8,128)} %shard_map.118), calls=%async_computation | async-start | bytes 393216 | tf_op jit(solution)/shard_map/all_to_all | solution.py:435
  31.9 10.0 %copy-start.2 = (bf16[768,768]{1,0:T(8,128)(2,1)S(1)}, bf16[768,768]{1,0:T(8,128)(2,1)}, u32[]{:S(2)}) copy-start(bf16[768,768]{1,0:T(8,128)(2,1)} %refs_1_) | copy-start | bytes 3538948
  31.9 4.2 %collective-permute-start.13 = (bf16[32,768]{1,0:T(8,128)(2,1)S(1)}, bf16[32,768]{1,0:T(8,128)(2,1)S(1)}, u32[]{:S(2)}, u32[]{:S(2)}) collective-permute-start(bf16[32,768]{1,0:T(8,128)(2,1)S(1)} %get-tuple-element.25.refs_0_), channel_id=1, source_target_pairs={{0,16},{16,0},{1,17},{17,1},{2,18},{18,2},{3,19},{19,3},{4,20},{20... | collective-permute-start | bytes 147464 | tf_op jit(solution)/shard_map/ppermute | solution.py:437
  36.5 5.4 %collective-permute-start.14 = (bf16[64,1152]{1,0:T(8,128)(2,1)S(1)}, bf16[64,1152]{1,0:T(8,128)(2,1)S(1)}, u32[]{:S(2)}, u32[]{:S(2)}) collective-permute-start(bf16[64,1152]{1,0:T(8,128)(2,1)S(1)} %shard_map.120.own_ref), channel_id=1, source_target_pairs={{0,16},{16,0},{1,17},{17,1},{2,18},{18,2},{3,19},{19,3},{4,20},{20... | collective-permute-start | bytes 442376 | tf_op jit(solution)/shard_map/ppermute | solution.py:450

commit v12 on v10

--- a/solution.py
+++ b/solution.py
@@ -69,7 +69,14 @@
 
 
 def prepare_kernel(heads, sites, stages, scalar_ref, factor_ref, offset_ref, *refs):
-    head_ref, order_ref, own_ref, slab_ref = refs
+    head_ref, order_ref, own_ref, slab_ref, pick_ref, spread_ref = refs
+    head = pick_ref.shape[0] // heads
+    row = lax.broadcasted_iota(jnp.int32, pick_ref.shape, 0)
+    lane = lax.broadcasted_iota(jnp.int32, pick_ref.shape, 1)
+    pick_ref[...] = (row // head == lane).astype(BF16)
+    row = lax.broadcasted_iota(jnp.int32, spread_ref.shape, 0)
+    lane = lax.broadcasted_iota(jnp.int32, spread_ref.shape, 1)
+    spread_ref[...] = (lane // head == row).astype(BF16)
     row = lax.broadcasted_iota(jnp.int32, head_ref.shape, 0)
     factors = jnp.zeros(head_ref.shape, F32)
     for h in range(heads):
@@ -104,8 +111,10 @@
         out_ref[lines, :] = jnp.concatenate([done[lines, :] for done in done_refs] + [total], axis=1)
 
 
-def softmax_kernel(factor, *refs):
-    parts, w_ref = refs[:-1], refs[-1]
+def softmax_kernel(factor, heads, *refs):
+    parts, (head_ref, order_ref, w_ref, pair_ref, held) = refs[:-5], refs[-5:]
+    rows, length = w_ref.shape
+    sites = rows // heads
     logits = parts[0][...]
     for part in parts[1:]:
         logits = logits + part[...]
@@ -113,12 +122,7 @@
     exponent = jnp.exp(logits - jnp.max(logits, axis=1, keepdims=True))
     shares = (exponent / jnp.sum(exponent, axis=1, keepdims=True)).astype(BF16)
     w_ref[...] = shares
-
-
-def pair_kernel(heads, w_ref, head_ref, order_ref, pair_ref, held):
-    rows, length = w_ref.shape
-    sites = rows // heads
-    shares = w_ref[...].astype(F32)
+    shares = shares.astype(F32)
     row_sum = jnp.sum(shares, axis=1, keepdims=True)
     lane = lax.broadcasted_iota(jnp.int32, (rows, length), 1)
     row = lax.broadcasted_iota(jnp.int32, (rows, length), 0) % sites
@@ -166,17 +170,12 @@
     out_ref[...] = dot_nn(normed, weight_ref[...]).astype(BF16)
 
 
-def column_attend(head, factor, query, keys, values, hidden_ref, closing_ref, out_ref, products, mixed):
+def column_attend(
+    factor, query, keys, values, hidden_ref, closing_ref, pick_ref, spread_ref, out_ref, products, mixed
+):
     rows, sites, embed = out_ref.shape
-    padded = round_up(embed // head, 128)
-    pick = (
-        lax.broadcasted_iota(jnp.int32, (embed, padded), 0) // head
-        == lax.broadcasted_iota(jnp.int32, (embed, padded), 1)
-    ).astype(BF16)
-    spread = (
-        lax.broadcasted_iota(jnp.int32, (padded, embed), 1) // head
-        == lax.broadcasted_iota(jnp.int32, (padded, embed), 0)
-    ).astype(BF16)
+    pick = pick_ref[...]
+    padded = pick.shape[1]
     seqs = len(keys)
     for s in range(rows):
         for t in range(seqs):
@@ -188,7 +187,7 @@
     scores = (dot_nn(high, pick) + dot_nn(low, pick)) * factor
     exponent = jnp.exp(scores).reshape(rows, seqs, sites, padded)
     shares = (exponent / jnp.sum(exponent, axis=1, keepdims=True)).astype(BF16)
-    wide = dot_nn(shares.reshape(rows * seqs * sites, padded), spread)
+    wide = dot_nn(shares.reshape(rows * seqs * sites, padded), spread_ref[...])
     for s in range(rows):
         total = None
         for t in range(seqs):
@@ -200,17 +199,17 @@
     out_ref[...] = out.reshape(rows, sites, embed).astype(BF16)
 
 
-def column_kernel(head, factor, query_ref, kv_ref, *refs):
-    rows, sites, embed = refs[2].shape
+def column_kernel(factor, query_ref, kv_ref, *refs):
+    rows, sites, embed = refs[4].shape
     kv = kv_ref[...].astype(F32)
     seqs = kv.shape[0] // sites
     keys = [kv[t * sites : (t + 1) * sites, 0:embed] for t in range(seqs)]
     values = [kv[t * sites : (t + 1) * sites, embed:] for t in range(seqs)]
-    column_attend(head, factor, query_ref[...].astype(F32), keys, values, *refs)
-
-
-def swapped_column_kernel(head, factor, own_ref, other_ref, *refs):
-    rows, sites, embed = refs[2].shape
+    column_attend(factor, query_ref[...].astype(F32), keys, values, *refs)
+
+
+def swapped_column_kernel(factor, own_ref, other_ref, *refs):
+    rows, sites, embed = refs[4].shape
     cells, columns = own_ref.shape
     half = cells // 2
 
@@ -236,7 +235,7 @@
             for t in range(half // sites):
                 keys.append(key[t * sites : (t + 1) * sites, :])
                 values.append(value[t * sites : (t + 1) * sites, :])
-        column_attend(head, factor, query, keys, values, *refs)
+        column_attend(factor, query, keys, values, *refs)
 
     seq_index = lax.axis_index("seq")
     pl.when(seq_index == 0)(functools.partial(attend, True))
@@ -385,13 +384,16 @@
             jax.ShapeDtypeStruct((heads * sites, length), F32),
             [masked, *far_parts, partial],
         )
-    head_factors, order, own_select, slab_select = call(
+    padded = round_up(heads, 128)
+    head_factors, order, own_select, slab_select, pick, spread = call(
         functools.partial(prepare_kernel, heads, sites, stages),
         (
             jax.ShapeDtypeStruct((head_rows + 8, 128), F32),
             jax.ShapeDtypeStruct((length, length), F32),
             jax.ShapeDtypeStruct((sites, length), F32),
             jax.ShapeDtypeStruct((length, slab_width), F32),
+            jax.ShapeDtypeStruct((embed, padded), BF16),
+            jax.ShapeDtypeStruct((padded, embed), BF16),
         ),
         [after(scalars, partial), regression_factors, regression_offset],
         smem=(0, 1, 2),
@@ -400,18 +402,15 @@
         partials = [partial, after(lax.ppermute(partial, "seq", swap), order)]
     else:
         partials = [lax.psum(partial, "seq")]
-    shares = call(
+    shares, pair_local = call(
         functools.partial(
-            softmax_kernel, 1.0 / (math.sqrt(head) * math.sqrt(rows * seq_count))
+            softmax_kernel, 1.0 / (math.sqrt(head) * math.sqrt(rows * seq_count)), heads
         ),
-        jax.ShapeDtypeStruct((heads * sites, length), BF16),
-        partials,
-    )
-
-    pair_local = call(
-        functools.partial(pair_kernel, heads),
-        jax.ShapeDtypeStruct((pos_count, head_rows + sites, length), F32),
-        [shares, head_factors, order],
+        (
+            jax.ShapeDtypeStruct((heads * sites, length), BF16),
+            jax.ShapeDtypeStruct((pos_count, head_rows + sites, length), F32),
+        ),
+        [*partials, head_factors, order],
         scratch=[pltpu.VMEM((head_rows + sites, length), F32)],
     )
     if len(stages) > 2:
@@ -441,7 +440,8 @@
     )
     if swapped:
         normed_all = [normed, lax.ppermute(normed, "seq", swap)]
-        weight = after(upright_threefold_linear, normed)
+        one = jnp.minimum(jnp.abs(normed[0, 0]) + 1, 1)
+        weight = upright_threefold_linear * one
     else:
         normed_all = [normed]
         weight = lax.all_gather(upright_threefold_linear, "seq", axis=1, tiled=True)
@@ -459,12 +459,14 @@
         key_value = lax.all_gather(projected[:, embed:], "seq", axis=0, tiled=True)
         column, column_inputs = column_kernel, [projected[:, :embed], key_value]
     alignment_output = call(
-        functools.partial(column, head, 1.0 / math.sqrt(head)),
+        functools.partial(column, 1.0 / math.sqrt(head)),
         jax.ShapeDtypeStruct((rows, sites, embed), BF16),
         [
             *column_inputs,
             hidden,
             after(upright_closing_linear, projected),
+            pick,
+            spread,
         ],
         scratch=[
             pltpu.VMEM((cells * rows * seq_count, embed), F32),

time: 44.6 us -> 44.7 us (level)
  starting transfers between devices: 23.3 us -> 24.9 us
  Pallas kernels: 7.05 us -> 6.01 us
  waiting for transfers between devices: 8.99 us -> 7.98 us
  between operations: 1.48 us -> 2.17 us
    all_to_all x1, waiting for transfers between devices: 0.24 us -> 1.7 us  [per_device(): lax.all_to_all(pair_local, 'pos', split_axis=0, concat_axis=0, tiled=True)]
    ppermute x1, waiting for transfers between devices: 2.54 us -> 1.09 us  [per_device(): lax.ppermute(projected, 'seq', swap)]
    pallas_call x10 -> x9, Pallas kernels: 7.05 us -> 6.01 us  [call(): pl.pallas_call(kernel, out_shape=out_shape, in_specs=specs, out_specs=jax...]
    ppermute x12, starting transfers between devices: 14.1 us -> 15 us  [send_pos(): return lax.ppermute(array, 'pos', pairs)]
    ppermute x1, waiting for transfers between devices: 2.6 us -> 1.73 us  [per_device(): normed_all = [normed, lax.ppermute(normed, 'seq', swap)]]
    all_to_all x1, starting transfers between devices: 4.51 us -> 5.33 us  [per_device(): lax.all_to_all(pair_local, 'pos', split_axis=0, concat_axis=0, tiled=True)]
    unnamed x20, local copies, waits for them, and re-layouts: 3.24 us -> 2.45 us
    slice x0 -> x1, local copies, waits for them, and re-layouts: none -> 0.51 us  [per_device(): one = jnp.minimum(jnp.abs(normed[0, 0]) + 1, 1)]
  transfers between devices with their start and end apart: 16 -> 16, of which waited for: 6 -> 6; matrix products, arithmetic and copies ran while one was open for 4% -> 5% of each run, Pallas kernels for 13% -> 10%
where the time goes in v12:
time: 44.7 us; the launch traced here: 44.3 us
  starting transfers between devices  24.9 us (56%)
  waiting for transfers between devices  7.98 us (18%)
  Pallas kernels  6.01 us (13%)
  local copies, waits for them, and re-layouts  2.98 us (7%)
  between operations  2.17 us (5%)
    ppermute x12, starting transfers between devices, send_pos(): return lax.ppermute(array, 'pos', pairs)  15 us
    pallas_call x9, Pallas kernels, call(): pl.pallas_call(kernel, out_shape=out_shape, in_specs=specs, out_specs=jax...  6.01 us
    all_to_all x1, starting transfers between devices, per_device(): lax.all_to_all(pair_local, 'pos', split_axis=0, concat_axis=0, tiled=True)  5.33 us
    ppermute x12, waiting for transfers between devices, send_pos(): return lax.ppermute(array, 'pos', pairs)  2.46 us
    unnamed x20, local copies, waits for them, and re-layouts  2.45 us
    ppermute x1, waiting for transfers between devices, per_device(): normed_all = [normed, lax.ppermute(normed, 'seq', swap)]  1.73 us
    all_to_all x1, waiting for transfers between devices, per_device(): lax.all_to_all(pair_local, 'pos', split_axis=0, concat_axis=0, tiled=True)  1.7 us
    ppermute x1, starting transfers between devices, per_device(): partials = [partial, after(lax.ppermute(partial, 'seq', swap), order)]  1.56 us
  transfers between devices with their start and end apart: 16, of which 6 were waited for; matrix products, arithmetic and copies ran while one was open for 5% of the time, Pallas kernels for 10%

profile of v12, /device:TPU:0, one launch (start us, length us, event | category | flops | bytes accessed | tf_op | source)
XLA Modules:
  0.0 44.3 jit_solution(14462735613925397792)
XLA Ops:
  0.6 4.1 %collective-permute-start.1 = (bf16[4,8,768]{2,1,0:T(8,128)(2,1)}, bf16[4,8,768]{2,1,0:T(8,128)(2,1)S(1)}, u32[]{:S(2)}, u32[]{:S(2)}) collective-permute-start(bf16[4,8,768]{2,1,0:T(8,128)(2,1)} %param.12), channel_id=1, source_target_pairs={{0,8},{1,9},{2,10},{3,11},{4,12},{5,13},{6,14},{7,15},{8,0},{9,1},... | collective-permute-start | bytes 147464 | tf_op jit(solution)/shard_map/ppermute | solution.py:312
  4.7 1.6 %collective-permute-start = (bf16[4,8,768]{2,1,0:T(8,128)(2,1)}, bf16[4,8,768]{2,1,0:T(8,128)(2,1)S(1)}, u32[]{:S(2)}, u32[]{:S(2)}) collective-permute-start(bf16[4,8,768]{2,1,0:T(8,128)(2,1)} %param.12), channel_id=1, source_target_pairs={{0,4},{1,5},{2,6},{3,7},{4,8},{5,9},{6,10},{7,11},{8,12},{9,13},{1... | collective-permute-start | bytes 147464 | tf_op jit(solution)/shard_map/ppermute | solution.py:312
  6.3 2.2 %collective-permute-start.2 = (bf16[4,8,768]{2,1,0:T(8,128)(2,1)}, bf16[4,8,768]{2,1,0:T(8,128)(2,1)S(1)}, u32[]{:S(2)}, u32[]{:S(2)}) collective-permute-start(bf16[4,8,768]{2,1,0:T(8,128)(2,1)} %param.12), channel_id=1, source_target_pairs={{0,12},{1,13},{2,14},{3,15},{4,0},{5,1},{6,2},{7,3},{8,4},{9,5},{1... | collective-permute-start | bytes 147464 | tf_op jit(solution)/shard_map/ppermute | solution.py:312
  8.6 0.0 collective-permute-start.7
  8.6 3.8 %collective-permute-start.9 = (bf16[4,8,768]{2,1,0:T(8,128)(2,1)}, bf16[4,8,768]{2,1,0:T(8,128)(2,1)S(1)}, u32[]{:S(2)}, u32[]{:S(2)}) collective-permute-start(bf16[4,8,768]{2,1,0:T(8,128)(2,1)} %param.13), channel_id=1, source_target_pairs={{0,12},{1,13},{2,14},{3,15},{4,0},{5,1},{6,2},{7,3},{8,4},{9,5},{1... | collective-permute-start | bytes 147464 | tf_op jit(solution)/shard_map/ppermute | solution.py:312
  12.4 0.8 %constant_dynamic-update-slice_fusion.3 = bf16[4,32,768]{2,1,0:T(8,128)(2,1)S(1)} fusion(bf16[4,8,768]{2,1,0:T(8,128)(2,1)} %param.12), kind=kLoop, calls=%fused_computation.4 | loop fusion | bytes 98304
  13.2 0.0 collective-permute-done
  13.2 0.0 collective-permute-start.8
  13.2 0.0 collective-permute-done.1
  13.2 0.0 collective-permute-done.2
  13.3 1.6 %collective-permute-start.4 = (bf16[4,32,768]{2,1,0:T(8,128)(2,1)S(1)}, bf16[4,32,768]{2,1,0:T(8,128)(2,1)S(1)}, u32[]{:S(2)}, u32[]{:S(2)}) collective-permute-start(bf16[4,32,768]{2,1,0:T(8,128)(2,1)S(1)} %constant_dynamic-update-slice_fusion.refs_1_), channel_id=1, source_target_pairs={{0,2},{1,3},{2,0},{3,1},{4,6},{5,7},{6,4},{7,5},{8,10},{9,11},{10,... | collective-permute-start | bytes 589832 | tf_op jit(solution)/shard_map/ppermute | solution.py:312
  14.9 0.0 collective-permute-start.3
  14.9 0.8 %copy-done.2 = bf16[4,8,768]{2,1,0:T(8,128)(2,1)S(1)} copy-done((bf16[4,8,768]{2,1,0:T(8,128)(2,1)S(1)}, bf16[4,8,768]{2,1,0:T(8,128)(2,1)}, u32[]{:S(2)}) %copy-start.2) | copy-done | bytes 49176
  15.7 0.1 shard_map.113.refs_0_
  15.8 0.0 collective-permute-done.7
  15.8 0.8 %constant_dynamic-update-slice_fusion.7 = bf16[4,32,768]{2,1,0:T(8,128)(2,1)S(1)} fusion(bf16[4,8,768]{2,1,0:T(8,128)(2,1)} %param.13), kind=kLoop, calls=%fused_computation.8 | loop fusion | bytes 98304
  16.6 1.8 %collective-permute-done.8 = bf16[4,8,768]{2,1,0:T(8,128)(2,1)S(1)} collective-permute-done((bf16[4,8,768]{2,1,0:T(8,128)(2,1)}, bf16[4,8,768]{2,1,0:T(8,128)(2,1)S(1)}, u32[]{:S(2)}, u32[]{:S(2)}) %collective-permute-start.8) | collective-permute-done | bytes 49184 | tf_op jit(solution)/shard_map/ppermute | solution.py:312
  18.4 0.6 %collective-permute-done.4.refs_2_ = bf16[4,32,768]{2,1,0:T(8,128)(2,1)S(1)} collective-permute-done((bf16[4,32,768]{2,1,0:T(8,128)(2,1)S(1)}, bf16[4,32,768]{2,1,0:T(8,128)(2,1)S(1)}, u32[]{:S(2)}, u32[]{:S(2)}) %collective-permute-start.4) | collective-permute-done | bytes 196640 | tf_op jit(solution)/shard_map/ppermute | solution.py:312
  19.0 0.0 collective-permute-start.5
  19.0 0.0 collective-permute-done.9
  19.0 1.6 %collective-permute-start.10 = (bf16[4,32,768]{2,1,0:T(8,128)(2,1)S(1)}, bf16[4,32,768]{2,1,0:T(8,128)(2,1)S(1)}, u32[]{:S(2)}, u32[]{:S(2)}) collective-permute-start(bf16[4,32,768]{2,1,0:T(8,128)(2,1)S(1)} %constant_dynamic-update-slice_fusion.4.refs_1_), channel_id=1, source_target_pairs={{0,2},{1,3},{2,0},{3,1},{4,6},{5,7},{6,4},{7,5},{8,10},{9,11},{10,... | collective-permute-start | bytes 589832 | tf_op jit(solution)/shard_map/ppermute | solution.py:312
  20.6 0.2 shard_map.114.refs_3_
  20.8 0.0 collective-permute-done.3.refs_1_
  20.8 0.0 collective-permute-done.5.refs_2_
  20.8 0.3 shard_map.115.refs_0_
  21.1 1.6 %collective-permute-start.6 = (f32[96,128]{1,0:T(8,128)S(1)}, f32[96,128]{1,0:T(8,128)S(1)}, u32[]{:S(2)}, u32[]{:S(2)}) collective-permute-start(f32[96,128]{1,0:T(8,128)S(1)} %shard_map.115.refs_0_), channel_id=1, source_target_pairs={{0,16},{16,0},{1,17},{17,1},{2,18},{18,2},{3,19},{19,3},{4,20},{20... | collective-permute-start | bytes 147464 | tf_op jit(solution)/shard_map/ppermute | solution.py:402
  22.7 0.1 pad_add_fusion.scalar_ref
  23.4 0.1 collective-permute-start.11
  23.5 0.8 %shard_map.116 = (f32[24,128]{1,0:T(8,128)S(1)}, f32[128,128]{1,0:T(8,128)S(1)}, f32[8,128]{1,0:T(8,128)S(1)}, f32[128,64]{1,0:T(8,128)S(1)}, bf16[768,128]{1,0:...) custom-call(s32[2]{0:T(128)S(1)} %pad_add_fusion.scalar_ref, f32[12]{0:T(128)S(1)} %copy-done.5, f32[1]{0:T(128)S(6)} %copy.18.offset_ref), custom_call_target="tpu_custom_call" | custom-call | flops 1000000 | bytes 1000000 | tf_op jit(solution)/shard_map/pallas_call | solution.py:284
  24.3 1.0 %collective-permute-done.6.refs_1_ = f32[96,128]{1,0:T(8,128)S(1)} collective-permute-done((f32[96,128]{1,0:T(8,128)S(1)}, f32[96,128]{1,0:T(8,128)S(1)}, u32[]{:S(2)}, u32[]{:S(2)}) %collective-permute-start.6) | collective-permute-done | bytes 49184 | tf_op jit(solution)/shard_map/ppermute | solution.py:402
  25.3 1.1 %shard_map.117 = (bf16[96,128]{1,0:T(8,128)(2,1)S(1)}, f32[16,24,128]{2,1,0:T(8,128)}) custom-call(f32[96,128]{1,0:T(8,128)S(1)} %shard_map.115.refs_0_, f32[96,128]{1,0:T(8,128)S(1)} %collective-permute-done.6.refs_1_, f32[24,128]{1,0:T(8,128)S(1)} %get-tuple-element.23.refs_2_.factor_ref, f32[128,128]{1,0:T(8,128)S(1)} %get-tuple-element.21.refs_3_), custom_call_target="tpu_custom_call" | custom-call | flops 1000000 | bytes 1000000 | tf_op jit(solution)/shard_map/pallas_call | solution.py:284
  26.4 0.0 collective-permute-done.10.refs_2_
  26.4 0.0 collective-permute-start.12
  26.4 5.3 %all-to-all-start = ((f32[16,24,128]{2,1,0:T(8,128)}), f32[16,24,128]{2,1,0:T(8,128)S(1)}, u32[]{:S(2)}, u32[]{:S(2)}) async-start(f32[16,24,128]{2,1,0:T(8,128)} %get-tuple-element.27), calls=%async_computation | async-start | bytes 393216 | tf_op jit(solution)/shard_map/all_to_all | solution.py:434
  31.7 0.0 copy-start.6
  31.8 0.0 collective-permute-done.12.refs_4_
  31.8 0.6 %shard_map.118 = (f32[32,768]{1,0:T(8,128)S(1)}, bf16[32,768]{1,0:T(8,128)(2,1)S(1)}) custom-call(bf16[96,128]{1,0:T(8,128)(2,1)S(1)} %get-tuple-element.24.refs_0_, bf16[4,32,768]{2,1,0:T(8,128)(2,1)S(1)} %constant_dynamic-update-slice_fusion.4.refs_1_, bf16[4,32,768]{2,1,0:T(8,128)(2,1)S(1)} %collective-permute-done.10.refs_2_, ...), custom_call_target="tpu_custom_call" | custom-call | flops 1000000 | bytes 1000000 | tf_op jit(solution)/shard_map/pallas_call | solution.py:284
  32.4 0.5 %slice.3 = bf16[1,1]{1,0:T(2,128)(2,1)} slice(bf16[32,768]{1,0:T(8,128)(2,1)S(1)} %get-tuple-element.29.refs_0_), slice={[0:1], [0:1]} | slice | bytes 4 | tf_op jit(solution)/shard_map/slice | solution.py:443
  33.0 1.5 %collective-permute-start.13 = (bf16[32,768]{1,0:T(8,128)(2,1)S(1)}, bf16[32,768]{1,0:T(8,128)(2,1)S(1)}, u32[]{:S(2)}, u32[]{:S(2)}) collective-permute-start(bf16[32,768]{1,0:T(8,128)(2,1)S(1)} %get-tuple-element.29.refs_0_), channel_id=1, source_target_pairs={{0,16},{16,0},{1,17},{17,1},{2,18},{18,2},{3,19},{19,3},{4,20},{20... | collective-permute-start | bytes 147464 | tf_op jit(solution)/shard_map/ppermute | solution.py:442
  35.1 0.2 broadcast_multiply_fusion.refs_2_
  35.3 0.0 copy-start.1
  35.3 1.7 %collective-permute-done.13.refs_1_ = bf16[32,768]{1,0:T(8,128)(2,1)S(1)} collective-permute-done((bf16[32,768]{1,0:T(8,128)(2,1)S(1)}, bf16[32,768]{1,0:T(8,128)(2,1)S(1)}, u32[]{:S(2)}, u32[]{:S(2)}) %collective-permute-start.13) | collective-permute-done | bytes 49184 | tf_op jit(solution)/shard_map/ppermute | solution.py:442
  37.0 0.4 shard_map.119.own_ref
  37.5 1.6 %collective-permute-start.14 = (bf16[64,1152]{1,0:T(8,128)(2,1)S(1)}, bf16[64,1152]{1,0:T(8,128)(2,1)S(1)}, u32[]{:S(2)}, u32[]{:S(2)}) collective-permute-start(bf16[64,1152]{1,0:T(8,128)(2,1)S(1)} %shard_map.119.own_ref), channel_id=1, source_target_pairs={{0,16},{16,0},{1,17},{17,1},{2,18},{18,2},{3,19},{19,3},{4,20},{20... | collective-permute-start | bytes 442376 | tf_op jit(solution)/shard_map/ppermute | solution.py:456
  39.0 1.7 %all-to-all-done.pair_ref = f32[16,24,128]{2,1,0:T(8,128)S(1)} async-done(((f32[16,24,128]{2,1,0:T(8,128)}), f32[16,24,128]{2,1,0:T(8,128)S(1)}, u32[]{:S(2)}, u32[]{:S(2)}) %all-to-all-start) | async-done | bytes 196640 | tf_op jit(solution)/shard_map/all_to_all | solution.py:434
  40.7 1.0 %shard_map.121 = f32[8,64]{1,0:T(8,128)} custom-call(f32[16,24,128]{2,1,0:T(8,128)S(1)} %all-to-all-done.pair_ref, f32[24,128]{1,0:T(8,128)S(1)} %get-tuple-element.23.refs_2_.factor_ref, f32[8,128]{1,0:T(8,128)S(1)} %get-tuple-element.34.own_ref, f32[128,64]{1,0:T(8,128)S(1)} %get-tuple-element.35.slab_ref), custom_call_target="tpu_custom_call" | custom-call | flops 1000000 | bytes 1000000 | tf_op jit(solution)/shard_map/pallas_call | solution.py:284
  41.8 1.1 %collective-permute-done.14.other_ref = bf16[64,1152]{1,0:T(8,128)(2,1)S(1)} collective-permute-done((bf16[64,1152]{1,0:T(8,128)(2,1)S(1)}, bf16[64,1152]{1,0:T(8,128)(2,1)S(1)}, u32[]{:S(2)}, u32[]{:S(2)}) %collective-permute-start.14) | collective-permute-done | bytes 147488 | tf_op jit(solution)/shard_map/ppermute | solution.py:456
  42.9 1.4 %shard_map.120 = bf16[4,8,768]{2,1,0:T(8,128)(2,1)} custom-call(bf16[64,1152]{1,0:T(8,128)(2,1)S(1)} %shard_map.119.own_ref, bf16[64,1152]{1,0:T(8,128)(2,1)S(1)} %collective-permute-done.14.other_ref, f32[32,768]{1,0:T(8,128)S(1)} %get-tuple-element.30.refs_0_, bf16[768,768]{1,0:T(8,128)(2,1)S(1)} %copy-done.1, ...), custom_call_target="tpu_custom_call" | custom-call | flops 1000000 | bytes 1000000 | tf_op jit(solution)/shard_map/pallas_call | solution.py:284
  (18 shorter events, 0.1 us)
Async XLA Ops:
  0.6 31.2 %copy-start = (bf16[768,768]{1,0:T(8,128)(2,1)S(1)}, bf16[768,768]{1,0:T(8,128)(2,1)}, u32[]{:S(2)}) copy-start(bf16[768,768]{1,0:T(8,128)(2,1)} %refs_5_.1) | copy-start | bytes 3538948
  0.6 12.6 %collective-permute-start.1 = (bf16[4,8,768]{2,1,0:T(8,128)(2,1)}, bf16[4,8,768]{2,1,0:T(8,128)(2,1)S(1)}, u32[]{:S(2)}, u32[]{:S(2)}) collective-permute-start(bf16[4,8,768]{2,1,0:T(8,128)(2,1)} %param.12), channel_id=1, source_target_pairs={{0,8},{1,9},{2,10},{3,11},{4,12},{5,13},{6,14},{7,15},{8,0},{9,1},... | collective-permute-start | bytes 147464 | tf_op jit(solution)/shard_map/ppermute | solution.py:312
  4.7 8.5 %collective-permute-start = (bf16[4,8,768]{2,1,0:T(8,128)(2,1)}, bf16[4,8,768]{2,1,0:T(8,128)(2,1)S(1)}, u32[]{:S(2)}, u32[]{:S(2)}) collective-permute-start(bf16[4,8,768]{2,1,0:T(8,128)(2,1)} %param.12), channel_id=1, source_target_pairs={{0,4},{1,5},{2,6},{3,7},{4,8},{5,9},{6,10},{7,11},{8,12},{9,13},{1... | collective-permute-start | bytes 147464 | tf_op jit(solution)/shard_map/ppermute | solution.py:312
  6.3 6.9 %collective-permute-start.2 = (bf16[4,8,768]{2,1,0:T(8,128)(2,1)}, bf16[4,8,768]{2,1,0:T(8,128)(2,1)S(1)}, u32[]{:S(2)}, u32[]{:S(2)}) collective-permute-start(bf16[4,8,768]{2,1,0:T(8,128)(2,1)} %param.12), channel_id=1, source_target_pairs={{0,12},{1,13},{2,14},{3,15},{4,0},{5,1},{6,2},{7,3},{8,4},{9,5},{1... | collective-permute-start | bytes 147464 | tf_op jit(solution)/shard_map/ppermute | solution.py:312
  8.6 7.2 %collective-permute-start.7 = (bf16[4,8,768]{2,1,0:T(8,128)(2,1)}, bf16[4,8,768]{2,1,0:T(8,128)(2,1)S(1)}, u32[]{:S(2)}, u32[]{:S(2)}) collective-permute-start(bf16[4,8,768]{2,1,0:T(8,128)(2,1)} %param.13), channel_id=1, source_target_pairs={{0,4},{1,5},{2,6},{3,7},{4,8},{5,9},{6,10},{7,11},{8,12},{9,13},{1... | collective-permute-start | bytes 147464 | tf_op jit(solution)/shard_map/ppermute | solution.py:312
  8.6 10.4 %collective-permute-start.9 = (bf16[4,8,768]{2,1,0:T(8,128)(2,1)}, bf16[4,8,768]{2,1,0:T(8,128)(2,1)S(1)}, u32[]{:S(2)}, u32[]{:S(2)}) collective-permute-start(bf16[4,8,768]{2,1,0:T(8,128)(2,1)} %param.13), channel_id=1, source_target_pairs={{0,12},{1,13},{2,14},{3,15},{4,0},{5,1},{6,2},{7,3},{8,4},{9,5},{1... | collective-permute-start | bytes 147464 | tf_op jit(solution)/shard_map/ppermute | solution.py:312
  13.2 5.2 %collective-permute-start.8 = (bf16[4,8,768]{2,1,0:T(8,128)(2,1)}, bf16[4,8,768]{2,1,0:T(8,128)(2,1)S(1)}, u32[]{:S(2)}, u32[]{:S(2)}) collective-permute-start(bf16[4,8,768]{2,1,0:T(8,128)(2,1)} %param.13), channel_id=1, source_target_pairs={{0,8},{1,9},{2,10},{3,11},{4,12},{5,13},{6,14},{7,15},{8,0},{9,1},... | collective-permute-start | bytes 147464 | tf_op jit(solution)/shard_map/ppermute | solution.py:312
  13.3 5.7 %collective-permute-start.4 = (bf16[4,32,768]{2,1,0:T(8,128)(2,1)S(1)}, bf16[4,32,768]{2,1,0:T(8,128)(2,1)S(1)}, u32[]{:S(2)}, u32[]{:S(2)}) collective-permute-start(bf16[4,32,768]{2,1,0:T(8,128)(2,1)S(1)} %constant_dynamic-update-slice_fusion.refs_1_), channel_id=1, source_target_pairs={{0,2},{1,3},{2,0},{3,1},{4,6},{5,7},{6,4},{7,5},{8,10},{9,11},{10,... | collective-permute-start | bytes 589832 | tf_op jit(solution)/shard_map/ppermute | solution.py:312
  14.9 6.0 %collective-permute-start.3 = (bf16[4,32,768]{2,1,0:T(8,128)(2,1)S(1)}, bf16[4,32,768]{2,1,0:T(8,128)(2,1)S(1)}, u32[]{:S(2)}, u32[]{:S(2)}) collective-permute-start(bf16[4,32,768]{2,1,0:T(8,128)(2,1)S(1)} %constant_dynamic-update-slice_fusion.refs_1_), channel_id=1, source_target_pairs={{0,1},{1,0},{2,3},{3,2},{4,5},{5,4},{6,7},{7,6},{8,9},{9,8},{10,11... | collective-permute-start | bytes 589832 | tf_op jit(solution)/shard_map/ppermute | solution.py:312
  14.9 0.8 %copy-start.2 = (bf16[4,8,768]{2,1,0:T(8,128)(2,1)S(1)}, bf16[4,8,768]{2,1,0:T(8,128)(2,1)}, u32[]{:S(2)}) copy-start(bf16[4,8,768]{2,1,0:T(8,128)(2,1)} %q_hbm) | copy-start | bytes 147460
  15.7 7.8 %copy-start.5 = (f32[12]{0:T(128)S(1)}, f32[12]{0:T(128)}, u32[]{:S(2)}) copy-start(f32[12]{0:T(128)} %factor_ref.1) | copy-start | bytes 148
  15.7 16.1 %copy-start.3 = (bf16[4,8,768]{2,1,0:T(8,128)(2,1)S(1)}, bf16[4,8,768]{2,1,0:T(8,128)(2,1)}, u32[]{:S(2)}) copy-start(bf16[4,8,768]{2,1,0:T(8,128)(2,1)} %refs_6_.1) | copy-start | bytes 147460
  15.7 16.1 %copy-start.4 = (f32[768]{0:T(1024)S(1)}, f32[768]{0:T(1024)}, u32[]{:S(2)}) copy-start(f32[768]{0:T(1024)} %refs_7_.1) | copy-start | bytes 9220
  19.0 1.8 %collective-permute-start.5 = (bf16[4,32,768]{2,1,0:T(8,128)(2,1)S(1)}, bf16[4,32,768]{2,1,0:T(8,128)(2,1)S(1)}, u32[]{:S(2)}, u32[]{:S(2)}) collective-permute-start(bf16[4,32,768]{2,1,0:T(8,128)(2,1)S(1)} %collective-permute-done.4.refs_2_), channel_id=1, source_target_pairs={{0,1},{1,0},{2,3},{3,2},{4,5},{5,4},{6,7},{7,6},{8,9},{9,8},{10,11... | collective-permute-start | bytes 589832 | tf_op jit(solution)/shard_map/ppermute | solution.py:312
  19.0 7.4 %collective-permute-start.10 = (bf16[4,32,768]{2,1,0:T(8,128)(2,1)S(1)}, bf16[4,32,768]{2,1,0:T(8,128)(2,1)S(1)}, u32[]{:S(2)}, u32[]{:S(2)}) collective-permute-start(bf16[4,32,768]{2,1,0:T(8,128)(2,1)S(1)} %constant_dynamic-update-slice_fusion.4.refs_1_), channel_id=1, source_target_pairs={{0,2},{1,3},{2,0},{3,1},{4,6},{5,7},{6,4},{7,5},{8,10},{9,11},{10,... | collective-permute-start | bytes 589832 | tf_op jit(solution)/shard_map/ppermute | solution.py:312
  21.1 4.2 %collective-permute-start.6 = (f32[96,128]{1,0:T(8,128)S(1)}, f32[96,128]{1,0:T(8,128)S(1)}, u32[]{:S(2)}, u32[]{:S(2)}) collective-permute-start(f32[96,128]{1,0:T(8,128)S(1)} %shard_map.115.refs_0_), channel_id=1, source_target_pairs={{0,16},{16,0},{1,17},{17,1},{2,18},{18,2},{3,19},{19,3},{4,20},{20... | collective-permute-start | bytes 147464 | tf_op jit(solution)/shard_map/ppermute | solution.py:402
  23.4 8.3 %collective-permute-start.11 = (bf16[4,32,768]{2,1,0:T(8,128)(2,1)S(1)}, bf16[4,32,768]{2,1,0:T(8,128)(2,1)S(1)}, u32[]{:S(2)}, u32[]{:S(2)}) collective-permute-start(bf16[4,32,768]{2,1,0:T(8,128)(2,1)S(1)} %constant_dynamic-update-slice_fusion.4.refs_1_), channel_id=1, source_target_pairs={{0,1},{1,0},{2,3},{3,2},{4,5},{5,4},{6,7},{7,6},{8,9},{9,8},{10,11... | collective-permute-start | bytes 589832 | tf_op jit(solution)/shard_map/ppermute | solution.py:312
  26.4 5.4 %collective-permute-start.12 = (bf16[4,32,768]{2,1,0:T(8,128)(2,1)S(1)}, bf16[4,32,768]{2,1,0:T(8,128)(2,1)S(1)}, u32[]{:S(2)}, u32[]{:S(2)}) collective-permute-start(bf16[4,32,768]{2,1,0:T(8,128)(2,1)S(1)} %collective-permute-done.10.refs_2_), channel_id=1, source_target_pairs={{0,1},{1,0},{2,3},{3,2},{4,5},{5,4},{6,7},{7,6},{8,9},{9,8},{10,11... | collective-permute-start | bytes 589832 | tf_op jit(solution)/shard_map/ppermute | solution.py:312
  26.4 14.3 %all-to-all-start = ((f32[16,24,128]{2,1,0:T(8,128)}), f32[16,24,128]{2,1,0:T(8,128)S(1)}, u32[]{:S(2)}, u32[]{:S(2)}) async-start(f32[16,24,128]{2,1,0:T(8,128)} %get-tuple-element.27), calls=%async_computation | async-start | bytes 393216 | tf_op jit(solution)/shard_map/all_to_all | solution.py:434
  31.7 3.4 %copy-start.6 = (bf16[768,1152]{1,0:T(8,128)(2,1)S(1)}, bf16[768,1152]{1,0:T(8,128)(2,1)}, u32[]{:S(2)}) copy-start(bf16[768,1152]{1,0:T(8,128)(2,1)} %param.16) | copy-start | bytes 5308420
  33.0 4.1 %collective-permute-start.13 = (bf16[32,768]{1,0:T(8,128)(2,1)S(1)}, bf16[32,768]{1,0:T(8,128)(2,1)S(1)}, u32[]{:S(2)}, u32[]{:S(2)}) collective-permute-start(bf16[32,768]{1,0:T(8,128)(2,1)S(1)} %get-tuple-element.29.refs_0_), channel_id=1, source_target_pairs={{0,16},{16,0},{1,17},{17,1},{2,18},{18,2},{3,19},{19,3},{4,20},{20... | collective-permute-start | bytes 147464 | tf_op jit(solution)/shard_map/ppermute | solution.py:442
  35.3 7.6 %copy-start.1 = (bf16[768,768]{1,0:T(8,128)(2,1)S(1)}, bf16[768,768]{1,0:T(8,128)(2,1)}, u32[]{:S(2)}) copy-start(bf16[768,768]{1,0:T(8,128)(2,1)} %refs_1_) | copy-start | bytes 3538948
  37.5 5.4 %collective-permute-start.14 = (bf16[64,1152]{1,0:T(8,128)(2,1)S(1)}, bf16[64,1152]{1,0:T(8,128)(2,1)S(1)}, u32[]{:S(2)}, u32[]{:S(2)}) collective-permute-start(bf16[64,1152]{1,0:T(8,128)(2,1)S(1)} %shard_map.119.own_ref), channel_id=1, source_target_pairs={{0,16},{16,0},{1,17},{17,1},{2,18},{18,2},{3,19},{19,3},{4,20},{20... | collective-permute-start | bytes 442376 | tf_op jit(solution)/shard_map/ppermute | solution.py:456

commit v13 on v12

--- a/solution.py
+++ b/solution.py
@@ -142,7 +142,8 @@
 
 def mix_kernel(head, v_count, *refs):
     w_ref, v_refs = refs[0], refs[1 : 1 + v_count]
-    closing_ref, skip_ref, gain_ref, hidden_ref, normed_ref, mixed = refs[1 + v_count :]
+    closing_ref, skip_ref, gain_ref, hidden_ref, normed_ref, one_ref, mixed = refs[1 + v_count :]
+    one_ref[...] = jnp.ones_like(one_ref)
     rows, sites, embed = skip_ref.shape
     width = lane_block(embed, head)
     group = width // head
@@ -357,7 +358,9 @@
     key_first = [lateral_matched_vectors] + send_all([lateral_matched_vectors], pos_count, outer)
     key_parts = [jnp.concatenate(key_first, axis=1)]
     value_first = [after(lateral_carried_vectors, key_parts[0])]
-    value_first += send_all([lateral_carried_vectors], pos_count, outer)
+    value_first += [
+        send_pos(lateral_carried_vectors, pos_count, *outer, delta) for delta in range(outer[1] - 1, 0, -1)
+    ][::-1]
     masked = call(
         functools.partial(query_kernel, head),
         jax.ShapeDtypeStruct((rows, heads * sites, width), BF16),
@@ -373,8 +376,11 @@
         jax.ShapeDtypeStruct((heads * sites, near), F32),
         [masked, *key_parts],
     )
-    value_first[1] = after(value_first[1], masked)
-    value_parts = [jnp.concatenate(value_first, axis=1)]
+    value_first[-1] = after(value_first[-1], masked)
+    value_own = jnp.zeros((rows, sites * outer[1], embed), BF16)
+    for delta in [0, *range(outer[1] - 1, 0, -1)]:
+        value_own = lax.dynamic_update_slice(value_own, value_first[delta], (0, delta * sites, 0))
+    value_parts = [value_own]
     if middle:
         value_parts += send_all(value_parts, pos_count, middle)
     if len(stages) > 2:
@@ -416,11 +422,12 @@
     if len(stages) > 2:
         value_parts = value_parts[:1] + [after(part, pair_local) for part in value_parts[1:]]
         value_parts += send_all(value_parts, pos_count, stages[2])
-    hidden, normed = call(
+    hidden, normed, one = call(
         functools.partial(mix_kernel, head, len(value_parts)),
         (
             jax.ShapeDtypeStruct((cells, embed), F32),
             jax.ShapeDtypeStruct((cells, embed), BF16),
+            jax.ShapeDtypeStruct((1, columns), BF16),
         ),
         [
             shares,
@@ -440,7 +447,6 @@
     )
     if swapped:
         normed_all = [normed, lax.ppermute(normed, "seq", swap)]
-        one = jnp.minimum(jnp.abs(normed[0, 0]) + 1, 1)
         weight = upright_threefold_linear * one
     else:
         normed_all = [normed]

time: 44.7 us -> 43 us (0.962)
  other arithmetic: 0.24 us -> 1.74 us
  starting transfers between devices: 24.9 us -> 23.8 us
  waiting for transfers between devices: 7.98 us -> 7.14 us
  between operations: 2.17 us -> 1.46 us
  local copies, waits for them, and re-layouts: 2.98 us -> 2.46 us
    ppermute x12, starting transfers between devices: 15 us -> 13.2 us  [send_pos(): return lax.ppermute(array, 'pos', pairs)]
    mul x1, other arithmetic: 0.16 us -> 1.64 us  [per_device(): weight = upright_threefold_linear * one]
    dynamic_update_slice x0 -> x4, local copies, waits for them, and re-layouts: none -> 0.83 us  [per_device(): lax.dynamic_update_slice(value_own, value_first[delta], (0, delta * sites...]
    unnamed x20 -> x15, local copies, waits for them, and re-layouts: 2.45 us -> 1.63 us
    ppermute x1, waiting for transfers between devices: 1.73 us -> 0.91 us  [per_device(): normed_all = [normed, lax.ppermute(normed, 'seq', swap)]]
    all_to_all x1, starting transfers between devices: 5.33 us -> 5.88 us  [per_device(): lax.all_to_all(pair_local, 'pos', split_axis=0, concat_axis=0, tiled=True)]
    slice x1 -> x0, local copies, waits for them, and re-layouts: 0.51 us -> none  [per_device(): one = jnp.minimum(jnp.abs(normed[0, 0]) + 1, 1)]
    ppermute x1, waiting for transfers between devices: 1.09 us -> 0.63 us  [per_device(): lax.ppermute(projected, 'seq', swap)]
  transfers between devices with their start and end apart: 16 -> 16, of which waited for: 6 -> 6; matrix products, arithmetic and copies ran while one was open for 5% -> 8% of each run, Pallas kernels for 10% -> 11%
where the time goes in v13:
time: 43 us; the launch traced here: 42.6 us
  starting transfers between devices  23.8 us (55%)
  waiting for transfers between devices  7.14 us (17%)
  Pallas kernels  6.02 us (14%)
  local copies, waits for them, and re-layouts  2.46 us (6%)
  other arithmetic  1.74 us (4%)
  between operations  1.46 us (3%)
    ppermute x12, starting transfers between devices, send_pos(): return lax.ppermute(array, 'pos', pairs)  13.2 us
    pallas_call x9, Pallas kernels, call(): pl.pallas_call(kernel, out_shape=out_shape, in_specs=specs, out_specs=jax...  6.02 us
    all_to_all x1, starting transfers between devices, per_device(): lax.all_to_all(pair_local, 'pos', split_axis=0, concat_axis=0, tiled=True)  5.88 us
    ppermute x12, waiting for transfers between devices, send_pos(): return lax.ppermute(array, 'pos', pairs)  2.43 us
    all_to_all x1, waiting for transfers between devices, per_device(): lax.all_to_all(pair_local, 'pos', split_axis=0, concat_axis=0, tiled=True)  2.15 us
    mul x1, other arithmetic, per_device(): weight = upright_threefold_linear * one  1.64 us
    unnamed x15, local copies, waits for them, and re-layouts  1.63 us
    ppermute x1, starting transfers between devices, per_device(): lax.ppermute(projected, 'seq', swap)  1.56 us
  transfers between devices with their start and end apart: 16, of which 6 were waited for; matrix products, arithmetic and copies ran while one was open for 8% of the time, Pallas kernels for 11%

profile of v13, /device:TPU:0, one launch (start us, length us, event | category | flops | bytes accessed | tf_op | source)
XLA Modules:
  0.0 42.6 jit_solution(5331263530381509590)
XLA Ops:
  0.6 0.0 copy-start
  0.6 4.1 %collective-permute-start.1 = (bf16[4,8,768]{2,1,0:T(8,128)(2,1)}, bf16[4,8,768]{2,1,0:T(8,128)(2,1)S(1)}, u32[]{:S(2)}, u32[]{:S(2)}) collective-permute-start(bf16[4,8,768]{2,1,0:T(8,128)(2,1)} %param.12), channel_id=1, source_target_pairs={{0,8},{1,9},{2,10},{3,11},{4,12},{5,13},{6,14},{7,15},{8,0},{9,1},... | collective-permute-start | bytes 147464 | tf_op jit(solution)/shard_map/ppermute | solution.py:313
  4.7 1.6 %collective-permute-start = (bf16[4,8,768]{2,1,0:T(8,128)(2,1)}, bf16[4,8,768]{2,1,0:T(8,128)(2,1)S(1)}, u32[]{:S(2)}, u32[]{:S(2)}) collective-permute-start(bf16[4,8,768]{2,1,0:T(8,128)(2,1)} %param.12), channel_id=1, source_target_pairs={{0,4},{1,5},{2,6},{3,7},{4,8},{5,9},{6,10},{7,11},{8,12},{9,13},{1... | collective-permute-start | bytes 147464 | tf_op jit(solution)/shard_map/ppermute | solution.py:313
  6.3 2.2 %collective-permute-start.2 = (bf16[4,8,768]{2,1,0:T(8,128)(2,1)}, bf16[4,8,768]{2,1,0:T(8,128)(2,1)S(1)}, u32[]{:S(2)}, u32[]{:S(2)}) collective-permute-start(bf16[4,8,768]{2,1,0:T(8,128)(2,1)} %param.12), channel_id=1, source_target_pairs={{0,12},{1,13},{2,14},{3,15},{4,0},{5,1},{6,2},{7,3},{8,4},{9,5},{1... | collective-permute-start | bytes 147464 | tf_op jit(solution)/shard_map/ppermute | solution.py:313
  8.6 0.0 collective-permute-start.7
  8.6 2.0 %collective-permute-start.9 = (bf16[4,8,768]{2,1,0:T(8,128)(2,1)}, bf16[4,8,768]{2,1,0:T(8,128)(2,1)S(1)}, u32[]{:S(2)}, u32[]{:S(2)}) collective-permute-start(bf16[4,8,768]{2,1,0:T(8,128)(2,1)} %param.13), channel_id=1, source_target_pairs={{0,4},{1,5},{2,6},{3,7},{4,8},{5,9},{6,10},{7,11},{8,12},{9,13},{1... | collective-permute-start | bytes 147464 | tf_op jit(solution)/shard_map/ppermute | solution.py:313
  10.6 0.8 %constant_dynamic-update-slice_fusion.3 = bf16[4,32,768]{2,1,0:T(8,128)(2,1)S(1)} fusion(bf16[4,8,768]{2,1,0:T(8,128)(2,1)} %param.12), kind=kLoop, calls=%fused_computation.4 | loop fusion | bytes 98304
  11.4 0.0 collective-permute-done
  11.4 0.0 collective-permute-start.8
  11.4 0.0 collective-permute-done.1
  11.5 0.0 collective-permute-done.2
  11.5 1.6 %collective-permute-start.4 = (bf16[4,32,768]{2,1,0:T(8,128)(2,1)S(1)}, bf16[4,32,768]{2,1,0:T(8,128)(2,1)S(1)}, u32[]{:S(2)}, u32[]{:S(2)}) collective-permute-start(bf16[4,32,768]{2,1,0:T(8,128)(2,1)S(1)} %constant_dynamic-update-slice_fusion.refs_1_), channel_id=1, source_target_pairs={{0,2},{1,3},{2,0},{3,1},{4,6},{5,7},{6,4},{7,5},{8,10},{9,11},{10,... | collective-permute-start | bytes 589832 | tf_op jit(solution)/shard_map/ppermute | solution.py:313
  13.1 0.0 collective-permute-start.3
  13.1 0.8 %copy-done.2 = bf16[4,8,768]{2,1,0:T(8,128)(2,1)S(1)} copy-done((bf16[4,8,768]{2,1,0:T(8,128)(2,1)S(1)}, bf16[4,8,768]{2,1,0:T(8,128)(2,1)}, u32[]{:S(2)}) %copy-start.2) | copy-done | bytes 49176
  13.9 0.1 shard_map.113.refs_0_
  14.0 0.0 collective-permute-done.7
  14.0 0.8 %dynamic_update_slice.12 = bf16[4,32,768]{2,1,0:T(8,128)(2,1)S(1)} pad(bf16[4,8,768]{2,1,0:T(8,128)(2,1)} %param.13, bf16[]{:T(256)} %constant.6.clone.1), padding=0_0x0_24x0_0 | pad | bytes 245762 | tf_op jit(solution)/shard_map/dynamic_update_slice | solution.py:382
  14.8 1.8 %collective-permute-done.8 = bf16[4,8,768]{2,1,0:T(8,128)(2,1)S(1)} collective-permute-done((bf16[4,8,768]{2,1,0:T(8,128)(2,1)}, bf16[4,8,768]{2,1,0:T(8,128)(2,1)S(1)}, u32[]{:S(2)}, u32[]{:S(2)}) %collective-permute-start.8) | collective-permute-done | bytes 49184 | tf_op jit(solution)/shard_map/ppermute | solution.py:313
  16.6 0.6 %collective-permute-done.4.refs_2_ = bf16[4,32,768]{2,1,0:T(8,128)(2,1)S(1)} collective-permute-done((bf16[4,32,768]{2,1,0:T(8,128)(2,1)S(1)}, bf16[4,32,768]{2,1,0:T(8,128)(2,1)S(1)}, u32[]{:S(2)}, u32[]{:S(2)}) %collective-permute-start.4) | collective-permute-done | bytes 196640 | tf_op jit(solution)/shard_map/ppermute | solution.py:313
  17.2 0.0 collective-permute-start.5
  17.2 0.0 collective-permute-done.9
  17.2 1.6 %collective-permute-start.10 = (bf16[4,32,768]{2,1,0:T(8,128)(2,1)S(1)}, bf16[4,32,768]{2,1,0:T(8,128)(2,1)S(1)}, u32[]{:S(2)}, u32[]{:S(2)}) collective-permute-start(bf16[4,32,768]{2,1,0:T(8,128)(2,1)S(1)} %constant_dynamic-update-slice_fusion.4.refs_1_), channel_id=1, source_target_pairs={{0,2},{1,3},{2,0},{3,1},{4,6},{5,7},{6,4},{7,5},{8,10},{9,11},{10,... | collective-permute-start | bytes 589832 | tf_op jit(solution)/shard_map/ppermute | solution.py:313
  18.8 0.2 shard_map.114.refs_3_
  19.0 0.0 collective-permute-done.3.refs_1_
  19.0 0.0 collective-permute-done.5.refs_2_
  19.1 0.3 shard_map.115.refs_0_
  19.4 1.6 %collective-permute-start.6 = (f32[96,128]{1,0:T(8,128)S(1)}, f32[96,128]{1,0:T(8,128)S(1)}, u32[]{:S(2)}, u32[]{:S(2)}) collective-permute-start(f32[96,128]{1,0:T(8,128)S(1)} %shard_map.115.refs_0_), channel_id=1, source_target_pairs={{0,16},{16,0},{1,17},{17,1},{2,18},{18,2},{3,19},{19,3},{4,20},{20... | collective-permute-start | bytes 147464 | tf_op jit(solution)/shard_map/ppermute | solution.py:408
  20.9 0.1 pad_add_fusion.scalar_ref
  21.6 0.1 collective-permute-start.11
  21.7 0.8 %shard_map.116 = (f32[24,128]{1,0:T(8,128)S(1)}, f32[128,128]{1,0:T(8,128)S(1)}, f32[8,128]{1,0:T(8,128)S(1)}, f32[128,64]{1,0:T(8,128)S(1)}, bf16[768,128]{1,0:...) custom-call(s32[2]{0:T(128)S(1)} %pad_add_fusion.scalar_ref, f32[12]{0:T(128)S(1)} %copy-done.5, f32[1]{0:T(128)S(6)} %copy.18.offset_ref), custom_call_target="tpu_custom_call" | custom-call | flops 1000000 | bytes 1000000 | tf_op jit(solution)/shard_map/pallas_call | solution.py:285
  22.5 1.0 %collective-permute-done.6.refs_1_ = f32[96,128]{1,0:T(8,128)S(1)} collective-permute-done((f32[96,128]{1,0:T(8,128)S(1)}, f32[96,128]{1,0:T(8,128)S(1)}, u32[]{:S(2)}, u32[]{:S(2)}) %collective-permute-start.6) | collective-permute-done | bytes 49184 | tf_op jit(solution)/shard_map/ppermute | solution.py:408
  23.5 1.1 %shard_map.117 = (bf16[96,128]{1,0:T(8,128)(2,1)S(1)}, f32[16,24,128]{2,1,0:T(8,128)}) custom-call(f32[96,128]{1,0:T(8,128)S(1)} %shard_map.115.refs_0_, f32[96,128]{1,0:T(8,128)S(1)} %collective-permute-done.6.refs_1_, f32[24,128]{1,0:T(8,128)S(1)} %get-tuple-element.24.refs_2_.factor_ref, f32[128,128]{1,0:T(8,128)S(1)} %get-tuple-element.22.refs_3_), custom_call_target="tpu_custom_call" | custom-call | flops 1000000 | bytes 1000000 | tf_op jit(solution)/shard_map/pallas_call | solution.py:285
  24.6 0.0 collective-permute-done.10.refs_2_
  24.6 0.0 collective-permute-start.12
  24.6 5.9 %all-to-all-start = ((f32[16,24,128]{2,1,0:T(8,128)}), f32[16,24,128]{2,1,0:T(8,128)S(1)}, u32[]{:S(2)}, u32[]{:S(2)}) async-start(f32[16,24,128]{2,1,0:T(8,128)} %get-tuple-element.28), calls=%async_computation | async-start | bytes 393216 | tf_op jit(solution)/shard_map/all_to_all | solution.py:441
  30.5 0.0 collective-permute-done.11.refs_3_
  30.5 0.0 collective-permute-done.12.refs_4_
  30.6 0.6 %shard_map.118 = (f32[32,768]{1,0:T(8,128)S(1)}, bf16[32,768]{1,0:T(8,128)(2,1)S(1)}, bf16[1,1152]{1,0:T(2,128)(2,1)S(1)}) custom-call(bf16[96,128]{1,0:T(8,128)(2,1)S(1)} %get-tuple-element.25.refs_0_, bf16[4,32,768]{2,1,0:T(8,128)(2,1)S(1)} %constant_dynamic-update-slice_fusion.4.refs_1_, bf16[4,32,768]{2,1,0:T(8,128)(2,1)S(1)} %collective-permute-done.10.refs_2_, ...), custom_call_target="tpu_custom_call" | custom-call | flops 1000000 | bytes 1000000 | tf_op jit(solution)/shard_map/pallas_call | solution.py:285
  31.2 1.6 %collective-permute-start.13 = (bf16[32,768]{1,0:T(8,128)(2,1)S(1)}, bf16[32,768]{1,0:T(8,128)(2,1)S(1)}, u32[]{:S(2)}, u32[]{:S(2)}) collective-permute-start(bf16[32,768]{1,0:T(8,128)(2,1)S(1)} %get-tuple-element.30.refs_0_), channel_id=1, source_target_pairs={{0,16},{16,0},{1,17},{17,1},{2,18},{18,2},{3,19},{19,3},{4,20},{20... | collective-permute-start | bytes 147464 | tf_op jit(solution)/shard_map/ppermute | solution.py:449
  32.8 1.6 %broadcast_multiply_fusion.refs_2_ = bf16[768,1152]{1,0:T(8,128)(2,1)S(1)} fusion(bf16[768,1152]{1,0:T(8,128)(2,1)} %param.16, bf16[1152]{0:T(1024)(128)(2,1)S(1)} %reduce), kind=kLoop, calls=%fused_computation | loop fusion | flops 884736 | bytes 3541248 | tf_op jit(solution)/shard_map/mul | solution.py:450
  34.4 0.0 copy-start.1
  34.4 0.9 %collective-permute-done.13.refs_1_ = bf16[32,768]{1,0:T(8,128)(2,1)S(1)} collective-permute-done((bf16[32,768]{1,0:T(8,128)(2,1)S(1)}, bf16[32,768]{1,0:T(8,128)(2,1)S(1)}, u32[]{:S(2)}, u32[]{:S(2)}) %collective-permute-start.13) | collective-permute-done | bytes 49184 | tf_op jit(solution)/shard_map/ppermute | solution.py:449
  35.4 0.4 %shard_map.119.own_ref = bf16[64,1152]{1,0:T(8,128)(2,1)S(1)} custom-call(bf16[32,768]{1,0:T(8,128)(2,1)S(1)} %get-tuple-element.30.refs_0_, bf16[32,768]{1,0:T(8,128)(2,1)S(1)} %collective-permute-done.13.refs_1_, bf16[768,1152]{1,0:T(8,128)(2,1)S(1)} %broadcast_multiply_fusion.refs_2_), custom_call_target="tpu_custom_call" | custom-call | flops 1000000 | bytes 1000000 | tf_op jit(solution)/shard_map/pallas_call | solution.py:285
  35.8 1.6 %collective-permute-start.14 = (bf16[64,1152]{1,0:T(8,128)(2,1)S(1)}, bf16[64,1152]{1,0:T(8,128)(2,1)S(1)}, u32[]{:S(2)}, u32[]{:S(2)}) collective-permute-start(bf16[64,1152]{1,0:T(8,128)(2,1)S(1)} %shard_map.119.own_ref), channel_id=1, source_target_pairs={{0,16},{16,0},{1,17},{17,1},{2,18},{18,2},{3,19},{19,3},{4,20},{20... | collective-permute-start | bytes 442376 | tf_op jit(solution)/shard_map/ppermute | solution.py:462
  37.3 2.2 %all-to-all-done.pair_ref = f32[16,24,128]{2,1,0:T(8,128)S(1)} async-done(((f32[16,24,128]{2,1,0:T(8,128)}), f32[16,24,128]{2,1,0:T(8,128)S(1)}, u32[]{:S(2)}, u32[]{:S(2)}) %all-to-all-start) | async-done | bytes 196640 | tf_op jit(solution)/shard_map/all_to_all | solution.py:441
  39.5 1.0 %shard_map.121 = f32[8,64]{1,0:T(8,128)} custom-call(f32[16,24,128]{2,1,0:T(8,128)S(1)} %all-to-all-done.pair_ref, f32[24,128]{1,0:T(8,128)S(1)} %get-tuple-element.24.refs_2_.factor_ref, f32[8,128]{1,0:T(8,128)S(1)} %get-tuple-element.36.own_ref, f32[128,64]{1,0:T(8,128)S(1)} %get-tuple-element.37.slab_ref), custom_call_target="tpu_custom_call" | custom-call | flops 1000000 | bytes 1000000 | tf_op jit(solution)/shard_map/pallas_call | solution.py:285
  40.5 0.6 %collective-permute-done.14.other_ref = bf16[64,1152]{1,0:T(8,128)(2,1)S(1)} collective-permute-done((bf16[64,1152]{1,0:T(8,128)(2,1)S(1)}, bf16[64,1152]{1,0:T(8,128)(2,1)S(1)}, u32[]{:S(2)}, u32[]{:S(2)}) %collective-permute-start.14) | collective-permute-done | bytes 147488 | tf_op jit(solution)/shard_map/ppermute | solution.py:462
  41.2 1.4 %shard_map.120 = bf16[4,8,768]{2,1,0:T(8,128)(2,1)} custom-call(bf16[64,1152]{1,0:T(8,128)(2,1)S(1)} %shard_map.119.own_ref, bf16[64,1152]{1,0:T(8,128)(2,1)S(1)} %collective-permute-done.14.other_ref, f32[32,768]{1,0:T(8,128)S(1)} %get-tuple-element.32.refs_0_, bf16[768,768]{1,0:T(8,128)(2,1)S(1)} %copy-done.1, ...), custom_call_target="tpu_custom_call" | custom-call | flops 1000000 | bytes 1000000 | tf_op jit(solution)/shard_map/pallas_call | solution.py:285
  (16 shorter events, 0.1 us)
Async XLA Ops:
  0.6 29.9 %copy-start = (bf16[768,768]{1,0:T(8,128)(2,1)S(1)}, bf16[768,768]{1,0:T(8,128)(2,1)}, u32[]{:S(2)}) copy-start(bf16[768,768]{1,0:T(8,128)(2,1)} %refs_5_.1) | copy-start | bytes 3538948
  0.6 10.8 %collective-permute-start.1 = (bf16[4,8,768]{2,1,0:T(8,128)(2,1)}, bf16[4,8,768]{2,1,0:T(8,128)(2,1)S(1)}, u32[]{:S(2)}, u32[]{:S(2)}) collective-permute-start(bf16[4,8,768]{2,1,0:T(8,128)(2,1)} %param.12), channel_id=1, source_target_pairs={{0,8},{1,9},{2,10},{3,11},{4,12},{5,13},{6,14},{7,15},{8,0},{9,1},... | collective-permute-start | bytes 147464 | tf_op jit(solution)/shard_map/ppermute | solution.py:313
  4.7 6.7 %collective-permute-start = (bf16[4,8,768]{2,1,0:T(8,128)(2,1)}, bf16[4,8,768]{2,1,0:T(8,128)(2,1)S(1)}, u32[]{:S(2)}, u32[]{:S(2)}) collective-permute-start(bf16[4,8,768]{2,1,0:T(8,128)(2,1)} %param.12), channel_id=1, source_target_pairs={{0,4},{1,5},{2,6},{3,7},{4,8},{5,9},{6,10},{7,11},{8,12},{9,13},{1... | collective-permute-start | bytes 147464 | tf_op jit(solution)/shard_map/ppermute | solution.py:313
  6.3 5.1 %collective-permute-start.2 = (bf16[4,8,768]{2,1,0:T(8,128)(2,1)}, bf16[4,8,768]{2,1,0:T(8,128)(2,1)S(1)}, u32[]{:S(2)}, u32[]{:S(2)}) collective-permute-start(bf16[4,8,768]{2,1,0:T(8,128)(2,1)} %param.12), channel_id=1, source_target_pairs={{0,12},{1,13},{2,14},{3,15},{4,0},{5,1},{6,2},{7,3},{8,4},{9,5},{1... | collective-permute-start | bytes 147464 | tf_op jit(solution)/shard_map/ppermute | solution.py:313
  8.6 5.4 %collective-permute-start.7 = (bf16[4,8,768]{2,1,0:T(8,128)(2,1)}, bf16[4,8,768]{2,1,0:T(8,128)(2,1)S(1)}, u32[]{:S(2)}, u32[]{:S(2)}) collective-permute-start(bf16[4,8,768]{2,1,0:T(8,128)(2,1)} %param.13), channel_id=1, source_target_pairs={{0,12},{1,13},{2,14},{3,15},{4,0},{5,1},{6,2},{7,3},{8,4},{9,5},{1... | collective-permute-start | bytes 147464 | tf_op jit(solution)/shard_map/ppermute | solution.py:313
  8.6 8.6 %collective-permute-start.9 = (bf16[4,8,768]{2,1,0:T(8,128)(2,1)}, bf16[4,8,768]{2,1,0:T(8,128)(2,1)S(1)}, u32[]{:S(2)}, u32[]{:S(2)}) collective-permute-start(bf16[4,8,768]{2,1,0:T(8,128)(2,1)} %param.13), channel_id=1, source_target_pairs={{0,4},{1,5},{2,6},{3,7},{4,8},{5,9},{6,10},{7,11},{8,12},{9,13},{1... | collective-permute-start | bytes 147464 | tf_op jit(solution)/shard_map/ppermute | solution.py:313
  11.4 5.2 %collective-permute-start.8 = (bf16[4,8,768]{2,1,0:T(8,128)(2,1)}, bf16[4,8,768]{2,1,0:T(8,128)(2,1)S(1)}, u32[]{:S(2)}, u32[]{:S(2)}) collective-permute-start(bf16[4,8,768]{2,1,0:T(8,128)(2,1)} %param.13), channel_id=1, source_target_pairs={{0,8},{1,9},{2,10},{3,11},{4,12},{5,13},{6,14},{7,15},{8,0},{9,1},... | collective-permute-start | bytes 147464 | tf_op jit(solution)/shard_map/ppermute | solution.py:313
  11.5 5.7 %collective-permute-start.4 = (bf16[4,32,768]{2,1,0:T(8,128)(2,1)S(1)}, bf16[4,32,768]{2,1,0:T(8,128)(2,1)S(1)}, u32[]{:S(2)}, u32[]{:S(2)}) collective-permute-start(bf16[4,32,768]{2,1,0:T(8,128)(2,1)S(1)} %constant_dynamic-update-slice_fusion.refs_1_), channel_id=1, source_target_pairs={{0,2},{1,3},{2,0},{3,1},{4,6},{5,7},{6,4},{7,5},{8,10},{9,11},{10,... | collective-permute-start | bytes 589832 | tf_op jit(solution)/shard_map/ppermute | solution.py:313
  13.1 6.0 %collective-permute-start.3 = (bf16[4,32,768]{2,1,0:T(8,128)(2,1)S(1)}, bf16[4,32,768]{2,1,0:T(8,128)(2,1)S(1)}, u32[]{:S(2)}, u32[]{:S(2)}) collective-permute-start(bf16[4,32,768]{2,1,0:T(8,128)(2,1)S(1)} %constant_dynamic-update-slice_fusion.refs_1_), channel_id=1, source_target_pairs={{0,1},{1,0},{2,3},{3,2},{4,5},{5,4},{6,7},{7,6},{8,9},{9,8},{10,11... | collective-permute-start | bytes 589832 | tf_op jit(solution)/shard_map/ppermute | solution.py:313
  13.1 0.8 %copy-start.2 = (bf16[4,8,768]{2,1,0:T(8,128)(2,1)S(1)}, bf16[4,8,768]{2,1,0:T(8,128)(2,1)}, u32[]{:S(2)}) copy-start(bf16[4,8,768]{2,1,0:T(8,128)(2,1)} %q_hbm) | copy-start | bytes 147460
  13.9 7.9 %copy-start.5 = (f32[12]{0:T(128)S(1)}, f32[12]{0:T(128)}, u32[]{:S(2)}) copy-start(f32[12]{0:T(128)} %factor_ref.1) | copy-start | bytes 148
  13.9 16.7 %copy-start.3 = (bf16[4,8,768]{2,1,0:T(8,128)(2,1)S(1)}, bf16[4,8,768]{2,1,0:T(8,128)(2,1)}, u32[]{:S(2)}) copy-start(bf16[4,8,768]{2,1,0:T(8,128)(2,1)} %refs_6_.1) | copy-start | bytes 147460
  13.9 16.7 %copy-start.4 = (f32[768]{0:T(1024)S(1)}, f32[768]{0:T(1024)}, u32[]{:S(2)}) copy-start(f32[768]{0:T(1024)} %refs_7_.1) | copy-start | bytes 9220
  17.2 1.8 %collective-permute-start.5 = (bf16[4,32,768]{2,1,0:T(8,128)(2,1)S(1)}, bf16[4,32,768]{2,1,0:T(8,128)(2,1)S(1)}, u32[]{:S(2)}, u32[]{:S(2)}) collective-permute-start(bf16[4,32,768]{2,1,0:T(8,128)(2,1)S(1)} %collective-permute-done.4.refs_2_), channel_id=1, source_target_pairs={{0,1},{1,0},{2,3},{3,2},{4,5},{5,4},{6,7},{7,6},{8,9},{9,8},{10,11... | collective-permute-start | bytes 589832 | tf_op jit(solution)/shard_map/ppermute | solution.py:313
  17.2 7.4 %collective-permute-start.10 = (bf16[4,32,768]{2,1,0:T(8,128)(2,1)S(1)}, bf16[4,32,768]{2,1,0:T(8,128)(2,1)S(1)}, u32[]{:S(2)}, u32[]{:S(2)}) collective-permute-start(bf16[4,32,768]{2,1,0:T(8,128)(2,1)S(1)} %constant_dynamic-update-slice_fusion.4.refs_1_), channel_id=1, source_target_pairs={{0,2},{1,3},{2,0},{3,1},{4,6},{5,7},{6,4},{7,5},{8,10},{9,11},{10,... | collective-permute-start | bytes 589832 | tf_op jit(solution)/shard_map/ppermute | solution.py:313
  19.4 4.2 %collective-permute-start.6 = (f32[96,128]{1,0:T(8,128)S(1)}, f32[96,128]{1,0:T(8,128)S(1)}, u32[]{:S(2)}, u32[]{:S(2)}) collective-permute-start(f32[96,128]{1,0:T(8,128)S(1)} %shard_map.115.refs_0_), channel_id=1, source_target_pairs={{0,16},{16,0},{1,17},{17,1},{2,18},{18,2},{3,19},{19,3},{4,20},{20... | collective-permute-start | bytes 147464 | tf_op jit(solution)/shard_map/ppermute | solution.py:408
  21.6 8.9 %collective-permute-start.11 = (bf16[4,32,768]{2,1,0:T(8,128)(2,1)S(1)}, bf16[4,32,768]{2,1,0:T(8,128)(2,1)S(1)}, u32[]{:S(2)}, u32[]{:S(2)}) collective-permute-start(bf16[4,32,768]{2,1,0:T(8,128)(2,1)S(1)} %constant_dynamic-update-slice_fusion.4.refs_1_), channel_id=1, source_target_pairs={{0,1},{1,0},{2,3},{3,2},{4,5},{5,4},{6,7},{7,6},{8,9},{9,8},{10,11... | collective-permute-start | bytes 589832 | tf_op jit(solution)/shard_map/ppermute | solution.py:313
  24.6 5.9 %collective-permute-start.12 = (bf16[4,32,768]{2,1,0:T(8,128)(2,1)S(1)}, bf16[4,32,768]{2,1,0:T(8,128)(2,1)S(1)}, u32[]{:S(2)}, u32[]{:S(2)}) collective-permute-start(bf16[4,32,768]{2,1,0:T(8,128)(2,1)S(1)} %collective-permute-done.10.refs_2_), channel_id=1, source_target_pairs={{0,1},{1,0},{2,3},{3,2},{4,5},{5,4},{6,7},{7,6},{8,9},{9,8},{10,11... | collective-permute-start | bytes 589832 | tf_op jit(solution)/shard_map/ppermute | solution.py:313
  24.6 14.9 %all-to-all-start = ((f32[16,24,128]{2,1,0:T(8,128)}), f32[16,24,128]{2,1,0:T(8,128)S(1)}, u32[]{:S(2)}, u32[]{:S(2)}) async-start(f32[16,24,128]{2,1,0:T(8,128)} %get-tuple-element.28), calls=%async_computation | async-start | bytes 393216 | tf_op jit(solution)/shard_map/all_to_all | solution.py:441
  31.2 4.2 %collective-permute-start.13 = (bf16[32,768]{1,0:T(8,128)(2,1)S(1)}, bf16[32,768]{1,0:T(8,128)(2,1)S(1)}, u32[]{:S(2)}, u32[]{:S(2)}) collective-permute-start(bf16[32,768]{1,0:T(8,128)(2,1)S(1)} %get-tuple-element.30.refs_0_), channel_id=1, source_target_pairs={{0,16},{16,0},{1,17},{17,1},{2,18},{18,2},{3,19},{19,3},{4,20},{20... | collective-permute-start | bytes 147464 | tf_op jit(solution)/shard_map/ppermute | solution.py:449
  34.4 6.8 %copy-start.1 = (bf16[768,768]{1,0:T(8,128)(2,1)S(1)}, bf16[768,768]{1,0:T(8,128)(2,1)}, u32[]{:S(2)}) copy-start(bf16[768,768]{1,0:T(8,128)(2,1)} %refs_1_) | copy-start | bytes 3538948
  35.8 5.4 %collective-permute-start.14 = (bf16[64,1152]{1,0:T(8,128)(2,1)S(1)}, bf16[64,1152]{1,0:T(8,128)(2,1)S(1)}, u32[]{:S(2)}, u32[]{:S(2)}) collective-permute-start(bf16[64,1152]{1,0:T(8,128)(2,1)S(1)} %shard_map.119.own_ref), channel_id=1, source_target_pairs={{0,16},{16,0},{1,17},{17,1},{2,18},{18,2},{3,19},{19,3},{4,20},{20... | collective-permute-start | bytes 442376 | tf_op jit(solution)/shard_map/ppermute | solution.py:462

commit v14 on v13

--- a/solution.py
+++ b/solution.py
@@ -86,7 +86,7 @@
     length = order_ref.shape[0]
     row = lax.broadcasted_iota(jnp.int32, (length, length), 0)
     lane = lax.broadcasted_iota(jnp.int32, (length, length), 1)
-    order_ref[...] = (arrival_place(pos_index, row, stages, sites) == lane).astype(F32)
+    order_ref[...] = (arrival_place(pos_index, row, stages, sites) == lane).astype(BF16)
     row = lax.broadcasted_iota(jnp.int32, own_ref.shape, 0)
     lane = lax.broadcasted_iota(jnp.int32, own_ref.shape, 1)
     own_ref[...] = (row + pos_index * sites == lane).astype(F32)
@@ -135,9 +135,13 @@
         term = shares[h * sites : (h + 1) * sites, :] * head_ref[h : h + 1, 0:1]
         merged = term if merged is None else merged + term
     held[head_rows : head_rows + sites, :] = merged
-    pair_ref[...] = jnp.broadcast_to(
-        dot_nn(held[...], order_ref[...], HIGHEST)[None], pair_ref.shape
-    )
+    rest, ordered = held[...], None
+    for _ in range(3):
+        part = rest.astype(BF16)
+        rest = rest - part.astype(F32)
+        term = dot_nn(part, order_ref[...])
+        ordered = term if ordered is None else ordered + term
+    pair_ref[...] = jnp.broadcast_to(ordered[None], pair_ref.shape)
 
 
 def mix_kernel(head, v_count, *refs):
@@ -318,6 +322,14 @@
     return [send_pos(part, count, stride, size, delta) for delta in range(1, size) for part in parts]
 
 
+def lay_together(parts, order):
+    size = parts[0].shape[1]
+    whole = jnp.zeros((parts[0].shape[0], size * len(parts), parts[0].shape[2]), parts[0].dtype)
+    for at in order:
+        whole = lax.dynamic_update_slice(whole, parts[at], (0, at * size, 0))
+    return whole
+
+
 def after(array, *others):
     return lax.optimization_barrier((array, *others))[0]
 
@@ -350,13 +362,14 @@
 
     stages = stages_of(pos_count)
     outer = stages[0]
+    size = outer[1]
     middle = stages[1] if len(stages) > 1 else None
 
     scalars = jnp.stack([seq_index, pos_index])
     head_rows = round_up(heads, 8)
     width = lane_block(embed, head)
     key_first = [lateral_matched_vectors] + send_all([lateral_matched_vectors], pos_count, outer)
-    key_parts = [jnp.concatenate(key_first, axis=1)]
+    key_parts = [lay_together(key_first, [0, 1, *range(3, size), *range(2, min(size, 3))])]
     value_first = [after(lateral_carried_vectors, key_parts[0])]
     value_first += [
         send_pos(lateral_carried_vectors, pos_count, *outer, delta) for delta in range(outer[1] - 1, 0, -1)
@@ -377,9 +390,9 @@
         [masked, *key_parts],
     )
     value_first[-1] = after(value_first[-1], masked)
-    value_own = jnp.zeros((rows, sites * outer[1], embed), BF16)
-    for delta in [0, *range(outer[1] - 1, 0, -1)]:
-        value_own = lax.dynamic_update_slice(value_own, value_first[delta], (0, delta * sites, 0))
+    value_own = lay_together(
+        value_first, [0, *range(size - 1, size - 2, -1), *range(1, size - 2), *range(max(size - 2, 1), size - 1)]
+    )
     value_parts = [value_own]
     if middle:
         value_parts += send_all(value_parts, pos_count, middle)
@@ -395,7 +408,7 @@
         functools.partial(prepare_kernel, heads, sites, stages),
         (
             jax.ShapeDtypeStruct((head_rows + 8, 128), F32),
-            jax.ShapeDtypeStruct((length, length), F32),
+            jax.ShapeDtypeStruct((length, length), BF16),
             jax.ShapeDtypeStruct((sites, length), F32),
             jax.ShapeDtypeStruct((length, slab_width), F32),
             jax.ShapeDtypeStruct((embed, padded), BF16),

time: 43 us -> 42.6 us (level)
  starting transfers between devices: 23.8 us -> 23.3 us
    dynamic_update_slice x4 -> x8, local copies, waits for them, and re-layouts: 0.83 us -> 1.66 us  [lay_together(): whole = lax.dynamic_update_slice(whole, parts[at], (0, at * size, 0))]
    unnamed x15 -> x12, local copies, waits for them, and re-layouts: 1.63 us -> 0.82 us
    ppermute x12, starting transfers between devices: 13.2 us -> 12.7 us  [send_pos(): return lax.ppermute(array, 'pos', pairs)]
  transfers between devices with their start and end apart: 16 -> 16, of which waited for: 6 -> 5; matrix products, arithmetic and copies ran while one was open for 8% -> 8% of each run, Pallas kernels for 11% -> 11%
where the time goes in v14:
time: 42.6 us; the launch traced here: 42.2 us
  starting transfers between devices  23.3 us (55%)
  waiting for transfers between devices  7.25 us (17%)
  Pallas kernels  6.02 us (14%)
  local copies, waits for them, and re-layouts  2.48 us (6%)
  other arithmetic  1.74 us (4%)
  between operations  1.49 us (3%)
    ppermute x12, starting transfers between devices, send_pos(): return lax.ppermute(array, 'pos', pairs)  12.7 us
    pallas_call x9, Pallas kernels, call(): pl.pallas_call(kernel, out_shape=out_shape, in_specs=specs, out_specs=jax...  6.02 us
    all_to_all x1, starting transfers between devices, per_device(): lax.all_to_all(pair_local, 'pos', split_axis=0, concat_axis=0, tiled=True)  5.85 us
    ppermute x12, waiting for transfers between devices, send_pos(): return lax.ppermute(array, 'pos', pairs)  2.54 us
    all_to_all x1, waiting for transfers between devices, per_device(): lax.all_to_all(pair_local, 'pos', split_axis=0, concat_axis=0, tiled=True)  2.15 us
    dynamic_update_slice x8, local copies, waits for them, and re-layouts, lay_together(): whole = lax.dynamic_update_slice(whole, parts[at], (0, at * size, 0))  1.66 us
    mul x1, other arithmetic, per_device(): weight = upright_threefold_linear * one  1.64 us
    ppermute x1, starting transfers between devices, per_device(): partials = [partial, after(lax.ppermute(partial, 'seq', swap), order)]  1.56 us
  transfers between devices with their start and end apart: 16, of which 5 were waited for; matrix products, arithmetic and copies ran while one was open for 8% of the time, Pallas kernels for 11%

profile of v14, /device:TPU:0, one launch (start us, length us, event | category | flops | bytes accessed | tf_op | source)
XLA Modules:
  0.0 42.2 jit_solution(14428885099833177471)
XLA Ops:
  0.6 0.0 copy-start
  0.6 3.1 %collective-permute-start = (bf16[4,8,768]{2,1,0:T(8,128)(2,1)}, bf16[4,8,768]{2,1,0:T(8,128)(2,1)S(1)}, u32[]{:S(2)}, u32[]{:S(2)}) collective-permute-start(bf16[4,8,768]{2,1,0:T(8,128)(2,1)} %param.12), channel_id=1, source_target_pairs={{0,4},{1,5},{2,6},{3,7},{4,8},{5,9},{6,10},{7,11},{8,12},{9,13},{1... | collective-permute-start | bytes 147464 | tf_op jit(solution)/shard_map/ppermute | solution.py:317
  3.7 2.6 %collective-permute-start.2 = (bf16[4,8,768]{2,1,0:T(8,128)(2,1)}, bf16[4,8,768]{2,1,0:T(8,128)(2,1)S(1)}, u32[]{:S(2)}, u32[]{:S(2)}) collective-permute-start(bf16[4,8,768]{2,1,0:T(8,128)(2,1)} %param.12), channel_id=1, source_target_pairs={{0,8},{1,9},{2,10},{3,11},{4,12},{5,13},{6,14},{7,15},{8,0},{9,1},... | collective-permute-start | bytes 147464 | tf_op jit(solution)/shard_map/ppermute | solution.py:317
  6.3 1.3 %collective-permute-start.1 = (bf16[4,8,768]{2,1,0:T(8,128)(2,1)}, bf16[4,8,768]{2,1,0:T(8,128)(2,1)S(1)}, u32[]{:S(2)}, u32[]{:S(2)}) collective-permute-start(bf16[4,8,768]{2,1,0:T(8,128)(2,1)} %param.12), channel_id=1, source_target_pairs={{0,12},{1,13},{2,14},{3,15},{4,0},{5,1},{6,2},{7,3},{8,4},{9,5},{1... | collective-permute-start | bytes 147464 | tf_op jit(solution)/shard_map/ppermute | solution.py:317
  7.7 0.4 %collective-permute-start.7 = (bf16[4,8,768]{2,1,0:T(8,128)(2,1)}, bf16[4,8,768]{2,1,0:T(8,128)(2,1)S(1)}, u32[]{:S(2)}, u32[]{:S(2)}) collective-permute-start(bf16[4,8,768]{2,1,0:T(8,128)(2,1)} %param.13), channel_id=1, source_target_pairs={{0,12},{1,13},{2,14},{3,15},{4,0},{5,1},{6,2},{7,3},{8,4},{9,5},{1... | collective-permute-start | bytes 147464 | tf_op jit(solution)/shard_map/ppermute | solution.py:317
  8.1 1.7 %collective-permute-start.9 = (bf16[4,8,768]{2,1,0:T(8,128)(2,1)}, bf16[4,8,768]{2,1,0:T(8,128)(2,1)S(1)}, u32[]{:S(2)}, u32[]{:S(2)}) collective-permute-start(bf16[4,8,768]{2,1,0:T(8,128)(2,1)} %param.13), channel_id=1, source_target_pairs={{0,8},{1,9},{2,10},{3,11},{4,12},{5,13},{6,14},{7,15},{8,0},{9,1},... | collective-permute-start | bytes 147464 | tf_op jit(solution)/shard_map/ppermute | solution.py:317
  9.8 0.8 %dynamic_update_slice.24 = bf16[4,32,768]{2,1,0:T(8,128)(2,1)S(1)} pad(bf16[4,8,768]{2,1,0:T(8,128)(2,1)} %param.12, bf16[]{:T(256)} %constant.3.clone.1), padding=0_0x0_24x0_0 | pad | bytes 245762 | tf_op jit(solution)/shard_map/dynamic_update_slice | solution.py:329
  10.6 0.0 collective-permute-done
  10.6 0.1 collective-permute-start.8
  10.8 0.0 collective-permute-done.1
  10.8 0.0 collective-permute-done.2
  10.8 1.7 %collective-permute-start.4 = (bf16[4,32,768]{2,1,0:T(8,128)(2,1)S(1)}, bf16[4,32,768]{2,1,0:T(8,128)(2,1)S(1)}, u32[]{:S(2)}, u32[]{:S(2)}) collective-permute-start(bf16[4,32,768]{2,1,0:T(8,128)(2,1)S(1)} %constant_dynamic-update-slice_fusion.3.refs_1_), channel_id=1, source_target_pairs={{0,2},{1,3},{2,0},{3,1},{4,6},{5,7},{6,4},{7,5},{8,10},{9,11},{10,... | collective-permute-start | bytes 589832 | tf_op jit(solution)/shard_map/ppermute | solution.py:317
  12.5 0.0 collective-permute-start.3
  12.5 0.8 %copy-done.2 = bf16[4,8,768]{2,1,0:T(8,128)(2,1)S(1)} copy-done((bf16[4,8,768]{2,1,0:T(8,128)(2,1)S(1)}, bf16[4,8,768]{2,1,0:T(8,128)(2,1)}, u32[]{:S(2)}) %copy-start.2) | copy-done | bytes 49176
  13.3 0.1 shard_map.113.refs_0_
  13.4 0.0 collective-permute-done.7
  13.4 0.8 %dynamic_update_slice.28 = bf16[4,32,768]{2,1,0:T(8,128)(2,1)S(1)} pad(bf16[4,8,768]{2,1,0:T(8,128)(2,1)} %param.13, bf16[]{:T(256)} %constant.3.clone.1), padding=0_0x0_24x0_0 | pad | bytes 245762 | tf_op jit(solution)/shard_map/dynamic_update_slice | solution.py:329
  14.3 2.5 %collective-permute-done.8 = bf16[4,8,768]{2,1,0:T(8,128)(2,1)S(1)} collective-permute-done((bf16[4,8,768]{2,1,0:T(8,128)(2,1)}, bf16[4,8,768]{2,1,0:T(8,128)(2,1)S(1)}, u32[]{:S(2)}, u32[]{:S(2)}) %collective-permute-start.8) | collective-permute-done | bytes 49184 | tf_op jit(solution)/shard_map/ppermute | solution.py:317
  16.8 0.0 collective-permute-done.4.refs_2_
  16.8 0.1 collective-permute-start.5
  16.9 0.0 collective-permute-done.9
  16.9 1.6 %collective-permute-start.10 = (bf16[4,32,768]{2,1,0:T(8,128)(2,1)S(1)}, bf16[4,32,768]{2,1,0:T(8,128)(2,1)S(1)}, u32[]{:S(2)}, u32[]{:S(2)}) collective-permute-start(bf16[4,32,768]{2,1,0:T(8,128)(2,1)S(1)} %constant_dynamic-update-slice_fusion.refs_1_), channel_id=1, source_target_pairs={{0,2},{1,3},{2,0},{3,1},{4,6},{5,7},{6,4},{7,5},{8,10},{9,11},{10,... | collective-permute-start | bytes 589832 | tf_op jit(solution)/shard_map/ppermute | solution.py:317
  18.5 0.2 shard_map.114.refs_3_
  18.7 0.0 collective-permute-done.3.refs_1_
  18.7 0.0 collective-permute-done.5.refs_2_
  18.7 0.3 shard_map.115.refs_0_
  19.0 1.6 %collective-permute-start.6 = (f32[96,128]{1,0:T(8,128)S(1)}, f32[96,128]{1,0:T(8,128)S(1)}, u32[]{:S(2)}, u32[]{:S(2)}) collective-permute-start(f32[96,128]{1,0:T(8,128)S(1)} %shard_map.115.refs_0_), channel_id=1, source_target_pairs={{0,16},{16,0},{1,17},{17,1},{2,18},{18,2},{3,19},{19,3},{4,20},{20... | collective-permute-start | bytes 147464 | tf_op jit(solution)/shard_map/ppermute | solution.py:421
  20.6 0.1 pad_add_fusion.scalar_ref
  21.3 0.1 collective-permute-start.11
  21.4 0.8 %shard_map.116 = (f32[24,128]{1,0:T(8,128)S(1)}, bf16[128,128]{1,0:T(8,128)(2,1)S(1)}, f32[8,128]{1,0:T(8,128)S(1)}, f32[128,64]{1,0:T(8,128)S(1)}, bf16[768,128...) custom-call(s32[2]{0:T(128)S(1)} %pad_add_fusion.scalar_ref, f32[12]{0:T(128)S(1)} %copy-done.5, f32[1]{0:T(128)S(6)} %copy.18.offset_ref), custom_call_target="tpu_custom_call" | custom-call | flops 1000000 | bytes 1000000 | tf_op jit(solution)/shard_map/pallas_call | solution.py:289
  22.2 1.0 %collective-permute-done.6.refs_1_ = f32[96,128]{1,0:T(8,128)S(1)} collective-permute-done((f32[96,128]{1,0:T(8,128)S(1)}, f32[96,128]{1,0:T(8,128)S(1)}, u32[]{:S(2)}, u32[]{:S(2)}) %collective-permute-start.6) | collective-permute-done | bytes 49184 | tf_op jit(solution)/shard_map/ppermute | solution.py:421
  23.2 1.1 %shard_map.117 = (bf16[96,128]{1,0:T(8,128)(2,1)S(1)}, f32[16,24,128]{2,1,0:T(8,128)}) custom-call(f32[96,128]{1,0:T(8,128)S(1)} %shard_map.115.refs_0_, f32[96,128]{1,0:T(8,128)S(1)} %collective-permute-done.6.refs_1_, f32[24,128]{1,0:T(8,128)S(1)} %get-tuple-element.24.refs_2_.factor_ref, bf16[128,128]{1,0:T(8,128)(2,1)S(1)} %get-tuple-element.22.refs_3_), custom_call_target="tpu_custom_call" | custom-call | flops 1000000 | bytes 1000000 | tf_op jit(solution)/shard_map/pallas_call | solution.py:289
  24.3 0.0 collective-permute-done.10.refs_2_
  24.3 0.0 collective-permute-start.12
  24.3 5.9 %all-to-all-start = ((f32[16,24,128]{2,1,0:T(8,128)}), f32[16,24,128]{2,1,0:T(8,128)S(1)}, u32[]{:S(2)}, u32[]{:S(2)}) async-start(f32[16,24,128]{2,1,0:T(8,128)} %get-tuple-element.28), calls=%async_computation | async-start | bytes 393216 | tf_op jit(solution)/shard_map/all_to_all | solution.py:454
  30.1 0.0 collective-permute-done.11.refs_3_
  30.1 0.0 collective-permute-done.12.refs_4_
  30.2 0.6 %shard_map.118 = (f32[32,768]{1,0:T(8,128)S(1)}, bf16[32,768]{1,0:T(8,128)(2,1)S(1)}, bf16[1,1152]{1,0:T(2,128)(2,1)S(1)}) custom-call(bf16[96,128]{1,0:T(8,128)(2,1)S(1)} %get-tuple-element.25.refs_0_, bf16[4,32,768]{2,1,0:T(8,128)(2,1)S(1)} %constant_dynamic-update-slice_fusion.refs_1_, bf16[4,32,768]{2,1,0:T(8,128)(2,1)S(1)} %collective-permute-done.10.refs_2_, ...), custom_call_target="tpu_custom_call" | custom-call | flops 1000000 | bytes 1000000 | tf_op jit(solution)/shard_map/pallas_call | solution.py:289
  30.8 1.6 %collective-permute-start.13 = (bf16[32,768]{1,0:T(8,128)(2,1)S(1)}, bf16[32,768]{1,0:T(8,128)(2,1)S(1)}, u32[]{:S(2)}, u32[]{:S(2)}) collective-permute-start(bf16[32,768]{1,0:T(8,128)(2,1)S(1)} %get-tuple-element.30.refs_0_), channel_id=1, source_target_pairs={{0,16},{16,0},{1,17},{17,1},{2,18},{18,2},{3,19},{19,3},{4,20},{20... | collective-permute-start | bytes 147464 | tf_op jit(solution)/shard_map/ppermute | solution.py:462
  32.4 1.6 %broadcast_multiply_fusion.refs_2_ = bf16[768,1152]{1,0:T(8,128)(2,1)S(1)} fusion(bf16[768,1152]{1,0:T(8,128)(2,1)} %param.16, bf16[1152]{0:T(1024)(128)(2,1)S(1)} %reduce), kind=kLoop, calls=%fused_computation | loop fusion | flops 884736 | bytes 3541248 | tf_op jit(solution)/shard_map/mul | solution.py:463
  34.0 0.0 copy-start.1
  34.1 0.9 %collective-permute-done.13.refs_1_ = bf16[32,768]{1,0:T(8,128)(2,1)S(1)} collective-permute-done((bf16[32,768]{1,0:T(8,128)(2,1)S(1)}, bf16[32,768]{1,0:T(8,128)(2,1)S(1)}, u32[]{:S(2)}, u32[]{:S(2)}) %collective-permute-start.13) | collective-permute-done | bytes 49184 | tf_op jit(solution)/shard_map/ppermute | solution.py:462
  35.0 0.4 %shard_map.119.own_ref = bf16[64,1152]{1,0:T(8,128)(2,1)S(1)} custom-call(bf16[32,768]{1,0:T(8,128)(2,1)S(1)} %get-tuple-element.30.refs_0_, bf16[32,768]{1,0:T(8,128)(2,1)S(1)} %collective-permute-done.13.refs_1_, bf16[768,1152]{1,0:T(8,128)(2,1)S(1)} %broadcast_multiply_fusion.refs_2_), custom_call_target="tpu_custom_call" | custom-call | flops 1000000 | bytes 1000000 | tf_op jit(solution)/shard_map/pallas_call | solution.py:289
  35.4 1.6 %collective-permute-start.14 = (bf16[64,1152]{1,0:T(8,128)(2,1)S(1)}, bf16[64,1152]{1,0:T(8,128)(2,1)S(1)}, u32[]{:S(2)}, u32[]{:S(2)}) collective-permute-start(bf16[64,1152]{1,0:T(8,128)(2,1)S(1)} %shard_map.119.own_ref), channel_id=1, source_target_pairs={{0,16},{16,0},{1,17},{17,1},{2,18},{18,2},{3,19},{19,3},{4,20},{20... | collective-permute-start | bytes 442376 | tf_op jit(solution)/shard_map/ppermute | solution.py:475
  37.0 2.2 %all-to-all-done.pair_ref = f32[16,24,128]{2,1,0:T(8,128)S(1)} async-done(((f32[16,24,128]{2,1,0:T(8,128)}), f32[16,24,128]{2,1,0:T(8,128)S(1)}, u32[]{:S(2)}, u32[]{:S(2)}) %all-to-all-start) | async-done | bytes 196640 | tf_op jit(solution)/shard_map/all_to_all | solution.py:454
  39.1 1.0 %shard_map.121 = f32[8,64]{1,0:T(8,128)} custom-call(f32[16,24,128]{2,1,0:T(8,128)S(1)} %all-to-all-done.pair_ref, f32[24,128]{1,0:T(8,128)S(1)} %get-tuple-element.24.refs_2_.factor_ref, f32[8,128]{1,0:T(8,128)S(1)} %get-tuple-element.36.own_ref, f32[128,64]{1,0:T(8,128)S(1)} %get-tuple-element.37.slab_ref), custom_call_target="tpu_custom_call" | custom-call | flops 1000000 | bytes 1000000 | tf_op jit(solution)/shard_map/pallas_call | solution.py:289
  40.2 0.6 %collective-permute-done.14.other_ref = bf16[64,1152]{1,0:T(8,128)(2,1)S(1)} collective-permute-done((bf16[64,1152]{1,0:T(8,128)(2,1)S(1)}, bf16[64,1152]{1,0:T(8,128)(2,1)S(1)}, u32[]{:S(2)}, u32[]{:S(2)}) %collective-permute-start.14) | collective-permute-done | bytes 147488 | tf_op jit(solution)/shard_map/ppermute | solution.py:475
  40.8 1.4 %shard_map.120 = bf16[4,8,768]{2,1,0:T(8,128)(2,1)} custom-call(bf16[64,1152]{1,0:T(8,128)(2,1)S(1)} %shard_map.119.own_ref, bf16[64,1152]{1,0:T(8,128)(2,1)S(1)} %collective-permute-done.14.other_ref, f32[32,768]{1,0:T(8,128)S(1)} %get-tuple-element.32.refs_0_, bf16[768,768]{1,0:T(8,128)(2,1)S(1)} %copy-done.1, ...), custom_call_target="tpu_custom_call" | custom-call | flops 1000000 | bytes 1000000 | tf_op jit(solution)/shard_map/pallas_call | solution.py:289
  (16 shorter events, 0.1 us)
Async XLA Ops:
  0.6 29.5 %copy-start = (bf16[768,768]{1,0:T(8,128)(2,1)S(1)}, bf16[768,768]{1,0:T(8,128)(2,1)}, u32[]{:S(2)}) copy-start(bf16[768,768]{1,0:T(8,128)(2,1)} %refs_5_.1) | copy-start | bytes 3538948
  0.6 10.0 %collective-permute-start = (bf16[4,8,768]{2,1,0:T(8,128)(2,1)}, bf16[4,8,768]{2,1,0:T(8,128)(2,1)S(1)}, u32[]{:S(2)}, u32[]{:S(2)}) collective-permute-start(bf16[4,8,768]{2,1,0:T(8,128)(2,1)} %param.12), channel_id=1, source_target_pairs={{0,4},{1,5},{2,6},{3,7},{4,8},{5,9},{6,10},{7,11},{8,12},{9,13},{1... | collective-permute-start | bytes 147464 | tf_op jit(solution)/shard_map/ppermute | solution.py:317
  3.7 7.1 %collective-permute-start.2 = (bf16[4,8,768]{2,1,0:T(8,128)(2,1)}, bf16[4,8,768]{2,1,0:T(8,128)(2,1)S(1)}, u32[]{:S(2)}, u32[]{:S(2)}) collective-permute-start(bf16[4,8,768]{2,1,0:T(8,128)(2,1)} %param.12), channel_id=1, source_target_pairs={{0,8},{1,9},{2,10},{3,11},{4,12},{5,13},{6,14},{7,15},{8,0},{9,1},... | collective-permute-start | bytes 147464 | tf_op jit(solution)/shard_map/ppermute | solution.py:317
  6.3 4.5 %collective-permute-start.1 = (bf16[4,8,768]{2,1,0:T(8,128)(2,1)}, bf16[4,8,768]{2,1,0:T(8,128)(2,1)S(1)}, u32[]{:S(2)}, u32[]{:S(2)}) collective-permute-start(bf16[4,8,768]{2,1,0:T(8,128)(2,1)} %param.12), channel_id=1, source_target_pairs={{0,12},{1,13},{2,14},{3,15},{4,0},{5,1},{6,2},{7,3},{8,4},{9,5},{1... | collective-permute-start | bytes 147464 | tf_op jit(solution)/shard_map/ppermute | solution.py:317
  7.7 5.8 %collective-permute-start.7 = (bf16[4,8,768]{2,1,0:T(8,128)(2,1)}, bf16[4,8,768]{2,1,0:T(8,128)(2,1)S(1)}, u32[]{:S(2)}, u32[]{:S(2)}) collective-permute-start(bf16[4,8,768]{2,1,0:T(8,128)(2,1)} %param.13), channel_id=1, source_target_pairs={{0,12},{1,13},{2,14},{3,15},{4,0},{5,1},{6,2},{7,3},{8,4},{9,5},{1... | collective-permute-start | bytes 147464 | tf_op jit(solution)/shard_map/ppermute | solution.py:317
  8.1 8.8 %collective-permute-start.9 = (bf16[4,8,768]{2,1,0:T(8,128)(2,1)}, bf16[4,8,768]{2,1,0:T(8,128)(2,1)S(1)}, u32[]{:S(2)}, u32[]{:S(2)}) collective-permute-start(bf16[4,8,768]{2,1,0:T(8,128)(2,1)} %param.13), channel_id=1, source_target_pairs={{0,8},{1,9},{2,10},{3,11},{4,12},{5,13},{6,14},{7,15},{8,0},{9,1},... | collective-permute-start | bytes 147464 | tf_op jit(solution)/shard_map/ppermute | solution.py:317
  10.6 6.2 %collective-permute-start.8 = (bf16[4,8,768]{2,1,0:T(8,128)(2,1)}, bf16[4,8,768]{2,1,0:T(8,128)(2,1)S(1)}, u32[]{:S(2)}, u32[]{:S(2)}) collective-permute-start(bf16[4,8,768]{2,1,0:T(8,128)(2,1)} %param.13), channel_id=1, source_target_pairs={{0,4},{1,5},{2,6},{3,7},{4,8},{5,9},{6,10},{7,11},{8,12},{9,13},{1... | collective-permute-start | bytes 147464 | tf_op jit(solution)/shard_map/ppermute | solution.py:317
  10.8 6.0 %collective-permute-start.4 = (bf16[4,32,768]{2,1,0:T(8,128)(2,1)S(1)}, bf16[4,32,768]{2,1,0:T(8,128)(2,1)S(1)}, u32[]{:S(2)}, u32[]{:S(2)}) collective-permute-start(bf16[4,32,768]{2,1,0:T(8,128)(2,1)S(1)} %constant_dynamic-update-slice_fusion.3.refs_1_), channel_id=1, source_target_pairs={{0,2},{1,3},{2,0},{3,1},{4,6},{5,7},{6,4},{7,5},{8,10},{9,11},{10,... | collective-permute-start | bytes 589832 | tf_op jit(solution)/shard_map/ppermute | solution.py:317
  12.5 6.2 %collective-permute-start.3 = (bf16[4,32,768]{2,1,0:T(8,128)(2,1)S(1)}, bf16[4,32,768]{2,1,0:T(8,128)(2,1)S(1)}, u32[]{:S(2)}, u32[]{:S(2)}) collective-permute-start(bf16[4,32,768]{2,1,0:T(8,128)(2,1)S(1)} %constant_dynamic-update-slice_fusion.3.refs_1_), channel_id=1, source_target_pairs={{0,1},{1,0},{2,3},{3,2},{4,5},{5,4},{6,7},{7,6},{8,9},{9,8},{10,11... | collective-permute-start | bytes 589832 | tf_op jit(solution)/shard_map/ppermute | solution.py:317
  12.5 0.8 %copy-start.2 = (bf16[4,8,768]{2,1,0:T(8,128)(2,1)S(1)}, bf16[4,8,768]{2,1,0:T(8,128)(2,1)}, u32[]{:S(2)}) copy-start(bf16[4,8,768]{2,1,0:T(8,128)(2,1)} %q_hbm) | copy-start | bytes 147460
  13.3 8.1 %copy-start.5 = (f32[12]{0:T(128)S(1)}, f32[12]{0:T(128)}, u32[]{:S(2)}) copy-start(f32[12]{0:T(128)} %factor_ref.1) | copy-start | bytes 148
  13.3 16.8 %copy-start.3 = (bf16[4,8,768]{2,1,0:T(8,128)(2,1)S(1)}, bf16[4,8,768]{2,1,0:T(8,128)(2,1)}, u32[]{:S(2)}) copy-start(bf16[4,8,768]{2,1,0:T(8,128)(2,1)} %refs_6_.1) | copy-start | bytes 147460
  13.3 16.8 %copy-start.4 = (f32[768]{0:T(1024)S(1)}, f32[768]{0:T(1024)}, u32[]{:S(2)}) copy-start(f32[768]{0:T(1024)} %refs_7_.1) | copy-start | bytes 9220
  16.8 1.9 %collective-permute-start.5 = (bf16[4,32,768]{2,1,0:T(8,128)(2,1)S(1)}, bf16[4,32,768]{2,1,0:T(8,128)(2,1)S(1)}, u32[]{:S(2)}, u32[]{:S(2)}) collective-permute-start(bf16[4,32,768]{2,1,0:T(8,128)(2,1)S(1)} %collective-permute-done.4.refs_2_), channel_id=1, source_target_pairs={{0,1},{1,0},{2,3},{3,2},{4,5},{5,4},{6,7},{7,6},{8,9},{9,8},{10,11... | collective-permute-start | bytes 589832 | tf_op jit(solution)/shard_map/ppermute | solution.py:317
  16.9 7.4 %collective-permute-start.10 = (bf16[4,32,768]{2,1,0:T(8,128)(2,1)S(1)}, bf16[4,32,768]{2,1,0:T(8,128)(2,1)S(1)}, u32[]{:S(2)}, u32[]{:S(2)}) collective-permute-start(bf16[4,32,768]{2,1,0:T(8,128)(2,1)S(1)} %constant_dynamic-update-slice_fusion.refs_1_), channel_id=1, source_target_pairs={{0,2},{1,3},{2,0},{3,1},{4,6},{5,7},{6,4},{7,5},{8,10},{9,11},{10,... | collective-permute-start | bytes 589832 | tf_op jit(solution)/shard_map/ppermute | solution.py:317
  19.0 4.2 %collective-permute-start.6 = (f32[96,128]{1,0:T(8,128)S(1)}, f32[96,128]{1,0:T(8,128)S(1)}, u32[]{:S(2)}, u32[]{:S(2)}) collective-permute-start(f32[96,128]{1,0:T(8,128)S(1)} %shard_map.115.refs_0_), channel_id=1, source_target_pairs={{0,16},{16,0},{1,17},{17,1},{2,18},{18,2},{3,19},{19,3},{4,20},{20... | collective-permute-start | bytes 147464 | tf_op jit(solution)/shard_map/ppermute | solution.py:421
  21.3 8.8 %collective-permute-start.11 = (bf16[4,32,768]{2,1,0:T(8,128)(2,1)S(1)}, bf16[4,32,768]{2,1,0:T(8,128)(2,1)S(1)}, u32[]{:S(2)}, u32[]{:S(2)}) collective-permute-start(bf16[4,32,768]{2,1,0:T(8,128)(2,1)S(1)} %constant_dynamic-update-slice_fusion.refs_1_), channel_id=1, source_target_pairs={{0,1},{1,0},{2,3},{3,2},{4,5},{5,4},{6,7},{7,6},{8,9},{9,8},{10,11... | collective-permute-start | bytes 589832 | tf_op jit(solution)/shard_map/ppermute | solution.py:317
  24.3 5.9 %collective-permute-start.12 = (bf16[4,32,768]{2,1,0:T(8,128)(2,1)S(1)}, bf16[4,32,768]{2,1,0:T(8,128)(2,1)S(1)}, u32[]{:S(2)}, u32[]{:S(2)}) collective-permute-start(bf16[4,32,768]{2,1,0:T(8,128)(2,1)S(1)} %collective-permute-done.10.refs_2_), channel_id=1, source_target_pairs={{0,1},{1,0},{2,3},{3,2},{4,5},{5,4},{6,7},{7,6},{8,9},{9,8},{10,11... | collective-permute-start | bytes 589832 | tf_op jit(solution)/shard_map/ppermute | solution.py:317
  24.3 14.9 %all-to-all-start = ((f32[16,24,128]{2,1,0:T(8,128)}), f32[16,24,128]{2,1,0:T(8,128)S(1)}, u32[]{:S(2)}, u32[]{:S(2)}) async-start(f32[16,24,128]{2,1,0:T(8,128)} %get-tuple-element.28), calls=%async_computation | async-start | bytes 393216 | tf_op jit(solution)/shard_map/all_to_all | solution.py:454
  30.8 4.2 %collective-permute-start.13 = (bf16[32,768]{1,0:T(8,128)(2,1)S(1)}, bf16[32,768]{1,0:T(8,128)(2,1)S(1)}, u32[]{:S(2)}, u32[]{:S(2)}) collective-permute-start(bf16[32,768]{1,0:T(8,128)(2,1)S(1)} %get-tuple-element.30.refs_0_), channel_id=1, source_target_pairs={{0,16},{16,0},{1,17},{17,1},{2,18},{18,2},{3,19},{19,3},{4,20},{20... | collective-permute-start | bytes 147464 | tf_op jit(solution)/shard_map/ppermute | solution.py:462
  34.0 6.8 %copy-start.1 = (bf16[768,768]{1,0:T(8,128)(2,1)S(1)}, bf16[768,768]{1,0:T(8,128)(2,1)}, u32[]{:S(2)}) copy-start(bf16[768,768]{1,0:T(8,128)(2,1)} %refs_1_) | copy-start | bytes 3538948
  35.4 5.4 %collective-permute-start.14 = (bf16[64,1152]{1,0:T(8,128)(2,1)S(1)}, bf16[64,1152]{1,0:T(8,128)(2,1)S(1)}, u32[]{:S(2)}, u32[]{:S(2)}) collective-permute-start(bf16[64,1152]{1,0:T(8,128)(2,1)S(1)} %shard_map.119.own_ref), channel_id=1, source_target_pairs={{0,16},{16,0},{1,17},{17,1},{2,18},{18,2},{3,19},{19,3},{4,20},{20... | collective-permute-start | bytes 442376 | tf_op jit(solution)/shard_map/ppermute | solution.py:475

commit v15 on v14

--- a/solution.py
+++ b/solution.py
@@ -397,7 +397,8 @@
     if middle:
         value_parts += send_all(value_parts, pos_count, middle)
     if len(stages) > 2:
-        far_parts = send_all(key_parts, pos_count, stages[2])
+        late_parts = [after(key_parts[0], *key_parts[1:])] + key_parts[1:]
+        far_parts = send_all(late_parts, pos_count, stages[2])
         partial = call(
             functools.partial(logits_kernel, len(far_parts)),
             jax.ShapeDtypeStruct((heads * sites, length), F32),
@@ -433,8 +434,8 @@
         scratch=[pltpu.VMEM((head_rows + sites, length), F32)],
     )
     if len(stages) > 2:
-        value_parts = value_parts[:1] + [after(part, pair_local) for part in value_parts[1:]]
-        value_parts += send_all(value_parts, pos_count, stages[2])
+        late_parts = [after(part, pair_local, *value_parts[1:]) for part in value_parts]
+        value_parts = value_parts + send_all(late_parts, pos_count, stages[2])
     hidden, normed, one = call(
         functools.partial(mix_kernel, head, len(value_parts)),
         (

time: 42.6 us -> 43 us (level)
    ppermute x12, starting transfers between devices: 12.7 us -> 13.7 us  [send_pos(): return lax.ppermute(array, 'pos', pairs)]
    all_to_all x1, starting transfers between devices: 5.85 us -> 5.28 us  [per_device(): lax.all_to_all(pair_local, 'pos', split_axis=0, concat_axis=0, tiled=True)]
where the time goes in v15:
time: 43 us; the launch traced here: 42.6 us
  starting transfers between devices  23.6 us (55%)
  waiting for transfers between devices  7.33 us (17%)
  Pallas kernels  6 us (14%)
  local copies, waits for them, and re-layouts  2.47 us (6%)
  other arithmetic  1.74 us (4%)
  between operations  1.47 us (3%)
    ppermute x12, starting transfers between devices, send_pos(): return lax.ppermute(array, 'pos', pairs)  13.7 us
    pallas_call x9, Pallas kernels, call(): pl.pallas_call(kernel, out_shape=out_shape, in_specs=specs, out_specs=jax...  6 us
    all_to_all x1, starting transfers between devices, per_device(): lax.all_to_all(pair_local, 'pos', split_axis=0, concat_axis=0, tiled=True)  5.28 us
    ppermute x12, waiting for transfers between devices, send_pos(): return lax.ppermute(array, 'pos', pairs)  2.54 us
    all_to_all x1, waiting for transfers between devices, per_device(): lax.all_to_all(pair_local, 'pos', split_axis=0, concat_axis=0, tiled=True)  2.15 us
    dynamic_update_slice x8, local copies, waits for them, and re-layouts, lay_together(): whole = lax.dynamic_update_slice(whole, parts[at], (0, at * size, 0))  1.66 us
    mul x1, other arithmetic, per_device(): weight = upright_threefold_linear * one  1.64 us
    ppermute x1, starting transfers between devices, per_device(): partials = [partial, after(lax.ppermute(partial, 'seq', swap), order)]  1.56 us
  transfers between devices with their start and end apart: 16, of which 5 were waited for; matrix products, arithmetic and copies ran while one was open for 8% of the time, Pallas kernels for 11%

profile of v15, /device:TPU:0, one launch (start us, length us, event | category | flops | bytes accessed | tf_op | source)
XLA Modules:
  0.0 42.6 jit_solution(7769345693265362757)
XLA Ops:
  0.6 0.0 copy-start
  0.6 3.1 %collective-permute-start = (bf16[4,8,768]{2,1,0:T(8,128)(2,1)}, bf16[4,8,768]{2,1,0:T(8,128)(2,1)S(1)}, u32[]{:S(2)}, u32[]{:S(2)}) collective-permute-start(bf16[4,8,768]{2,1,0:T(8,128)(2,1)} %param.12), channel_id=1, source_target_pairs={{0,4},{1,5},{2,6},{3,7},{4,8},{5,9},{6,10},{7,11},{8,12},{9,13},{1... | collective-permute-start | bytes 147464 | tf_op jit(solution)/shard_map/ppermute | solution.py:317
  3.7 2.6 %collective-permute-start.2 = (bf16[4,8,768]{2,1,0:T(8,128)(2,1)}, bf16[4,8,768]{2,1,0:T(8,128)(2,1)S(1)}, u32[]{:S(2)}, u32[]{:S(2)}) collective-permute-start(bf16[4,8,768]{2,1,0:T(8,128)(2,1)} %param.12), channel_id=1, source_target_pairs={{0,8},{1,9},{2,10},{3,11},{4,12},{5,13},{6,14},{7,15},{8,0},{9,1},... | collective-permute-start | bytes 147464 | tf_op jit(solution)/shard_map/ppermute | solution.py:317
  6.3 1.3 %collective-permute-start.1 = (bf16[4,8,768]{2,1,0:T(8,128)(2,1)}, bf16[4,8,768]{2,1,0:T(8,128)(2,1)S(1)}, u32[]{:S(2)}, u32[]{:S(2)}) collective-permute-start(bf16[4,8,768]{2,1,0:T(8,128)(2,1)} %param.12), channel_id=1, source_target_pairs={{0,12},{1,13},{2,14},{3,15},{4,0},{5,1},{6,2},{7,3},{8,4},{9,5},{1... | collective-permute-start | bytes 147464 | tf_op jit(solution)/shard_map/ppermute | solution.py:317
  7.7 0.4 %collective-permute-start.7 = (bf16[4,8,768]{2,1,0:T(8,128)(2,1)}, bf16[4,8,768]{2,1,0:T(8,128)(2,1)S(1)}, u32[]{:S(2)}, u32[]{:S(2)}) collective-permute-start(bf16[4,8,768]{2,1,0:T(8,128)(2,1)} %param.13), channel_id=1, source_target_pairs={{0,12},{1,13},{2,14},{3,15},{4,0},{5,1},{6,2},{7,3},{8,4},{9,5},{1... | collective-permute-start | bytes 147464 | tf_op jit(solution)/shard_map/ppermute | solution.py:317
  8.1 1.7 %collective-permute-start.9 = (bf16[4,8,768]{2,1,0:T(8,128)(2,1)}, bf16[4,8,768]{2,1,0:T(8,128)(2,1)S(1)}, u32[]{:S(2)}, u32[]{:S(2)}) collective-permute-start(bf16[4,8,768]{2,1,0:T(8,128)(2,1)} %param.13), channel_id=1, source_target_pairs={{0,8},{1,9},{2,10},{3,11},{4,12},{5,13},{6,14},{7,15},{8,0},{9,1},... | collective-permute-start | bytes 147464 | tf_op jit(solution)/shard_map/ppermute | solution.py:317
  9.8 0.8 %dynamic_update_slice.24 = bf16[4,32,768]{2,1,0:T(8,128)(2,1)S(1)} pad(bf16[4,8,768]{2,1,0:T(8,128)(2,1)} %param.12, bf16[]{:T(256)} %constant.3.clone.1), padding=0_0x0_24x0_0 | pad | bytes 245762 | tf_op jit(solution)/shard_map/dynamic_update_slice | solution.py:329
  10.6 0.0 collective-permute-done
  10.6 0.1 collective-permute-start.8
  10.8 0.0 collective-permute-done.1
  10.8 0.0 collective-permute-done.2
  10.8 1.7 %collective-permute-start.3 = (bf16[4,32,768]{2,1,0:T(8,128)(2,1)S(1)}, bf16[4,32,768]{2,1,0:T(8,128)(2,1)S(1)}, u32[]{:S(2)}, u32[]{:S(2)}) collective-permute-start(bf16[4,32,768]{2,1,0:T(8,128)(2,1)S(1)} %constant_dynamic-update-slice_fusion.3.refs_1_), channel_id=1, source_target_pairs={{0,2},{1,3},{2,0},{3,1},{4,6},{5,7},{6,4},{7,5},{8,10},{9,11},{10,... | collective-permute-start | bytes 589832 | tf_op jit(solution)/shard_map/ppermute | solution.py:317
  12.5 0.8 %copy-done.2 = bf16[4,8,768]{2,1,0:T(8,128)(2,1)S(1)} copy-done((bf16[4,8,768]{2,1,0:T(8,128)(2,1)S(1)}, bf16[4,8,768]{2,1,0:T(8,128)(2,1)}, u32[]{:S(2)}) %copy-start.2) | copy-done | bytes 49176
  13.3 0.1 shard_map.113.refs_0_
  13.4 0.0 collective-permute-done.7
  13.4 0.8 %dynamic_update_slice.28 = bf16[4,32,768]{2,1,0:T(8,128)(2,1)S(1)} pad(bf16[4,8,768]{2,1,0:T(8,128)(2,1)} %param.13, bf16[]{:T(256)} %constant.3.clone.1), padding=0_0x0_24x0_0 | pad | bytes 245762 | tf_op jit(solution)/shard_map/dynamic_update_slice | solution.py:329
  14.3 2.5 %collective-permute-done.8 = bf16[4,8,768]{2,1,0:T(8,128)(2,1)S(1)} collective-permute-done((bf16[4,8,768]{2,1,0:T(8,128)(2,1)}, bf16[4,8,768]{2,1,0:T(8,128)(2,1)S(1)}, u32[]{:S(2)}, u32[]{:S(2)}) %collective-permute-start.8) | collective-permute-done | bytes 49184 | tf_op jit(solution)/shard_map/ppermute | solution.py:317
  16.8 0.0 collective-permute-done.3.refs_2_
  16.8 0.1 collective-permute-start.4
  16.9 0.5 %collective-permute-start.5 = (bf16[4,32,768]{2,1,0:T(8,128)(2,1)S(1)}, bf16[4,32,768]{2,1,0:T(8,128)(2,1)S(1)}, u32[]{:S(2)}, u32[]{:S(2)}) collective-permute-start(bf16[4,32,768]{2,1,0:T(8,128)(2,1)S(1)} %collective-permute-done.3.refs_2_), channel_id=1, source_target_pairs={{0,1},{1,0},{2,3},{3,2},{4,5},{5,4},{6,7},{7,6},{8,9},{9,8},{10,11... | collective-permute-start | bytes 589832 | tf_op jit(solution)/shard_map/ppermute | solution.py:317
  17.4 0.0 collective-permute-done.9
  17.4 1.6 %collective-permute-start.10 = (bf16[4,32,768]{2,1,0:T(8,128)(2,1)S(1)}, bf16[4,32,768]{2,1,0:T(8,128)(2,1)S(1)}, u32[]{:S(2)}, u32[]{:S(2)}) collective-permute-start(bf16[4,32,768]{2,1,0:T(8,128)(2,1)S(1)} %constant_dynamic-update-slice_fusion.refs_1_), channel_id=1, source_target_pairs={{0,2},{1,3},{2,0},{3,1},{4,6},{5,7},{6,4},{7,5},{8,10},{9,11},{10,... | collective-permute-start | bytes 589832 | tf_op jit(solution)/shard_map/ppermute | solution.py:317
  18.9 0.2 shard_map.114.refs_3_
  19.2 0.0 collective-permute-done.4.refs_1_
  19.2 0.0 collective-permute-done.5.refs_2_
  19.2 0.3 shard_map.115.refs_0_
  19.5 1.6 %collective-permute-start.6 = (f32[96,128]{1,0:T(8,128)S(1)}, f32[96,128]{1,0:T(8,128)S(1)}, u32[]{:S(2)}, u32[]{:S(2)}) collective-permute-start(f32[96,128]{1,0:T(8,128)S(1)} %shard_map.115.refs_0_), channel_id=1, source_target_pairs={{0,16},{16,0},{1,17},{17,1},{2,18},{18,2},{3,19},{19,3},{4,20},{20... | collective-permute-start | bytes 147464 | tf_op jit(solution)/shard_map/ppermute | solution.py:422
  21.0 0.1 pad_add_fusion.scalar_ref
  21.8 0.8 %shard_map.116 = (f32[24,128]{1,0:T(8,128)S(1)}, bf16[128,128]{1,0:T(8,128)(2,1)S(1)}, f32[8,128]{1,0:T(8,128)S(1)}, f32[128,64]{1,0:T(8,128)S(1)}, bf16[768,128...) custom-call(s32[2]{0:T(128)S(1)} %pad_add_fusion.scalar_ref, f32[12]{0:T(128)S(1)} %copy-done.5, f32[1]{0:T(128)S(6)} %copy.18.offset_ref), custom_call_target="tpu_custom_call" | custom-call | flops 1000000 | bytes 1000000 | tf_op jit(solution)/shard_map/pallas_call | solution.py:289
  22.6 1.1 %collective-permute-done.6.refs_1_ = f32[96,128]{1,0:T(8,128)S(1)} collective-permute-done((f32[96,128]{1,0:T(8,128)S(1)}, f32[96,128]{1,0:T(8,128)S(1)}, u32[]{:S(2)}, u32[]{:S(2)}) %collective-permute-start.6) | collective-permute-done | bytes 49184 | tf_op jit(solution)/shard_map/ppermute | solution.py:422
  23.6 1.1 %shard_map.117 = (bf16[96,128]{1,0:T(8,128)(2,1)S(1)}, f32[16,24,128]{2,1,0:T(8,128)}) custom-call(f32[96,128]{1,0:T(8,128)S(1)} %shard_map.115.refs_0_, f32[96,128]{1,0:T(8,128)S(1)} %collective-permute-done.6.refs_1_, f32[24,128]{1,0:T(8,128)S(1)} %get-tuple-element.27.refs_2_.factor_ref, bf16[128,128]{1,0:T(8,128)(2,1)S(1)} %get-tuple-element.25.refs_3_), custom_call_target="tpu_custom_call" | custom-call | flops 1000000 | bytes 1000000 | tf_op jit(solution)/shard_map/pallas_call | solution.py:289
  24.7 0.0 collective-permute-done.10.refs_2_
  24.7 0.0 collective-permute-start.11
  24.7 0.5 %collective-permute-start.12 = (bf16[4,32,768]{2,1,0:T(8,128)(2,1)S(1)}, bf16[4,32,768]{2,1,0:T(8,128)(2,1)S(1)}, u32[]{:S(2)}, u32[]{:S(2)}) collective-permute-start(bf16[4,32,768]{2,1,0:T(8,128)(2,1)S(1)} %collective-permute-done.10.refs_2_), channel_id=1, source_target_pairs={{0,1},{1,0},{2,3},{3,2},{4,5},{5,4},{6,7},{7,6},{8,9},{9,8},{10,11... | collective-permute-start | bytes 589832 | tf_op jit(solution)/shard_map/ppermute | solution.py:317
  25.2 5.3 %all-to-all-start = ((f32[16,24,128]{2,1,0:T(8,128)}), f32[16,24,128]{2,1,0:T(8,128)S(1)}, u32[]{:S(2)}, u32[]{:S(2)}) async-start(f32[16,24,128]{2,1,0:T(8,128)} %get-tuple-element.31), calls=%async_computation | async-start | bytes 393216 | tf_op jit(solution)/shard_map/all_to_all | solution.py:455
  30.5 0.0 collective-permute-done.11.refs_3_
  30.5 0.0 collective-permute-done.12.refs_4_
  30.6 0.6 %shard_map.118 = (f32[32,768]{1,0:T(8,128)S(1)}, bf16[32,768]{1,0:T(8,128)(2,1)S(1)}, bf16[1,1152]{1,0:T(2,128)(2,1)S(1)}) custom-call(bf16[96,128]{1,0:T(8,128)(2,1)S(1)} %get-tuple-element.28.refs_0_, bf16[4,32,768]{2,1,0:T(8,128)(2,1)S(1)} %constant_dynamic-update-slice_fusion.refs_1_, bf16[4,32,768]{2,1,0:T(8,128)(2,1)S(1)} %collective-permute-done.10.refs_2_, ...), custom_call_target="tpu_custom_call" | custom-call | flops 1000000 | bytes 1000000 | tf_op jit(solution)/shard_map/pallas_call | solution.py:289
  31.2 1.6 %collective-permute-start.13 = (bf16[32,768]{1,0:T(8,128)(2,1)S(1)}, bf16[32,768]{1,0:T(8,128)(2,1)S(1)}, u32[]{:S(2)}, u32[]{:S(2)}) collective-permute-start(bf16[32,768]{1,0:T(8,128)(2,1)S(1)} %get-tuple-element.34.refs_0_), channel_id=1, source_target_pairs={{0,16},{16,0},{1,17},{17,1},{2,18},{18,2},{3,19},{19,3},{4,20},{20... | collective-permute-start | bytes 147464 | tf_op jit(solution)/shard_map/ppermute | solution.py:463
  32.8 1.6 %broadcast_multiply_fusion.refs_2_ = bf16[768,1152]{1,0:T(8,128)(2,1)S(1)} fusion(bf16[768,1152]{1,0:T(8,128)(2,1)} %param.16, bf16[1152]{0:T(1024)(128)(2,1)S(1)} %reduce), kind=kLoop, calls=%fused_computation | loop fusion | flops 884736 | bytes 3541248 | tf_op jit(solution)/shard_map/mul | solution.py:464
  34.4 0.0 copy-start.1
  34.5 0.9 %collective-permute-done.13.refs_1_ = bf16[32,768]{1,0:T(8,128)(2,1)S(1)} collective-permute-done((bf16[32,768]{1,0:T(8,128)(2,1)S(1)}, bf16[32,768]{1,0:T(8,128)(2,1)S(1)}, u32[]{:S(2)}, u32[]{:S(2)}) %collective-permute-start.13) | collective-permute-done | bytes 49184 | tf_op jit(solution)/shard_map/ppermute | solution.py:463
  35.4 0.4 %shard_map.119.own_ref = bf16[64,1152]{1,0:T(8,128)(2,1)S(1)} custom-call(bf16[32,768]{1,0:T(8,128)(2,1)S(1)} %get-tuple-element.34.refs_0_, bf16[32,768]{1,0:T(8,128)(2,1)S(1)} %collective-permute-done.13.refs_1_, bf16[768,1152]{1,0:T(8,128)(2,1)S(1)} %broadcast_multiply_fusion.refs_2_), custom_call_target="tpu_custom_call" | custom-call | flops 1000000 | bytes 1000000 | tf_op jit(solution)/shard_map/pallas_call | solution.py:289
  35.8 1.6 %collective-permute-start.14 = (bf16[64,1152]{1,0:T(8,128)(2,1)S(1)}, bf16[64,1152]{1,0:T(8,128)(2,1)S(1)}, u32[]{:S(2)}, u32[]{:S(2)}) collective-permute-start(bf16[64,1152]{1,0:T(8,128)(2,1)S(1)} %shard_map.119.own_ref), channel_id=1, source_target_pairs={{0,16},{16,0},{1,17},{17,1},{2,18},{18,2},{3,19},{19,3},{4,20},{20... | collective-permute-start | bytes 442376 | tf_op jit(solution)/shard_map/ppermute | solution.py:476
  37.4 2.2 %all-to-all-done.pair_ref = f32[16,24,128]{2,1,0:T(8,128)S(1)} async-done(((f32[16,24,128]{2,1,0:T(8,128)}), f32[16,24,128]{2,1,0:T(8,128)S(1)}, u32[]{:S(2)}, u32[]{:S(2)}) %all-to-all-start) | async-done | bytes 196640 | tf_op jit(solution)/shard_map/all_to_all | solution.py:455
  39.5 1.0 %shard_map.121 = f32[8,64]{1,0:T(8,128)} custom-call(f32[16,24,128]{2,1,0:T(8,128)S(1)} %all-to-all-done.pair_ref, f32[24,128]{1,0:T(8,128)S(1)} %get-tuple-element.27.refs_2_.factor_ref, f32[8,128]{1,0:T(8,128)S(1)} %get-tuple-element.40.own_ref, f32[128,64]{1,0:T(8,128)S(1)} %get-tuple-element.41.slab_ref), custom_call_target="tpu_custom_call" | custom-call | flops 1000000 | bytes 1000000 | tf_op jit(solution)/shard_map/pallas_call | solution.py:289
  40.6 0.6 %collective-permute-done.14.other_ref = bf16[64,1152]{1,0:T(8,128)(2,1)S(1)} collective-permute-done((bf16[64,1152]{1,0:T(8,128)(2,1)S(1)}, bf16[64,1152]{1,0:T(8,128)(2,1)S(1)}, u32[]{:S(2)}, u32[]{:S(2)}) %collective-permute-start.14) | collective-permute-done | bytes 147488 | tf_op jit(solution)/shard_map/ppermute | solution.py:476
  41.2 1.4 %shard_map.120 = bf16[4,8,768]{2,1,0:T(8,128)(2,1)} custom-call(bf16[64,1152]{1,0:T(8,128)(2,1)S(1)} %shard_map.119.own_ref, bf16[64,1152]{1,0:T(8,128)(2,1)S(1)} %collective-permute-done.14.other_ref, f32[32,768]{1,0:T(8,128)S(1)} %get-tuple-element.36.refs_0_, bf16[768,768]{1,0:T(8,128)(2,1)S(1)} %copy-done.1, ...), custom_call_target="tpu_custom_call" | custom-call | flops 1000000 | bytes 1000000 | tf_op jit(solution)/shard_map/pallas_call | solution.py:289
  (16 shorter events, 0.1 us)
Async XLA Ops:
  0.6 29.9 %copy-start = (bf16[768,768]{1,0:T(8,128)(2,1)S(1)}, bf16[768,768]{1,0:T(8,128)(2,1)}, u32[]{:S(2)}) copy-start(bf16[768,768]{1,0:T(8,128)(2,1)} %refs_5_.1) | copy-start | bytes 3538948
  0.6 10.0 %collective-permute-start = (bf16[4,8,768]{2,1,0:T(8,128)(2,1)}, bf16[4,8,768]{2,1,0:T(8,128)(2,1)S(1)}, u32[]{:S(2)}, u32[]{:S(2)}) collective-permute-start(bf16[4,8,768]{2,1,0:T(8,128)(2,1)} %param.12), channel_id=1, source_target_pairs={{0,4},{1,5},{2,6},{3,7},{4,8},{5,9},{6,10},{7,11},{8,12},{9,13},{1... | collective-permute-start | bytes 147464 | tf_op jit(solution)/shard_map/ppermute | solution.py:317
  3.7 7.1 %collective-permute-start.2 = (bf16[4,8,768]{2,1,0:T(8,128)(2,1)}, bf16[4,8,768]{2,1,0:T(8,128)(2,1)S(1)}, u32[]{:S(2)}, u32[]{:S(2)}) collective-permute-start(bf16[4,8,768]{2,1,0:T(8,128)(2,1)} %param.12), channel_id=1, source_target_pairs={{0,8},{1,9},{2,10},{3,11},{4,12},{5,13},{6,14},{7,15},{8,0},{9,1},... | collective-permute-start | bytes 147464 | tf_op jit(solution)/shard_map/ppermute | solution.py:317
  6.3 4.5 %collective-permute-start.1 = (bf16[4,8,768]{2,1,0:T(8,128)(2,1)}, bf16[4,8,768]{2,1,0:T(8,128)(2,1)S(1)}, u32[]{:S(2)}, u32[]{:S(2)}) collective-permute-start(bf16[4,8,768]{2,1,0:T(8,128)(2,1)} %param.12), channel_id=1, source_target_pairs={{0,12},{1,13},{2,14},{3,15},{4,0},{5,1},{6,2},{7,3},{8,4},{9,5},{1... | collective-permute-start | bytes 147464 | tf_op jit(solution)/shard_map/ppermute | solution.py:317
  7.7 5.8 %collective-permute-start.7 = (bf16[4,8,768]{2,1,0:T(8,128)(2,1)}, bf16[4,8,768]{2,1,0:T(8,128)(2,1)S(1)}, u32[]{:S(2)}, u32[]{:S(2)}) collective-permute-start(bf16[4,8,768]{2,1,0:T(8,128)(2,1)} %param.13), channel_id=1, source_target_pairs={{0,12},{1,13},{2,14},{3,15},{4,0},{5,1},{6,2},{7,3},{8,4},{9,5},{1... | collective-permute-start | bytes 147464 | tf_op jit(solution)/shard_map/ppermute | solution.py:317
  8.1 9.3 %collective-permute-start.9 = (bf16[4,8,768]{2,1,0:T(8,128)(2,1)}, bf16[4,8,768]{2,1,0:T(8,128)(2,1)S(1)}, u32[]{:S(2)}, u32[]{:S(2)}) collective-permute-start(bf16[4,8,768]{2,1,0:T(8,128)(2,1)} %param.13), channel_id=1, source_target_pairs={{0,8},{1,9},{2,10},{3,11},{4,12},{5,13},{6,14},{7,15},{8,0},{9,1},... | collective-permute-start | bytes 147464 | tf_op jit(solution)/shard_map/ppermute | solution.py:317
  10.6 6.2 %collective-permute-start.8 = (bf16[4,8,768]{2,1,0:T(8,128)(2,1)}, bf16[4,8,768]{2,1,0:T(8,128)(2,1)S(1)}, u32[]{:S(2)}, u32[]{:S(2)}) collective-permute-start(bf16[4,8,768]{2,1,0:T(8,128)(2,1)} %param.13), channel_id=1, source_target_pairs={{0,4},{1,5},{2,6},{3,7},{4,8},{5,9},{6,10},{7,11},{8,12},{9,13},{1... | collective-permute-start | bytes 147464 | tf_op jit(solution)/shard_map/ppermute | solution.py:317
  10.8 6.0 %collective-permute-start.3 = (bf16[4,32,768]{2,1,0:T(8,128)(2,1)S(1)}, bf16[4,32,768]{2,1,0:T(8,128)(2,1)S(1)}, u32[]{:S(2)}, u32[]{:S(2)}) collective-permute-start(bf16[4,32,768]{2,1,0:T(8,128)(2,1)S(1)} %constant_dynamic-update-slice_fusion.3.refs_1_), channel_id=1, source_target_pairs={{0,2},{1,3},{2,0},{3,1},{4,6},{5,7},{6,4},{7,5},{8,10},{9,11},{10,... | collective-permute-start | bytes 589832 | tf_op jit(solution)/shard_map/ppermute | solution.py:317
  12.5 0.8 %copy-start.2 = (bf16[4,8,768]{2,1,0:T(8,128)(2,1)S(1)}, bf16[4,8,768]{2,1,0:T(8,128)(2,1)}, u32[]{:S(2)}) copy-start(bf16[4,8,768]{2,1,0:T(8,128)(2,1)} %q_hbm) | copy-start | bytes 147460
  13.3 8.4 %copy-start.5 = (f32[12]{0:T(128)S(1)}, f32[12]{0:T(128)}, u32[]{:S(2)}) copy-start(f32[12]{0:T(128)} %factor_ref.1) | copy-start | bytes 148
  13.3 17.2 %copy-start.3 = (bf16[4,8,768]{2,1,0:T(8,128)(2,1)S(1)}, bf16[4,8,768]{2,1,0:T(8,128)(2,1)}, u32[]{:S(2)}) copy-start(bf16[4,8,768]{2,1,0:T(8,128)(2,1)} %refs_6_.1) | copy-start | bytes 147460
  13.3 17.2 %copy-start.4 = (f32[768]{0:T(1024)S(1)}, f32[768]{0:T(1024)}, u32[]{:S(2)}) copy-start(f32[768]{0:T(1024)} %refs_7_.1) | copy-start | bytes 9220
  16.8 2.4 %collective-permute-start.4 = (bf16[4,32,768]{2,1,0:T(8,128)(2,1)S(1)}, bf16[4,32,768]{2,1,0:T(8,128)(2,1)S(1)}, u32[]{:S(2)}, u32[]{:S(2)}) collective-permute-start(bf16[4,32,768]{2,1,0:T(8,128)(2,1)S(1)} %constant_dynamic-update-slice_fusion.3.refs_1_), channel_id=1, source_target_pairs={{0,1},{1,0},{2,3},{3,2},{4,5},{5,4},{6,7},{7,6},{8,9},{9,8},{10,11... | collective-permute-start | bytes 589832 | tf_op jit(solution)/shard_map/ppermute | solution.py:317
  16.9 2.3 %collective-permute-start.5 = (bf16[4,32,768]{2,1,0:T(8,128)(2,1)S(1)}, bf16[4,32,768]{2,1,0:T(8,128)(2,1)S(1)}, u32[]{:S(2)}, u32[]{:S(2)}) collective-permute-start(bf16[4,32,768]{2,1,0:T(8,128)(2,1)S(1)} %collective-permute-done.3.refs_2_), channel_id=1, source_target_pairs={{0,1},{1,0},{2,3},{3,2},{4,5},{5,4},{6,7},{7,6},{8,9},{9,8},{10,11... | collective-permute-start | bytes 589832 | tf_op jit(solution)/shard_map/ppermute | solution.py:317
  17.4 7.4 %collective-permute-start.10 = (bf16[4,32,768]{2,1,0:T(8,128)(2,1)S(1)}, bf16[4,32,768]{2,1,0:T(8,128)(2,1)S(1)}, u32[]{:S(2)}, u32[]{:S(2)}) collective-permute-start(bf16[4,32,768]{2,1,0:T(8,128)(2,1)S(1)} %constant_dynamic-update-slice_fusion.refs_1_), channel_id=1, source_target_pairs={{0,2},{1,3},{2,0},{3,1},{4,6},{5,7},{6,4},{7,5},{8,10},{9,11},{10,... | collective-permute-start | bytes 589832 | tf_op jit(solution)/shard_map/ppermute | solution.py:317
  19.5 4.2 %collective-permute-start.6 = (f32[96,128]{1,0:T(8,128)S(1)}, f32[96,128]{1,0:T(8,128)S(1)}, u32[]{:S(2)}, u32[]{:S(2)}) collective-permute-start(f32[96,128]{1,0:T(8,128)S(1)} %shard_map.115.refs_0_), channel_id=1, source_target_pairs={{0,16},{16,0},{1,17},{17,1},{2,18},{18,2},{3,19},{19,3},{4,20},{20... | collective-permute-start | bytes 147464 | tf_op jit(solution)/shard_map/ppermute | solution.py:422
  24.7 5.8 %collective-permute-start.11 = (bf16[4,32,768]{2,1,0:T(8,128)(2,1)S(1)}, bf16[4,32,768]{2,1,0:T(8,128)(2,1)S(1)}, u32[]{:S(2)}, u32[]{:S(2)}) collective-permute-start(bf16[4,32,768]{2,1,0:T(8,128)(2,1)S(1)} %constant_dynamic-update-slice_fusion.refs_1_), channel_id=1, source_target_pairs={{0,1},{1,0},{2,3},{3,2},{4,5},{5,4},{6,7},{7,6},{8,9},{9,8},{10,11... | collective-permute-start | bytes 589832 | tf_op jit(solution)/shard_map/ppermute | solution.py:317
  24.7 5.8 %collective-permute-start.12 = (bf16[4,32,768]{2,1,0:T(8,128)(2,1)S(1)}, bf16[4,32,768]{2,1,0:T(8,128)(2,1)S(1)}, u32[]{:S(2)}, u32[]{:S(2)}) collective-permute-start(bf16[4,32,768]{2,1,0:T(8,128)(2,1)S(1)} %collective-permute-done.10.refs_2_), channel_id=1, source_target_pairs={{0,1},{1,0},{2,3},{3,2},{4,5},{5,4},{6,7},{7,6},{8,9},{9,8},{10,11... | collective-permute-start | bytes 589832 | tf_op jit(solution)/shard_map/ppermute | solution.py:317
  25.2 14.3 %all-to-all-start = ((f32[16,24,128]{2,1,0:T(8,128)}), f32[16,24,128]{2,1,0:T(8,128)S(1)}, u32[]{:S(2)}, u32[]{:S(2)}) async-start(f32[16,24,128]{2,1,0:T(8,128)} %get-tuple-element.31), calls=%async_computation | async-start | bytes 393216 | tf_op jit(solution)/shard_map/all_to_all | solution.py:455
  31.2 4.2 %collective-permute-start.13 = (bf16[32,768]{1,0:T(8,128)(2,1)S(1)}, bf16[32,768]{1,0:T(8,128)(2,1)S(1)}, u32[]{:S(2)}, u32[]{:S(2)}) collective-permute-start(bf16[32,768]{1,0:T(8,128)(2,1)S(1)} %get-tuple-element.34.refs_0_), channel_id=1, source_target_pairs={{0,16},{16,0},{1,17},{17,1},{2,18},{18,2},{3,19},{19,3},{4,20},{20... | collective-permute-start | bytes 147464 | tf_op jit(solution)/shard_map/ppermute | solution.py:463
  34.4 6.8 %copy-start.1 = (bf16[768,768]{1,0:T(8,128)(2,1)S(1)}, bf16[768,768]{1,0:T(8,128)(2,1)}, u32[]{:S(2)}) copy-start(bf16[768,768]{1,0:T(8,128)(2,1)} %refs_1_) | copy-start | bytes 3538948
  35.8 5.4 %collective-permute-start.14 = (bf16[64,1152]{1,0:T(8,128)(2,1)S(1)}, bf16[64,1152]{1,0:T(8,128)(2,1)S(1)}, u32[]{:S(2)}, u32[]{:S(2)}) collective-permute-start(bf16[64,1152]{1,0:T(8,128)(2,1)S(1)} %shard_map.119.own_ref), channel_id=1, source_target_pairs={{0,16},{16,0},{1,17},{17,1},{2,18},{18,2},{3,19},{19,3},{4,20},{20... | collective-permute-start | bytes 442376 | tf_op jit(solution)/shard_map/ppermute | solution.py:476

commit v16 on v14

--- a/solution.py
+++ b/solution.py
@@ -383,12 +383,6 @@
     )
     if middle:
         key_parts += send_all(key_parts, pos_count, middle)
-    near = sum(part.shape[1] for part in key_parts)
-    partial = call(
-        functools.partial(logits_kernel, len(key_parts)),
-        jax.ShapeDtypeStruct((heads * sites, near), F32),
-        [masked, *key_parts],
-    )
     value_first[-1] = after(value_first[-1], masked)
     value_own = lay_together(
         value_first, [0, *range(size - 1, size - 2, -1), *range(1, size - 2), *range(max(size - 2, 1), size - 1)]
@@ -397,12 +391,12 @@
     if middle:
         value_parts += send_all(value_parts, pos_count, middle)
     if len(stages) > 2:
-        far_parts = send_all(key_parts, pos_count, stages[2])
-        partial = call(
-            functools.partial(logits_kernel, len(far_parts)),
-            jax.ShapeDtypeStruct((heads * sites, length), F32),
-            [masked, *far_parts, partial],
-        )
+        key_parts += send_all(key_parts, pos_count, stages[2])
+    partial = call(
+        functools.partial(logits_kernel, len(key_parts)),
+        jax.ShapeDtypeStruct((heads * sites, length), F32),
+        [masked, *key_parts],
+    )
     padded = round_up(heads, 128)
     head_factors, order, own_select, slab_select, pick, spread = call(
         functools.partial(prepare_kernel, heads, sites, stages),

time: 42.6 us -> 44.3 us (1.040)
  waiting for transfers between devices: 7.25 us -> 8.65 us
    ppermute x12, waiting for transfers between devices: 2.54 us -> 3.95 us  [send_pos(): return lax.ppermute(array, 'pos', pairs)]
    pallas_call x9 -> x8, Pallas kernels: 6.02 us -> 5.85 us  [call(): pl.pallas_call(kernel, out_shape=out_shape, in_specs=specs, out_specs=jax...]
  transfers between devices with their start and end apart: 16 -> 16, of which waited for: 5 -> 7; matrix products, arithmetic and copies ran while one was open for 8% -> 8% of each run, Pallas kernels for 11% -> 10%
where the time goes in v16:
time: 44.3 us; the launch traced here: 43.9 us
  starting transfers between devices  23.7 us (53%)
  waiting for transfers between devices  8.65 us (20%)
  Pallas kernels  5.85 us (13%)
  local copies, waits for them, and re-layouts  2.47 us (6%)
  other arithmetic  1.74 us (4%)
  between operations  1.47 us (3%)
    ppermute x12, starting transfers between devices, send_pos(): return lax.ppermute(array, 'pos', pairs)  12.9 us
    all_to_all x1, starting transfers between devices, per_device(): lax.all_to_all(pair_local, 'pos', split_axis=0, concat_axis=0, tiled=True)  6.19 us
    pallas_call x8, Pallas kernels, call(): pl.pallas_call(kernel, out_shape=out_shape, in_specs=specs, out_specs=jax...  5.85 us
    ppermute x12, waiting for transfers between devices, send_pos(): return lax.ppermute(array, 'pos', pairs)  3.95 us
    all_to_all x1, waiting for transfers between devices, per_device(): lax.all_to_all(pair_local, 'pos', split_axis=0, concat_axis=0, tiled=True)  2.15 us
    dynamic_update_slice x8, local copies, waits for them, and re-layouts, lay_together(): whole = lax.dynamic_update_slice(whole, parts[at], (0, at * size, 0))  1.66 us
    mul x1, other arithmetic, per_device(): weight = upright_threefold_linear * one  1.64 us
    ppermute x1, starting transfers between devices, per_device(): lax.ppermute(projected, 'seq', swap)  1.56 us
  transfers between devices with their start and end apart: 16, of which 7 were waited for; matrix products, arithmetic and copies ran while one was open for 8% of the time, Pallas kernels for 10%

profile of v16, /device:TPU:0, one launch (start us, length us, event | category | flops | bytes accessed | tf_op | source)
XLA Modules:
  0.0 43.9 jit_solution(2182151027384572739)
XLA Ops:
  0.6 0.0 copy-start
  0.6 3.1 %collective-permute-start = (bf16[4,8,768]{2,1,0:T(8,128)(2,1)}, bf16[4,8,768]{2,1,0:T(8,128)(2,1)S(1)}, u32[]{:S(2)}, u32[]{:S(2)}) collective-permute-start(bf16[4,8,768]{2,1,0:T(8,128)(2,1)} %param.12), channel_id=1, source_target_pairs={{0,4},{1,5},{2,6},{3,7},{4,8},{5,9},{6,10},{7,11},{8,12},{9,13},{1... | collective-permute-start | bytes 147464 | tf_op jit(solution)/shard_map/ppermute | solution.py:317
  3.7 2.6 %collective-permute-start.2 = (bf16[4,8,768]{2,1,0:T(8,128)(2,1)}, bf16[4,8,768]{2,1,0:T(8,128)(2,1)S(1)}, u32[]{:S(2)}, u32[]{:S(2)}) collective-permute-start(bf16[4,8,768]{2,1,0:T(8,128)(2,1)} %param.12), channel_id=1, source_target_pairs={{0,8},{1,9},{2,10},{3,11},{4,12},{5,13},{6,14},{7,15},{8,0},{9,1},... | collective-permute-start | bytes 147464 | tf_op jit(solution)/shard_map/ppermute | solution.py:317
  6.3 1.3 %collective-permute-start.1 = (bf16[4,8,768]{2,1,0:T(8,128)(2,1)}, bf16[4,8,768]{2,1,0:T(8,128)(2,1)S(1)}, u32[]{:S(2)}, u32[]{:S(2)}) collective-permute-start(bf16[4,8,768]{2,1,0:T(8,128)(2,1)} %param.12), channel_id=1, source_target_pairs={{0,12},{1,13},{2,14},{3,15},{4,0},{5,1},{6,2},{7,3},{8,4},{9,5},{1... | collective-permute-start | bytes 147464 | tf_op jit(solution)/shard_map/ppermute | solution.py:317
  7.7 0.4 %collective-permute-start.7 = (bf16[4,8,768]{2,1,0:T(8,128)(2,1)}, bf16[4,8,768]{2,1,0:T(8,128)(2,1)S(1)}, u32[]{:S(2)}, u32[]{:S(2)}) collective-permute-start(bf16[4,8,768]{2,1,0:T(8,128)(2,1)} %param.13), channel_id=1, source_target_pairs={{0,12},{1,13},{2,14},{3,15},{4,0},{5,1},{6,2},{7,3},{8,4},{9,5},{1... | collective-permute-start | bytes 147464 | tf_op jit(solution)/shard_map/ppermute | solution.py:317
  8.1 1.7 %collective-permute-start.9 = (bf16[4,8,768]{2,1,0:T(8,128)(2,1)}, bf16[4,8,768]{2,1,0:T(8,128)(2,1)S(1)}, u32[]{:S(2)}, u32[]{:S(2)}) collective-permute-start(bf16[4,8,768]{2,1,0:T(8,128)(2,1)} %param.13), channel_id=1, source_target_pairs={{0,8},{1,9},{2,10},{3,11},{4,12},{5,13},{6,14},{7,15},{8,0},{9,1},... | collective-permute-start | bytes 147464 | tf_op jit(solution)/shard_map/ppermute | solution.py:317
  9.8 0.8 %dynamic_update_slice.24 = bf16[4,32,768]{2,1,0:T(8,128)(2,1)S(1)} pad(bf16[4,8,768]{2,1,0:T(8,128)(2,1)} %param.12, bf16[]{:T(256)} %constant.3.clone.1), padding=0_0x0_24x0_0 | pad | bytes 245762 | tf_op jit(solution)/shard_map/dynamic_update_slice | solution.py:329
  10.6 0.0 collective-permute-done
  10.6 0.1 collective-permute-start.8
  10.8 0.0 collective-permute-done.1
  10.8 0.0 collective-permute-done.2
  10.8 0.1 collective-permute-start.4
  10.9 1.7 %collective-permute-start.3 = (bf16[4,32,768]{2,1,0:T(8,128)(2,1)S(1)}, bf16[4,32,768]{2,1,0:T(8,128)(2,1)S(1)}, u32[]{:S(2)}, u32[]{:S(2)}) collective-permute-start(bf16[4,32,768]{2,1,0:T(8,128)(2,1)S(1)} %constant_dynamic-update-slice_fusion.3.refs_1_), channel_id=1, source_target_pairs={{0,2},{1,3},{2,0},{3,1},{4,6},{5,7},{6,4},{7,5},{8,10},{9,11},{10,... | collective-permute-start | bytes 589832 | tf_op jit(solution)/shard_map/ppermute | solution.py:317
  12.6 0.8 %copy-done.2 = bf16[4,8,768]{2,1,0:T(8,128)(2,1)S(1)} copy-done((bf16[4,8,768]{2,1,0:T(8,128)(2,1)S(1)}, bf16[4,8,768]{2,1,0:T(8,128)(2,1)}, u32[]{:S(2)}) %copy-start.2) | copy-done | bytes 49176
  13.4 0.1 shard_map.113.refs_0_
  13.5 0.0 collective-permute-done.7
  13.5 0.8 %dynamic_update_slice.28 = bf16[4,32,768]{2,1,0:T(8,128)(2,1)S(1)} pad(bf16[4,8,768]{2,1,0:T(8,128)(2,1)} %param.13, bf16[]{:T(256)} %constant.3.clone.1), padding=0_0x0_24x0_0 | pad | bytes 245762 | tf_op jit(solution)/shard_map/dynamic_update_slice | solution.py:329
  14.3 2.4 %collective-permute-done.8 = bf16[4,8,768]{2,1,0:T(8,128)(2,1)S(1)} collective-permute-done((bf16[4,8,768]{2,1,0:T(8,128)(2,1)}, bf16[4,8,768]{2,1,0:T(8,128)(2,1)S(1)}, u32[]{:S(2)}, u32[]{:S(2)}) %collective-permute-start.8) | collective-permute-done | bytes 49184 | tf_op jit(solution)/shard_map/ppermute | solution.py:317
  16.8 1.4 %collective-permute-done.3.refs_2_ = bf16[4,32,768]{2,1,0:T(8,128)(2,1)S(1)} collective-permute-done((bf16[4,32,768]{2,1,0:T(8,128)(2,1)S(1)}, bf16[4,32,768]{2,1,0:T(8,128)(2,1)S(1)}, u32[]{:S(2)}, u32[]{:S(2)}) %collective-permute-start.3) | collective-permute-done | bytes 196640 | tf_op jit(solution)/shard_map/ppermute | solution.py:317
  18.2 0.0 collective-permute-start.5
  18.2 0.0 collective-permute-done.9
  18.2 1.7 %collective-permute-start.10 = (bf16[4,32,768]{2,1,0:T(8,128)(2,1)S(1)}, bf16[4,32,768]{2,1,0:T(8,128)(2,1)S(1)}, u32[]{:S(2)}, u32[]{:S(2)}) collective-permute-start(bf16[4,32,768]{2,1,0:T(8,128)(2,1)S(1)} %constant_dynamic-update-slice_fusion.refs_1_), channel_id=1, source_target_pairs={{0,2},{1,3},{2,0},{3,1},{4,6},{5,7},{6,4},{7,5},{8,10},{9,11},{10,... | collective-permute-start | bytes 589832 | tf_op jit(solution)/shard_map/ppermute | solution.py:317
  19.9 0.0 collective-permute-done.4.refs_3_
  19.9 0.0 collective-permute-done.5.refs_4_
  19.9 0.4 shard_map.114.refs_0_
  20.3 1.5 %collective-permute-start.6 = (f32[96,128]{1,0:T(8,128)S(1)}, f32[96,128]{1,0:T(8,128)S(1)}, u32[]{:S(2)}, u32[]{:S(2)}) collective-permute-start(f32[96,128]{1,0:T(8,128)S(1)} %shard_map.114.refs_0_), channel_id=1, source_target_pairs={{0,16},{16,0},{1,17},{17,1},{2,18},{18,2},{3,19},{19,3},{4,20},{20... | collective-permute-start | bytes 147464 | tf_op jit(solution)/shard_map/ppermute | solution.py:415
  21.8 0.1 pad_add_fusion.scalar_ref
  22.5 0.1 collective-permute-start.11
  22.6 0.0 copy-done.5
  22.6 0.8 %shard_map.115 = (f32[24,128]{1,0:T(8,128)S(1)}, bf16[128,128]{1,0:T(8,128)(2,1)S(1)}, f32[8,128]{1,0:T(8,128)S(1)}, f32[128,64]{1,0:T(8,128)S(1)}, bf16[768,128...) custom-call(s32[2]{0:T(128)S(1)} %pad_add_fusion.scalar_ref, f32[12]{0:T(128)S(1)} %copy-done.5, f32[1]{0:T(128)S(6)} %copy.18.offset_ref), custom_call_target="tpu_custom_call" | custom-call | flops 1000000 | bytes 1000000 | tf_op jit(solution)/shard_map/pallas_call | solution.py:289
  23.4 1.0 %collective-permute-done.6.refs_1_ = f32[96,128]{1,0:T(8,128)S(1)} collective-permute-done((f32[96,128]{1,0:T(8,128)S(1)}, f32[96,128]{1,0:T(8,128)S(1)}, u32[]{:S(2)}, u32[]{:S(2)}) %collective-permute-start.6) | collective-permute-done | bytes 49184 | tf_op jit(solution)/shard_map/ppermute | solution.py:415
  24.4 1.1 %shard_map.116 = (bf16[96,128]{1,0:T(8,128)(2,1)S(1)}, f32[16,24,128]{2,1,0:T(8,128)}) custom-call(f32[96,128]{1,0:T(8,128)S(1)} %shard_map.114.refs_0_, f32[96,128]{1,0:T(8,128)S(1)} %collective-permute-done.6.refs_1_, f32[24,128]{1,0:T(8,128)S(1)} %get-tuple-element.24.refs_2_.factor_ref, bf16[128,128]{1,0:T(8,128)(2,1)S(1)} %get-tuple-element.22.refs_3_), custom_call_target="tpu_custom_call" | custom-call | flops 1000000 | bytes 1000000 | tf_op jit(solution)/shard_map/pallas_call | solution.py:289
  25.5 0.1 collective-permute-done.10.refs_2_
  25.6 0.0 collective-permute-start.12
  25.6 6.2 %all-to-all-start = ((f32[16,24,128]{2,1,0:T(8,128)}), f32[16,24,128]{2,1,0:T(8,128)S(1)}, u32[]{:S(2)}, u32[]{:S(2)}) async-start(f32[16,24,128]{2,1,0:T(8,128)} %get-tuple-element.28), calls=%async_computation | async-start | bytes 393216 | tf_op jit(solution)/shard_map/all_to_all | solution.py:448
  31.8 0.0 collective-permute-done.11.refs_3_
  31.8 0.0 collective-permute-done.12.refs_4_
  31.8 0.6 %shard_map.117 = (f32[32,768]{1,0:T(8,128)S(1)}, bf16[32,768]{1,0:T(8,128)(2,1)S(1)}, bf16[1,1152]{1,0:T(2,128)(2,1)S(1)}) custom-call(bf16[96,128]{1,0:T(8,128)(2,1)S(1)} %get-tuple-element.25.refs_0_, bf16[4,32,768]{2,1,0:T(8,128)(2,1)S(1)} %constant_dynamic-update-slice_fusion.refs_1_, bf16[4,32,768]{2,1,0:T(8,128)(2,1)S(1)} %collective-permute-done.10.refs_2_, ...), custom_call_target="tpu_custom_call" | custom-call | flops 1000000 | bytes 1000000 | tf_op jit(solution)/shard_map/pallas_call | solution.py:289
  32.5 1.6 %collective-permute-start.13 = (bf16[32,768]{1,0:T(8,128)(2,1)S(1)}, bf16[32,768]{1,0:T(8,128)(2,1)S(1)}, u32[]{:S(2)}, u32[]{:S(2)}) collective-permute-start(bf16[32,768]{1,0:T(8,128)(2,1)S(1)} %get-tuple-element.30.refs_0_), channel_id=1, source_target_pairs={{0,16},{16,0},{1,17},{17,1},{2,18},{18,2},{3,19},{19,3},{4,20},{20... | collective-permute-start | bytes 147464 | tf_op jit(solution)/shard_map/ppermute | solution.py:456
  34.1 1.6 %broadcast_multiply_fusion.refs_2_ = bf16[768,1152]{1,0:T(8,128)(2,1)S(1)} fusion(bf16[768,1152]{1,0:T(8,128)(2,1)} %param.16, bf16[1152]{0:T(1024)(128)(2,1)S(1)} %reduce), kind=kLoop, calls=%fused_computation | loop fusion | flops 884736 | bytes 3541248 | tf_op jit(solution)/shard_map/mul | solution.py:457
  35.7 0.0 copy-start.1
  35.7 0.9 %collective-permute-done.13.refs_1_ = bf16[32,768]{1,0:T(8,128)(2,1)S(1)} collective-permute-done((bf16[32,768]{1,0:T(8,128)(2,1)S(1)}, bf16[32,768]{1,0:T(8,128)(2,1)S(1)}, u32[]{:S(2)}, u32[]{:S(2)}) %collective-permute-start.13) | collective-permute-done | bytes 49184 | tf_op jit(solution)/shard_map/ppermute | solution.py:456
  36.6 0.4 shard_map.118.own_ref
  37.1 1.6 %collective-permute-start.14 = (bf16[64,1152]{1,0:T(8,128)(2,1)S(1)}, bf16[64,1152]{1,0:T(8,128)(2,1)S(1)}, u32[]{:S(2)}, u32[]{:S(2)}) collective-permute-start(bf16[64,1152]{1,0:T(8,128)(2,1)S(1)} %shard_map.118.own_ref), channel_id=1, source_target_pairs={{0,16},{16,0},{1,17},{17,1},{2,18},{18,2},{3,19},{19,3},{4,20},{20... | collective-permute-start | bytes 442376 | tf_op jit(solution)/shard_map/ppermute | solution.py:469
  38.6 2.2 %all-to-all-done.pair_ref = f32[16,24,128]{2,1,0:T(8,128)S(1)} async-done(((f32[16,24,128]{2,1,0:T(8,128)}), f32[16,24,128]{2,1,0:T(8,128)S(1)}, u32[]{:S(2)}, u32[]{:S(2)}) %all-to-all-start) | async-done | bytes 196640 | tf_op jit(solution)/shard_map/all_to_all | solution.py:448
  40.8 1.0 %shard_map.120 = f32[8,64]{1,0:T(8,128)} custom-call(f32[16,24,128]{2,1,0:T(8,128)S(1)} %all-to-all-done.pair_ref, f32[24,128]{1,0:T(8,128)S(1)} %get-tuple-element.24.refs_2_.factor_ref, f32[8,128]{1,0:T(8,128)S(1)} %get-tuple-element.36.own_ref, f32[128,64]{1,0:T(8,128)S(1)} %get-tuple-element.37.slab_ref), custom_call_target="tpu_custom_call" | custom-call | flops 1000000 | bytes 1000000 | tf_op jit(solution)/shard_map/pallas_call | solution.py:289
  41.8 0.6 %collective-permute-done.14.other_ref = bf16[64,1152]{1,0:T(8,128)(2,1)S(1)} collective-permute-done((bf16[64,1152]{1,0:T(8,128)(2,1)S(1)}, bf16[64,1152]{1,0:T(8,128)(2,1)S(1)}, u32[]{:S(2)}, u32[]{:S(2)}) %collective-permute-start.14) | collective-permute-done | bytes 147488 | tf_op jit(solution)/shard_map/ppermute | solution.py:469
  42.5 1.4 %shard_map.119 = bf16[4,8,768]{2,1,0:T(8,128)(2,1)} custom-call(bf16[64,1152]{1,0:T(8,128)(2,1)S(1)} %shard_map.118.own_ref, bf16[64,1152]{1,0:T(8,128)(2,1)S(1)} %collective-permute-done.14.other_ref, f32[32,768]{1,0:T(8,128)S(1)} %get-tuple-element.32.refs_0_, bf16[768,768]{1,0:T(8,128)(2,1)S(1)} %copy-done.1, ...), custom_call_target="tpu_custom_call" | custom-call | flops 1000000 | bytes 1000000 | tf_op jit(solution)/shard_map/pallas_call | solution.py:289
  (15 shorter events, 0.1 us)
Async XLA Ops:
  0.6 31.2 %copy-start = (bf16[768,768]{1,0:T(8,128)(2,1)S(1)}, bf16[768,768]{1,0:T(8,128)(2,1)}, u32[]{:S(2)}) copy-start(bf16[768,768]{1,0:T(8,128)(2,1)} %refs_5_.1) | copy-start | bytes 3538948
  0.6 10.0 %collective-permute-start = (bf16[4,8,768]{2,1,0:T(8,128)(2,1)}, bf16[4,8,768]{2,1,0:T(8,128)(2,1)S(1)}, u32[]{:S(2)}, u32[]{:S(2)}) collective-permute-start(bf16[4,8,768]{2,1,0:T(8,128)(2,1)} %param.12), channel_id=1, source_target_pairs={{0,4},{1,5},{2,6},{3,7},{4,8},{5,9},{6,10},{7,11},{8,12},{9,13},{1... | collective-permute-start | bytes 147464 | tf_op jit(solution)/shard_map/ppermute | solution.py:317
  3.7 7.1 %collective-permute-start.2 = (bf16[4,8,768]{2,1,0:T(8,128)(2,1)}, bf16[4,8,768]{2,1,0:T(8,128)(2,1)S(1)}, u32[]{:S(2)}, u32[]{:S(2)}) collective-permute-start(bf16[4,8,768]{2,1,0:T(8,128)(2,1)} %param.12), channel_id=1, source_target_pairs={{0,8},{1,9},{2,10},{3,11},{4,12},{5,13},{6,14},{7,15},{8,0},{9,1},... | collective-permute-start | bytes 147464 | tf_op jit(solution)/shard_map/ppermute | solution.py:317
  6.3 4.5 %collective-permute-start.1 = (bf16[4,8,768]{2,1,0:T(8,128)(2,1)}, bf16[4,8,768]{2,1,0:T(8,128)(2,1)S(1)}, u32[]{:S(2)}, u32[]{:S(2)}) collective-permute-start(bf16[4,8,768]{2,1,0:T(8,128)(2,1)} %param.12), channel_id=1, source_target_pairs={{0,12},{1,13},{2,14},{3,15},{4,0},{5,1},{6,2},{7,3},{8,4},{9,5},{1... | collective-permute-start | bytes 147464 | tf_op jit(solution)/shard_map/ppermute | solution.py:317
  7.7 5.9 %collective-permute-start.7 = (bf16[4,8,768]{2,1,0:T(8,128)(2,1)}, bf16[4,8,768]{2,1,0:T(8,128)(2,1)S(1)}, u32[]{:S(2)}, u32[]{:S(2)}) collective-permute-start(bf16[4,8,768]{2,1,0:T(8,128)(2,1)} %param.13), channel_id=1, source_target_pairs={{0,12},{1,13},{2,14},{3,15},{4,0},{5,1},{6,2},{7,3},{8,4},{9,5},{1... | collective-permute-start | bytes 147464 | tf_op jit(solution)/shard_map/ppermute | solution.py:317
  8.1 10.1 %collective-permute-start.9 = (bf16[4,8,768]{2,1,0:T(8,128)(2,1)}, bf16[4,8,768]{2,1,0:T(8,128)(2,1)S(1)}, u32[]{:S(2)}, u32[]{:S(2)}) collective-permute-start(bf16[4,8,768]{2,1,0:T(8,128)(2,1)} %param.13), channel_id=1, source_target_pairs={{0,8},{1,9},{2,10},{3,11},{4,12},{5,13},{6,14},{7,15},{8,0},{9,1},... | collective-permute-start | bytes 147464 | tf_op jit(solution)/shard_map/ppermute | solution.py:317
  10.6 6.2 %collective-permute-start.8 = (bf16[4,8,768]{2,1,0:T(8,128)(2,1)}, bf16[4,8,768]{2,1,0:T(8,128)(2,1)S(1)}, u32[]{:S(2)}, u32[]{:S(2)}) collective-permute-start(bf16[4,8,768]{2,1,0:T(8,128)(2,1)} %param.13), channel_id=1, source_target_pairs={{0,4},{1,5},{2,6},{3,7},{4,8},{5,9},{6,10},{7,11},{8,12},{9,13},{1... | collective-permute-start | bytes 147464 | tf_op jit(solution)/shard_map/ppermute | solution.py:317
  10.8 9.1 %collective-permute-start.4 = (bf16[4,32,768]{2,1,0:T(8,128)(2,1)S(1)}, bf16[4,32,768]{2,1,0:T(8,128)(2,1)S(1)}, u32[]{:S(2)}, u32[]{:S(2)}) collective-permute-start(bf16[4,32,768]{2,1,0:T(8,128)(2,1)S(1)} %constant_dynamic-update-slice_fusion.3.refs_1_), channel_id=1, source_target_pairs={{0,1},{1,0},{2,3},{3,2},{4,5},{5,4},{6,7},{7,6},{8,9},{9,8},{10,11... | collective-permute-start | bytes 589832 | tf_op jit(solution)/shard_map/ppermute | solution.py:317
  10.9 7.3 %collective-permute-start.3 = (bf16[4,32,768]{2,1,0:T(8,128)(2,1)S(1)}, bf16[4,32,768]{2,1,0:T(8,128)(2,1)S(1)}, u32[]{:S(2)}, u32[]{:S(2)}) collective-permute-start(bf16[4,32,768]{2,1,0:T(8,128)(2,1)S(1)} %constant_dynamic-update-slice_fusion.3.refs_1_), channel_id=1, source_target_pairs={{0,2},{1,3},{2,0},{3,1},{4,6},{5,7},{6,4},{7,5},{8,10},{9,11},{10,... | collective-permute-start | bytes 589832 | tf_op jit(solution)/shard_map/ppermute | solution.py:317
  12.6 0.8 %copy-start.2 = (bf16[4,8,768]{2,1,0:T(8,128)(2,1)S(1)}, bf16[4,8,768]{2,1,0:T(8,128)(2,1)}, u32[]{:S(2)}) copy-start(bf16[4,8,768]{2,1,0:T(8,128)(2,1)} %q_hbm) | copy-start | bytes 147460
  13.4 9.2 %copy-start.5 = (f32[12]{0:T(128)S(1)}, f32[12]{0:T(128)}, u32[]{:S(2)}) copy-start(f32[12]{0:T(128)} %factor_ref.1) | copy-start | bytes 148
  13.4 18.4 %copy-start.3 = (bf16[4,8,768]{2,1,0:T(8,128)(2,1)S(1)}, bf16[4,8,768]{2,1,0:T(8,128)(2,1)}, u32[]{:S(2)}) copy-start(bf16[4,8,768]{2,1,0:T(8,128)(2,1)} %refs_6_.1) | copy-start | bytes 147460
  13.4 18.4 %copy-start.4 = (f32[768]{0:T(1024)S(1)}, f32[768]{0:T(1024)}, u32[]{:S(2)}) copy-start(f32[768]{0:T(1024)} %refs_7_.1) | copy-start | bytes 9220
  18.2 1.7 %collective-permute-start.5 = (bf16[4,32,768]{2,1,0:T(8,128)(2,1)S(1)}, bf16[4,32,768]{2,1,0:T(8,128)(2,1)S(1)}, u32[]{:S(2)}, u32[]{:S(2)}) collective-permute-start(bf16[4,32,768]{2,1,0:T(8,128)(2,1)S(1)} %collective-permute-done.3.refs_2_), channel_id=1, source_target_pairs={{0,1},{1,0},{2,3},{3,2},{4,5},{5,4},{6,7},{7,6},{8,9},{9,8},{10,11... | collective-permute-start | bytes 589832 | tf_op jit(solution)/shard_map/ppermute | solution.py:317
  18.2 7.4 %collective-permute-start.10 = (bf16[4,32,768]{2,1,0:T(8,128)(2,1)S(1)}, bf16[4,32,768]{2,1,0:T(8,128)(2,1)S(1)}, u32[]{:S(2)}, u32[]{:S(2)}) collective-permute-start(bf16[4,32,768]{2,1,0:T(8,128)(2,1)S(1)} %constant_dynamic-update-slice_fusion.refs_1_), channel_id=1, source_target_pairs={{0,2},{1,3},{2,0},{3,1},{4,6},{5,7},{6,4},{7,5},{8,10},{9,11},{10,... | collective-permute-start | bytes 589832 | tf_op jit(solution)/shard_map/ppermute | solution.py:317
  20.3 4.1 %collective-permute-start.6 = (f32[96,128]{1,0:T(8,128)S(1)}, f32[96,128]{1,0:T(8,128)S(1)}, u32[]{:S(2)}, u32[]{:S(2)}) collective-permute-start(f32[96,128]{1,0:T(8,128)S(1)} %shard_map.114.refs_0_), channel_id=1, source_target_pairs={{0,16},{16,0},{1,17},{17,1},{2,18},{18,2},{3,19},{19,3},{4,20},{20... | collective-permute-start | bytes 147464 | tf_op jit(solution)/shard_map/ppermute | solution.py:415
  22.5 9.3 %collective-permute-start.11 = (bf16[4,32,768]{2,1,0:T(8,128)(2,1)S(1)}, bf16[4,32,768]{2,1,0:T(8,128)(2,1)S(1)}, u32[]{:S(2)}, u32[]{:S(2)}) collective-permute-start(bf16[4,32,768]{2,1,0:T(8,128)(2,1)S(1)} %constant_dynamic-update-slice_fusion.refs_1_), channel_id=1, source_target_pairs={{0,1},{1,0},{2,3},{3,2},{4,5},{5,4},{6,7},{7,6},{8,9},{9,8},{10,11... | collective-permute-start | bytes 589832 | tf_op jit(solution)/shard_map/ppermute | solution.py:317
  25.6 6.2 %collective-permute-start.12 = (bf16[4,32,768]{2,1,0:T(8,128)(2,1)S(1)}, bf16[4,32,768]{2,1,0:T(8,128)(2,1)S(1)}, u32[]{:S(2)}, u32[]{:S(2)}) collective-permute-start(bf16[4,32,768]{2,1,0:T(8,128)(2,1)S(1)} %collective-permute-done.10.refs_2_), channel_id=1, source_target_pairs={{0,1},{1,0},{2,3},{3,2},{4,5},{5,4},{6,7},{7,6},{8,9},{9,8},{10,11... | collective-permute-start | bytes 589832 | tf_op jit(solution)/shard_map/ppermute | solution.py:317
  25.6 15.2 %all-to-all-start = ((f32[16,24,128]{2,1,0:T(8,128)}), f32[16,24,128]{2,1,0:T(8,128)S(1)}, u32[]{:S(2)}, u32[]{:S(2)}) async-start(f32[16,24,128]{2,1,0:T(8,128)} %get-tuple-element.28), calls=%async_computation | async-start | bytes 393216 | tf_op jit(solution)/shard_map/all_to_all | solution.py:448
  32.5 4.2 %collective-permute-start.13 = (bf16[32,768]{1,0:T(8,128)(2,1)S(1)}, bf16[32,768]{1,0:T(8,128)(2,1)S(1)}, u32[]{:S(2)}, u32[]{:S(2)}) collective-permute-start(bf16[32,768]{1,0:T(8,128)(2,1)S(1)} %get-tuple-element.30.refs_0_), channel_id=1, source_target_pairs={{0,16},{16,0},{1,17},{17,1},{2,18},{18,2},{3,19},{19,3},{4,20},{20... | collective-permute-start | bytes 147464 | tf_op jit(solution)/shard_map/ppermute | solution.py:456
  35.7 6.8 %copy-start.1 = (bf16[768,768]{1,0:T(8,128)(2,1)S(1)}, bf16[768,768]{1,0:T(8,128)(2,1)}, u32[]{:S(2)}) copy-start(bf16[768,768]{1,0:T(8,128)(2,1)} %refs_1_) | copy-start | bytes 3538948
  37.1 5.4 %collective-permute-start.14 = (bf16[64,1152]{1,0:T(8,128)(2,1)S(1)}, bf16[64,1152]{1,0:T(8,128)(2,1)S(1)}, u32[]{:S(2)}, u32[]{:S(2)}) collective-permute-start(bf16[64,1152]{1,0:T(8,128)(2,1)S(1)} %shard_map.118.own_ref), channel_id=1, source_target_pairs={{0,16},{16,0},{1,17},{17,1},{2,18},{18,2},{3,19},{19,3},{4,20},{20... | collective-permute-start | bytes 442376 | tf_op jit(solution)/shard_map/ppermute | solution.py:469

commit v17 on v16

--- a/solution.py
+++ b/solution.py
@@ -391,7 +391,8 @@
     if middle:
         value_parts += send_all(value_parts, pos_count, middle)
     if len(stages) > 2:
-        key_parts += send_all(key_parts, pos_count, stages[2])
+        late_parts = [after(key_parts[0], *key_parts[1:])] + key_parts[1:]
+        key_parts += send_all(late_parts, pos_count, stages[2])
     partial = call(
         functools.partial(logits_kernel, len(key_parts)),
         jax.ShapeDtypeStruct((heads * sites, length), F32),

time: 44.3 us -> 42.7 us (0.964)
  waiting for transfers between devices: 8.65 us -> 7.24 us
    ppermute x12, waiting for transfers between devices: 3.95 us -> 2.53 us  [send_pos(): return lax.ppermute(array, 'pos', pairs)]
    all_to_all x1, starting transfers between devices: 6.19 us -> 5.61 us  [per_device(): lax.all_to_all(pair_local, 'pos', split_axis=0, concat_axis=0, tiled=True)]
  transfers between devices with their start and end apart: 16 -> 16, of which waited for: 7 -> 5; matrix products, arithmetic and copies ran while one was open for 8% -> 8% of each run, Pallas kernels for 10% -> 10%
where the time goes in v17:
time: 42.7 us; the launch traced here: 42.3 us
  starting transfers between devices  23.5 us (55%)
  waiting for transfers between devices  7.24 us (17%)
  Pallas kernels  5.86 us (14%)
  local copies, waits for them, and re-layouts  2.47 us (6%)
  other arithmetic  1.74 us (4%)
  between operations  1.47 us (3%)
    ppermute x12, starting transfers between devices, send_pos(): return lax.ppermute(array, 'pos', pairs)  13.2 us
    pallas_call x8, Pallas kernels, call(): pl.pallas_call(kernel, out_shape=out_shape, in_specs=specs, out_specs=jax...  5.86 us
    all_to_all x1, starting transfers between devices, per_device(): lax.all_to_all(pair_local, 'pos', split_axis=0, concat_axis=0, tiled=True)  5.61 us
    ppermute x12, waiting for transfers between devices, send_pos(): return lax.ppermute(array, 'pos', pairs)  2.53 us
    all_to_all x1, waiting for transfers between devices, per_device(): lax.all_to_all(pair_local, 'pos', split_axis=0, concat_axis=0, tiled=True)  2.15 us
    dynamic_update_slice x8, local copies, waits for them, and re-layouts, lay_together(): whole = lax.dynamic_update_slice(whole, parts[at], (0, at * size, 0))  1.66 us
    mul x1, other arithmetic, per_device(): weight = upright_threefold_linear * one  1.64 us
    ppermute x1, starting transfers between devices, per_device(): normed_all = [normed, lax.ppermute(normed, 'seq', swap)]  1.56 us
  transfers between devices with their start and end apart: 16, of which 5 were waited for; matrix products, arithmetic and copies ran while one was open for 8% of the time, Pallas kernels for 10%

profile of v17, /device:TPU:0, one launch (start us, length us, event | category | flops | bytes accessed | tf_op | source)
XLA Modules:
  0.0 42.3 jit_solution(7675127667312852219)
XLA Ops:
  0.6 3.1 %collective-permute-start = (bf16[4,8,768]{2,1,0:T(8,128)(2,1)}, bf16[4,8,768]{2,1,0:T(8,128)(2,1)S(1)}, u32[]{:S(2)}, u32[]{:S(2)}) collective-permute-start(bf16[4,8,768]{2,1,0:T(8,128)(2,1)} %param.12), channel_id=1, source_target_pairs={{0,4},{1,5},{2,6},{3,7},{4,8},{5,9},{6,10},{7,11},{8,12},{9,13},{1... | collective-permute-start | bytes 147464 | tf_op jit(solution)/shard_map/ppermute | solution.py:317
  3.7 2.6 %collective-permute-start.2 = (bf16[4,8,768]{2,1,0:T(8,128)(2,1)}, bf16[4,8,768]{2,1,0:T(8,128)(2,1)S(1)}, u32[]{:S(2)}, u32[]{:S(2)}) collective-permute-start(bf16[4,8,768]{2,1,0:T(8,128)(2,1)} %param.12), channel_id=1, source_target_pairs={{0,8},{1,9},{2,10},{3,11},{4,12},{5,13},{6,14},{7,15},{8,0},{9,1},... | collective-permute-start | bytes 147464 | tf_op jit(solution)/shard_map/ppermute | solution.py:317
  6.3 1.3 %collective-permute-start.1 = (bf16[4,8,768]{2,1,0:T(8,128)(2,1)}, bf16[4,8,768]{2,1,0:T(8,128)(2,1)S(1)}, u32[]{:S(2)}, u32[]{:S(2)}) collective-permute-start(bf16[4,8,768]{2,1,0:T(8,128)(2,1)} %param.12), channel_id=1, source_target_pairs={{0,12},{1,13},{2,14},{3,15},{4,0},{5,1},{6,2},{7,3},{8,4},{9,5},{1... | collective-permute-start | bytes 147464 | tf_op jit(solution)/shard_map/ppermute | solution.py:317
  7.7 0.4 %collective-permute-start.7 = (bf16[4,8,768]{2,1,0:T(8,128)(2,1)}, bf16[4,8,768]{2,1,0:T(8,128)(2,1)S(1)}, u32[]{:S(2)}, u32[]{:S(2)}) collective-permute-start(bf16[4,8,768]{2,1,0:T(8,128)(2,1)} %param.13), channel_id=1, source_target_pairs={{0,12},{1,13},{2,14},{3,15},{4,0},{5,1},{6,2},{7,3},{8,4},{9,5},{1... | collective-permute-start | bytes 147464 | tf_op jit(solution)/shard_map/ppermute | solution.py:317
  8.1 1.7 %collective-permute-start.9 = (bf16[4,8,768]{2,1,0:T(8,128)(2,1)}, bf16[4,8,768]{2,1,0:T(8,128)(2,1)S(1)}, u32[]{:S(2)}, u32[]{:S(2)}) collective-permute-start(bf16[4,8,768]{2,1,0:T(8,128)(2,1)} %param.13), channel_id=1, source_target_pairs={{0,8},{1,9},{2,10},{3,11},{4,12},{5,13},{6,14},{7,15},{8,0},{9,1},... | collective-permute-start | bytes 147464 | tf_op jit(solution)/shard_map/ppermute | solution.py:317
  9.8 0.8 %dynamic_update_slice.24 = bf16[4,32,768]{2,1,0:T(8,128)(2,1)S(1)} pad(bf16[4,8,768]{2,1,0:T(8,128)(2,1)} %param.12, bf16[]{:T(256)} %constant.3.clone.1), padding=0_0x0_24x0_0 | pad | bytes 245762 | tf_op jit(solution)/shard_map/dynamic_update_slice | solution.py:329
  10.6 0.0 collective-permute-done
  10.6 0.1 collective-permute-start.8
  10.8 0.0 collective-permute-done.1
  10.8 0.0 collective-permute-done.2
  10.8 1.7 %collective-permute-start.3 = (bf16[4,32,768]{2,1,0:T(8,128)(2,1)S(1)}, bf16[4,32,768]{2,1,0:T(8,128)(2,1)S(1)}, u32[]{:S(2)}, u32[]{:S(2)}) collective-permute-start(bf16[4,32,768]{2,1,0:T(8,128)(2,1)S(1)} %constant_dynamic-update-slice_fusion.3.refs_1_), channel_id=1, source_target_pairs={{0,2},{1,3},{2,0},{3,1},{4,6},{5,7},{6,4},{7,5},{8,10},{9,11},{10,... | collective-permute-start | bytes 589832 | tf_op jit(solution)/shard_map/ppermute | solution.py:317
  12.5 0.8 %copy-done.2 = bf16[4,8,768]{2,1,0:T(8,128)(2,1)S(1)} copy-done((bf16[4,8,768]{2,1,0:T(8,128)(2,1)S(1)}, bf16[4,8,768]{2,1,0:T(8,128)(2,1)}, u32[]{:S(2)}) %copy-start.2) | copy-done | bytes 49176
  13.3 0.1 shard_map.113.refs_0_
  13.4 0.0 collective-permute-done.7
  13.4 0.8 %dynamic_update_slice.28 = bf16[4,32,768]{2,1,0:T(8,128)(2,1)S(1)} pad(bf16[4,8,768]{2,1,0:T(8,128)(2,1)} %param.13, bf16[]{:T(256)} %constant.3.clone.1), padding=0_0x0_24x0_0 | pad | bytes 245762 | tf_op jit(solution)/shard_map/dynamic_update_slice | solution.py:329
  14.3 2.5 %collective-permute-done.8 = bf16[4,8,768]{2,1,0:T(8,128)(2,1)S(1)} collective-permute-done((bf16[4,8,768]{2,1,0:T(8,128)(2,1)}, bf16[4,8,768]{2,1,0:T(8,128)(2,1)S(1)}, u32[]{:S(2)}, u32[]{:S(2)}) %collective-permute-start.8) | collective-permute-done | bytes 49184 | tf_op jit(solution)/shard_map/ppermute | solution.py:317
  16.8 0.0 collective-permute-done.3.refs_2_
  16.8 0.1 collective-permute-start.4
  16.9 0.5 %collective-permute-start.5 = (bf16[4,32,768]{2,1,0:T(8,128)(2,1)S(1)}, bf16[4,32,768]{2,1,0:T(8,128)(2,1)S(1)}, u32[]{:S(2)}, u32[]{:S(2)}) collective-permute-start(bf16[4,32,768]{2,1,0:T(8,128)(2,1)S(1)} %collective-permute-done.3.refs_2_), channel_id=1, source_target_pairs={{0,1},{1,0},{2,3},{3,2},{4,5},{5,4},{6,7},{7,6},{8,9},{9,8},{10,11... | collective-permute-start | bytes 589832 | tf_op jit(solution)/shard_map/ppermute | solution.py:317
  17.4 0.0 collective-permute-done.9
  17.4 1.6 %collective-permute-start.10 = (bf16[4,32,768]{2,1,0:T(8,128)(2,1)S(1)}, bf16[4,32,768]{2,1,0:T(8,128)(2,1)S(1)}, u32[]{:S(2)}, u32[]{:S(2)}) collective-permute-start(bf16[4,32,768]{2,1,0:T(8,128)(2,1)S(1)} %constant_dynamic-update-slice_fusion.refs_1_), channel_id=1, source_target_pairs={{0,2},{1,3},{2,0},{3,1},{4,6},{5,7},{6,4},{7,5},{8,10},{9,11},{10,... | collective-permute-start | bytes 589832 | tf_op jit(solution)/shard_map/ppermute | solution.py:317
  18.9 0.0 collective-permute-done.4.refs_3_
  19.0 0.0 collective-permute-done.5.refs_4_
  19.0 0.4 shard_map.114.refs_0_
  19.3 1.5 %collective-permute-start.6 = (f32[96,128]{1,0:T(8,128)S(1)}, f32[96,128]{1,0:T(8,128)S(1)}, u32[]{:S(2)}, u32[]{:S(2)}) collective-permute-start(f32[96,128]{1,0:T(8,128)S(1)} %shard_map.114.refs_0_), channel_id=1, source_target_pairs={{0,16},{16,0},{1,17},{17,1},{2,18},{18,2},{3,19},{19,3},{4,20},{20... | collective-permute-start | bytes 147464 | tf_op jit(solution)/shard_map/ppermute | solution.py:416
  20.8 0.1 pad_add_fusion.scalar_ref
  21.5 0.1 collective-permute-start.11
  21.6 0.8 %shard_map.115 = (f32[24,128]{1,0:T(8,128)S(1)}, bf16[128,128]{1,0:T(8,128)(2,1)S(1)}, f32[8,128]{1,0:T(8,128)S(1)}, f32[128,64]{1,0:T(8,128)S(1)}, bf16[768,128...) custom-call(s32[2]{0:T(128)S(1)} %pad_add_fusion.scalar_ref, f32[12]{0:T(128)S(1)} %copy-done.5, f32[1]{0:T(128)S(6)} %copy.18.offset_ref), custom_call_target="tpu_custom_call" | custom-call | flops 1000000 | bytes 1000000 | tf_op jit(solution)/shard_map/pallas_call | solution.py:289
  22.4 1.0 %collective-permute-done.6.refs_1_ = f32[96,128]{1,0:T(8,128)S(1)} collective-permute-done((f32[96,128]{1,0:T(8,128)S(1)}, f32[96,128]{1,0:T(8,128)S(1)}, u32[]{:S(2)}, u32[]{:S(2)}) %collective-permute-start.6) | collective-permute-done | bytes 49184 | tf_op jit(solution)/shard_map/ppermute | solution.py:416
  23.4 1.1 %shard_map.116 = (bf16[96,128]{1,0:T(8,128)(2,1)S(1)}, f32[16,24,128]{2,1,0:T(8,128)}) custom-call(f32[96,128]{1,0:T(8,128)S(1)} %shard_map.114.refs_0_, f32[96,128]{1,0:T(8,128)S(1)} %collective-permute-done.6.refs_1_, f32[24,128]{1,0:T(8,128)S(1)} %get-tuple-element.26.refs_2_.factor_ref, bf16[128,128]{1,0:T(8,128)(2,1)S(1)} %get-tuple-element.24.refs_3_), custom_call_target="tpu_custom_call" | custom-call | flops 1000000 | bytes 1000000 | tf_op jit(solution)/shard_map/pallas_call | solution.py:289
  24.5 0.0 collective-permute-done.10.refs_2_
  24.5 0.0 collective-permute-start.12
  24.5 5.6 %all-to-all-start = ((f32[16,24,128]{2,1,0:T(8,128)}), f32[16,24,128]{2,1,0:T(8,128)S(1)}, u32[]{:S(2)}, u32[]{:S(2)}) async-start(f32[16,24,128]{2,1,0:T(8,128)} %get-tuple-element.30), calls=%async_computation | async-start | bytes 393216 | tf_op jit(solution)/shard_map/all_to_all | solution.py:449
  30.1 0.0 collective-permute-done.11.refs_3_
  30.1 0.0 collective-permute-done.12.refs_4_
  30.2 0.0 copy-done
  30.2 0.0 copy-done.3
  30.2 0.6 %shard_map.117 = (f32[32,768]{1,0:T(8,128)S(1)}, bf16[32,768]{1,0:T(8,128)(2,1)S(1)}, bf16[1,1152]{1,0:T(2,128)(2,1)S(1)}) custom-call(bf16[96,128]{1,0:T(8,128)(2,1)S(1)} %get-tuple-element.27.refs_0_, bf16[4,32,768]{2,1,0:T(8,128)(2,1)S(1)} %constant_dynamic-update-slice_fusion.refs_1_, bf16[4,32,768]{2,1,0:T(8,128)(2,1)S(1)} %collective-permute-done.10.refs_2_, ...), custom_call_target="tpu_custom_call" | custom-call | flops 1000000 | bytes 1000000 | tf_op jit(solution)/shard_map/pallas_call | solution.py:289
  30.8 1.6 %collective-permute-start.13 = (bf16[32,768]{1,0:T(8,128)(2,1)S(1)}, bf16[32,768]{1,0:T(8,128)(2,1)S(1)}, u32[]{:S(2)}, u32[]{:S(2)}) collective-permute-start(bf16[32,768]{1,0:T(8,128)(2,1)S(1)} %get-tuple-element.32.refs_0_), channel_id=1, source_target_pairs={{0,16},{16,0},{1,17},{17,1},{2,18},{18,2},{3,19},{19,3},{4,20},{20... | collective-permute-start | bytes 147464 | tf_op jit(solution)/shard_map/ppermute | solution.py:457
  32.4 1.6 %broadcast_multiply_fusion.refs_2_ = bf16[768,1152]{1,0:T(8,128)(2,1)S(1)} fusion(bf16[768,1152]{1,0:T(8,128)(2,1)} %param.16, bf16[1152]{0:T(1024)(128)(2,1)S(1)} %reduce), kind=kLoop, calls=%fused_computation | loop fusion | flops 884736 | bytes 3541248 | tf_op jit(solution)/shard_map/mul | solution.py:458
  34.1 0.0 copy-start.1
  34.1 0.9 %collective-permute-done.13.refs_1_ = bf16[32,768]{1,0:T(8,128)(2,1)S(1)} collective-permute-done((bf16[32,768]{1,0:T(8,128)(2,1)S(1)}, bf16[32,768]{1,0:T(8,128)(2,1)S(1)}, u32[]{:S(2)}, u32[]{:S(2)}) %collective-permute-start.13) | collective-permute-done | bytes 49184 | tf_op jit(solution)/shard_map/ppermute | solution.py:457
  35.0 0.4 %shard_map.118.own_ref = bf16[64,1152]{1,0:T(8,128)(2,1)S(1)} custom-call(bf16[32,768]{1,0:T(8,128)(2,1)S(1)} %get-tuple-element.32.refs_0_, bf16[32,768]{1,0:T(8,128)(2,1)S(1)} %collective-permute-done.13.refs_1_, bf16[768,1152]{1,0:T(8,128)(2,1)S(1)} %broadcast_multiply_fusion.refs_2_), custom_call_target="tpu_custom_call" | custom-call | flops 1000000 | bytes 1000000 | tf_op jit(solution)/shard_map/pallas_call | solution.py:289
  35.4 1.6 %collective-permute-start.14 = (bf16[64,1152]{1,0:T(8,128)(2,1)S(1)}, bf16[64,1152]{1,0:T(8,128)(2,1)S(1)}, u32[]{:S(2)}, u32[]{:S(2)}) collective-permute-start(bf16[64,1152]{1,0:T(8,128)(2,1)S(1)} %shard_map.118.own_ref), channel_id=1, source_target_pairs={{0,16},{16,0},{1,17},{17,1},{2,18},{18,2},{3,19},{19,3},{4,20},{20... | collective-permute-start | bytes 442376 | tf_op jit(solution)/shard_map/ppermute | solution.py:470
  37.0 2.2 %all-to-all-done.pair_ref = f32[16,24,128]{2,1,0:T(8,128)S(1)} async-done(((f32[16,24,128]{2,1,0:T(8,128)}), f32[16,24,128]{2,1,0:T(8,128)S(1)}, u32[]{:S(2)}, u32[]{:S(2)}) %all-to-all-start) | async-done | bytes 196640 | tf_op jit(solution)/shard_map/all_to_all | solution.py:449
  39.1 1.0 %shard_map.120 = f32[8,64]{1,0:T(8,128)} custom-call(f32[16,24,128]{2,1,0:T(8,128)S(1)} %all-to-all-done.pair_ref, f32[24,128]{1,0:T(8,128)S(1)} %get-tuple-element.26.refs_2_.factor_ref, f32[8,128]{1,0:T(8,128)S(1)} %get-tuple-element.38.own_ref, f32[128,64]{1,0:T(8,128)S(1)} %get-tuple-element.39.slab_ref), custom_call_target="tpu_custom_call" | custom-call | flops 1000000 | bytes 1000000 | tf_op jit(solution)/shard_map/pallas_call | solution.py:289
  40.2 0.6 %collective-permute-done.14.other_ref = bf16[64,1152]{1,0:T(8,128)(2,1)S(1)} collective-permute-done((bf16[64,1152]{1,0:T(8,128)(2,1)S(1)}, bf16[64,1152]{1,0:T(8,128)(2,1)S(1)}, u32[]{:S(2)}, u32[]{:S(2)}) %collective-permute-start.14) | collective-permute-done | bytes 147488 | tf_op jit(solution)/shard_map/ppermute | solution.py:470
  40.8 1.4 %shard_map.119 = bf16[4,8,768]{2,1,0:T(8,128)(2,1)} custom-call(bf16[64,1152]{1,0:T(8,128)(2,1)S(1)} %shard_map.118.own_ref, bf16[64,1152]{1,0:T(8,128)(2,1)S(1)} %collective-permute-done.14.other_ref, f32[32,768]{1,0:T(8,128)S(1)} %get-tuple-element.34.refs_0_, bf16[768,768]{1,0:T(8,128)(2,1)S(1)} %copy-done.1, ...), custom_call_target="tpu_custom_call" | custom-call | flops 1000000 | bytes 1000000 | tf_op jit(solution)/shard_map/pallas_call | solution.py:289
  (15 shorter events, 0.1 us)
Async XLA Ops:
  0.6 29.5 %copy-start = (bf16[768,768]{1,0:T(8,128)(2,1)S(1)}, bf16[768,768]{1,0:T(8,128)(2,1)}, u32[]{:S(2)}) copy-start(bf16[768,768]{1,0:T(8,128)(2,1)} %refs_5_.1) | copy-start | bytes 3538948
  0.6 10.0 %collective-permute-start = (bf16[4,8,768]{2,1,0:T(8,128)(2,1)}, bf16[4,8,768]{2,1,0:T(8,128)(2,1)S(1)}, u32[]{:S(2)}, u32[]{:S(2)}) collective-permute-start(bf16[4,8,768]{2,1,0:T(8,128)(2,1)} %param.12), channel_id=1, source_target_pairs={{0,4},{1,5},{2,6},{3,7},{4,8},{5,9},{6,10},{7,11},{8,12},{9,13},{1... | collective-permute-start | bytes 147464 | tf_op jit(solution)/shard_map/ppermute | solution.py:317
  3.7 7.1 %collective-permute-start.2 = (bf16[4,8,768]{2,1,0:T(8,128)(2,1)}, bf16[4,8,768]{2,1,0:T(8,128)(2,1)S(1)}, u32[]{:S(2)}, u32[]{:S(2)}) collective-permute-start(bf16[4,8,768]{2,1,0:T(8,128)(2,1)} %param.12), channel_id=1, source_target_pairs={{0,8},{1,9},{2,10},{3,11},{4,12},{5,13},{6,14},{7,15},{8,0},{9,1},... | collective-permute-start | bytes 147464 | tf_op jit(solution)/shard_map/ppermute | solution.py:317
  6.3 4.5 %collective-permute-start.1 = (bf16[4,8,768]{2,1,0:T(8,128)(2,1)}, bf16[4,8,768]{2,1,0:T(8,128)(2,1)S(1)}, u32[]{:S(2)}, u32[]{:S(2)}) collective-permute-start(bf16[4,8,768]{2,1,0:T(8,128)(2,1)} %param.12), channel_id=1, source_target_pairs={{0,12},{1,13},{2,14},{3,15},{4,0},{5,1},{6,2},{7,3},{8,4},{9,5},{1... | collective-permute-start | bytes 147464 | tf_op jit(solution)/shard_map/ppermute | solution.py:317
  7.7 5.8 %collective-permute-start.7 = (bf16[4,8,768]{2,1,0:T(8,128)(2,1)}, bf16[4,8,768]{2,1,0:T(8,128)(2,1)S(1)}, u32[]{:S(2)}, u32[]{:S(2)}) collective-permute-start(bf16[4,8,768]{2,1,0:T(8,128)(2,1)} %param.13), channel_id=1, source_target_pairs={{0,12},{1,13},{2,14},{3,15},{4,0},{5,1},{6,2},{7,3},{8,4},{9,5},{1... | collective-permute-start | bytes 147464 | tf_op jit(solution)/shard_map/ppermute | solution.py:317
  8.1 9.3 %collective-permute-start.9 = (bf16[4,8,768]{2,1,0:T(8,128)(2,1)}, bf16[4,8,768]{2,1,0:T(8,128)(2,1)S(1)}, u32[]{:S(2)}, u32[]{:S(2)}) collective-permute-start(bf16[4,8,768]{2,1,0:T(8,128)(2,1)} %param.13), channel_id=1, source_target_pairs={{0,8},{1,9},{2,10},{3,11},{4,12},{5,13},{6,14},{7,15},{8,0},{9,1},... | collective-permute-start | bytes 147464 | tf_op jit(solution)/shard_map/ppermute | solution.py:317
  10.6 6.2 %collective-permute-start.8 = (bf16[4,8,768]{2,1,0:T(8,128)(2,1)}, bf16[4,8,768]{2,1,0:T(8,128)(2,1)S(1)}, u32[]{:S(2)}, u32[]{:S(2)}) collective-permute-start(bf16[4,8,768]{2,1,0:T(8,128)(2,1)} %param.13), channel_id=1, source_target_pairs={{0,4},{1,5},{2,6},{3,7},{4,8},{5,9},{6,10},{7,11},{8,12},{9,13},{1... | collective-permute-start | bytes 147464 | tf_op jit(solution)/shard_map/ppermute | solution.py:317
  10.8 6.0 %collective-permute-start.3 = (bf16[4,32,768]{2,1,0:T(8,128)(2,1)S(1)}, bf16[4,32,768]{2,1,0:T(8,128)(2,1)S(1)}, u32[]{:S(2)}, u32[]{:S(2)}) collective-permute-start(bf16[4,32,768]{2,1,0:T(8,128)(2,1)S(1)} %constant_dynamic-update-slice_fusion.3.refs_1_), channel_id=1, source_target_pairs={{0,2},{1,3},{2,0},{3,1},{4,6},{5,7},{6,4},{7,5},{8,10},{9,11},{10,... | collective-permute-start | bytes 589832 | tf_op jit(solution)/shard_map/ppermute | solution.py:317
  12.5 0.8 %copy-start.2 = (bf16[4,8,768]{2,1,0:T(8,128)(2,1)S(1)}, bf16[4,8,768]{2,1,0:T(8,128)(2,1)}, u32[]{:S(2)}) copy-start(bf16[4,8,768]{2,1,0:T(8,128)(2,1)} %q_hbm) | copy-start | bytes 147460
  13.3 8.3 %copy-start.5 = (f32[12]{0:T(128)S(1)}, f32[12]{0:T(128)}, u32[]{:S(2)}) copy-start(f32[12]{0:T(128)} %factor_ref.1) | copy-start | bytes 148
  13.3 16.8 %copy-start.3 = (bf16[4,8,768]{2,1,0:T(8,128)(2,1)S(1)}, bf16[4,8,768]{2,1,0:T(8,128)(2,1)}, u32[]{:S(2)}) copy-start(bf16[4,8,768]{2,1,0:T(8,128)(2,1)} %refs_6_.1) | copy-start | bytes 147460
  13.3 16.8 %copy-start.4 = (f32[768]{0:T(1024)S(1)}, f32[768]{0:T(1024)}, u32[]{:S(2)}) copy-start(f32[768]{0:T(1024)} %refs_7_.1) | copy-start | bytes 9220
  16.8 2.2 %collective-permute-start.4 = (bf16[4,32,768]{2,1,0:T(8,128)(2,1)S(1)}, bf16[4,32,768]{2,1,0:T(8,128)(2,1)S(1)}, u32[]{:S(2)}, u32[]{:S(2)}) collective-permute-start(bf16[4,32,768]{2,1,0:T(8,128)(2,1)S(1)} %constant_dynamic-update-slice_fusion.3.refs_1_), channel_id=1, source_target_pairs={{0,1},{1,0},{2,3},{3,2},{4,5},{5,4},{6,7},{7,6},{8,9},{9,8},{10,11... | collective-permute-start | bytes 589832 | tf_op jit(solution)/shard_map/ppermute | solution.py:317
  16.9 2.1 %collective-permute-start.5 = (bf16[4,32,768]{2,1,0:T(8,128)(2,1)S(1)}, bf16[4,32,768]{2,1,0:T(8,128)(2,1)S(1)}, u32[]{:S(2)}, u32[]{:S(2)}) collective-permute-start(bf16[4,32,768]{2,1,0:T(8,128)(2,1)S(1)} %collective-permute-done.3.refs_2_), channel_id=1, source_target_pairs={{0,1},{1,0},{2,3},{3,2},{4,5},{5,4},{6,7},{7,6},{8,9},{9,8},{10,11... | collective-permute-start | bytes 589832 | tf_op jit(solution)/shard_map/ppermute | solution.py:317
  17.4 7.1 %collective-permute-start.10 = (bf16[4,32,768]{2,1,0:T(8,128)(2,1)S(1)}, bf16[4,32,768]{2,1,0:T(8,128)(2,1)S(1)}, u32[]{:S(2)}, u32[]{:S(2)}) collective-permute-start(bf16[4,32,768]{2,1,0:T(8,128)(2,1)S(1)} %constant_dynamic-update-slice_fusion.refs_1_), channel_id=1, source_target_pairs={{0,2},{1,3},{2,0},{3,1},{4,6},{5,7},{6,4},{7,5},{8,10},{9,11},{10,... | collective-permute-start | bytes 589832 | tf_op jit(solution)/shard_map/ppermute | solution.py:317
  19.3 4.1 %collective-permute-start.6 = (f32[96,128]{1,0:T(8,128)S(1)}, f32[96,128]{1,0:T(8,128)S(1)}, u32[]{:S(2)}, u32[]{:S(2)}) collective-permute-start(f32[96,128]{1,0:T(8,128)S(1)} %shard_map.114.refs_0_), channel_id=1, source_target_pairs={{0,16},{16,0},{1,17},{17,1},{2,18},{18,2},{3,19},{19,3},{4,20},{20... | collective-permute-start | bytes 147464 | tf_op jit(solution)/shard_map/ppermute | solution.py:416
  21.5 8.6 %collective-permute-start.11 = (bf16[4,32,768]{2,1,0:T(8,128)(2,1)S(1)}, bf16[4,32,768]{2,1,0:T(8,128)(2,1)S(1)}, u32[]{:S(2)}, u32[]{:S(2)}) collective-permute-start(bf16[4,32,768]{2,1,0:T(8,128)(2,1)S(1)} %constant_dynamic-update-slice_fusion.refs_1_), channel_id=1, source_target_pairs={{0,1},{1,0},{2,3},{3,2},{4,5},{5,4},{6,7},{7,6},{8,9},{9,8},{10,11... | collective-permute-start | bytes 589832 | tf_op jit(solution)/shard_map/ppermute | solution.py:317
  24.5 5.6 %collective-permute-start.12 = (bf16[4,32,768]{2,1,0:T(8,128)(2,1)S(1)}, bf16[4,32,768]{2,1,0:T(8,128)(2,1)S(1)}, u32[]{:S(2)}, u32[]{:S(2)}) collective-permute-start(bf16[4,32,768]{2,1,0:T(8,128)(2,1)S(1)} %collective-permute-done.10.refs_2_), channel_id=1, source_target_pairs={{0,1},{1,0},{2,3},{3,2},{4,5},{5,4},{6,7},{7,6},{8,9},{9,8},{10,11... | collective-permute-start | bytes 589832 | tf_op jit(solution)/shard_map/ppermute | solution.py:317
  24.5 14.6 %all-to-all-start = ((f32[16,24,128]{2,1,0:T(8,128)}), f32[16,24,128]{2,1,0:T(8,128)S(1)}, u32[]{:S(2)}, u32[]{:S(2)}) async-start(f32[16,24,128]{2,1,0:T(8,128)} %get-tuple-element.30), calls=%async_computation | async-start | bytes 393216 | tf_op jit(solution)/shard_map/all_to_all | solution.py:449
  30.8 4.2 %collective-permute-start.13 = (bf16[32,768]{1,0:T(8,128)(2,1)S(1)}, bf16[32,768]{1,0:T(8,128)(2,1)S(1)}, u32[]{:S(2)}, u32[]{:S(2)}) collective-permute-start(bf16[32,768]{1,0:T(8,128)(2,1)S(1)} %get-tuple-element.32.refs_0_), channel_id=1, source_target_pairs={{0,16},{16,0},{1,17},{17,1},{2,18},{18,2},{3,19},{19,3},{4,20},{20... | collective-permute-start | bytes 147464 | tf_op jit(solution)/shard_map/ppermute | solution.py:457
  34.1 6.8 %copy-start.1 = (bf16[768,768]{1,0:T(8,128)(2,1)S(1)}, bf16[768,768]{1,0:T(8,128)(2,1)}, u32[]{:S(2)}) copy-start(bf16[768,768]{1,0:T(8,128)(2,1)} %refs_1_) | copy-start | bytes 3538948
  35.4 5.4 %collective-permute-start.14 = (bf16[64,1152]{1,0:T(8,128)(2,1)S(1)}, bf16[64,1152]{1,0:T(8,128)(2,1)S(1)}, u32[]{:S(2)}, u32[]{:S(2)}) collective-permute-start(bf16[64,1152]{1,0:T(8,128)(2,1)S(1)} %shard_map.118.own_ref), channel_id=1, source_target_pairs={{0,16},{16,0},{1,17},{17,1},{2,18},{18,2},{3,19},{19,3},{4,20},{20... | collective-permute-start | bytes 442376 | tf_op jit(solution)/shard_map/ppermute | solution.py:470

commit v18 on v17

--- a/solution.py
+++ b/solution.py
@@ -183,13 +183,13 @@
     padded = pick.shape[1]
     seqs = len(keys)
     for s in range(rows):
-        for t in range(seqs):
-            at = (s * seqs + t) * sites
-            products[at : at + sites, :] = query[s * sites : (s + 1) * sites, :] * keys[t]
-    product = products[...]
-    high = product.astype(BF16)
-    low = (product - high.astype(F32)).astype(BF16)
-    scores = (dot_nn(high, pick) + dot_nn(low, pick)) * factor
+        own = query[s * sites : (s + 1) * sites, :]
+        product = jnp.concatenate([own * key for key in keys], axis=0)
+        high = product.astype(BF16)
+        low = (product - high.astype(F32)).astype(BF16)
+        at = s * seqs * sites
+        products[at : at + seqs * sites, 0:padded] = dot_nn(high, pick) + dot_nn(low, pick)
+    scores = products[:, 0:padded] * factor
     exponent = jnp.exp(scores).reshape(rows, seqs, sites, padded)
     shares = (exponent / jnp.sum(exponent, axis=1, keepdims=True)).astype(BF16)
     wide = dot_nn(shares.reshape(rows * seqs * sites, padded), spread_ref[...])

time: 42.7 us -> 42.7 us (level)
  no operation moved by 1% of the time
where the time goes in v18:
time: 42.7 us; the launch traced here: 42.3 us
  starting transfers between devices  23.5 us (55%)
  waiting for transfers between devices  7.24 us (17%)
  Pallas kernels  5.88 us (14%)
  local copies, waits for them, and re-layouts  2.47 us (6%)
  other arithmetic  1.74 us (4%)
  between operations  1.47 us (3%)
    ppermute x12, starting transfers between devices, send_pos(): return lax.ppermute(array, 'pos', pairs)  13.2 us
    pallas_call x8, Pallas kernels, call(): pl.pallas_call(kernel, out_shape=out_shape, in_specs=specs, out_specs=jax...  5.88 us
    all_to_all x1, starting transfers between devices, per_device(): lax.all_to_all(pair_local, 'pos', split_axis=0, concat_axis=0, tiled=True)  5.61 us
    ppermute x12, waiting for transfers between devices, send_pos(): return lax.ppermute(array, 'pos', pairs)  2.53 us
    all_to_all x1, waiting for transfers between devices, per_device(): lax.all_to_all(pair_local, 'pos', split_axis=0, concat_axis=0, tiled=True)  2.15 us
    dynamic_update_slice x8, local copies, waits for them, and re-layouts, lay_together(): whole = lax.dynamic_update_slice(whole, parts[at], (0, at * size, 0))  1.66 us
    mul x1, other arithmetic, per_device(): weight = upright_threefold_linear * one  1.64 us
    ppermute x1, starting transfers between devices, per_device(): normed_all = [normed, lax.ppermute(normed, 'seq', swap)]  1.56 us
  transfers between devices with their start and end apart: 16, of which 5 were waited for; matrix products, arithmetic and copies ran while one was open for 8% of the time, Pallas kernels for 10%

profile of v18, /device:TPU:0, one launch (start us, length us, event | category | flops | bytes accessed | tf_op | source)
XLA Modules:
  0.0 42.3 jit_solution(7285366393043714730)
XLA Ops:
  0.6 0.0 copy-start
  0.6 3.1 %collective-permute-start = (bf16[4,8,768]{2,1,0:T(8,128)(2,1)}, bf16[4,8,768]{2,1,0:T(8,128)(2,1)S(1)}, u32[]{:S(2)}, u32[]{:S(2)}) collective-permute-start(bf16[4,8,768]{2,1,0:T(8,128)(2,1)} %param.12), channel_id=1, source_target_pairs={{0,4},{1,5},{2,6},{3,7},{4,8},{5,9},{6,10},{7,11},{8,12},{9,13},{1... | collective-permute-start | bytes 147464 | tf_op jit(solution)/shard_map/ppermute | solution.py:317
  3.7 2.6 %collective-permute-start.2 = (bf16[4,8,768]{2,1,0:T(8,128)(2,1)}, bf16[4,8,768]{2,1,0:T(8,128)(2,1)S(1)}, u32[]{:S(2)}, u32[]{:S(2)}) collective-permute-start(bf16[4,8,768]{2,1,0:T(8,128)(2,1)} %param.12), channel_id=1, source_target_pairs={{0,8},{1,9},{2,10},{3,11},{4,12},{5,13},{6,14},{7,15},{8,0},{9,1},... | collective-permute-start | bytes 147464 | tf_op jit(solution)/shard_map/ppermute | solution.py:317
  6.3 1.3 %collective-permute-start.1 = (bf16[4,8,768]{2,1,0:T(8,128)(2,1)}, bf16[4,8,768]{2,1,0:T(8,128)(2,1)S(1)}, u32[]{:S(2)}, u32[]{:S(2)}) collective-permute-start(bf16[4,8,768]{2,1,0:T(8,128)(2,1)} %param.12), channel_id=1, source_target_pairs={{0,12},{1,13},{2,14},{3,15},{4,0},{5,1},{6,2},{7,3},{8,4},{9,5},{1... | collective-permute-start | bytes 147464 | tf_op jit(solution)/shard_map/ppermute | solution.py:317
  7.7 0.4 %collective-permute-start.7 = (bf16[4,8,768]{2,1,0:T(8,128)(2,1)}, bf16[4,8,768]{2,1,0:T(8,128)(2,1)S(1)}, u32[]{:S(2)}, u32[]{:S(2)}) collective-permute-start(bf16[4,8,768]{2,1,0:T(8,128)(2,1)} %param.13), channel_id=1, source_target_pairs={{0,12},{1,13},{2,14},{3,15},{4,0},{5,1},{6,2},{7,3},{8,4},{9,5},{1... | collective-permute-start | bytes 147464 | tf_op jit(solution)/shard_map/ppermute | solution.py:317
  8.1 1.7 %collective-permute-start.9 = (bf16[4,8,768]{2,1,0:T(8,128)(2,1)}, bf16[4,8,768]{2,1,0:T(8,128)(2,1)S(1)}, u32[]{:S(2)}, u32[]{:S(2)}) collective-permute-start(bf16[4,8,768]{2,1,0:T(8,128)(2,1)} %param.13), channel_id=1, source_target_pairs={{0,8},{1,9},{2,10},{3,11},{4,12},{5,13},{6,14},{7,15},{8,0},{9,1},... | collective-permute-start | bytes 147464 | tf_op jit(solution)/shard_map/ppermute | solution.py:317
  9.8 0.8 %dynamic_update_slice.24 = bf16[4,32,768]{2,1,0:T(8,128)(2,1)S(1)} pad(bf16[4,8,768]{2,1,0:T(8,128)(2,1)} %param.12, bf16[]{:T(256)} %constant.3.clone.1), padding=0_0x0_24x0_0 | pad | bytes 245762 | tf_op jit(solution)/shard_map/dynamic_update_slice | solution.py:329
  10.6 0.0 collective-permute-done
  10.6 0.1 collective-permute-start.8
  10.8 0.0 collective-permute-done.1
  10.8 0.0 collective-permute-done.2
  10.8 1.7 %collective-permute-start.3 = (bf16[4,32,768]{2,1,0:T(8,128)(2,1)S(1)}, bf16[4,32,768]{2,1,0:T(8,128)(2,1)S(1)}, u32[]{:S(2)}, u32[]{:S(2)}) collective-permute-start(bf16[4,32,768]{2,1,0:T(8,128)(2,1)S(1)} %constant_dynamic-update-slice_fusion.3.refs_1_), channel_id=1, source_target_pairs={{0,2},{1,3},{2,0},{3,1},{4,6},{5,7},{6,4},{7,5},{8,10},{9,11},{10,... | collective-permute-start | bytes 589832 | tf_op jit(solution)/shard_map/ppermute | solution.py:317
  12.5 0.8 %copy-done.2 = bf16[4,8,768]{2,1,0:T(8,128)(2,1)S(1)} copy-done((bf16[4,8,768]{2,1,0:T(8,128)(2,1)S(1)}, bf16[4,8,768]{2,1,0:T(8,128)(2,1)}, u32[]{:S(2)}) %copy-start.2) | copy-done | bytes 49176
  13.3 0.1 shard_map.113.refs_0_
  13.4 0.0 collective-permute-done.7
  13.4 0.8 %dynamic_update_slice.28 = bf16[4,32,768]{2,1,0:T(8,128)(2,1)S(1)} pad(bf16[4,8,768]{2,1,0:T(8,128)(2,1)} %param.13, bf16[]{:T(256)} %constant.3.clone.1), padding=0_0x0_24x0_0 | pad | bytes 245762 | tf_op jit(solution)/shard_map/dynamic_update_slice | solution.py:329
  14.3 2.5 %collective-permute-done.8 = bf16[4,8,768]{2,1,0:T(8,128)(2,1)S(1)} collective-permute-done((bf16[4,8,768]{2,1,0:T(8,128)(2,1)}, bf16[4,8,768]{2,1,0:T(8,128)(2,1)S(1)}, u32[]{:S(2)}, u32[]{:S(2)}) %collective-permute-start.8) | collective-permute-done | bytes 49184 | tf_op jit(solution)/shard_map/ppermute | solution.py:317
  16.8 0.0 collective-permute-done.3.refs_2_
  16.8 0.1 collective-permute-start.4
  16.9 0.5 %collective-permute-start.5 = (bf16[4,32,768]{2,1,0:T(8,128)(2,1)S(1)}, bf16[4,32,768]{2,1,0:T(8,128)(2,1)S(1)}, u32[]{:S(2)}, u32[]{:S(2)}) collective-permute-start(bf16[4,32,768]{2,1,0:T(8,128)(2,1)S(1)} %collective-permute-done.3.refs_2_), channel_id=1, source_target_pairs={{0,1},{1,0},{2,3},{3,2},{4,5},{5,4},{6,7},{7,6},{8,9},{9,8},{10,11... | collective-permute-start | bytes 589832 | tf_op jit(solution)/shard_map/ppermute | solution.py:317
  17.4 0.0 collective-permute-done.9
  17.4 1.6 %collective-permute-start.10 = (bf16[4,32,768]{2,1,0:T(8,128)(2,1)S(1)}, bf16[4,32,768]{2,1,0:T(8,128)(2,1)S(1)}, u32[]{:S(2)}, u32[]{:S(2)}) collective-permute-start(bf16[4,32,768]{2,1,0:T(8,128)(2,1)S(1)} %constant_dynamic-update-slice_fusion.refs_1_), channel_id=1, source_target_pairs={{0,2},{1,3},{2,0},{3,1},{4,6},{5,7},{6,4},{7,5},{8,10},{9,11},{10,... | collective-permute-start | bytes 589832 | tf_op jit(solution)/shard_map/ppermute | solution.py:317
  18.9 0.0 collective-permute-done.4.refs_3_
  19.0 0.0 collective-permute-done.5.refs_4_
  19.0 0.4 shard_map.114.refs_0_
  19.3 1.5 %collective-permute-start.6 = (f32[96,128]{1,0:T(8,128)S(1)}, f32[96,128]{1,0:T(8,128)S(1)}, u32[]{:S(2)}, u32[]{:S(2)}) collective-permute-start(f32[96,128]{1,0:T(8,128)S(1)} %shard_map.114.refs_0_), channel_id=1, source_target_pairs={{0,16},{16,0},{1,17},{17,1},{2,18},{18,2},{3,19},{19,3},{4,20},{20... | collective-permute-start | bytes 147464 | tf_op jit(solution)/shard_map/ppermute | solution.py:416
  20.8 0.1 pad_add_fusion.scalar_ref
  21.5 0.1 collective-permute-start.11
  21.6 0.0 copy-done.5
  21.6 0.8 %shard_map.115 = (f32[24,128]{1,0:T(8,128)S(1)}, bf16[128,128]{1,0:T(8,128)(2,1)S(1)}, f32[8,128]{1,0:T(8,128)S(1)}, f32[128,64]{1,0:T(8,128)S(1)}, bf16[768,128...) custom-call(s32[2]{0:T(128)S(1)} %pad_add_fusion.scalar_ref, f32[12]{0:T(128)S(1)} %copy-done.5, f32[1]{0:T(128)S(6)} %copy.18.offset_ref), custom_call_target="tpu_custom_call" | custom-call | flops 1000000 | bytes 1000000 | tf_op jit(solution)/shard_map/pallas_call | solution.py:289
  22.4 1.0 %collective-permute-done.6.refs_1_ = f32[96,128]{1,0:T(8,128)S(1)} collective-permute-done((f32[96,128]{1,0:T(8,128)S(1)}, f32[96,128]{1,0:T(8,128)S(1)}, u32[]{:S(2)}, u32[]{:S(2)}) %collective-permute-start.6) | collective-permute-done | bytes 49184 | tf_op jit(solution)/shard_map/ppermute | solution.py:416
  23.4 1.1 %shard_map.116 = (bf16[96,128]{1,0:T(8,128)(2,1)S(1)}, f32[16,24,128]{2,1,0:T(8,128)}) custom-call(f32[96,128]{1,0:T(8,128)S(1)} %shard_map.114.refs_0_, f32[96,128]{1,0:T(8,128)S(1)} %collective-permute-done.6.refs_1_, f32[24,128]{1,0:T(8,128)S(1)} %get-tuple-element.26.refs_2_.factor_ref, bf16[128,128]{1,0:T(8,128)(2,1)S(1)} %get-tuple-element.24.refs_3_), custom_call_target="tpu_custom_call" | custom-call | flops 1000000 | bytes 1000000 | tf_op jit(solution)/shard_map/pallas_call | solution.py:289
  24.5 0.0 collective-permute-done.10.refs_2_
  24.5 0.0 collective-permute-start.12
  24.5 5.6 %all-to-all-start = ((f32[16,24,128]{2,1,0:T(8,128)}), f32[16,24,128]{2,1,0:T(8,128)S(1)}, u32[]{:S(2)}, u32[]{:S(2)}) async-start(f32[16,24,128]{2,1,0:T(8,128)} %get-tuple-element.30), calls=%async_computation | async-start | bytes 393216 | tf_op jit(solution)/shard_map/all_to_all | solution.py:449
  30.1 0.0 collective-permute-done.11.refs_3_
  30.1 0.0 collective-permute-done.12.refs_4_
  30.2 0.6 %shard_map.117 = (f32[32,768]{1,0:T(8,128)S(1)}, bf16[32,768]{1,0:T(8,128)(2,1)S(1)}, bf16[1,1152]{1,0:T(2,128)(2,1)S(1)}) custom-call(bf16[96,128]{1,0:T(8,128)(2,1)S(1)} %get-tuple-element.27.refs_0_, bf16[4,32,768]{2,1,0:T(8,128)(2,1)S(1)} %constant_dynamic-update-slice_fusion.refs_1_, bf16[4,32,768]{2,1,0:T(8,128)(2,1)S(1)} %collective-permute-done.10.refs_2_, ...), custom_call_target="tpu_custom_call" | custom-call | flops 1000000 | bytes 1000000 | tf_op jit(solution)/shard_map/pallas_call | solution.py:289
  30.8 1.6 %collective-permute-start.13 = (bf16[32,768]{1,0:T(8,128)(2,1)S(1)}, bf16[32,768]{1,0:T(8,128)(2,1)S(1)}, u32[]{:S(2)}, u32[]{:S(2)}) collective-permute-start(bf16[32,768]{1,0:T(8,128)(2,1)S(1)} %get-tuple-element.32.refs_0_), channel_id=1, source_target_pairs={{0,16},{16,0},{1,17},{17,1},{2,18},{18,2},{3,19},{19,3},{4,20},{20... | collective-permute-start | bytes 147464 | tf_op jit(solution)/shard_map/ppermute | solution.py:457
  32.4 1.6 %broadcast_multiply_fusion.refs_2_ = bf16[768,1152]{1,0:T(8,128)(2,1)S(1)} fusion(bf16[768,1152]{1,0:T(8,128)(2,1)} %param.16, bf16[1152]{0:T(1024)(128)(2,1)S(1)} %reduce), kind=kLoop, calls=%fused_computation | loop fusion | flops 884736 | bytes 3541248 | tf_op jit(solution)/shard_map/mul | solution.py:458
  34.1 0.0 copy-start.1
  34.1 0.9 %collective-permute-done.13.refs_1_ = bf16[32,768]{1,0:T(8,128)(2,1)S(1)} collective-permute-done((bf16[32,768]{1,0:T(8,128)(2,1)S(1)}, bf16[32,768]{1,0:T(8,128)(2,1)S(1)}, u32[]{:S(2)}, u32[]{:S(2)}) %collective-permute-start.13) | collective-permute-done | bytes 49184 | tf_op jit(solution)/shard_map/ppermute | solution.py:457
  35.0 0.4 %shard_map.118.own_ref = bf16[64,1152]{1,0:T(8,128)(2,1)S(1)} custom-call(bf16[32,768]{1,0:T(8,128)(2,1)S(1)} %get-tuple-element.32.refs_0_, bf16[32,768]{1,0:T(8,128)(2,1)S(1)} %collective-permute-done.13.refs_1_, bf16[768,1152]{1,0:T(8,128)(2,1)S(1)} %broadcast_multiply_fusion.refs_2_), custom_call_target="tpu_custom_call" | custom-call | flops 1000000 | bytes 1000000 | tf_op jit(solution)/shard_map/pallas_call | solution.py:289
  35.4 1.6 %collective-permute-start.14 = (bf16[64,1152]{1,0:T(8,128)(2,1)S(1)}, bf16[64,1152]{1,0:T(8,128)(2,1)S(1)}, u32[]{:S(2)}, u32[]{:S(2)}) collective-permute-start(bf16[64,1152]{1,0:T(8,128)(2,1)S(1)} %shard_map.118.own_ref), channel_id=1, source_target_pairs={{0,16},{16,0},{1,17},{17,1},{2,18},{18,2},{3,19},{19,3},{4,20},{20... | collective-permute-start | bytes 442376 | tf_op jit(solution)/shard_map/ppermute | solution.py:470
  37.0 2.2 %all-to-all-done.pair_ref = f32[16,24,128]{2,1,0:T(8,128)S(1)} async-done(((f32[16,24,128]{2,1,0:T(8,128)}), f32[16,24,128]{2,1,0:T(8,128)S(1)}, u32[]{:S(2)}, u32[]{:S(2)}) %all-to-all-start) | async-done | bytes 196640 | tf_op jit(solution)/shard_map/all_to_all | solution.py:449
  39.1 1.0 %shard_map.120 = f32[8,64]{1,0:T(8,128)} custom-call(f32[16,24,128]{2,1,0:T(8,128)S(1)} %all-to-all-done.pair_ref, f32[24,128]{1,0:T(8,128)S(1)} %get-tuple-element.26.refs_2_.factor_ref, f32[8,128]{1,0:T(8,128)S(1)} %get-tuple-element.38.own_ref, f32[128,64]{1,0:T(8,128)S(1)} %get-tuple-element.39.slab_ref), custom_call_target="tpu_custom_call" | custom-call | flops 1000000 | bytes 1000000 | tf_op jit(solution)/shard_map/pallas_call | solution.py:289
  40.2 0.6 %collective-permute-done.14.other_ref = bf16[64,1152]{1,0:T(8,128)(2,1)S(1)} collective-permute-done((bf16[64,1152]{1,0:T(8,128)(2,1)S(1)}, bf16[64,1152]{1,0:T(8,128)(2,1)S(1)}, u32[]{:S(2)}, u32[]{:S(2)}) %collective-permute-start.14) | collective-permute-done | bytes 147488 | tf_op jit(solution)/shard_map/ppermute | solution.py:470
  40.8 1.5 %shard_map.119 = bf16[4,8,768]{2,1,0:T(8,128)(2,1)} custom-call(bf16[64,1152]{1,0:T(8,128)(2,1)S(1)} %shard_map.118.own_ref, bf16[64,1152]{1,0:T(8,128)(2,1)S(1)} %collective-permute-done.14.other_ref, f32[32,768]{1,0:T(8,128)S(1)} %get-tuple-element.34.refs_0_, bf16[768,768]{1,0:T(8,128)(2,1)S(1)} %copy-done.1, ...), custom_call_target="tpu_custom_call" | custom-call | flops 1000000 | bytes 1000000 | tf_op jit(solution)/shard_map/pallas_call | solution.py:289
  (15 shorter events, 0.1 us)
Async XLA Ops:
  0.6 29.5 %copy-start = (bf16[768,768]{1,0:T(8,128)(2,1)S(1)}, bf16[768,768]{1,0:T(8,128)(2,1)}, u32[]{:S(2)}) copy-start(bf16[768,768]{1,0:T(8,128)(2,1)} %refs_5_.1) | copy-start | bytes 3538948
  0.6 10.0 %collective-permute-start = (bf16[4,8,768]{2,1,0:T(8,128)(2,1)}, bf16[4,8,768]{2,1,0:T(8,128)(2,1)S(1)}, u32[]{:S(2)}, u32[]{:S(2)}) collective-permute-start(bf16[4,8,768]{2,1,0:T(8,128)(2,1)} %param.12), channel_id=1, source_target_pairs={{0,4},{1,5},{2,6},{3,7},{4,8},{5,9},{6,10},{7,11},{8,12},{9,13},{1... | collective-permute-start | bytes 147464 | tf_op jit(solution)/shard_map/ppermute | solution.py:317
  3.7 7.1 %collective-permute-start.2 = (bf16[4,8,768]{2,1,0:T(8,128)(2,1)}, bf16[4,8,768]{2,1,0:T(8,128)(2,1)S(1)}, u32[]{:S(2)}, u32[]{:S(2)}) collective-permute-start(bf16[4,8,768]{2,1,0:T(8,128)(2,1)} %param.12), channel_id=1, source_target_pairs={{0,8},{1,9},{2,10},{3,11},{4,12},{5,13},{6,14},{7,15},{8,0},{9,1},... | collective-permute-start | bytes 147464 | tf_op jit(solution)/shard_map/ppermute | solution.py:317
  6.3 4.5 %collective-permute-start.1 = (bf16[4,8,768]{2,1,0:T(8,128)(2,1)}, bf16[4,8,768]{2,1,0:T(8,128)(2,1)S(1)}, u32[]{:S(2)}, u32[]{:S(2)}) collective-permute-start(bf16[4,8,768]{2,1,0:T(8,128)(2,1)} %param.12), channel_id=1, source_target_pairs={{0,12},{1,13},{2,14},{3,15},{4,0},{5,1},{6,2},{7,3},{8,4},{9,5},{1... | collective-permute-start | bytes 147464 | tf_op jit(solution)/shard_map/ppermute | solution.py:317
  7.7 5.8 %collective-permute-start.7 = (bf16[4,8,768]{2,1,0:T(8,128)(2,1)}, bf16[4,8,768]{2,1,0:T(8,128)(2,1)S(1)}, u32[]{:S(2)}, u32[]{:S(2)}) collective-permute-start(bf16[4,8,768]{2,1,0:T(8,128)(2,1)} %param.13), channel_id=1, source_target_pairs={{0,12},{1,13},{2,14},{3,15},{4,0},{5,1},{6,2},{7,3},{8,4},{9,5},{1... | collective-permute-start | bytes 147464 | tf_op jit(solution)/shard_map/ppermute | solution.py:317
  8.1 9.3 %collective-permute-start.9 = (bf16[4,8,768]{2,1,0:T(8,128)(2,1)}, bf16[4,8,768]{2,1,0:T(8,128)(2,1)S(1)}, u32[]{:S(2)}, u32[]{:S(2)}) collective-permute-start(bf16[4,8,768]{2,1,0:T(8,128)(2,1)} %param.13), channel_id=1, source_target_pairs={{0,8},{1,9},{2,10},{3,11},{4,12},{5,13},{6,14},{7,15},{8,0},{9,1},... | collective-permute-start | bytes 147464 | tf_op jit(solution)/shard_map/ppermute | solution.py:317
  10.6 6.2 %collective-permute-start.8 = (bf16[4,8,768]{2,1,0:T(8,128)(2,1)}, bf16[4,8,768]{2,1,0:T(8,128)(2,1)S(1)}, u32[]{:S(2)}, u32[]{:S(2)}) collective-permute-start(bf16[4,8,768]{2,1,0:T(8,128)(2,1)} %param.13), channel_id=1, source_target_pairs={{0,4},{1,5},{2,6},{3,7},{4,8},{5,9},{6,10},{7,11},{8,12},{9,13},{1... | collective-permute-start | bytes 147464 | tf_op jit(solution)/shard_map/ppermute | solution.py:317
  10.8 6.0 %collective-permute-start.3 = (bf16[4,32,768]{2,1,0:T(8,128)(2,1)S(1)}, bf16[4,32,768]{2,1,0:T(8,128)(2,1)S(1)}, u32[]{:S(2)}, u32[]{:S(2)}) collective-permute-start(bf16[4,32,768]{2,1,0:T(8,128)(2,1)S(1)} %constant_dynamic-update-slice_fusion.3.refs_1_), channel_id=1, source_target_pairs={{0,2},{1,3},{2,0},{3,1},{4,6},{5,7},{6,4},{7,5},{8,10},{9,11},{10,... | collective-permute-start | bytes 589832 | tf_op jit(solution)/shard_map/ppermute | solution.py:317
  12.5 0.8 %copy-start.2 = (bf16[4,8,768]{2,1,0:T(8,128)(2,1)S(1)}, bf16[4,8,768]{2,1,0:T(8,128)(2,1)}, u32[]{:S(2)}) copy-start(bf16[4,8,768]{2,1,0:T(8,128)(2,1)} %q_hbm) | copy-start | bytes 147460
  13.3 8.3 %copy-start.5 = (f32[12]{0:T(128)S(1)}, f32[12]{0:T(128)}, u32[]{:S(2)}) copy-start(f32[12]{0:T(128)} %factor_ref.1) | copy-start | bytes 148
  13.3 16.8 %copy-start.3 = (bf16[4,8,768]{2,1,0:T(8,128)(2,1)S(1)}, bf16[4,8,768]{2,1,0:T(8,128)(2,1)}, u32[]{:S(2)}) copy-start(bf16[4,8,768]{2,1,0:T(8,128)(2,1)} %refs_6_.1) | copy-start | bytes 147460
  13.3 16.8 %copy-start.4 = (f32[768]{0:T(1024)S(1)}, f32[768]{0:T(1024)}, u32[]{:S(2)}) copy-start(f32[768]{0:T(1024)} %refs_7_.1) | copy-start | bytes 9220
  16.8 2.2 %collective-permute-start.4 = (bf16[4,32,768]{2,1,0:T(8,128)(2,1)S(1)}, bf16[4,32,768]{2,1,0:T(8,128)(2,1)S(1)}, u32[]{:S(2)}, u32[]{:S(2)}) collective-permute-start(bf16[4,32,768]{2,1,0:T(8,128)(2,1)S(1)} %constant_dynamic-update-slice_fusion.3.refs_1_), channel_id=1, source_target_pairs={{0,1},{1,0},{2,3},{3,2},{4,5},{5,4},{6,7},{7,6},{8,9},{9,8},{10,11... | collective-permute-start | bytes 589832 | tf_op jit(solution)/shard_map/ppermute | solution.py:317
  16.9 2.1 %collective-permute-start.5 = (bf16[4,32,768]{2,1,0:T(8,128)(2,1)S(1)}, bf16[4,32,768]{2,1,0:T(8,128)(2,1)S(1)}, u32[]{:S(2)}, u32[]{:S(2)}) collective-permute-start(bf16[4,32,768]{2,1,0:T(8,128)(2,1)S(1)} %collective-permute-done.3.refs_2_), channel_id=1, source_target_pairs={{0,1},{1,0},{2,3},{3,2},{4,5},{5,4},{6,7},{7,6},{8,9},{9,8},{10,11... | collective-permute-start | bytes 589832 | tf_op jit(solution)/shard_map/ppermute | solution.py:317
  17.4 7.1 %collective-permute-start.10 = (bf16[4,32,768]{2,1,0:T(8,128)(2,1)S(1)}, bf16[4,32,768]{2,1,0:T(8,128)(2,1)S(1)}, u32[]{:S(2)}, u32[]{:S(2)}) collective-permute-start(bf16[4,32,768]{2,1,0:T(8,128)(2,1)S(1)} %constant_dynamic-update-slice_fusion.refs_1_), channel_id=1, source_target_pairs={{0,2},{1,3},{2,0},{3,1},{4,6},{5,7},{6,4},{7,5},{8,10},{9,11},{10,... | collective-permute-start | bytes 589832 | tf_op jit(solution)/shard_map/ppermute | solution.py:317
  19.3 4.1 %collective-permute-start.6 = (f32[96,128]{1,0:T(8,128)S(1)}, f32[96,128]{1,0:T(8,128)S(1)}, u32[]{:S(2)}, u32[]{:S(2)}) collective-permute-start(f32[96,128]{1,0:T(8,128)S(1)} %shard_map.114.refs_0_), channel_id=1, source_target_pairs={{0,16},{16,0},{1,17},{17,1},{2,18},{18,2},{3,19},{19,3},{4,20},{20... | collective-permute-start | bytes 147464 | tf_op jit(solution)/shard_map/ppermute | solution.py:416
  21.5 8.6 %collective-permute-start.11 = (bf16[4,32,768]{2,1,0:T(8,128)(2,1)S(1)}, bf16[4,32,768]{2,1,0:T(8,128)(2,1)S(1)}, u32[]{:S(2)}, u32[]{:S(2)}) collective-permute-start(bf16[4,32,768]{2,1,0:T(8,128)(2,1)S(1)} %constant_dynamic-update-slice_fusion.refs_1_), channel_id=1, source_target_pairs={{0,1},{1,0},{2,3},{3,2},{4,5},{5,4},{6,7},{7,6},{8,9},{9,8},{10,11... | collective-permute-start | bytes 589832 | tf_op jit(solution)/shard_map/ppermute | solution.py:317
  24.5 5.6 %collective-permute-start.12 = (bf16[4,32,768]{2,1,0:T(8,128)(2,1)S(1)}, bf16[4,32,768]{2,1,0:T(8,128)(2,1)S(1)}, u32[]{:S(2)}, u32[]{:S(2)}) collective-permute-start(bf16[4,32,768]{2,1,0:T(8,128)(2,1)S(1)} %collective-permute-done.10.refs_2_), channel_id=1, source_target_pairs={{0,1},{1,0},{2,3},{3,2},{4,5},{5,4},{6,7},{7,6},{8,9},{9,8},{10,11... | collective-permute-start | bytes 589832 | tf_op jit(solution)/shard_map/ppermute | solution.py:317
  24.5 14.6 %all-to-all-start = ((f32[16,24,128]{2,1,0:T(8,128)}), f32[16,24,128]{2,1,0:T(8,128)S(1)}, u32[]{:S(2)}, u32[]{:S(2)}) async-start(f32[16,24,128]{2,1,0:T(8,128)} %get-tuple-element.30), calls=%async_computation | async-start | bytes 393216 | tf_op jit(solution)/shard_map/all_to_all | solution.py:449
  30.8 4.2 %collective-permute-start.13 = (bf16[32,768]{1,0:T(8,128)(2,1)S(1)}, bf16[32,768]{1,0:T(8,128)(2,1)S(1)}, u32[]{:S(2)}, u32[]{:S(2)}) collective-permute-start(bf16[32,768]{1,0:T(8,128)(2,1)S(1)} %get-tuple-element.32.refs_0_), channel_id=1, source_target_pairs={{0,16},{16,0},{1,17},{17,1},{2,18},{18,2},{3,19},{19,3},{4,20},{20... | collective-permute-start | bytes 147464 | tf_op jit(solution)/shard_map/ppermute | solution.py:457
  34.1 6.8 %copy-start.1 = (bf16[768,768]{1,0:T(8,128)(2,1)S(1)}, bf16[768,768]{1,0:T(8,128)(2,1)}, u32[]{:S(2)}) copy-start(bf16[768,768]{1,0:T(8,128)(2,1)} %refs_1_) | copy-start | bytes 3538948
  35.4 5.4 %collective-permute-start.14 = (bf16[64,1152]{1,0:T(8,128)(2,1)S(1)}, bf16[64,1152]{1,0:T(8,128)(2,1)S(1)}, u32[]{:S(2)}, u32[]{:S(2)}) collective-permute-start(bf16[64,1152]{1,0:T(8,128)(2,1)S(1)} %shard_map.118.own_ref), channel_id=1, source_target_pairs={{0,16},{16,0},{1,17},{17,1},{2,18},{18,2},{3,19},{19,3},{4,20},{20... | collective-permute-start | bytes 442376 | tf_op jit(solution)/shard_map/ppermute | solution.py:470
